TPU v7x, 32 devices: a whole 2x2x4 slice. The times are simulated.
32 devices in a mesh: dp: 8 (over z, core), shard: 4 (over y, x).
Axes of the slice: x: 2, y: 2, z: 4, core: 2. Of those that a mesh axis runs over, the one named last changes fastest.
Arguments:
- tokens: bfloat16 [32768, 1024], P(('dp', 'shard')), may hold values from -6 to 6
- cotangent: bfloat16 [32768, 1024], P(('dp', 'shard')), may hold values from -6 to 6
- lengths: int32 [32, 4], P(('dp', 'shard')), may hold values from 0 to 1024, as said below
- attn_w: float32 [1024, 4096], P('shard')
- attn_m: float32 [1024, 4096], P('shard')
- attn_v: float32 [1024, 4096], P('shard'), as said below
- mlp_w: float32 [1024, 8192], P('shard'), may hold values from -0.1875 to 0.1875
- mlp_m: float32 [1024, 8192], P('shard')
- mlp_v: float32 [1024, 8192], P('shard'), as said below
- small: float32 [12288], P('shard')
- small_m: float32 [12288], P('shard')
- small_v: float32 [12288], P('shard'), as said below
Outputs:
- output: bfloat16 [32768, 1024], P(('dp', 'shard'))
- grad_input: float32 [32768, 1024], P(('dp', 'shard'))
- attn_w_new: float32 [1024, 4096], P('shard')
- attn_m_new: float32 [1024, 4096], P('shard')
- attn_v_new: float32 [1024, 4096], P('shard')
- mlp_w_new: float32 [1024, 8192], P('shard')
- mlp_m_new: float32 [1024, 8192], P('shard')
- mlp_v_new: float32 [1024, 8192], P('shard')
- small_new: float32 [12288], P('shard')
- small_m_new: float32 [12288], P('shard')
- small_v_new: float32 [12288], P('shard')
Inputs may be any that keep to these rules, and one draw needn't show every extreme that they name: Row b lists the document lengths of block b; zero entries are empty slots; a row sums to 512 or more and to 1024 at most; in every draw some row holds a single document of 1024. `attn_v`: Positive. `mlp_v`: Positive. `small_v`: Positive.
All inputs are finite; a program needn't handle non-finite values.
Results may differ from a plain program's by a relative error of at most 0.012.
The roundings to bfloat16 on the way count: a program that leaves them out, or rounds other values in their place, can miss the bound.
Values may be sent and summed in bfloat16 or wider, within the bound.
No kernel may reach another device: no remote copies, remote signals or barrier semaphores. Data moves between devices by JAX's collectives and lax.ppermute only.
A program may use at most 384 MiB of HBM per device.

v0:
```python
import jax
import jax.numpy as jnp
from jax import lax
from jax.sharding import PartitionSpec as P

HD = 64
QB = 512
STEP = 10


beta_one = 0.9
beta_two = 0.95
adam_eps = 1e-08
norm_eps = 1e-05


def layer_norm(values, gain, shift):
    center = values - jnp.mean(values, axis=-1, keepdims=True)
    spread = jnp.mean(center * center, axis=-1, keepdims=True)
    return center * lax.rsqrt(spread + norm_eps) * gain + shift


def gelu_tanh(values):
    return jax.nn.gelu(values, approximate=True)


def rows_product(left, right):
    return lax.dot_general(
        left, right, (((0,), (0,)), ((), ())), preferred_element_type=jnp.float32
    )


def cols_product(left, right):
    return lax.dot_general(
        left, right, (((1,), (1,)), ((), ())), preferred_element_type=jnp.float32
    )


def block_allowed(seg, start, count, keys):
    query_pos = start + jnp.arange(count, dtype=jnp.int32)
    key_pos = jnp.arange(keys, dtype=jnp.int32)
    same = seg[start : start + count][:, None] == seg[:keys][None, :]
    return (query_pos[:, None] >= key_pos[None, :]) & same


def attend_forward(query, keys, values, seg, heads):
    rows = query.shape[0]
    span = min(QB, rows)
    scale = HD ** (-0.5)
    qh = query.reshape(rows, heads, HD)
    kh = keys.reshape(rows, heads, HD)
    vh = values.reshape(rows, heads, HD)
    outs = []
    sums = []
    for start in range(0, rows, span):
        end = start + span
        scores = (
            jnp.einsum("qhd,khd->hqk", qh[start:end], kh[:end], preferred_element_type=jnp.float32)
            * scale
        )
        allowed = block_allowed(seg, start, span, end)
        scores = jnp.where(allowed[None], scores, -1e30)
        top = jnp.max(scores, axis=-1, keepdims=True)
        expo = jnp.exp(scores - top)
        total = jnp.sum(expo, axis=-1, keepdims=True)
        probs = (expo / total).astype(jnp.bfloat16)
        mixed = jnp.einsum("hqk,khd->qhd", probs, vh[:end], preferred_element_type=jnp.float32)
        outs.append(mixed.reshape(span, heads * HD))
        sums.append(top + jnp.log(total))
    return (jnp.concatenate(outs, axis=0), sums)


def attend_backward(query, keys, values, seg, sums, grad_mixed, heads):
    rows = query.shape[0]
    span = min(QB, rows)
    scale = HD ** (-0.5)
    qh = query.reshape(rows, heads, HD)
    kh = keys.reshape(rows, heads, HD)
    vh = values.reshape(rows, heads, HD)
    gh = grad_mixed.reshape(rows, heads, HD)
    grad_keys = jnp.zeros((rows, heads, HD), jnp.float32)
    grad_vals = jnp.zeros((rows, heads, HD), jnp.float32)
    grad_queries = []
    for number, start in enumerate(range(0, rows, span)):
        end = start + span
        scores = (
            jnp.einsum("qhd,khd->hqk", qh[start:end], kh[:end], preferred_element_type=jnp.float32)
            * scale
        )
        allowed = block_allowed(seg, start, span, end)
        scores = jnp.where(allowed[None], scores, -1e30)
        probs = jnp.exp(scores - sums[number])
        probs_low = probs.astype(jnp.bfloat16)
        grad_probs = jnp.einsum(
            "qhd,khd->hqk", gh[start:end], vh[:end], preferred_element_type=jnp.float32
        )
        grad_vals = grad_vals.at[:end].add(
            jnp.einsum("hqk,qhd->khd", probs_low, gh[start:end], preferred_element_type=jnp.float32)
        )
        inner = jnp.sum(probs * grad_probs, axis=-1, keepdims=True)
        grad_scores = (probs * (grad_probs - inner)).astype(jnp.bfloat16)
        grad_queries.append(
            jnp.einsum("hqk,khd->qhd", grad_scores, kh[:end], preferred_element_type=jnp.float32)
            * scale
        )
        grad_keys = grad_keys.at[:end].add(
            jnp.einsum(
                "hqk,qhd->khd", grad_scores, qh[start:end], preferred_element_type=jnp.float32
            )
            * scale
        )
    width = heads * HD
    grad_q = jnp.concatenate(grad_queries, axis=0).reshape(rows, width)
    return (grad_q, grad_keys.reshape(rows, width), grad_vals.reshape(rows, width))


def adamw(weight, first, second, grad, rate, decay):
    first_new = beta_one * first + (1.0 - beta_one) * grad
    second_new = beta_two * second + (1.0 - beta_two) * grad * grad
    first_hat = first_new / (1.0 - beta_one**STEP)
    second_hat = second_new / (1.0 - beta_two**STEP)
    weight_new = weight - rate * (first_hat / (jnp.sqrt(second_hat) + adam_eps) + decay * weight)
    return (weight_new, first_new, second_new)


def settle(grads, states, rates, decays):
    owned = (
        lax.psum_scatter(grads[0], "shard", scatter_dimension=0, tiled=True),
        lax.psum_scatter(grads[1], "shard", scatter_dimension=0, tiled=True),
        lax.psum_scatter(grads[2], "shard", scatter_dimension=0, tiled=True),
    )
    summed = lax.psum((owned[0], owned[1], owned[2]), "dp")
    return tuple(
        (
            adamw(state[0], state[1], state[2], grad, rate, decay)
            for grad, state, rate, decay in zip(summed, states, rates, decays)
        )
    )


def body(
    tokens, cotangent, lengths, attn_w, attn_m, attn_v, mlp_w, mlp_m, mlp_v, small, small_m, small_v
):
    full_attn, full_mlp, full_small = (
        lax.all_gather(attn_w.astype(jnp.bfloat16), "shard", axis=0, tiled=True),
        lax.all_gather(mlp_w.astype(jnp.bfloat16), "shard", axis=0, tiled=True),
        lax.all_gather(small.astype(jnp.bfloat16), "shard", axis=0, tiled=True),
    )
    rows = tokens.shape[0]
    width = tokens.shape[1]
    hidden = full_mlp.shape[1] // 2
    heads = width // HD
    params = full_small.astype(jnp.float32)
    bias_q = params[0:width]
    bias_v = params[width : 2 * width]
    bias_o = params[2 * width : 3 * width]
    bias_up = params[3 * width : 3 * width + hidden]
    bias_dn = params[3 * width + hidden : 4 * width + hidden]
    gain_one = params[4 * width + hidden : 5 * width + hidden]
    shift_one = params[5 * width + hidden : 6 * width + hidden]
    gain_two = params[6 * width + hidden : 7 * width + hidden]
    shift_two = params[7 * width + hidden : 8 * width + hidden]
    w_qkv = full_attn[:, : 3 * width]
    w_out = full_attn[:, 3 * width :]
    w_up = full_mlp[:, :hidden]
    w_down = full_mlp[:, hidden:]
    ends = jnp.cumsum(lengths[0], dtype=jnp.int32)
    places = jnp.arange(rows, dtype=jnp.int32)
    seg = jnp.sum((places[:, None] >= ends[None, :]).astype(jnp.int32), axis=1)
    live = (places < ends[-1]).astype(jnp.float32)
    start = tokens.astype(jnp.float32)
    hidden_one = layer_norm(start, gain_one, shift_one).astype(jnp.bfloat16)
    joint = jnp.dot(hidden_one, w_qkv, preferred_element_type=jnp.float32)
    query = (joint[:, :width] + bias_q).astype(jnp.bfloat16)
    keys = joint[:, width : 2 * width].astype(jnp.bfloat16)
    vals = (joint[:, 2 * width :] + bias_v).astype(jnp.bfloat16)
    mixed_f, sums = attend_forward(query, keys, vals, seg, heads)
    mixed = mixed_f.astype(jnp.bfloat16)
    after = start + jnp.dot(mixed, w_out, preferred_element_type=jnp.float32) + bias_o
    hidden_two = layer_norm(after, gain_two, shift_two).astype(jnp.bfloat16)
    upper = jnp.dot(hidden_two, w_up, preferred_element_type=jnp.float32) + bias_up
    active = gelu_tanh(upper).astype(jnp.bfloat16)
    output = (after + cols_product(active, w_down) + bias_dn).astype(jnp.bfloat16)
    grad_out = cotangent.astype(jnp.float32) * live[:, None]
    grad_low = grad_out.astype(jnp.bfloat16)
    grad_bias_dn = jnp.sum(grad_out, axis=0)
    grad_w_down = rows_product(grad_low, active)
    grad_active = jnp.dot(grad_low, w_down, preferred_element_type=jnp.float32)
    gelu_value, gelu_pull = jax.vjp(gelu_tanh, upper)
    grad_upper = gelu_pull(grad_active)[0].astype(jnp.bfloat16)
    grad_bias_up = jnp.sum(grad_upper.astype(jnp.float32), axis=0)
    grad_w_up = rows_product(hidden_two, grad_upper)
    grad_hidden_two = cols_product(grad_upper, w_up)
    norm_value, norm_pull = jax.vjp(layer_norm, after, gain_two, shift_two)
    grad_after_norm, grad_gain_two, grad_shift_two = norm_pull(grad_hidden_two)
    grad_after = grad_out + grad_after_norm
    grad_mlp = jnp.concatenate([grad_w_up, grad_w_down], axis=1)
    mlp_state = (mlp_w, mlp_m, mlp_v)
    grad_branch = grad_after.astype(jnp.bfloat16)
    grad_bias_o = jnp.sum(grad_branch.astype(jnp.float32), axis=0)
    grad_w_out = rows_product(mixed, grad_branch)
    grad_mixed = cols_product(grad_branch, w_out).astype(jnp.bfloat16)
    grad_q, grad_k, grad_v = attend_backward(query, keys, vals, seg, sums, grad_mixed, heads)
    grad_joint = jnp.concatenate(
        [grad_q.astype(jnp.bfloat16), grad_k.astype(jnp.bfloat16), grad_v.astype(jnp.bfloat16)],
        axis=1,
    )
    grad_bias_q = jnp.sum(grad_joint[:, :width].astype(jnp.float32), axis=0)
    grad_bias_v = jnp.sum(grad_joint[:, 2 * width :].astype(jnp.float32), axis=0)
    grad_w_qkv = rows_product(hidden_one, grad_joint)
    grad_hidden_one = cols_product(grad_joint, w_qkv)
    first_value, first_pull = jax.vjp(layer_norm, start, gain_one, shift_one)
    grad_start_norm, grad_gain_one, grad_shift_one = first_pull(grad_hidden_one)
    grad_input = grad_after + grad_start_norm
    grad_attn = jnp.concatenate([grad_w_qkv, grad_w_out], axis=1)
    grad_small = jnp.concatenate(
        [
            grad_bias_q,
            grad_bias_v,
            grad_bias_o,
            grad_bias_up,
            grad_bias_dn,
            grad_gain_one,
            grad_shift_one,
            grad_gain_two,
            grad_shift_two,
        ],
        axis=0,
    )
    attn_state = (attn_w, attn_m, attn_v)
    small_state = (small, small_m, small_v)
    attn_result, mlp_result, small_result = settle(
        (grad_attn, grad_mlp, grad_small),
        (attn_state, mlp_state, small_state),
        (0.05, 0.05, 0.4),
        (0.1, 0.1, 0.0),
    )
    return (
        output,
        grad_input,
        attn_result[0],
        attn_result[1],
        attn_result[2],
        mlp_result[0],
        mlp_result[1],
        mlp_result[2],
        small_result[0],
        small_result[1],
        small_result[2],
    )


def solution(mesh):
    placed = (
        P(("dp", "shard"), None),
        P(("dp", "shard"), None),
        P(("dp", "shard"), None),
        P("shard", None),
        P("shard", None),
        P("shard", None),
        P("shard", None),
        P("shard", None),
        P("shard", None),
        P("shard"),
        P("shard"),
        P("shard"),
    )
    return jax.shard_map(
        body,
        mesh=mesh,
        in_specs=placed,
        out_specs=(
            P(("dp", "shard"), None),
            P(("dp", "shard"), None),
            P("shard", None),
            P("shard", None),
            P("shard", None),
            P("shard", None),
            P("shard", None),
            P("shard", None),
            P("shard"),
            P("shard"),
            P("shard"),
        ),
        check_vma=False,
    )
```

profile of v0, /device:TPU:0, one launch (start us, length us, event | category | flops | bytes accessed | tf_op | source)
XLA Modules:
  0.0 1233.7 jit_solution(8972866082699710707)
XLA Ops:
  40.8 60.8 %all-gather.3.cloned.1.call-done = bf16[1024,4096]{1,0:T(8,128)(2,1)} async-done(((bf16[256,4096]{1,0:T(8,128)(2,1)}), bf16[1024,4096]{1,0:T(8,128)(2,1)}) %all-gather.3.cloned.1.call-update) | async-done | bytes 8388624 | tf_op jit(solution)/shard_map/all_gather | solution.py:145
  159.1 18.0 %fusion.94 = (f32[16,512]{1,0:T(8,128)S(1)}, f32[16,512,1024]{2,1,0:T(8,128)}) fusion(bf16[512,16,64]{0,2,1:T(8,128)(2,1)S(1)} %bitcast.65, bf16[1024,16,64]{0,2,1:T(8,128)(2,1)} %bitcast.63, pred[512,1024]{1,0:T(8,128)(4,1)S(1)} %copy-done.22), kind=kOutput, calls=%fused_computation.155 | convolution fusion | flops 1098899456 | bytes 37257216 | tf_op jit(solution)/shard_map/qhd,khd->hqk/dot_general | solution.py:58
  177.1 14.4 %fusion = f32[16,512]{1,0:T(8,128)S(1)} fusion(f32[16,512,1024]{2,1,0:T(8,128)} %get-tuple-element.161, f32[16,512]{1,0:T(8,128)S(1)} %get-tuple-element.160), kind=kLoop, calls=%fused_computation.7 | loop fusion | flops 16769024 | bytes 33619968 | tf_op jit(solution)/shard_map/reduce_sum | solution.py:65
  199.2 13.1 %fusion.69 = bf16[16,64,512]{2,1,0:T(8,128)(2,1)S(1)} fusion(bf16[1024,16,64]{0,2,1:T(8,128)(2,1)S(1)} %bitcast.69, f32[16,512,1024]{2,1,0:T(8,128)} %get-tuple-element.161, f32[16,512]{1,0:T(8,128)S(1)} %fusion, f32[16,512]{1,0:T(8,128)S(1)} %get-tuple-element.160), kind=kOutput, calls=%fused_computation.109 | convolution fusion | flops 1099431936 | bytes 36765696 | tf_op jit(solution)/shard_map/hqk,khd->qhd/dot_general | solution.py:67
  220.7 40.7 %all-gather.5.cloned.1.call-done = bf16[1024,8192]{1,0:T(8,128)(2,1)} async-done(((bf16[256,8192]{1,0:T(8,128)(2,1)}), bf16[1024,8192]{1,0:T(8,128)(2,1)}) %all-gather.5.cloned.1.call-update) | async-done | bytes 16777232 | tf_op jit(solution)/shard_map/all_gather | solution.py:146
  261.5 17.0 %fusion.26 = f32[1024,4096]{1,0:T(8,128)} fusion(bf16[1024,8192]{1,0:T(8,128)(2,1)} %all-gather.5.cloned.1.call-done, f32[1024,1024]{0,1:T(8,128)} %copy-done.3, f32[1024]{0:T(1024)S(1)} %get-tuple-element.149, f32[1024]{0:T(1024)S(1)} %get-tuple-element.148, f32[1024]{0:T(1024)S(1)} %fusion.76, f32[1024]{0:T(1024)S(1)} %broadcast_multiply_fusion), kind=kOutput, calls=%fused_computation.45 | convolution fusion | flops 8595177472 | bytes 29376512 | tf_op jit(solution)/shard_map/dot_general | solution.py:181
  278.5 26.7 %convert_reduce_fusion = (f32[4096]{0:T(1024)}, bf16[1024,4096]{1,0:T(8,128)(2,1)}) fusion(f32[1024,4096]{1,0:T(8,128)} %fusion.26, f32[4096]{0:T(1024)S(1)} %copy-done.52, bf16[1024,8192]{1,0:T(8,128)(2,1)} %all-gather.5.cloned.1.call-done, bf16[1024,1024]{0,1:T(8,128)(2,1)S(1)} %copy-done.11, f32[1024]{0:T(1024)S(1)} %copy-done.43), kind=kOutput, calls=%fused_computation.20 | convolution fusion | flops 8689545216 | bytes 35688448 | tf_op jit(solution)/shard_map/dot_general | solution.py:188
  305.2 15.6 %fusion.98 = (f32[1024]{0:T(1024)}, f32[1024,1024]{1,0:T(8,128)}) fusion(bf16[1024,4096]{1,0:T(8,128)(2,1)} %get-tuple-element.173, bf16[1024,8192]{1,0:T(8,128)(2,1)} %all-gather.5.cloned.1.call-done), kind=kOutput, calls=%fused_computation.159 | convolution fusion | flops 8590982144 | bytes 20975616 | tf_op jit(solution)/shard_map/dot_general | solution.py:34
  374.7 22.4 %multiply_reduce_fusion = (f32[16,512]{1,0:T(8,128)S(1)}, f32[16,512,1024]{2,1,0:T(8,128)}) fusion(f32[16,512,1024]{2,1,0:T(8,128)} %get-tuple-element.161, f32[16,512]{1,0:T(8,128)S(1)} %copy-done.28, bf16[512,16,64]{0,2,1:T(8,128)(2,1)S(1)} %bitcast.71, bf16[1024,16,64]{0,2,1:T(8,128)(2,1)S(1)} %bitcast.70), kind=kOutput, calls=%fused_computation.2 | convolution fusion | flops 1098899456 | bytes 70320128 | tf_op jit(solution)/shard_map/qhd,khd->hqk/dot_general | solution.py:94
  397.1 15.3 %convert_reduce_fusion.3 = (f32[16,64]{1,0:T(8,128)}, bf16[1024,16,64]{0,2,1:T(8,128)(2,1)}) fusion(bf16[512,16,64]{0,2,1:T(8,128)(2,1)S(1)} %bitcast.72, f32[16,512,1024]{2,1,0:T(8,128)} %get-tuple-element.161, f32[16,512]{1,0:T(8,128)S(1)} %copy-done.28, f32[512,16,64]{0,2,1:T(8,128)S(1)} %copy-done.19), kind=kOutput, calls=%fused_computation.82 | convolution fusion | flops 1094712320 | bytes 38834176 | tf_op jit(solution)/shard_map/hqk,qhd->khd/dot_general | solution.py:98
  412.4 28.3 %multiply_convert_fusion = bf16[16,512,1024]{2,1,0:T(8,128)(2,1)} fusion(f32[16,512,1024]{2,1,0:T(8,128)} %get-tuple-element.169, f32[16,512,1024]{2,1,0:T(8,128)} %get-tuple-element.161, f32[16,512]{1,0:T(8,128)S(1)} %get-tuple-element.168, f32[16,512]{1,0:T(8,128)S(1)} %copy-done.28), kind=kLoop, calls=%fused_computation.1 | loop fusion | flops 33554432 | bytes 83951616 | tf_op jit(solution)/shard_map/convert_element_type | solution.py:101
  440.7 12.0 multiply_bitcast_fusion.1
  466.1 13.1 %fusion.53 = f32[1024,3072]{1,0:T(8,128)} fusion(bf16[1024,1024]{0,1:T(8,128)(2,1)S(1)} %bitcast.82, bf16[1024,1024]{0,1:T(8,128)(2,1)S(1)} %bitcast.79, bf16[1024,1024]{0,1:T(8,128)(2,1)} %bitcast.83, bf16[1024,1024]{0,1:T(8,128)(2,1)S(1)} %copy-done.1, f32[1024]{0:T(1024)S(1)} %copy-done.61, f32[1024]{0:T(1024)S(1)} %copy-done.34, ...), kind=kOutput, calls=%fused_computation.95 | convolution fusion | flops 6467616768 | bytes 20987904 | tf_op jit(solution)/shard_map/dot_general | solution.py:28
  490.5 16.9 %fusion.83 = f32[1024,4096]{1,0:T(8,128)} fusion(bf16[1024,4096]{1,0:T(8,128)(2,1)} %get-tuple-element.173, f32[1024,1024]{0,1:T(8,128)} %copy-done.3, f32[1024]{0:T(1024)S(1)} %copy-done.59, f32[1024]{0:T(1024)S(1)} %copy-done.38, f32[1024]{0:T(1024)S(1)} %copy-done.40, f32[1024]{0:T(1024)S(1)} %copy-done.32), kind=kOutput, calls=%fused_computation.148 | convolution fusion | flops 8595177472 | bytes 29376512 | tf_op jit(solution)/shard_map/dot_general | solution.py:28
  507.4 16.3 %fusion.62 = f32[1024,4096]{1,0:T(8,128)} fusion(bf16[1024,1024]{0,1:T(8,128)(2,1)S(1)} %copy-done.12, f32[1024]{0:T(1024)S(1)} %copy-done.44, f32[1024,4096]{1,0:T(8,128)} %fusion.26, f32[4096]{0:T(1024)S(1)} %copy-done.53), kind=kOutput, calls=%fused_computation.106 | convolution fusion | flops 8635023360 | bytes 35672064 | tf_op jit(solution)/shard_map/dot_general | solution.py:28
  523.6 23.6 %pad_maximum_fusion = f32[1024,8192]{1,0:T(8,128)} fusion(f32[1024,4096]{1,0:T(8,128)} %fusion.62, f32[1024,4096]{1,0:T(8,128)} %fusion.83), kind=kLoop, calls=%fused_computation | loop fusion | flops 8388608 | bytes 67108864 | tf_op jit(solution)/shard_map/concatenate | solution.py:197
  549.1 94.6 %reduce-scatter.3.cloned.1.call-done = f32[256,4096]{1,0:T(8,128)} async-done(((f32[1024,4096]{1,0:T(8,128)}), f32[256,4096]{1,0:T(8,128)}) %reduce-scatter.3.cloned.1.call-update) | async-done | bytes 4194320 | tf_op jit(solution)/shard_map/reduce_scatter | solution.py:128
  643.8 291.6 %reduce-scatter.5.cloned.1.call-done = f32[256,8192]{1,0:T(8,128)} async-done(((f32[1024,8192]{1,0:T(8,128)}), f32[256,8192]{1,0:T(8,128)}) %reduce-scatter.5.cloned.1.call-update) | async-done | bytes 8388624 | tf_op jit(solution)/shard_map/reduce_scatter | solution.py:129
  936.1 16.9 %add_convert_fusion = bf16[1024,1024]{0,1:T(8,128)(2,1)} fusion(f32[1024,1024]{0,1:T(8,128)} %copy-done.3, bf16[1024,8192]{1,0:T(8,128)(2,1)} %all-gather.5.cloned.1.call-done, f32[1024]{0:T(1024)S(1)} %copy-done.57, f32[1024,4096]{1,0:T(8,128)} %fusion.26, f32[4096]{0:T(1024)S(1)} %copy-done.53), kind=kOutput, calls=%fused_computation.92 | convolution fusion | flops 8635023360 | bytes 31477760 | tf_op jit(solution)/shard_map/dot_general | solution.py:34
  957.1 12.2 fusion.97
  990.3 15.8 %all-reduce.2 = f32[12288]{0:T(1024)S(1)} all-reduce(f32[12288]{0:T(1024)S(1)} %constant_dynamic-update-slice_fusion), channel_id=4, replica_groups=mesh['dp'=8,'shard'=4] {'shard'}, use_global_device_ids=true, to_apply=%region_29.30.clone | all-reduce | flops 12288 | bytes 98304
  1006.0 27.9 %psum.23 = f32[3072]{0:T(1024)S(1)} all-reduce(f32[3072]{0:T(1024)S(1)} %dynamic-slice.26), channel_id=1, replica_groups=mesh['dp'=8,'shard'=4] {'dp'}, use_global_device_ids=true, to_apply=%region_30.31 | all-reduce | flops 3072 | bytes 24576 | tf_op jit(solution)/shard_map/psum | solution.py:132
  1034.6 158.8 %all-reduce.6.cloned.1.call-done = (f32[256,4096]{1,0:T(8,128)}, f32[256,8192]{1,0:T(8,128)}) async-done(((f32[256,4096]{1,0:T(8,128)}, f32[256,8192]{1,0:T(8,128)}), (f32[256,4096]{1,0:T(8,128)}, f32[256,8192]{1,0:T(8,128)})) %all-reduce.6.cloned.1.call-update) | async-done | bytes 12582928 | tf_op jit(solution)/shard_map/psum | solution.py:132
  1204.5 22.2 %multiply_subtract_fusion = (f32[256,8192]{1,0:T(8,128)}, f32[256,8192]{1,0:T(8,128)}, f32[256,8192]{1,0:T(8,128)}) fusion(f32[256,8192]{1,0:T(8,128)} %param.30, f32[256,8192]{1,0:T(8,128)} %get-tuple-element.124, f32[256,8192]{1,0:T(8,128)} %param.31, f32[256,8192]{1,0:T(8,128)} %param.32), kind=kLoop, calls=%fused_computation.35 | loop fusion | flops 31457280 | bytes 58720256 | tf_op jit(solution)/shard_map/sub | solution.py:122
  (233 shorter events, 223.8 us)
Async XLA Ops:
  7.2 94.4 %all-gather.3.cloned.1.call-start = ((), (), s32[]{:S(2)}) async-start(), calls=%async_computation.2 | async-start | bytes 10485760 | tf_op jit(solution)/shard_map/all_gather | solution.py:145
  11.0 250.4 %all-gather.5.cloned.1.call-start = ((), (), s32[]{:S(2)}) async-start(), calls=%async_computation.3 | async-start | bytes 20971520 | tf_op jit(solution)/shard_map/all_gather | solution.py:146
  17.1 626.7 %reduce-scatter.3.cloned.1.call-start = ((), (), s32[]{:S(2)}) async-start(), calls=%async_computation.4 | async-start | bytes 20971520 | tf_op jit(solution)/shard_map/reduce_scatter | solution.py:128
  31.7 180.7 %copy-start = (bf16[1024,1024]{0,1:T(8,128)(2,1)}, bf16[1024,1024]{0,1:T(8,128)(2,1)S(1)}, u32[]{:S(2)}) copy-start(bf16[1024,1024]{0,1:T(8,128)(2,1)S(1)} %copy.89) | copy-start | bytes 6291460
  38.0 75.2 %copy-start.29 = (f32[1024]{0:T(1024)}, f32[1024]{0:T(1024)S(1)}, u32[]{:S(2)}) copy-start(f32[1024]{0:T(1024)S(1)} %broadcast_multiply_fusion.1) | copy-start | bytes 12292
  38.6 74.5 %copy-start.45 = (f32[1024]{0:T(1024)}, f32[1024]{0:T(1024)S(1)}, u32[]{:S(2)}) copy-start(f32[1024]{0:T(1024)S(1)} %fusion.75) | copy-start | bytes 12292
  39.2 73.9 %copy-start.33 = (f32[1024]{0:T(1024)}, f32[1024]{0:T(1024)S(1)}, u32[]{:S(2)}) copy-start(f32[1024]{0:T(1024)S(1)} %get-tuple-element.153) | copy-start | bytes 12292
  39.2 73.9 %copy-start.60 = (f32[1024]{0:T(1024)}, f32[1024]{0:T(1024)S(1)}, u32[]{:S(2)}) copy-start(f32[1024]{0:T(1024)S(1)} %get-tuple-element.154) | copy-start | bytes 12292
  39.2 222.2 %copy-start.58 = (f32[1024]{0:T(1024)}, f32[1024]{0:T(1024)S(1)}, u32[]{:S(2)}) copy-start(f32[1024]{0:T(1024)S(1)} %get-tuple-element.149) | copy-start | bytes 12292
  39.3 292.5 %copy-start.37 = (f32[1024]{0:T(1024)}, f32[1024]{0:T(1024)S(1)}, u32[]{:S(2)}) copy-start(f32[1024]{0:T(1024)S(1)} %get-tuple-element.148) | copy-start | bytes 12292
  131.8 27.3 %copy-start.9 = (bf16[512,1024]{0,1:T(8,128)(2,1)}, bf16[512,1024]{0,1:T(8,128)(2,1)S(1)}, u32[]{:S(2)}) copy-start(bf16[512,1024]{0,1:T(8,128)(2,1)S(1)} %copy.95) | copy-start | bytes 3145732
  217.0 114.8 %copy-start.31 = (f32[1024]{0:T(1024)}, f32[1024]{0:T(1024)S(1)}, u32[]{:S(2)}) copy-start(f32[1024]{0:T(1024)S(1)} %broadcast_multiply_fusion) | copy-start | bytes 12292
  219.5 112.3 %copy-start.39 = (f32[1024]{0:T(1024)}, f32[1024]{0:T(1024)S(1)}, u32[]{:S(2)}) copy-start(f32[1024]{0:T(1024)S(1)} %fusion.76) | copy-start | bytes 12292
  261.5 17.0 %copy-start.43 = (f32[1024]{0:T(1024)S(1)}, f32[1024]{0:T(1024)}, u32[]{:S(2)}) copy-start(f32[1024]{0:T(1024)} %fusion.74) | copy-start | bytes 12292
  261.5 17.0 %copy-start.52 = (f32[4096]{0:T(1024)S(1)}, f32[4096]{0:T(1024)}, u32[]{:S(2)}) copy-start(f32[4096]{0:T(1024)} %slice.237) | copy-start | bytes 49156
  374.7 22.4 %copy-start.19 = (f32[512,16,64]{0,2,1:T(8,128)S(1)}, f32[512,16,64]{0,2,1:T(8,128)}, u32[]{:S(2)}) copy-start(f32[512,16,64]{0,2,1:T(8,128)} %fusion.65) | copy-start | bytes 6291460
  412.4 28.3 %copy-start.8 = (bf16[1024,1024]{0,1:T(8,128)(2,1)S(1)}, bf16[1024,1024]{0,1:T(8,128)(2,1)}, u32[]{:S(2)}) copy-start(bf16[1024,1024]{0,1:T(8,128)(2,1)} %copy.96) | copy-start | bytes 6291460
  489.8 17.6 %copy-start.44 = (f32[1024]{0:T(1024)S(1)}, f32[1024]{0:T(1024)}, u32[]{:S(2)}) copy-start(f32[1024]{0:T(1024)} %fusion.74) | copy-start | bytes 12292
  489.8 17.6 %copy-start.53 = (f32[4096]{0:T(1024)S(1)}, f32[4096]{0:T(1024)}, u32[]{:S(2)}) copy-start(f32[4096]{0:T(1024)} %slice.237) | copy-start | bytes 49156
  489.8 445.6 %reduce-scatter.5.cloned.1.call-start = ((), (), s32[]{:S(2)}) async-start(), calls=%async_computation.5 | async-start | bytes 41943040 | tf_op jit(solution)/shard_map/reduce_scatter | solution.py:129
  547.3 646.1 %all-reduce.6.cloned.1.call-start = ((), (), s32[]{:S(2)}) async-start(), calls=%async_computation.6 | async-start | bytes 25165824 | tf_op jit(solution)/shard_map/psum | solution.py:132
  984.7 49.3 %copy-start.36 = (f32[3072]{0:T(1024)S(1)}, f32[3072]{0:T(1024)}, u32[]{:S(2)}) copy-start(f32[3072]{0:T(1024)} %param.33) | copy-start | bytes 36868
  984.7 49.3 %copy-start.55 = (f32[3072]{0:T(1024)S(1)}, f32[3072]{0:T(1024)}, u32[]{:S(2)}) copy-start(f32[3072]{0:T(1024)} %param.34) | copy-start | bytes 36868
  984.7 49.2 %copy-start.56 = (f32[3072]{0:T(1024)S(1)}, f32[3072]{0:T(1024)}, u32[]{:S(2)}) copy-start(f32[3072]{0:T(1024)} %param.35) | copy-start | bytes 36868
  (52 other events, 273.9 us)
Sparse Core Ops, SparseCore 0:
  11.2 90.3 all-gather.2
  104.0 157.4 all-gather.4
  489.9 153.8 reduce-scatter.2
  646.7 288.6 reduce-scatter.4
  937.8 255.5 all-reduce.5
where the time goes:
time: 1240 us; the launch traced here: 1230 us
  waiting for transfers between devices  647 us (52%)
  matrix products  289 us (23%)
  other arithmetic  164 us (13%)
  local copies, waits for them, and re-layouts  64.7 us (5%)
  blocking collectives  53.5 us (4%)
  between operations  15.6 us (1%)
    reduce_scatter x1, waiting for transfers between devices, settle(): lax.psum_scatter(grads[1], 'shard', scatter_dimension=0, tiled=True)  292 us
    psum x1, waiting for transfers between devices, settle(): summed = lax.psum((owned[0], owned[1], owned[2]), 'dp')  159 us
    reduce_scatter x1, waiting for transfers between devices, settle(): lax.psum_scatter(grads[0], 'shard', scatter_dimension=0, tiled=True)  94.6 us
    all_gather x1, waiting for transfers between devices, body(): lax.all_gather(attn_w.astype(jnp.bfloat16), 'shard', axis=0, tiled=True)  60.8 us
    dot_general x4, matrix products, rows_product(): lax.dot_general(left, right, (((0,), (0,)), ((), ())), preferred_element_...  50.6 us
    dot_general x4, matrix products, cols_product(): lax.dot_general(left, right, (((1,), (1,)), ((), ())), preferred_element_...  48.8 us
    all_gather x1, waiting for transfers between devices, body(): lax.all_gather(mlp_w.astype(jnp.bfloat16), 'shard', axis=0, tiled=True)  40.7 us
    convert_element_type x2, other arithmetic, attend_backward(): grad_scores = (probs * (grad_probs - inner)).astype(jnp.bfloat16)  36.6 us
  transfers between devices with their start and end apart: 5, of which 5 were waited for; matrix products, arithmetic and copies ran while one was open for 20% of the time, Pallas kernels for 0%

commit v1 on v0

v1 whole, which is shorter than its diff:
```python
import functools

import jax
import jax.numpy as jnp
from jax import lax
from jax.experimental import pallas as pl
from jax.experimental.pallas import tpu as pltpu
from jax.sharding import PartitionSpec as P

HD = 64
STEP = 10
LANES = 128
MASKED = -1e30
SAFE = 60.0
GELU_IN = 0.7978845608028654
GELU_CUBE = 0.044715

beta_one = 0.9
beta_two = 0.95
adam_eps = 1e-08
norm_eps = 1e-05

F32 = jnp.float32
BF16 = jnp.bfloat16
MIB = 1024 * 1024
VMEM_MIB = 64

ANY = pl.BlockSpec(memory_space=pl.ANY)
SMEM = pl.BlockSpec(memory_space=pltpu.SMEM)


def dot_nn(left, right):
    return lax.dot_general(left, right, (((1,), (0,)), ((), ())), preferred_element_type=F32)


def dot_nt(left, right):
    return lax.dot_general(left, right, (((1,), (1,)), ((), ())), preferred_element_type=F32)


def dot_tn(left, right):
    return lax.dot_general(left, right, (((0,), (0,)), ((), ())), preferred_element_type=F32)


def whole(shape):
    return pl.BlockSpec(shape, lambda *_: (0,) * len(shape))


def call(kernel, grid, ins, outs, after=(), reuse=(), prefetch=(), scratch=(), cost=None, name=None):
    known = len(prefetch) + len(ins)
    idle = [*after, *(array for array, _ in reuse)]

    def run(*refs):
        kernel(*refs[:known], *refs[known + len(idle) :])

    def placed(array, spec):
        if spec is SMEM:
            return array
        return pltpu.with_memory_space_constraint(array, pltpu.HBM)

    return pl.pallas_call(
        run,
        grid_spec=pltpu.PrefetchScalarGridSpec(
            num_scalar_prefetch=len(prefetch),
            grid=grid,
            in_specs=[spec for _, spec in ins] + [ANY] * len(idle),
            out_specs=[spec for _, _, spec in outs],
            scratch_shapes=list(scratch),
        ),
        out_shape=[pltpu.HBM(shape, dtype) for shape, dtype, _ in outs],
        input_output_aliases={
            known + len(after) + number: output for number, (_, output) in enumerate(reuse)
        },
        compiler_params=pltpu.CompilerParams(vmem_limit_bytes=VMEM_MIB * MIB),
        cost_estimate=pl.CostEstimate(flops=0, bytes_accessed=0, transcendentals=0),
        name=name,
    )(*prefetch, *(placed(*item) for item in ins), *(placed(array, ANY) for array in idle))


def param(small, number, width):
    return (small, pl.BlockSpec((1, width), lambda *_: (0, number)))


def cost(flops, moved, exps=0):
    return pl.CostEstimate(flops=int(flops), bytes_accessed=int(moved), transcendentals=int(exps))


def store_turned(turned_ref, toff, block, half, value, columns):
    turned = value.astype(BF16).T
    for part in range(LANES // half):
        offset = pl.multiple_of(toff[block * (LANES // half) + part], half)
        turned_ref[pl.ds(offset, half), columns] = turned[part * half : (part + 1) * half]


def norm_stats(values):
    center = values - jnp.mean(values, axis=-1, keepdims=True)
    spread = jnp.mean(center * center, axis=-1, keepdims=True)
    scale = lax.rsqrt(spread + norm_eps)
    return center * scale, scale


def norm_back(hat, scale, grad_hat):
    mean = jnp.mean(grad_hat, axis=-1, keepdims=True)
    along = jnp.mean(grad_hat * hat, axis=-1, keepdims=True)
    return scale * (grad_hat - mean - hat * along)


def accumulate(ref, value, first):
    @pl.when(first)
    def _():
        ref[...] = value

    @pl.when(jnp.logical_not(first))
    def _():
        ref[...] += value


class Weights:
    def __init__(self, pieces, plan, offs, first=0):
        self.pieces, self.plan, self.offs, self.first = pieces, plan, offs, first

    def at(self, first):
        return Weights(self.pieces, self.plan, self.offs, self.first + first)

    def inputs(self):
        return [(self.offs, SMEM)] + [(piece, ANY) for piece in self.pieces]

    def sems(self):
        return pltpu.SemaphoreType.DMA((len(self.plan),))

    def rest(self, refs):
        return refs[1 + len(self.pieces) :]

    def copies(self, refs, size, target, sems, start=None):
        offs, refs = refs[0], refs[1:]
        columns = slice(self.first, self.first + size)
        if start is not None:
            columns = pl.ds(pl.multiple_of(self.first + start, LANES), size)
        made = []
        for number, (piece, first, rows, index) in enumerate(self.plan):
            offset = pl.multiple_of(offs[index], rows)
            made.append(
                pltpu.make_async_copy(
                    refs[piece].at[pl.ds(first, rows), columns],
                    target(offset, rows),
                    sems.at[number],
                )
            )
        return made, refs[len(self.pieces) :]


def start_all(copies):
    @pl.when(pl.program_id(0) == 0)
    def _():
        for copy in copies:
            copy.start()


def wait_all(copies):
    @pl.when(pl.program_id(0) == 0)
    def _():
        for copy in copies:
            copy.wait()


def cot_kernel(half, toff, ends, cot_ref, dy_ref, turned_ref, bias_ref):
    rows = cot_ref.shape[0]
    place = lax.broadcasted_iota(jnp.int32, (rows, LANES), 0)
    live = (place < ends[ends.shape[0] - 1]).astype(F32)
    for block in range(cot_ref.shape[1] // LANES):
        columns = slice(block * LANES, (block + 1) * LANES)
        value = cot_ref[:, columns].astype(F32) * live
        dy_ref[:, columns] = value.astype(BF16)
        bias_ref[:, columns] = jnp.sum(value, axis=0, keepdims=True)
        store_turned(turned_ref, toff, block, half, value, slice(None))


def run_cot(half, toff, ends, cot, after=()):
    rows, width = cot.shape
    return call(
        functools.partial(cot_kernel, half),
        (1,),
        [(toff, SMEM), (ends, SMEM), (cot, whole(cot.shape))],
        [
            ((rows, width), BF16, whole((rows, width))),
            ((width, rows), BF16, whole((width, rows))),
            ((1, width), F32, whole((1, width))),
        ],
        after=after,
        cost=cost(0, 6 * rows * width),
        name="cotangent",
    )


def run_qkv(half, weights, toff, x, small, numbers, after=()):
    rows, width = x.shape
    span = 256

    def kernel(*refs):
        weight, sems = refs[-2:]
        copies, refs = weights.copies(
            refs, 3 * width, lambda at, size: weight.at[pl.ds(at, size), :], sems
        )
        toff_ref, x_ref, bias_q, bias_v, gain_ref, shift_ref, qkv_ref, turned_ref = refs[:8]
        start_all(copies)
        hat, _ = norm_stats(x_ref[...].astype(F32))
        normed = hat * gain_ref[...] + shift_ref[...]
        for block in range(width // LANES):
            columns = slice(block * LANES, (block + 1) * LANES)
            store_turned(turned_ref, toff_ref, block, half, normed[:, columns], slice(None))
        wait_all(copies)
        low = normed.astype(BF16)
        for part in range(3):
            columns = slice(part * width, (part + 1) * width)
            value = dot_nn(low, weight[:, columns])
            if part == 2:
                value += bias_v[...]
            if part == 0:
                value = (value + bias_q[...]).astype(BF16).astype(F32) * HD ** (-0.5)
            qkv_ref[:, columns] = value.astype(BF16)

    return call(
        kernel,
        (rows // span,),
        weights.inputs()
        + [
            (toff, SMEM),
            (x, pl.BlockSpec((span, width), lambda i: (i, 0))),
        ]
        + [param(small, number, width) for number in numbers],
        [
            ((rows, 3 * width), BF16, pl.BlockSpec((span, 3 * width), lambda i: (i, 0))),
            ((width, rows), BF16, pl.BlockSpec((width, span), lambda i: (0, i))),
        ],
        after=after,
        scratch=[pltpu.VMEM((width, 3 * width), BF16), weights.sems()],
        cost=cost(6 * rows * width * width, 16 * rows * width),
        name="qkv",
    )


def first_of_row(ends, place):
    first = jnp.zeros_like(place)
    for number in range(ends.shape[0]):
        first = jnp.where(place >= ends[number], ends[number], first)
    return first


def attend_kernel(ends, q_ref, k_ref, v_ref, o_ref, lse_ref, allow):
    rows = q_ref.shape[0]
    span = min(256, rows)

    @pl.when(pl.program_id(0) == 0)
    def _():
        for start in range(0, rows, span):
            keys = start + span
            place = lax.broadcasted_iota(jnp.int32, (span, 1), 0) + start
            first = first_of_row(ends, place)
            key = lax.broadcasted_iota(jnp.int32, (span, keys), 1)
            allow[start:keys, :keys] = jnp.where((key <= place) & (key >= first), 0.0, MASKED)

    lane = lax.broadcasted_iota(jnp.int32, (1, LANES), 1)
    low_lane = lane < HD
    one = low_lane.astype(BF16)
    masks = (one, 1 - one)

    same = (lax.broadcasted_iota(jnp.int32, (LANES, LANES), 0) < HD) == (
        lax.broadcasted_iota(jnp.int32, (LANES, LANES), 1) < HD
    )
    same = same.astype(F32).astype(BF16)
    longest = [
        jnp.max(dot_nn(ref[...] * ref[...], same), axis=0, keepdims=True) for ref in (q_ref, k_ref)
    ]
    bounded = jnp.max(longest[0] * longest[1]) < SAFE * SAFE

    def attend(shift):
        mixed = [v_ref[...] * mask + (1 - mask) for mask in masks]
        for start in range(0, rows, span):
            keys = start + span
            sums = []
            tops = []
            for head in range(2):
                query = q_ref[start:keys, :] * masks[head]
                scores = dot_nt(query, k_ref[:keys, :]) + allow[start:keys, :keys]
                if shift:
                    top = jnp.max(scores, axis=1, keepdims=True)
                    tops.append(top)
                    scores = scores - top
                probs = jnp.exp(scores).astype(BF16)
                sums.append(dot_nn(probs, mixed[head][:keys]))
            total = pltpu.roll(jnp.where(low_lane, sums[1], sums[0]), HD, 1)
            out = jnp.where(low_lane, sums[0], sums[1]) / total
            o_ref[start:keys, :] = out.astype(BF16)
            lse = jnp.log(total)
            if shift:
                lse += jnp.where(low_lane, tops[0], tops[1])
            lse = lse.T
            lse_ref[0, 0:1, start:keys] = lse[0:1]
            lse_ref[0, 1:2, start:keys] = lse[HD : HD + 1]

    @pl.when(bounded)
    def _():
        attend(False)

    @pl.when(jnp.logical_not(bounded))
    def _():
        attend(True)


def run_attend(ends, qkv, first, count, earlier=None, after=()):
    rows = qkv.shape[0]
    width = qkv.shape[1] // 3
    pairs = width // LANES
    column = lambda shift: pl.BlockSpec((rows, LANES), lambda i: (0, i + shift))
    return call(
        attend_kernel,
        (count,),
        [(ends, SMEM)] + [(qkv, column(first + part * pairs)) for part in range(3)],
        [
            ((rows, width), BF16, column(first)),
            ((pairs, 2, rows), F32, pl.BlockSpec((1, 2, rows), lambda i: (i + first, 0, 0))),
        ],
        after=after,
        reuse=[] if earlier is None else [(earlier[0], 0), (earlier[1], 1)],
        scratch=[pltpu.VMEM((rows, rows), F32)],
        cost=cost(8 * rows * rows * LANES * count, 8 * rows * LANES * count, 2 * rows * rows * count),
        name="attend",
    )


def run_after(half, weights, toffs, mixed, x, small, numbers, after=()):
    rows, width = x.shape
    span = 256

    def kernel(*refs):
        weight, sems = refs[-2:]
        copies, refs = weights.copies(
            refs, width, lambda at, size: weight.at[pl.ds(at, size), :], sems
        )
        mixed_toff, low_toff, mixed_ref, x_ref, bias_ref, gain_ref, shift_ref = refs[:7]
        after_ref, low_ref, turned_ref, mixed_turned_ref = refs[7:11]
        start_all(copies)
        for block in range(width // LANES):
            columns = slice(block * LANES, (block + 1) * LANES)
            store_turned(mixed_turned_ref, mixed_toff, block, half, mixed_ref[:, columns], slice(None))
        wait_all(copies)
        value = x_ref[...].astype(F32) + dot_nn(mixed_ref[...], weight[...]) + bias_ref[...]
        after_ref[...] = value
        hat, _ = norm_stats(value)
        normed = hat * gain_ref[...] + shift_ref[...]
        low_ref[...] = normed.astype(BF16)
        for block in range(width // LANES):
            columns = slice(block * LANES, (block + 1) * LANES)
            store_turned(turned_ref, low_toff, block, half, normed[:, columns], slice(None))

    by_row = pl.BlockSpec((span, width), lambda i: (i, 0))
    by_column = pl.BlockSpec((width, span), lambda i: (0, i))
    return call(
        kernel,
        (rows // span,),
        weights.inputs()
        + [(toff, SMEM) for toff in toffs]
        + [(mixed, by_row), (x, by_row)]
        + [param(small, number, width) for number in numbers],
        [
            ((rows, width), F32, by_row),
            ((rows, width), BF16, by_row),
            ((width, rows), BF16, by_column),
            ((width, rows), BF16, by_column),
        ],
        after=after,
        scratch=[pltpu.VMEM((width, width), BF16), weights.sems()],
        cost=cost(2 * rows * width * width, 14 * rows * width),
        name="after",
    )


def run_feed(up_weights, down_weights, low, turned, dy, dyt, small, first, begin, block, earlier, after=()):
    rows, width = low.shape
    hidden = earlier[0].shape[1] if earlier is not None else block_total(small, width)
    span = 256
    mid = width // 2
    count = block // span
    by_column = lambda size: pl.BlockSpec((size, span), lambda i: (0, i))
    shifted = pl.BlockSpec((rows, span), lambda i: (0, begin // span + i))
    grad = ((2, mid, block), BF16, pl.BlockSpec((2, mid, span), lambda i: (0, 0, i)))

    def kernel(*refs):
        up, down, up_sems, down_sems = refs[-4:]
        step = pl.program_id(0)

        def copies(number):
            columns = pl.ds(pl.multiple_of(number * span, span), span)
            made, rest = up_weights.copies(
                refs,
                span,
                lambda at, size: up.at[pl.ds(at, size), columns],
                up_sems.at[number],
                number * span,
            )
            more, _ = down_weights.copies(
                rest,
                span,
                lambda at, size: down.at[pl.ds(at, size), columns],
                down_sems.at[number],
                number * span,
            )
            return made + more

        @pl.when(step == 0)
        def _():
            for copy in copies(0):
                copy.start()

        @pl.when(step + 1 < count)
        def _():
            for copy in copies(step + 1):
                copy.start()

        for copy in copies(step):
            copy.wait()
        low_ref, turned_ref, dy_ref, dyt_ref, bias_ref, act_ref, du_ref, own_ref, sib_ref, gbias_ref = (
            down_weights.rest(up_weights.rest(refs))[:10]
        )
        columns = pl.ds(pl.multiple_of(step * span, span), span)
        upper = dot_nn(low_ref[...], up[:, columns]) + bias_ref[...]
        grad_act = dot_nn(dy_ref[...], down[:, columns])
        square = (GELU_IN * GELU_CUBE) * (upper * upper)
        tanh = jnp.tanh(upper * (GELU_IN + square))
        share = 0.5 + 0.5 * tanh
        act = upper * share
        slope = share + act * (1.0 - tanh) * (GELU_IN + 3.0 * square)
        act = act.astype(BF16)
        du = (grad_act * slope).astype(BF16)
        act_ref[...] = act
        du_ref[...] = du
        gbias_ref[...] = jnp.sum(du.astype(F32), axis=0, keepdims=True)
        grad_up = dot_nn(turned_ref[...], du).astype(BF16)
        own_ref[0] = grad_up[:mid]
        sib_ref[0] = grad_up[mid:]
        grad_dn = dot_nn(dyt_ref[...], act).astype(BF16)
        own_ref[1] = grad_dn[:mid]
        sib_ref[1] = grad_dn[mid:]

    return call(
        kernel,
        (count,),
        up_weights.inputs()
        + down_weights.inputs()
        + [
            (low, whole((rows, width))),
            (turned, whole((width, rows))),
            (dy, whole((rows, width))),
            (dyt, whole((width, rows))),
            (small, pl.BlockSpec((1, span), lambda i: (0, first // span + i))),
        ],
        [
            ((rows, hidden), BF16, shifted),
            ((rows, hidden), BF16, shifted),
            grad,
            grad,
            ((1, block), F32, by_column(1)),
        ],
        after=after,
        reuse=[] if earlier is None else [(earlier[0], 0), (earlier[1], 1)],
        scratch=[
            pltpu.VMEM((width, block), BF16),
            pltpu.VMEM((width, block), BF16),
            pltpu.SemaphoreType.DMA((count, len(up_weights.plan))),
            pltpu.SemaphoreType.DMA((count, len(down_weights.plan))),
        ],
        cost=cost(8 * rows * width * block, 24 * width * block, rows * block),
        name="feed",
    )


def block_total(small, width):
    return small.shape[1] - 8 * width


class Stream:
    def __init__(self):
        self.parts = []

    def add(self, copies):
        self.parts.append(copies)

    def start(self):
        for copies in self.parts:
            for copy in copies:
                copy.start()

    def wait(self, number):
        for copy in self.parts[number]:
            copy.wait()


def run_output(weights, acts, after_value, small, number, after=()):
    rows, width = after_value.shape
    hidden = acts.shape[1]
    part = width
    parts = hidden // part
    places = [
        (item.at(start)) for size, item in weights for start in range(0, size, part)
    ]
    most = max(len(item.plan) for item in places)

    def kernel(*refs):
        act, down, start_value, sems, own_sems = refs[-5:]
        stream = Stream()
        for index, item in enumerate(places):
            columns = slice(index * part, (index + 1) * part)
            copies, refs = item.copies(
                refs,
                part,
                lambda at, size, columns=columns: down.at[pl.ds(at, size), columns],
                sems.at[index],
            )
            stream.add(copies)
        act_ref, after_ref, bias_ref, out_ref = refs[:4]
        for index in range(parts):
            columns = slice(index * part, (index + 1) * part)
            stream.parts[index].append(
                pltpu.make_async_copy(
                    act_ref.at[:, columns], act.at[:, columns], own_sems.at[index]
                )
            )
        stream.add([pltpu.make_async_copy(after_ref, start_value, own_sems.at[parts])])
        stream.start()
        total = None
        for index in range(parts):
            columns = slice(index * part, (index + 1) * part)
            stream.wait(index)
            value = dot_nt(act[:, columns], down[:, columns])
            total = value if total is None else total + value
        stream.wait(parts)
        out_ref[...] = (total + start_value[...] + bias_ref[...]).astype(BF16)

    (out,) = call(
        kernel,
        (1,),
        [item for place in places for item in place.inputs()]
        + [(acts, ANY), (after_value, ANY), param(small, number, width)],
        [((rows, width), BF16, whole((rows, width)))],
        after=after,
        scratch=[
            pltpu.VMEM((rows, hidden), BF16),
            pltpu.VMEM((width, hidden), BF16),
            pltpu.VMEM((rows, width), F32),
            pltpu.SemaphoreType.DMA((parts, most)),
            pltpu.SemaphoreType.DMA((parts + 1,)),
        ],
        cost=cost(2 * rows * width * hidden, 22 * rows * width),
        name="output",
    )
    return out


def run_middle(weights, out_weights, dus, after_value, dy, small, number, turned, after=()):
    rows, width = after_value.shape
    hidden = dus.shape[1]
    part = width
    parts = hidden // part
    span = 256
    mid = width // 2
    places = [
        (item.at(start)) for size, item in weights for start in range(0, size, part)
    ]
    most = max(len(item.plan) for item in places)

    def kernel(*refs):
        du, up, value_in, dy_in, turned_in, out_weight, branch, sems, out_sems, own_sems = refs[-10:]
        stream = Stream()
        for index, item in enumerate(places):
            columns = slice(index * part, (index + 1) * part)
            copies, refs = item.copies(
                refs,
                part,
                lambda at, size, columns=columns: up.at[pl.ds(at, size), columns],
                sems.at[index],
            )
            stream.add(copies)
        more, refs = out_weights.copies(
            refs, width, lambda at, size: out_weight.at[pl.ds(at, size), :], out_sems
        )
        du_ref, after_ref, dy_ref, gain_ref, turned_ref = refs[:5]
        grad_ref, dmix_ref, own_ref, sib_ref, gbias_ref, ggain_ref, gshift_ref = refs[5:12]
        for index in range(parts):
            columns = slice(index * part, (index + 1) * part)
            stream.parts[index].append(
                pltpu.make_async_copy(du_ref.at[:, columns], du.at[:, columns], own_sems.at[index])
            )
        stream.add(
            [
                pltpu.make_async_copy(after_ref, value_in, own_sems.at[parts]),
                pltpu.make_async_copy(dy_ref, dy_in, own_sems.at[parts + 1]),
            ]
        )
        stream.add([pltpu.make_async_copy(turned_ref, turned_in, own_sems.at[parts + 2]), *more])
        stream.start()
        total = None
        for index in range(parts):
            columns = slice(index * part, (index + 1) * part)
            stream.wait(index)
            value = dot_nt(du[:, columns], up[:, columns])
            total = value if total is None else total + value
        stream.wait(parts)
        gain = gain_ref[...]
        sums = [jnp.zeros((1, width), F32)] * 3
        for start in range(0, rows, span):
            lines = slice(start, start + span)
            grad = total[lines]
            hat, scale = norm_stats(value_in[lines, :])
            full = dy_in[lines, :].astype(F32) + norm_back(hat, scale, grad * gain)
            grad_ref[lines, :] = full
            low = full.astype(BF16)
            branch[lines, :] = low
            for index, value in enumerate((low.astype(F32), grad * hat, grad)):
                sums[index] = sums[index] + jnp.sum(value, axis=0, keepdims=True)
        gbias_ref[...], ggain_ref[...], gshift_ref[...] = sums
        stream.wait(parts + 1)
        dmix_ref[...] = dot_nt(branch[...], out_weight[...]).astype(BF16)
        for side in range(2):
            columns = slice(side * (width // 2), (side + 1) * (width // 2))
            value = dot_nn(turned_in[...], branch[:, columns]).astype(BF16)
            own_ref[side] = value[:mid]
            sib_ref[side] = value[mid:]

    grads = ((2, mid, width // 2), BF16, whole((2, mid, width // 2)))
    vector = ((1, width), F32, whole((1, width)))
    full = whole((rows, width))
    return call(
        kernel,
        (1,),
        [item for place in places for item in place.inputs()]
        + out_weights.inputs()
        + [(dus, ANY), (after_value, ANY), (dy, ANY), param(small, number, width), (turned, ANY)],
        [((rows, width), F32, full), ((rows, width), BF16, full), grads, grads] + [vector] * 3,
        after=after,
        scratch=[
            pltpu.VMEM((rows, hidden), BF16),
            pltpu.VMEM((width, hidden), BF16),
            pltpu.VMEM((rows, width), F32),
            pltpu.VMEM((rows, width), BF16),
            pltpu.VMEM((width, rows), BF16),
            pltpu.VMEM((width, width), BF16),
            pltpu.VMEM((rows, width), BF16),
            pltpu.SemaphoreType.DMA((parts, most)),
            out_weights.sems(),
            pltpu.SemaphoreType.DMA((parts + 3,)),
        ],
        cost=cost(2 * rows * width * (hidden + 2 * width), 30 * rows * width),
        name="middle",
    )


def attend_back_kernel(
    ends,
    q_ref,
    k_ref,
    v_ref,
    o_ref,
    do_ref,
    lse_ref,
    dq_ref,
    dk_ref,
    dv_ref,
    gq_ref,
    gv_ref,
    allow,
    total,
):
    rows = q_ref.shape[0]
    span = min(256, rows)

    @pl.when(pl.program_id(0) == 0)
    def _():
        for start in range(0, rows, span):
            query = lax.broadcasted_iota(jnp.int32, (1, rows - start), 1) + start
            first = first_of_row(ends, query)
            key = lax.broadcasted_iota(jnp.int32, (span, rows - start), 0) + start
            allow[start : start + span, start:] = jnp.where(
                (key <= query) & (key >= first), 0.0, MASKED
            )

    lane = lax.broadcasted_iota(jnp.int32, (1, LANES), 1)
    low_lane = lane < HD
    one = low_lane.astype(BF16)
    masks = (one, 1 - one)
    product = (o_ref[...].astype(F32) * do_ref[...].astype(F32)).T
    inner = (
        jnp.sum(product[:HD], axis=0, keepdims=True),
        jnp.sum(product[HD:], axis=0, keepdims=True),
    )
    for start in range(0, rows, span):
        stop = start + span
        grads = []
        for head in range(2):
            keys = k_ref[start:stop, :] * masks[head]
            vals = v_ref[start:stop, :] * masks[head]
            scores = dot_nt(keys, q_ref[start:, :]) + allow[start:stop, start:]
            probs = jnp.exp(scores - lse_ref[0, head : head + 1, start:])
            grad_probs = dot_nt(vals, do_ref[start:, :])
            grad_scores = (probs * (grad_probs - inner[head][:, start:])).astype(BF16)
            grad_vals = dot_nn(probs.astype(BF16), do_ref[start:, :])
            grad_keys = dot_nn(grad_scores, q_ref[start:, :])
            grads.append((grad_keys, grad_vals))
            update = dot_tn(grad_scores, keys)
            if start == 0 and head == 0:
                total[...] = update
            else:
                total[start:, :] += update
        dk_ref[start:stop, :] = jnp.where(low_lane, grads[0][0], grads[1][0]).astype(BF16)
        dv_ref[start:stop, :] = jnp.where(low_lane, grads[0][1], grads[1][1]).astype(BF16)
    grad_query = (total[...] * HD ** (-0.5)).astype(BF16)
    dq_ref[...] = grad_query
    gq_ref[...] = jnp.sum(grad_query.astype(F32), axis=0, keepdims=True)
    gv_ref[...] = jnp.sum(dv_ref[...].astype(F32), axis=0, keepdims=True)


def run_attend_back(ends, qkv, mixed, dmix, lse, first, count, after=()):
    rows, width = mixed.shape
    pairs = width // LANES
    column = lambda shift: pl.BlockSpec((rows, LANES), lambda i: (0, i + shift))
    return call(
        attend_back_kernel,
        (count,),
        [(ends, SMEM)]
        + [(qkv, column(first + part * pairs)) for part in range(3)]
        + [
            (mixed, column(first)),
            (dmix, column(first)),
            (lse, pl.BlockSpec((1, 2, rows), lambda i: (i + first, 0, 0))),
        ],
        [((rows, LANES * count), BF16, column(0))] * 3
        + [((1, LANES * count), F32, pl.BlockSpec((1, LANES), lambda i: (0, i)))] * 2,
        after=after,
        scratch=[pltpu.VMEM((rows, rows), F32), pltpu.VMEM((rows, LANES), F32)],
        cost=cost(
            20 * rows * rows * LANES * count, 16 * rows * LANES * count, 2 * rows * rows * count
        ),
        name="attend_back",
    )


def project_kernel(turned_ref, dq_ref, dk_ref, dv_ref, own_ref, sib_ref):
    mid = own_ref.shape[1]
    size = dq_ref.shape[1]
    left = jnp.concatenate([dq_ref[...], dk_ref[:, : size // 2]], axis=1)
    right = jnp.concatenate([dk_ref[:, size // 2 :], dv_ref[...]], axis=1)
    for side, columns in enumerate((left, right)):
        own_ref[side] = dot_nn(turned_ref[:mid], columns).astype(BF16)
        sib_ref[side] = dot_nn(turned_ref[mid:], columns).astype(BF16)


def run_project(turned, dq, dk, dv, after=()):
    width, rows = turned.shape
    size = dq.shape[1]
    mid = width // 2
    grad = ((2, mid, 3 * size // 2), BF16, whole((2, mid, 3 * size // 2)))
    return call(
        project_kernel,
        (1,),
        [(turned, whole((width, rows)))] + [(value, whole((rows, size))) for value in (dq, dk, dv)],
        [grad, grad],
        after=after,
        cost=cost(6 * rows * width * size, 14 * rows * size),
        name="project",
    )


def run_input(weights, grads, x, grad_after, small, number, after=()):
    rows, width = x.shape
    span = 256
    size = grads[0][0].shape[1]
    flat = [value for group in grads for value in group]
    count = len(flat)

    def kernel(*refs):
        held, weight, x_in, grad_in, sems, own_sems = refs[-6:]
        pieces = refs
        refs = weights.rest(refs)
        grad_refs = refs[:count]
        x_ref, grad_ref, gain_ref, out_ref, ggain_ref, gshift_ref = refs[count : count + 6]
        stream = Stream()
        begins = []
        for index in range(count):
            group, part = divmod(index, 3)
            begin = part * width + group * size
            begins.append(begin)
            columns = slice(begin, begin + size)
            copies, _ = weights.at(begin).copies(
                pieces,
                size,
                lambda at, lines, columns=columns: weight.at[pl.ds(at, lines), columns],
                sems.at[index],
            )
            copies.append(
                pltpu.make_async_copy(grad_refs[index], held.at[index], own_sems.at[index])
            )
            stream.add(copies)
        stream.add(
            [
                pltpu.make_async_copy(x_ref, x_in, own_sems.at[count]),
                pltpu.make_async_copy(grad_ref, grad_in, own_sems.at[count + 1]),
            ]
        )
        stream.start()
        total = None
        for index in range(count):
            stream.wait(index)
            columns = slice(begins[index], begins[index] + size)
            value = dot_nt(held[index], weight[:, columns])
            total = value if total is None else total + value
        stream.wait(count)
        gain = gain_ref[...]
        sums = [jnp.zeros((1, width), F32)] * 2
        for start in range(0, rows, span):
            lines = slice(start, start + span)
            grad = total[lines]
            hat, scale = norm_stats(x_in[lines, :].astype(F32))
            out_ref[lines, :] = grad_in[lines, :] + norm_back(hat, scale, grad * gain)
            for index, value in enumerate((grad * hat, grad)):
                sums[index] = sums[index] + jnp.sum(value, axis=0, keepdims=True)
        ggain_ref[...], gshift_ref[...] = sums

    vector = ((1, width), F32, whole((1, width)))
    return call(
        kernel,
        (1,),
        weights.inputs()
        + [(value, ANY) for value in flat]
        + [(x, ANY), (grad_after, ANY), param(small, number, width)],
        [((rows, width), F32, whole((rows, width))), vector, vector],
        after=after,
        scratch=[
            pltpu.VMEM((count, rows, size), BF16),
            pltpu.VMEM((width, 3 * width), BF16),
            pltpu.VMEM((rows, width), BF16),
            pltpu.VMEM((rows, width), F32),
            pltpu.SemaphoreType.DMA((count, len(weights.plan))),
            pltpu.SemaphoreType.DMA((count + 2,)),
        ],
        cost=cost(6 * rows * width * width, 22 * rows * width),
        name="grad_input",
    )


def adamw(weight, first, second, grad, rate, decay):
    first_new = beta_one * first + (1.0 - beta_one) * grad
    second_new = beta_two * second + (1.0 - beta_two) * grad * grad
    first_hat = first_new / (1.0 - beta_one**STEP)
    second_hat = second_new / (1.0 - beta_two**STEP)
    weight_new = weight - rate * (first_hat / (jnp.sqrt(second_hat) + adam_eps) + decay * weight)
    return (weight_new, first_new, second_new)


def run_adam(core, state, groups, span, places, pick, earlier, after=()):
    half = groups[0][0].shape[1]
    count = len(places)
    table = jnp.array(places, jnp.int32)
    place = pl.BlockSpec((half, span), lambda p, h, c, t: (jnp.bitwise_xor(h, c[0]), t[p]))
    flat = [value for group in groups for value in group]

    def kernel(core_ref, table_ref, w_ref, m_ref, v_ref, *refs):
        w_out, m_out, v_out, grad_ref = refs[-4:]
        for side in range(2):
            mine = refs[side : 2 * len(groups) : 2]
            for block in range(count):

                @pl.when((pl.program_id(1) == side) & (pl.program_id(0) == block))
                def _(mine=mine, block=block):
                    start = 0
                    for value in pick(block, mine):
                        grad_ref[:, start : start + value.shape[1]] = value
                        start += value.shape[1]

        w_out[...], m_out[...], v_out[...] = adamw(
            w_ref[...], m_ref[...], v_ref[...], grad_ref[...].astype(F32), 0.05, 0.1
        )

    moved = 2 * half * count * span
    return call(
        kernel,
        (count, 2),
        [(value, place) for value in state] + [(value, whole(value.shape)) for value in flat],
        [(state[0].shape, F32, place)] * 3,
        after=after,
        reuse=[] if earlier is None else [(value, n) for n, value in enumerate(earlier)],
        prefetch=(core, table),
        scratch=[pltpu.VMEM((half, span), BF16)],
        cost=cost(20 * moved, 26 * moved),
        name="adam",
    )


def run_side(core, jobs, after=(), steps=4):
    counts = [(len(job[0]), len(job[1])) for job in jobs]
    total_in = sum(count[0] for count in counts)

    def kernel(core_ref, *refs):
        ins = refs[:total_in]
        outs = refs[total_in:]
        for job, (have, give) in zip(jobs, counts):
            more = (core_ref,) if "places" in job[2].__code__.co_varnames else ()
            job[2](ins[:have], outs[:give], *more)
            ins = ins[have:]
            outs = outs[give:]

    def spec(block, index):
        return pl.BlockSpec(block, lambda i, c: index(i, c))

    moved = sum(array.size * 2 for job in jobs for array, _, _ in job[0])
    results = call(
        kernel,
        (steps,),
        [(array, spec(block, index)) for job in jobs for array, block, index in job[0]],
        [(shape, dtype, spec(block, index)) for job in jobs for shape, dtype, block, index in job[1]],
        after=after,
        prefetch=(core,),
        cost=cost(0, 2 * moved),
        name="side",
    )
    split = []
    for _, give in counts:
        split.append(results[:give])
        results = results[give:]
    return split


def job_cast(rows, columns, by_core, steps):
    span = rows // steps
    total = sum(size for _, _, size in columns)
    ins = []
    for state, number, size in columns:
        index = lambda i, c, number=number: (c[0] * steps * by_core + i, number)
        ins.append((state, (span, size), index))
    outs = [((rows, total), BF16, (span, total), lambda i, c: (i, 0))]

    def run(have, give):
        start = 0
        for ref, (_, _, size) in zip(have, columns):
            give[0][:, start : start + size] = ref[...].astype(BF16)
            start += size

    return ins, outs, run


def job_join(pairs, steps):
    blocks, rows, size = pairs[0][0].shape[1:]
    span = rows // steps
    four = lambda i, c: (0, 0, i, 0)
    count = 2 * len(pairs)
    ins = [(value, (2, blocks, span, size), four) for pair in pairs for value in pair]
    outs = [((blocks, count, rows, size), BF16, (blocks, count, span, size), four)]

    def run(have, give):
        for number in range(len(pairs)):
            left, right = have[2 * number : 2 * number + 2]
            for side in range(2):
                for block in range(blocks):
                    give[0][block, 2 * number + side] = left[side, block] + right[side, block]

    return ins, outs, run


def job_copy(value, first, rows):
    size = value.shape[1]
    ins = [(value, value.shape, lambda i, c: (0, 0))]
    outs = [((rows, size), value.dtype, (rows, size), lambda i, c: (0, 0))]

    def run(have, give):
        give[0][...] = have[0][first : first + rows, :]

    return ins, outs, run


def job_add(left, right, steps):
    at = left.ndim - 2
    if left.shape[at] == 1:
        same = lambda i, c: (0,) * left.ndim

        def run_whole(have, give):
            give[0][...] = have[0][...] + have[1][...]

        return (
            [(left, left.shape, same), (right, right.shape, same)],
            [(left.shape, left.dtype, left.shape, same)],
            run_whole,
        )
    block = tuple(size // steps if axis == at else size for axis, size in enumerate(left.shape))
    index = lambda i, c: (0,) * at + (i, 0)

    def run(have, give):
        give[0][...] = have[0][...] + have[1][...]

    return [(left, block, index), (right, block, index)], [(left.shape, left.dtype, block, index)], run


def job_pick(own, received, steps):
    count, rows, size = own.shape
    block = (count, rows // steps, size)
    index = lambda i, c: (0, i, 0)

    def run(have, give, places):
        give[0][...] = jnp.where(places[2] == 1, have[0][...], have[1][...])

    return [(own, block, index), (received, block, index)], [(own.shape, own.dtype, block, index)], run


def job_sum(groups, keep, send, steps):
    _, blocks, rows, _ = groups[0][0].shape
    span = rows // steps
    total = sum(own.shape[3] for own, _ in groups)
    four = lambda i, c: (0, 0, i, 0)
    three = lambda i, c: (0, i, 0)
    ins = []
    for own, received in groups:
        size = own.shape[3]
        ins.append((own, (2, blocks, span, size), four))
        if len(received) == 1:
            ins.append((received[0], (2, blocks, span, size), four))
        else:
            ins += [(value, (blocks, span, size), three) for value in received]
    kept = len(keep[0])
    outs = [((2, kept, rows, total), BF16, (2, kept, span, total), four)]
    if len(send) == 1:
        gone = len(send[0])
        outs.append(((2, gone, rows, total), BF16, (2, gone, span, total), four))
    else:
        for side in range(2):
            if send[side]:
                gone = len(send[side])
                outs.append(((gone, rows, total), BF16, (gone, span, total), three))

    def run(have, give):
        start = 0
        for own, received in groups:
            size = own.shape[3]
            columns = slice(start, start + size)
            start += size
            for side in range(2):
                for block in range(blocks):
                    other = have[1][side, block] if len(received) == 1 else have[1 + side][block]
                    value = have[0][side, block] + other
                    if block in keep[side]:
                        give[0][side, keep[side].index(block), :, columns] = value
                    elif len(send) == 1:
                        give[1][side, send[0].index(block), :, columns] = value
                    else:
                        give[1 + side][send[side].index(block), :, columns] = value
            have = have[1 + len(received) :]

    return ins, outs, run


def job_params(rows, shards, small_size):
    ins = []
    for array, row in rows:
        if array.shape[0] == 1:
            ins.append((array, array.shape, lambda i, c: (0, 0)))
        else:
            size = array.shape[1]
            ins.append((array, (16, size), lambda i, c, row=row: (row // 16, 0)))
    shape = (1, shards * small_size)
    outs = [(shape, F32, shape, lambda i, c: (0, 0))]

    def run(have, give, places):
        for number, ref in enumerate(have):
            owner = jnp.bitwise_xor(places[1], number)
            start = pl.multiple_of(owner * small_size, LANES)
            value = ref[0:1, :small_size].astype(BF16).astype(F32)
            give[0][:, pl.ds(start, small_size)] = value

    return ins, outs, run


def job_lay(values):
    total = sum(value.shape[1] for value in values)
    same = lambda i, c: (0, 0)
    ins = [(value, value.shape, same) for value in values]

    def run(have, give):
        start = 0
        for ref in have:
            give[0][:, start : start + ref.shape[1]] = ref[...]
            start += ref.shape[1]

    return ins, [((1, total), F32, (1, total), same)], run


class Links:
    def __init__(self, sizes, shard_rows):
        self.replicas, self.shards = sizes
        dp = lax.axis_index("dp")
        self.shard = lax.axis_index("shard")
        self.core = lax.rem(dp, 2)
        place = dp // 2
        self.inner = (place > 0) & (place < sizes[0] // 2 - 1)
        self.core_arr = jnp.stack([self.core, self.shard, self.inner]).astype(jnp.int32)
        self.rows = shard_rows
        self.half = shard_rows // 2
        self.fast = sizes == (8, 4)

    def swap(self, value):
        return self.across_dp(value, 1)

    def across_dp(self, value, bit):
        return lax.ppermute(value, "dp", [(d, d ^ bit) for d in range(self.replicas)])

    def along_dp(self, value, step):
        hops = ([(0, 1), (3, 2)], [(1, 2), (2, 1)], [(1, 0), (2, 3)])[step]
        pairs = [(2 * a + core, 2 * b + core) for a, b in hops for core in range(2)]
        return lax.ppermute(value, "dp", pairs)

    def across_shard(self, value, bit):
        return lax.ppermute(value, "shard", [(s, s ^ bit) for s in range(self.shards)])

    def turned_offsets(self, around):
        blocks = jnp.arange(2 * self.shards, dtype=jnp.int32)
        owner = blocks // 2
        if around:
            owner = jnp.bitwise_xor(owner, self.shard)
        away = jnp.bitwise_xor(lax.rem(blocks, 2), self.core)
        return away * (self.shards * self.half) + owner * self.half

    def gather(self, half_rows):
        return lax.all_gather(half_rows, "shard", axis=0, tiled=True)

    def gathered(self, mine, behind=None):
        if behind is not None:
            mine, _ = lax.optimization_barrier((mine, behind))
        first = jnp.arange(self.shards, dtype=jnp.int32) * self.rows
        offs = jnp.concatenate([first + self.core * self.half, first + (1 - self.core) * self.half])
        stride = mine.shape[0] // self.shards
        plan = tuple((0, t * stride, self.half, t) for t in range(self.shards)) + tuple(
            (1, t * stride, self.half, self.shards + t) for t in range(self.shards)
        )
        return Weights((mine, self.swap(mine)), plan, offs.astype(jnp.int32))

    def over_dp(self, values):
        groups = [[d for d in range(self.replicas) if d % 2 == c] for c in range(2)]
        return lax.psum(values, "dp", axis_index_groups=groups)


class Gather:
    def __init__(self, links, half_rows, own):
        self.links = links
        self.own = own
        self.by_x = links.across_shard(half_rows, 1)
        self.by_y = links.across_shard(half_rows, 2)

    def jobs(self):
        part = self.links.half // 2
        rest = self.by_x.shape[0] - part
        return [job_copy(self.by_y, 0, part), job_copy(self.by_x, part, rest)]

    def forward(self, results):
        links = self.links
        self.far = (
            links.across_shard(results[0], 1),
            links.across_shard(results[1], 2),
        )
        self.near = (links.swap(self.by_x), links.swap(self.by_y))

    def weights(self):
        links = self.links
        half, rows = links.half, links.rows
        part = half // 2
        far = tuple(links.swap(value) for value in self.far)
        pieces = (self.own, self.by_x, self.by_y, *self.near, *self.far, *far)
        plan = ((0, 0, rows, 0),)
        plan += tuple((n, 0, half, n) for n in range(1, 5))
        plan += tuple((n, 0, part, n) for n in range(5, 9))
        at = lambda bits: jnp.bitwise_xor(links.shard, bits) * rows
        mine = links.core * half
        other = (1 - links.core) * half
        offs = [at(0), at(1) + mine, at(2) + mine, at(1) + other, at(2) + other]
        offs += [at(3) + mine, at(3) + mine + part, at(3) + other, at(3) + other + part]
        return Weights(pieces, plan, jnp.stack(offs).astype(jnp.int32))


class Reduce:
    def __init__(self, links, line):
        self.links = links
        self.line = line
        self.stage = 0
        self.groups = []

    def add(self, own, sib):
        shape = (2, self.links.shards, self.links.half, own.shape[2])
        self.groups.append((own.reshape(shape), (self.links.swap(sib).reshape(shape),)))
        return self

    def job(self, steps):
        if self.stage > 2:
            own, received = self.groups[0]
            if self.line and self.stage == 5:
                return job_pick(own, received, steps)
            return job_add(own, received, steps)
        blocks = self.groups[0][0].shape[1]
        odd = lambda block: block % 2 == 1
        late = lambda block: block >= blocks // 2
        goes = [odd, late]
        if blocks == 2:
            goes = [odd, odd]
        if blocks == 1:
            goes = [lambda block: False] * 2
        keep = [[block for block in range(blocks) if not go(block)] for go in goes]
        send = [[block for block in range(blocks) if go(block)] for go in goes]
        return job_sum(self.groups, keep, send, steps)

    def advance(self, results):
        links = self.links
        own = results[0]
        stage = self.stage
        self.stage += 1
        if stage < 2:
            bits = (1, 2) if stage == 0 else (2, 1)
            received = tuple(
                links.across_shard(value, bit) for value, bit in zip(results[1:], bits)
            )
            self.groups = [(own, received)]
            return
        if stage == 2:
            own = own.reshape(2, own.shape[2], own.shape[3])
        if self.line and stage < 5:
            self.groups = [(own, links.along_dp(own, stage - 2))]
        elif not self.line and stage < 4:
            self.groups = [(own, links.across_dp(own, 2 * (stage - 1)))]
        else:
            self.grads = (own, links.swap(own))


class Wide:
    def __init__(self, links, joined):
        self.links = links
        self.stage = 0
        count, half, size = joined.shape[1:]
        flat = joined.reshape(links.shards * count * half, size)
        mine = lax.psum_scatter(flat, "shard", scatter_dimension=0, tiled=True)
        self.own = mine.reshape(count, half, size)

    def send(self):
        before = self.own
        self.received = self.links.along_dp(before, 0)
        return before

    def job(self, steps):
        if self.stage == 2:
            return job_pick(self.own, self.received, steps)
        return job_add(self.own, self.received, steps)

    def advance(self, results):
        self.own = results[0]
        self.stage += 1
        if self.stage < 3:
            self.received = self.links.along_dp(self.own, self.stage)
        else:
            self.grads = (self.own, self.links.swap(self.own))


class Side:
    def __init__(self, links):
        self.links = links
        self.order = ()

    def jobs(self, jobs, steps=1, after=()):
        results = run_side(self.links.core_arr, jobs, after=(*self.order, *after), steps=steps)
        self.order = (results[0][0],)
        return [result[0] for result in results]

    def reduce(self, reduces, jobs=(), steps=2):
        work = [item.job(steps) for item in reduces] + list(jobs)
        results = run_side(self.links.core_arr, work, after=self.order, steps=steps)
        for item, result in zip(reduces, results):
            item.advance(result)
        self.order = (results[0][0],)
        return [result[0] for result in results[len(reduces) :]]

    def then(self, results):
        self.order = (results[0],)
        return results


def small_parts(small, width, hidden):
    bounds = [width] * 3 + [hidden] + [width] * 5
    parts = []
    start = 0
    for size in bounds:
        parts.append(small[:, start : start + size])
        start += size
    return parts


def body(sizes, *args):
    tokens, cotangent, lengths = args[:3]
    attn_state, mlp_state, small_state = args[3:6], args[6:9], args[9:12]
    rows, width = tokens.shape
    links = Links(sizes, attn_state[0].shape[0])
    half = links.half
    hidden = mlp_state[0].shape[1] // 2
    pairs = width // LANES
    pad = 16
    core_arr = links.core_arr
    by_owner = links.turned_offsets(False)
    around = links.turned_offsets(True) if links.fast else by_owner
    side = Side(links)

    ends = jnp.cumsum(lengths[0], dtype=jnp.int32)
    small_own = small_state[0][None]
    small_size = small_own.shape[1]
    (
        BIAS_Q,
        BIAS_V,
        BIAS_O,
        BIAS_UP,
    ) = range(4)
    BIAS_DN, GAIN_ONE, SHIFT_ONE, GAIN_TWO, SHIFT_TWO = range(
        BIAS_UP + hidden // width, BIAS_UP + hidden // width + 5
    )

    def first_job():
        ins = [
            (attn_state[0], (half, 3 * width), lambda i, c: (c[0], 0)),
            (small_own, (1, small_size), lambda i, c: (0, 0)),
        ]
        outs = [((half + pad, 3 * width), BF16, (half + pad, 3 * width), lambda i, c: (0, 0))]

        def job(have, give):
            give[0][:half] = have[0][...].astype(BF16)
            row = have[1][...].astype(BF16)
            give[0][half:, :small_size] = jnp.broadcast_to(row, (pad, small_size))

        return ins, outs, job

    blocks = 4
    block = hidden // blocks
    columns = [(attn_state[0], 3, width)]
    columns += [(mlp_state[0], number, block) for number in (0, 1, blocks, blocks + 1)]
    more_columns = [
        (mlp_state[0], number, block) for number in (2, 3, blocks + 2, blocks + 3)
    ]
    (first_half,) = side.jobs([first_job()])
    if links.fast:
        qkv_gather = Gather(links, first_half, None)
    else:
        qkv_weights = links.gathered(links.gather(first_half))
    dy, dyt, grad_bias_dn = side.then(run_cot(half, by_owner, ends, cotangent, after=side.order))
    if links.fast:
        (qkv_gather.own,) = side.jobs(
            [job_cast(links.rows, [(attn_state[0], 0, 3 * width)], 0, 4)], steps=4
        )
        qkv_gather.forward(side.jobs(qkv_gather.jobs()))
    (out_half,) = side.jobs([job_cast(half, columns, 1, 4)], steps=4)
    wide = links.gather(out_half)
    (feed_half,) = side.jobs([job_cast(half, more_columns, 1, 4)], steps=4)
    more_wide = links.gather(feed_half)
    if links.fast:
        qkv_weights = qkv_gather.weights()
        rows_of = [
            (small_own, 0),
            (qkv_gather.by_x, half),
            (qkv_gather.by_y, half),
            (qkv_gather.far[1], half // 2),
        ]
        (small,) = side.jobs([job_params(rows_of, links.shards, small_size)])
    else:
        small = qkv_weights.pieces[0].reshape(links.shards, half + pad, 3 * width)
        small = small[:, half, :small_size].astype(F32).reshape(1, -1)

    qkv, turned_one = side.then(
        run_qkv(
            half,
            qkv_weights,
            around,
            tokens,
            small,
            (BIAS_Q, BIAS_V, GAIN_ONE, SHIFT_ONE),
            after=side.order,
        )
    )
    attended = side.then(run_attend(ends, qkv, 0, pairs // 2, after=side.order))
    wide = links.gathered(wide, attended[1])
    mixed, lse = side.then(
        run_attend(ends, qkv, pairs // 2, pairs // 2, attended, after=(wide.pieces[0],))
    )
    after, low_two, turned_two, turned_mixed = side.then(
        run_after(
            half,
            wide,
            (around, by_owner),
            mixed,
            tokens,
            small,
            (BIAS_O, GAIN_TWO, SHIFT_TWO),
            after=side.order,
        )
    )

    passed, grad_bias_up, mlp_grads = [None], [], []
    feeds = [(0, 2 * block, wide.at(width), wide.at(width + 2 * block))]

    def feed(number):
        start, size, up_weights, down_weights = feeds[number]
        act, du, own, sib, gbias = side.then(
            run_feed(
                up_weights,
                down_weights,
                low_two,
                turned_two,
                dy,
                dyt,
                small,
                BIAS_UP * width + start,
                start,
                size,
                passed[-1],
                after=side.order,
            )
        )
        side.order = (own,)
        passed.append((act, du))
        grad_bias_up.append(gbias)
        shape = (2, links.shards, half, size)
        mlp_grads.append((own.reshape(shape), links.swap(sib).reshape(shape)))

    def join(pairs):
        return side.jobs([job_join(pairs, half // 16)], steps=half // 16)[0]

    feed(0)
    more_wide = links.gathered(more_wide, grad_bias_up[0])
    feeds += [
        (2 * block, block, more_wide, more_wide.at(2 * block)),
        (3 * block, block, more_wide.at(block), more_wide.at(3 * block)),
    ]
    feed(1)
    reduces = [Wide(links, join([mlp_grads[0]]))]
    feed(2)
    (
        grad_after,
        dmix,
        own_out,
        sib_out,
        grad_bias_o,
        grad_gain_two,
        grad_shift_two,
    ) = side.then(
        run_middle(
            [(item[1], item[2]) for item in feeds],
            wide,
            passed[-1][1],
            after,
            dy,
            small,
            GAIN_TWO,
            turned_mixed,
            after=side.order,
        )
    )
    reduces.append(Wide(links, join([mlp_grads[1], mlp_grads[2]])))
    if links.fast:
        reduces.append(Reduce(links, True).add(own_out, sib_out))
    else:
        reduces.append((own_out, sib_out))
    grads, biases = [], []

    def attend_back(first):
        dq, dk, dv, gq, gv = side.then(
            run_attend_back(ends, qkv, mixed, dmix, lse, first, pairs // 2, after=side.order)
        )
        grads.append((dq, dk, dv))
        biases.append((gq, gv))

    def project(group):
        own, sib = side.then(run_project(turned_one, *grads[group], after=side.order))
        if not links.fast:
            reduces.append((own, sib))
        elif group == 0:
            reduces[2].add(own, sib)
        else:
            reduces.append(Reduce(links, False).add(own, sib))

    def reduce(numbers, jobs=()):
        if links.fast:
            return side.reduce([reduces[number] for number in numbers], jobs)
        return side.jobs(jobs) if jobs else None

    attend_back(0)
    if links.fast:
        side.order += (reduces[0].send(),)
    project(0)
    attend_back(pairs // 2)
    reduce([0, 2])
    if links.fast:
        side.order += (reduces[1].send(),)
    project(1)
    reduce([2])
    grad_input, grad_gain_one, grad_shift_one = side.then(
        run_input(
            qkv_weights, grads, tokens, grad_after, small, GAIN_ONE, after=side.order
        )
    )
    small_grads = [biases[0][0], biases[1][0], biases[0][1], biases[1][1], grad_bias_o]
    small_grads += grad_bias_up
    small_grads += [grad_bias_dn, grad_gain_one, grad_shift_one, grad_gain_two, grad_shift_two]
    (grad_small,) = reduce([0, 1, 2, 3], [job_lay(small_grads)])
    output = run_output(
        [(item[1], item[3]) for item in feeds],
        passed[-1][0],
        after,
        small,
        BIAS_DN,
        after=side.order,
    )
    side.then([output])

    out_block = width // 2
    pick_mlp = (
        lambda number, arrays: [arrays[0][number]],
        lambda number, arrays: [arrays[0][number], arrays[0][2 + number]],
    )

    def pick_heads(number, arrays):
        skip = arrays[0].shape[2] - 3 * out_block // 2
        left, right = arrays[0][0], arrays[0][1]
        split = skip + out_block // 2
        return (
            [left[:, skip : skip + out_block]],
            [left[:, skip + out_block :], right[:, skip:split]],
            [right[:, split:]],
            [left[:, :skip]],
            [right[:, :skip]],
        )[number]

    def adam_attn(group, earlier):
        places = [0, 2, 4, 6, 7] if group == 0 else [1, 3, 5]
        return side.then(
            run_adam(
                core_arr,
                attn_state,
                [reduces[2 + group].grads],
                out_block,
                places,
                pick_heads,
                earlier,
                after=side.order,
            )
        )

    def adam_mlp(group, earlier):
        return side.then(
            run_adam(
                core_arr,
                mlp_state,
                [reduces[group].grads],
                2 * block,
                [group, blocks // 2 + group],
                pick_mlp[group],
                earlier,
                after=side.order,
            )
        )

    if links.fast:

        def step(numbers, move):
            (total,) = reduce(numbers, [job_add(grad_small, moved, 2)])
            return total, move(total) if move else None

        across = lambda bit: functools.partial(links.across_dp, bit=bit)
        reduce([0, 1, 2, 3])
        moved = links.across_shard(grad_small, 1)
        mlp_new = adam_mlp(0, None)
        grad_small, moved = step([1, 2, 3], functools.partial(links.across_shard, bit=2))
        mlp_new = adam_mlp(1, mlp_new)
        grad_small, moved = step([2, 3], links.swap)
        attn_new = adam_attn(0, None)
        grad_small, moved = step([3], across(2))
        grad_small, moved = step([], across(4))
        attn_new = adam_attn(1, attn_new)
        grad_small, _ = step([], None)
    else:
        blocked = lambda value: value.reshape(2, links.shards, half, value.shape[2])
        for number in range(2, len(reduces)):
            own, sib = reduces[number]
            pair = (blocked(own), blocked(links.swap(sib)))
            reduces[number] = Wide(links, join([pair]))
        for item in reduces:
            item.own = links.over_dp(item.own)
            item.grads = (item.own, links.swap(item.own))
        mine = jnp.concatenate([reduces[2].own, reduces[3].own], axis=2)
        reduces[2].grads = (mine, links.swap(mine))
        reduces[3] = reduces.pop()
        grad_small = lax.psum(grad_small, ("dp", "shard"))
        mlp_new = adam_mlp(1, adam_mlp(0, None))
        attn_new = adam_attn(1, adam_attn(0, None))
    grad_small = lax.dynamic_slice_in_dim(grad_small, links.shard * small_size, small_size, 1)[0]
    small_new = adamw(*small_state, grad_small, 0.4, 0.0)
    return (output, grad_input, *attn_new, *mlp_new, *small_new)


def solution(mesh):
    tokens = P(("dp", "shard"), None)
    state = P("shard", None)
    vector = P("shard")
    return jax.shard_map(
        functools.partial(body, (mesh.shape["dp"], mesh.shape["shard"])),
        mesh=mesh,
        in_specs=(tokens,) * 3 + (state,) * 6 + (vector,) * 3,
        out_specs=(tokens,) * 2 + (state,) * 6 + (vector,) * 3,
        check_vma=False,
    )
```

time: 1240 us -> 535 us (0.43)
  waiting for transfers between devices: 647 us -> 101 us
  Pallas kernels: 0 us -> 352 us
  matrix products: 289 us -> 0 us
  other arithmetic: 164 us -> 5.5 us
  local copies, waits for them, and re-layouts: 64.7 us -> 1.32 us
  blocking collectives: 53.5 us -> 0 us
  starting transfers between devices: 0.21 us -> 51.3 us
    reduce_scatter x2, waiting for transfers between devices: 386 us -> 0.03 us  [__init__(): mine = lax.psum_scatter(flat, 'shard', scatter_dimension=0, tiled=True)]
    pallas_call x0 -> x36, Pallas kernels: none -> 352 us  [call(): pl.pallas_call(run, grid_spec=pltpu.PrefetchScalarGridSpec(num_scalar_pre...]
    dot_general x24 -> x0, matrix products: 289 us -> none  [the longest x4 50.6 us: rows_product(): lax.dot_general(left, right, (((0,), (0,)), ((), ())), preferred_element_...]
    psum x1 -> x0, waiting for transfers between devices: 159 us -> none  [settle(): summed = lax.psum((owned[0], owned[1], owned[2]), 'dp')]
    all_gather x2, waiting for transfers between devices: 102 us -> 15.6 us  [gather(): return lax.all_gather(half_rows, 'shard', axis=0, tiled=True)]
    ppermute x0 -> x44, waiting for transfers between devices: none -> 85 us  [the longest x14 41.7 us: across_shard(): lax.ppermute(value, 'shard', [(s, s ^ bit) for s in range(self.shards)])]
    ppermute x0 -> x44, starting transfers between devices: none -> 51.1 us  [the longest x9 27.8 us: along_dp(): return lax.ppermute(value, 'dp', pairs)]
    convert_element_type x7 -> x0, other arithmetic: 50.2 us -> none  [the longest x2 36.6 us: attend_backward(): grad_scores = (probs * (grad_probs - inner)).astype(jnp.bfloat16)]
  transfers between devices with their start and end apart: 5 -> 48, of which waited for: 5 -> 14; matrix products, arithmetic and copies ran while one was open for 20% -> 1% of each run, Pallas kernels for 0% -> 58%
where the time goes in v1:
time: 535 us; the launch traced here: 525 us
  Pallas kernels  352 us (66%)
  waiting for transfers between devices  101 us (19%)
  starting transfers between devices  51.3 us (10%)
  between operations  14.6 us (3%)
  other arithmetic  5.5 us (1%)
    pallas_call x36, Pallas kernels, call(): pl.pallas_call(run, grid_spec=pltpu.PrefetchScalarGridSpec(num_scalar_pre...  352 us
    ppermute x14, waiting for transfers between devices, across_shard(): lax.ppermute(value, 'shard', [(s, s ^ bit) for s in range(self.shards)])  41.7 us
    ppermute x21, waiting for transfers between devices, across_dp(): lax.ppermute(value, 'dp', [(d, d ^ bit) for d in range(self.replicas)])  31 us
    ppermute x9, starting transfers between devices, along_dp(): return lax.ppermute(value, 'dp', pairs)  27.8 us
    ppermute x14, starting transfers between devices, across_shard(): lax.ppermute(value, 'shard', [(s, s ^ bit) for s in range(self.shards)])  15.7 us
    all_gather x2, waiting for transfers between devices, gather(): return lax.all_gather(half_rows, 'shard', axis=0, tiled=True)  15.6 us
    ppermute x9, waiting for transfers between devices, along_dp(): return lax.ppermute(value, 'dp', pairs)  12.2 us
  transfers between devices with their start and end apart: 48, of which 14 were waited for; matrix products, arithmetic and copies ran while one was open for 1% of the time, Pallas kernels for 58%

profile of v1, /device:TPU:0, one launch (start us, length us, event | category | flops | bytes accessed | tf_op | source)
XLA Modules:
  0.0 525.4 jit_solution(6017223203571692516)
XLA Ops:
  26.4 7.5 %collective-permute-done.refs_1_.refs_3_ = bf16[144,3072]{1,0:T(8,128)(2,1)} collective-permute-done((bf16[144,3072]{1,0:T(8,128)(2,1)}, bf16[144,3072]{1,0:T(8,128)(2,1)}, u32[]{:S(2)}, u32[]{:S(2)}) %collective-permute-start) | collective-permute-done | bytes 884768 | tf_op jit(solution)/shard_map/ppermute | solution.py:1116
  49.9 16.6 %collective-permute-done.5.refs_4_.refs_7_ = bf16[80,3072]{1,0:T(8,128)(2,1)} collective-permute-done((bf16[80,3072]{1,0:T(8,128)(2,1)}, bf16[80,3072]{1,0:T(8,128)(2,1)}, u32[]{:S(2)}, u32[]{:S(2)}) %collective-permute-start.5) | collective-permute-done | bytes 491552 | tf_op jit(solution)/shard_map/ppermute | solution.py:1116
  70.5 14.4 %qkv.1 = (bf16[1024,3072]{1,0:T(8,128)(2,1)}, bf16[1024,1024]{1,0:T(8,128)(2,1)}) custom-call(s32[9]{0:T(128)} %stack.59.refs_0_, bf16[256,3072]{1,0:T(8,128)(2,1)} %side.18.refs_3_.refs_1_, bf16[144,3072]{1,0:T(8,128)(2,1)} %collective-permute-done.1.refs_2_, bf16[144,3072]{1,0:T(8,128)(2,1)} %collective-permute-done.refs_1_.refs_3_, ...), custom_call_target="tpu_custom_call" | custom-call | tf_op jit(solution)/shard_map/qkv/pallas_call | solution.py:60
  84.8 12.6 %attend.2 = (bf16[1024,1024]{1,0:T(8,128)(2,1)}, f32[8,2,1024]{2,1,0:T(2,128)}) custom-call(s32[4]{0:T(128)} %bitcast.56, bf16[1024,3072]{1,0:T(8,128)(2,1)} %get-tuple-element.111.refs_1_.refs_2_.refs_3_.refs_4_, bf16[1024,3072]{1,0:T(8,128)(2,1)} %get-tuple-element.111.refs_1_.refs_2_.refs_3_.refs_4_, ...), custom_call_target="tpu_custom_call" | custom-call | tf_op jit(solution)/shard_map/attend/pallas_call | solution.py:60
  97.4 13.7 %all-gather.3.cloned.1.call-done.refs_4_.refs_1_.refs_13_ = bf16[512,5120]{1,0:T(8,128)(2,1)} async-done(((bf16[128,5120]{1,0:T(8,128)(2,1)}), bf16[512,5120]{1,0:T(8,128)(2,1)}) %all-gather.3.cloned.1.call-update) | async-done | bytes 5242896 | tf_op jit(solution)/shard_map/all_gather | solution.py:1127
  111.7 12.8 %attend.3 = (bf16[1024,1024]{1,0:T(8,128)(2,1)}, f32[8,2,1024]{2,1,0:T(2,128)}) custom-call(s32[4]{0:T(128)} %bitcast.57, bf16[1024,3072]{1,0:T(8,128)(2,1)} %get-tuple-element.111.refs_1_.refs_2_.refs_3_.refs_4_, bf16[1024,3072]{1,0:T(8,128)(2,1)} %get-tuple-element.111.refs_1_.refs_2_.refs_3_.refs_4_, ...), custom_call_target="tpu_custom_call", output_to_operand_aliasing={{0}: (5, {}), {1}: (6, {})} | custom-call | tf_op jit(solution)/shard_map/attend/pallas_call | solution.py:60
  124.5 10.3 %after.1 = (f32[1024,1024]{1,0:T(8,128)}, bf16[1024,1024]{1,0:T(8,128)(2,1)}, bf16[1024,1024]{1,0:T(8,128)(2,1)}, bf16[1024,1024]{1,0:T(8,128)(2,1)}) custom-call(s32[8]{0:T(128)} %pad_add_fusion.refs_0_.refs_3_.refs_6_.refs_9_.refs_12_, bf16[512,5120]{1,0:T(8,128)(2,1)} %all-gather.3.cloned.1.call-done.refs_4_.refs_1_.refs_13_, ...), custom_call_target="tpu_custom_call" | custom-call | tf_op jit(solution)/shard_map/after/pallas_call | solution.py:60
  134.8 28.9 %feed.3 = (bf16[1024,4096]{1,0:T(8,128)(2,1)}, bf16[1024,4096]{1,0:T(8,128)(2,1)}, bf16[2,512,2048]{2,1,0:T(8,128)(2,1)}, bf16[2,512,2048]{2,1,0:T(8,128)(2,1)}, f32[1,2048]{1,0:T(1,128)}) custom-call(s32[8]{0:T(128)} %pad_add_fusion.refs_0_.refs_3_.refs_6_.refs_9_.refs_12_, bf16[512,5120]{1,0:T(8,128)(2,1)} %all-gather.3.cloned.1.call-done.refs_4_.refs_1_.refs_13_, ...), custom_call_target="tpu_custom_call" | custom-call | tf_op jit(solution)/shard_map/feed/pallas_call | solution.py:60
  173.2 17.3 %feed.4 = (bf16[1024,4096]{1,0:T(8,128)(2,1)}, bf16[1024,4096]{1,0:T(8,128)(2,1)}, bf16[2,512,1024]{2,1,0:T(8,128)(2,1)}, bf16[2,512,1024]{2,1,0:T(8,128)(2,1)}, f32[1,1024]{1,0:T(1,128)}) custom-call(s32[8]{0:T(128)} %pad_add_fusion.refs_0_.refs_3_.refs_6_.refs_9_.refs_12_, ...), custom_call_target="tpu_custom_call", output_to_operand_aliasing={{0}: (12, {}), {1}: (13, {})} | custom-call | tf_op jit(solution)/shard_map/feed/pallas_call | solution.py:60
  190.5 8.3 %side.23.refs_11_ = bf16[4,2,128,2048]{3,2,1,0:T(8,128)(2,1)} custom-call(s32[3]{0:T(128)} %pad_add_fusion.1.refs_0_, bf16[2,4,128,2048]{3,2,1,0:T(8,128)(2,1)} %bitcast.36, bf16[2,4,128,2048]{3,2,1,0:T(8,128)(2,1)} %bitcast.16.refs_2_, bf16[2,512,1024]{2,1,0:T(8,128)(2,1)} %get-tuple-element.126.refs_3_), custom_call_target="tpu_custom_call" | custom-call | tf_op jit(solution)/shard_map/side/pallas_call | solution.py:60
  198.9 25.7 %feed.5 = (bf16[1024,4096]{1,0:T(8,128)(2,1)}, bf16[1024,4096]{1,0:T(8,128)(2,1)}, bf16[2,512,1024]{2,1,0:T(8,128)(2,1)}, bf16[2,512,1024]{2,1,0:T(8,128)(2,1)}, f32[1,1024]{1,0:T(1,128)}) custom-call(s32[8]{0:T(128)} %pad_add_fusion.refs_0_.refs_3_.refs_6_.refs_9_.refs_12_, ...), custom_call_target="tpu_custom_call", output_to_operand_aliasing={{0}: (12, {}), {1}: (13, {})} | custom-call | tf_op jit(solution)/shard_map/feed/pallas_call | solution.py:60
  225.1 24.5 %middle.1 = (f32[1024,1024]{1,0:T(8,128)}, bf16[1024,1024]{1,0:T(8,128)(2,1)}, bf16[2,512,512]{2,1,0:T(8,128)(2,1)}, bf16[2,512,512]{2,1,0:T(8,128)(2,1)}, f32[1...) custom-call(s32[8]{0:T(128)} %pad_add_fusion.refs_0_.refs_3_.refs_6_.refs_9_.refs_12_, ...), custom_call_target="tpu_custom_call" | custom-call | tf_op jit(solution)/shard_map/middle/pallas_call | solution.py:60
  249.7 8.2 %side.24.refs_7_ = bf16[4,4,128,1024]{3,2,1,0:T(8,128)(2,1)} custom-call(s32[3]{0:T(128)} %pad_add_fusion.1.refs_0_, bf16[2,4,128,1024]{3,2,1,0:T(8,128)(2,1)} %bitcast.38, bf16[2,4,128,1024]{3,2,1,0:T(8,128)(2,1)} %bitcast.22.refs_2_, bf16[2,4,128,1024]{3,2,1,0:T(8,128)(2,1)} %bitcast.37, bf16[2,4,128,1024]{3,2,1,0:T(8,128)(2,1)} %bitcast.24.refs_4_, ...), custom_call_target="tpu_custom_call" | custom-call | tf_op jit(solution)/shard_map/side/pallas_call | solution.py:60
  258.0 18.8 %attend_back.2 = (bf16[1024,512]{1,0:T(8,128)(2,1)}, bf16[1024,512]{1,0:T(8,128)(2,1)}, bf16[1024,512]{1,0:T(8,128)(2,1)}, f32[1,512]{1,0:T(1,128)}, f32[1,512]{1,0:T(1,128)}) custom-call(s32[4]{0:T(128)} %bitcast.58, bf16[1024,3072]{1,0:T(8,128)(2,1)} %get-tuple-element.111.refs_1_.refs_2_.refs_3_.refs_4_, ...), custom_call_target="tpu_custom_call" | custom-call | tf_op jit(solution)/shard_map/attend_back/pallas_call | solution.py:60
  288.8 19.2 %attend_back.3 = (bf16[1024,512]{1,0:T(8,128)(2,1)}, bf16[1024,512]{1,0:T(8,128)(2,1)}, bf16[1024,512]{1,0:T(8,128)(2,1)}, f32[1,512]{1,0:T(1,128)}, f32[1,512]{1,0:T(1,128)}) custom-call(s32[4]{0:T(128)} %bitcast.59, bf16[1024,3072]{1,0:T(8,128)(2,1)} %get-tuple-element.111.refs_1_.refs_2_.refs_3_.refs_4_, ...), custom_call_target="tpu_custom_call" | custom-call | tf_op jit(solution)/shard_map/attend_back/pallas_call | solution.py:60
  333.9 14.9 %collective-permute-done.18.refs_2_ = bf16[2,128,1280]{2,1,0:T(8,128)(2,1)} collective-permute-done((bf16[2,128,1280]{2,1,0:T(8,128)(2,1)}, bf16[2,128,1280]{2,1,0:T(8,128)(2,1)}, u32[]{:S(2)}, u32[]{:S(2)}) %collective-permute-start.18) | collective-permute-done | bytes 655392 | tf_op jit(solution)/shard_map/ppermute | solution.py:1116
  355.5 17.6 %grad_input.1 = (f32[1024,1024]{1,0:T(8,128)}, f32[1,1024]{1,0:T(1,128)}, f32[1,1024]{1,0:T(1,128)}) custom-call(s32[9]{0:T(128)} %stack.59.refs_0_, bf16[256,3072]{1,0:T(8,128)(2,1)} %side.18.refs_3_.refs_1_, bf16[144,3072]{1,0:T(8,128)(2,1)} %collective-permute-done.1.refs_2_, bf16[144,3072]{1,0:T(8,128)(2,1)} %collective-permute-done.refs_1_.refs_3_, ...), custom_call_target="tpu_custom_call" | custom-call | tf_op jit(solution)/shard_map/grad_input/pallas_call | solution.py:60
  391.8 16.7 %output.1.refs_10_ = bf16[1024,1024]{1,0:T(8,128)(2,1)} custom-call(s32[8]{0:T(128)} %pad_add_fusion.refs_0_.refs_3_.refs_6_.refs_9_.refs_12_, bf16[512,5120]{1,0:T(8,128)(2,1)} %all-gather.3.cloned.1.call-done.refs_4_.refs_1_.refs_13_, bf16[512,5120]{1,0:T(8,128)(2,1)} %collective-permute-done.8.refs_2_.refs_5_.refs_14_, ...), custom_call_target="tpu_custom_call" | custom-call | tf_op jit(solution)/shard_map/output/pallas_call | solution.py:60
  419.6 12.4 %adam.4 = (f32[256,8192]{1,0:T(8,128)}, f32[256,8192]{1,0:T(8,128)}, f32[256,8192]{1,0:T(8,128)}) custom-call(s32[3]{0:T(128)} %pad_add_fusion.1.refs_0_, s32[2]{0:T(128)} %iota_multiply_fusion.1.refs_1_, f32[256,8192]{1,0:T(8,128)} %refs_2_.11, f32[256,8192]{1,0:T(8,128)} %refs_3_.9, f32[256,8192]{1,0:T(8,128)} %refs_4_.9, ...), custom_call_target="tpu_custom_call" | custom-call | tf_op jit(solution)/shard_map/adam/pallas_call | solution.py:60
  432.1 9.4 %collective-permute-done.28.refs_2_ = bf16[4,128,1024]{2,1,0:T(8,128)(2,1)} collective-permute-done((bf16[4,128,1024]{2,1,0:T(8,128)(2,1)}, bf16[4,128,1024]{2,1,0:T(8,128)(2,1)}, u32[]{:S(2)}, u32[]{:S(2)}) %collective-permute-start.28) | collective-permute-done | bytes 1048608 | tf_op jit(solution)/shard_map/ppermute | solution.py:1113
  451.2 12.4 %adam.5 = (f32[256,8192]{1,0:T(8,128)}, f32[256,8192]{1,0:T(8,128)}, f32[256,8192]{1,0:T(8,128)}) custom-call(s32[3]{0:T(128)} %pad_add_fusion.1.refs_0_, s32[2]{0:T(128)} %constant.89.clone.refs_1_, f32[256,8192]{1,0:T(8,128)} %refs_2_.11, f32[256,8192]{1,0:T(8,128)} %refs_3_.9, ...), custom_call_target="tpu_custom_call", output_to_operand_aliasing={{0}: (8, {}), {1}: (9, {}), {2}: (10, {})} | custom-call | tf_op jit(solution)/shard_map/adam/pallas_call | solution.py:60
  463.6 9.7 %collective-permute-done.35.refs_4_ = bf16[2,128,768]{2,1,0:T(8,128)(2,1)} collective-permute-done((bf16[2,128,768]{2,1,0:T(8,128)(2,1)}, bf16[2,128,768]{2,1,0:T(8,128)(2,1)}, u32[]{:S(2)}, u32[]{:S(2)}) %collective-permute-start.35) | collective-permute-done | bytes 393248 | tf_op jit(solution)/shard_map/ppermute | solution.py:1108
  479.0 10.3 %adam.6 = (f32[256,4096]{1,0:T(8,128)}, f32[256,4096]{1,0:T(8,128)}, f32[256,4096]{1,0:T(8,128)}) custom-call(s32[3]{0:T(128)} %pad_add_fusion.1.refs_0_, s32[5]{0:T(128)} %constant.90.clone.refs_1_, f32[256,4096]{1,0:T(8,128)} %refs_2_.13, f32[256,4096]{1,0:T(8,128)} %refs_3_.11, f32[256,4096]{1,0:T(8,128)} %refs_4_.11, ...), custom_call_target="tpu_custom_call" | custom-call | tf_op jit(solution)/shard_map/adam/pallas_call | solution.py:60
  489.3 8.1 %collective-permute-done.38.refs_2_ = bf16[2,128,768]{2,1,0:T(8,128)(2,1)} collective-permute-done((bf16[2,128,768]{2,1,0:T(8,128)(2,1)}, bf16[2,128,768]{2,1,0:T(8,128)(2,1)}, u32[]{:S(2)}, u32[]{:S(2)}) %collective-permute-start.38) | collective-permute-done | bytes 393248 | tf_op jit(solution)/shard_map/ppermute | solution.py:1108
  (122 shorter events, 160.4 us)
Async XLA Ops:
  7.2 103.9 %all-gather.3.cloned.1.call-start = ((), (), s32[]{:S(2)}) async-start(), calls=%async_computation.2 | async-start | bytes 6553600 | tf_op jit(solution)/shard_map/all_gather | solution.py:1127
  11.0 22.9 %collective-permute-start = (bf16[144,3072]{1,0:T(8,128)(2,1)}, bf16[144,3072]{1,0:T(8,128)(2,1)}, u32[]{:S(2)}, u32[]{:S(2)}) collective-permute-start(bf16[144,3072]{1,0:T(8,128)(2,1)} %side.17.refs_3_), channel_id=1, source_target_pairs={{0,2},{1,3},{2,0},{3,1},{4,6},{5,7},{6,4},{7,5},{8,10},{9,11},{10,... | collective-permute-start | bytes 2654216 | tf_op jit(solution)/shard_map/ppermute | solution.py:1116
  14.0 21.4 %collective-permute-start.1 = (bf16[144,3072]{1,0:T(8,128)(2,1)}, bf16[144,3072]{1,0:T(8,128)(2,1)}, u32[]{:S(2)}, u32[]{:S(2)}) collective-permute-start(bf16[144,3072]{1,0:T(8,128)(2,1)} %side.17.refs_3_), channel_id=1, source_target_pairs={{0,1},{1,0},{2,3},{3,2},{4,5},{5,4},{6,7},{7,6},{8,9},{9,8},{10,11... | collective-permute-start | bytes 2654216 | tf_op jit(solution)/shard_map/ppermute | solution.py:1116
  42.9 122.7 %all-gather.5.cloned.1.call-start = ((), (), s32[]{:S(2)}) async-start(), calls=%async_computation.3 | async-start | bytes 5242880 | tf_op jit(solution)/shard_map/all_gather | solution.py:1127
  47.3 229.5 %reduce-scatter.3.cloned.1.call-start = ((), (), s32[]{:S(2)}) async-start(), calls=%async_computation.4 | async-start | bytes 5242880 | tf_op jit(solution)/shard_map/reduce_scatter | solution.py:1240
  47.7 22.8 %collective-permute-start.2 = (bf16[144,3072]{1,0:T(8,128)(2,1)}, bf16[144,3072]{1,0:T(8,128)(2,1)}, u32[]{:S(2)}, u32[]{:S(2)}) collective-permute-start(bf16[144,3072]{1,0:T(8,128)(2,1)} %collective-permute-done.1.refs_2_), channel_id=1, source_target_pairs={{0,4},{4,0},{8,12},{12,8},{16,20},{20,16},{24,28},{28,24},{1,5},{5... | collective-permute-start | bytes 2654216 | tf_op jit(solution)/shard_map/ppermute | solution.py:1108
  47.7 22.8 %collective-permute-start.3 = (bf16[144,3072]{1,0:T(8,128)(2,1)}, bf16[144,3072]{1,0:T(8,128)(2,1)}, u32[]{:S(2)}, u32[]{:S(2)}) collective-permute-start(bf16[144,3072]{1,0:T(8,128)(2,1)} %collective-permute-done.refs_1_.refs_3_), channel_id=1, source_target_pairs={{0,4},{4,0},{8,12},{12,8},{16,20},{20,16},{24,28},{28,24},{1,5},{5... | collective-permute-start | bytes 2654216 | tf_op jit(solution)/shard_map/ppermute | solution.py:1108
  165.7 24.8 %collective-permute-start.10 = (bf16[2,512,2048]{2,1,0:T(8,128)(2,1)}, bf16[2,512,2048]{2,1,0:T(8,128)(2,1)}, u32[]{:S(2)}, u32[]{:S(2)}) collective-permute-start(bf16[2,512,2048]{2,1,0:T(8,128)(2,1)} %get-tuple-element.123), channel_id=1, source_target_pairs={{0,4},{4,0},{8,12},{12,8},{16,20},{20,16},{24,28},{28,24},{1,5},{5... | collective-permute-start | bytes 12582920 | tf_op jit(solution)/shard_map/ppermute | solution.py:1108
  198.8 117.3 %reduce-scatter.5.cloned.1.call-start = ((), (), s32[]{:S(2)}) async-start(), calls=%async_computation.5 | async-start | bytes 5242880 | tf_op jit(solution)/shard_map/reduce_scatter | solution.py:1240
  224.6 25.1 %collective-permute-start.14 = (bf16[2,512,1024]{2,1,0:T(8,128)(2,1)}, bf16[2,512,1024]{2,1,0:T(8,128)(2,1)}, u32[]{:S(2)}, u32[]{:S(2)}) collective-permute-start(bf16[2,512,1024]{2,1,0:T(8,128)(2,1)} %get-tuple-element.139), channel_id=1, source_target_pairs={{0,4},{4,0},{8,12},{12,8},{16,20},{20,16},{24,28},{28,24},{1,5},{5... | collective-permute-start | bytes 6291464 | tf_op jit(solution)/shard_map/ppermute | solution.py:1108
  224.7 25.0 %collective-permute-start.13 = (bf16[2,512,1024]{2,1,0:T(8,128)(2,1)}, bf16[2,512,1024]{2,1,0:T(8,128)(2,1)}, u32[]{:S(2)}, u32[]{:S(2)}) collective-permute-start(bf16[2,512,1024]{2,1,0:T(8,128)(2,1)} %get-tuple-element.138), channel_id=1, source_target_pairs={{0,4},{4,0},{8,12},{12,8},{16,20},{20,16},{24,28},{28,24},{1,5},{5... | collective-permute-start | bytes 6291464 | tf_op jit(solution)/shard_map/ppermute | solution.py:1108
  283.9 27.0 %collective-permute-start.15 = (bf16[2,512,768]{2,1,0:T(8,128)(2,1)}, bf16[2,512,768]{2,1,0:T(8,128)(2,1)}, u32[]{:S(2)}, u32[]{:S(2)}) collective-permute-start(bf16[2,512,768]{2,1,0:T(8,128)(2,1)} %get-tuple-element.145), channel_id=1, source_target_pairs={{0,4},{4,0},{8,12},{12,8},{16,20},{20,16},{24,28},{28,24},{1,5},{5... | collective-permute-start | bytes 4718600 | tf_op jit(solution)/shard_map/ppermute | solution.py:1108
  284.1 24.0 %collective-permute-start.12 = (bf16[2,512,512]{2,1,0:T(8,128)(2,1)}, bf16[2,512,512]{2,1,0:T(8,128)(2,1)}, u32[]{:S(2)}, u32[]{:S(2)}) collective-permute-start(bf16[2,512,512]{2,1,0:T(8,128)(2,1)} %get-tuple-element.134), channel_id=1, source_target_pairs={{0,4},{4,0},{8,12},{12,8},{16,20},{20,16},{24,28},{28,24},{1,5},{5... | collective-permute-start | bytes 3145736 | tf_op jit(solution)/shard_map/ppermute | solution.py:1108
  284.4 26.4 %collective-permute-start.11 = (bf16[2,128,2048]{2,1,0:T(8,128)(2,1)}, bf16[2,128,2048]{2,1,0:T(8,128)(2,1)}, u32[]{:S(2)}, u32[]{:S(2)}) collective-permute-start(bf16[2,128,2048]{2,1,0:T(8,128)(2,1)} %bitcast.45), channel_id=1, source_target_pairs={{0,8},{4,12},{24,16},{28,20},{1,9},{5,13},{25,17},{29,21},{2,10},{... | collective-permute-start | bytes 3145736 | tf_op jit(solution)/shard_map/ppermute | solution.py:1113
  323.1 50.0 %collective-permute-start.22 = (bf16[2,512,768]{2,1,0:T(8,128)(2,1)}, bf16[2,512,768]{2,1,0:T(8,128)(2,1)}, u32[]{:S(2)}, u32[]{:S(2)}) collective-permute-start(bf16[2,512,768]{2,1,0:T(8,128)(2,1)} %get-tuple-element.157), channel_id=1, source_target_pairs={{0,4},{4,0},{8,12},{12,8},{16,20},{20,16},{24,28},{28,24},{1,5},{5... | collective-permute-start | bytes 4718600 | tf_op jit(solution)/shard_map/ppermute | solution.py:1108
  323.1 50.0 %collective-permute-start.16 = (bf16[2,128,2048]{2,1,0:T(8,128)(2,1)}, bf16[2,128,2048]{2,1,0:T(8,128)(2,1)}, u32[]{:S(2)}, u32[]{:S(2)}) collective-permute-start(bf16[2,128,2048]{2,1,0:T(8,128)(2,1)} %get-tuple-element.147.refs_4_.refs_1_), channel_id=1, source_target_pairs={{8,16},{12,20},{16,8},{20,12},{9,17},{13,21},{17,9},{21,13},{10,18... | collective-permute-start | bytes 3145736 | tf_op jit(solution)/shard_map/ppermute | solution.py:1113
  324.8 48.3 %collective-permute-start.17 = (bf16[4,128,1024]{2,1,0:T(8,128)(2,1)}, bf16[4,128,1024]{2,1,0:T(8,128)(2,1)}, u32[]{:S(2)}, u32[]{:S(2)}) collective-permute-start(bf16[4,128,1024]{2,1,0:T(8,128)(2,1)} %bitcast.42), channel_id=1, source_target_pairs={{0,8},{4,12},{24,16},{28,20},{1,9},{5,13},{25,17},{29,21},{2,10},{... | collective-permute-start | bytes 3145736 | tf_op jit(solution)/shard_map/ppermute | solution.py:1113
  379.4 29.2 %collective-permute-start.23 = (bf16[2,128,2048]{2,1,0:T(8,128)(2,1)}, bf16[2,128,2048]{2,1,0:T(8,128)(2,1)}, u32[]{:S(2)}, u32[]{:S(2)}) collective-permute-start(bf16[2,128,2048]{2,1,0:T(8,128)(2,1)} %get-tuple-element.171.refs_15_.refs_1_), channel_id=1, source_target_pairs={{8,0},{12,4},{16,24},{20,28},{9,1},{13,5},{17,25},{21,29},{10,2},{... | collective-permute-start | bytes 3145736 | tf_op jit(solution)/shard_map/ppermute | solution.py:1113
  380.7 27.9 %collective-permute-start.24 = (bf16[4,128,1024]{2,1,0:T(8,128)(2,1)}, bf16[4,128,1024]{2,1,0:T(8,128)(2,1)}, u32[]{:S(2)}, u32[]{:S(2)}) collective-permute-start(bf16[4,128,1024]{2,1,0:T(8,128)(2,1)} %get-tuple-element.172.refs_3_), channel_id=1, source_target_pairs={{8,16},{12,20},{16,8},{20,12},{9,17},{13,21},{17,9},{21,13},{10,18... | collective-permute-start | bytes 3145736 | tf_op jit(solution)/shard_map/ppermute | solution.py:1113
  382.3 26.2 %collective-permute-start.25 = (bf16[2,128,1280]{2,1,0:T(8,128)(2,1)}, bf16[2,128,1280]{2,1,0:T(8,128)(2,1)}, u32[]{:S(2)}, u32[]{:S(2)}) collective-permute-start(bf16[2,128,1280]{2,1,0:T(8,128)(2,1)} %bitcast.48), channel_id=1, source_target_pairs={{0,8},{4,12},{24,16},{28,20},{1,9},{5,13},{25,17},{29,21},{2,10},{... | collective-permute-start | bytes 1966088 | tf_op jit(solution)/shard_map/ppermute | solution.py:1113
  413.7 27.8 %collective-permute-start.28 = (bf16[4,128,1024]{2,1,0:T(8,128)(2,1)}, bf16[4,128,1024]{2,1,0:T(8,128)(2,1)}, u32[]{:S(2)}, u32[]{:S(2)}) collective-permute-start(bf16[4,128,1024]{2,1,0:T(8,128)(2,1)} %get-tuple-element.177.refs_1_), channel_id=1, source_target_pairs={{8,0},{12,4},{16,24},{20,28},{9,1},{13,5},{17,25},{21,29},{10,2},{... | collective-permute-start | bytes 3145736 | tf_op jit(solution)/shard_map/ppermute | solution.py:1113
  445.5 27.8 %collective-permute-start.34 = (bf16[2,128,1280]{2,1,0:T(8,128)(2,1)}, bf16[2,128,1280]{2,1,0:T(8,128)(2,1)}, u32[]{:S(2)}, u32[]{:S(2)}) collective-permute-start(bf16[2,128,1280]{2,1,0:T(8,128)(2,1)} %get-tuple-element.185.refs_1_), channel_id=1, source_target_pairs={{8,0},{12,4},{16,24},{20,28},{9,1},{13,5},{17,25},{21,29},{10,2},{... | collective-permute-start | bytes 1966088 | tf_op jit(solution)/shard_map/ppermute | solution.py:1113
  447.1 26.2 %collective-permute-start.35 = (bf16[2,128,768]{2,1,0:T(8,128)(2,1)}, bf16[2,128,768]{2,1,0:T(8,128)(2,1)}, u32[]{:S(2)}, u32[]{:S(2)}) collective-permute-start(bf16[2,128,768]{2,1,0:T(8,128)(2,1)} %bitcast.50), channel_id=1, source_target_pairs={{0,8},{4,12},{8,0},{12,4},{16,24},{20,28},{24,16},{28,20},{1,9},{5... | collective-permute-start | bytes 1179656 | tf_op jit(solution)/shard_map/ppermute | solution.py:1108
  476.5 20.9 %collective-permute-start.38 = (bf16[2,128,768]{2,1,0:T(8,128)(2,1)}, bf16[2,128,768]{2,1,0:T(8,128)(2,1)}, u32[]{:S(2)}, u32[]{:S(2)}) collective-permute-start(bf16[2,128,768]{2,1,0:T(8,128)(2,1)} %get-tuple-element.192.refs_1_), channel_id=1, source_target_pairs={{0,16},{4,20},{8,24},{12,28},{16,0},{20,4},{24,8},{28,12},{1,17},{... | collective-permute-start | bytes 1179656 | tf_op jit(solution)/shard_map/ppermute | solution.py:1108
  (24 other events, 293.8 us)
Sparse Core Ops, SparseCore 0:
  43.0 67.9 all-gather.2
  112.9 52.6 all-gather.4
  198.9 52.6 reduce-scatter.2
  258.1 52.7 reduce-scatter.4

commit v2 on v1

--- a/solution.py
+++ b/solution.py
@@ -71,7 +71,7 @@
             known + len(after) + number: output for number, (_, output) in enumerate(reuse)
         },
         compiler_params=pltpu.CompilerParams(vmem_limit_bytes=VMEM_MIB * MIB),
-        cost_estimate=pl.CostEstimate(flops=0, bytes_accessed=0, transcendentals=0),
+        cost_estimate=cost,
         name=name,
     )(*prefetch, *(placed(*item) for item in ins), *(placed(array, ANY) for array in idle))
 
@@ -497,58 +497,43 @@
 def run_output(weights, acts, after_value, small, number, after=()):
     rows, width = after_value.shape
     hidden = acts.shape[1]
-    part = width
-    parts = hidden // part
-    places = [
-        (item.at(start)) for size, item in weights for start in range(0, size, part)
-    ]
-    most = max(len(item.plan) for item in places)
+    span = 256
+    bounds = [0]
+    for size, _ in weights:
+        bounds.append(bounds[-1] + size)
+    by_row = lambda size: pl.BlockSpec((span, size), lambda i: (i, 0))
 
     def kernel(*refs):
-        act, down, start_value, sems, own_sems = refs[-5:]
-        stream = Stream()
-        for index, item in enumerate(places):
-            columns = slice(index * part, (index + 1) * part)
+        down = refs[-1 - len(weights)]
+        sems = refs[-len(weights) :]
+        stream = []
+        for index, (size, item) in enumerate(weights):
+            columns = slice(bounds[index], bounds[index + 1])
             copies, refs = item.copies(
                 refs,
-                part,
-                lambda at, size, columns=columns: down.at[pl.ds(at, size), columns],
-                sems.at[index],
+                size,
+                lambda at, lines, columns=columns: down.at[pl.ds(at, lines), columns],
+                sems[index],
             )
-            stream.add(copies)
+            stream.append(copies)
         act_ref, after_ref, bias_ref, out_ref = refs[:4]
-        for index in range(parts):
-            columns = slice(index * part, (index + 1) * part)
-            stream.parts[index].append(
-                pltpu.make_async_copy(
-                    act_ref.at[:, columns], act.at[:, columns], own_sems.at[index]
-                )
-            )
-        stream.add([pltpu.make_async_copy(after_ref, start_value, own_sems.at[parts])])
-        stream.start()
-        total = None
-        for index in range(parts):
-            columns = slice(index * part, (index + 1) * part)
-            stream.wait(index)
-            value = dot_nt(act[:, columns], down[:, columns])
-            total = value if total is None else total + value
-        stream.wait(parts)
-        out_ref[...] = (total + start_value[...] + bias_ref[...]).astype(BF16)
+        for copies in stream:
+            start_all(copies)
+        total = after_ref[...] + bias_ref[...]
+        for index, copies in enumerate(stream):
+            wait_all(copies)
+            columns = slice(bounds[index], bounds[index + 1])
+            total += dot_nt(act_ref[:, columns], down[:, columns])
+        out_ref[...] = total.astype(BF16)
 
     (out,) = call(
         kernel,
-        (1,),
-        [item for place in places for item in place.inputs()]
-        + [(acts, ANY), (after_value, ANY), param(small, number, width)],
-        [((rows, width), BF16, whole((rows, width)))],
+        (rows // span,),
+        [item for _, weight in weights for item in weight.inputs()]
+        + [(acts, by_row(hidden)), (after_value, by_row(width)), param(small, number, width)],
+        [((rows, width), BF16, by_row(width))],
         after=after,
-        scratch=[
-            pltpu.VMEM((rows, hidden), BF16),
-            pltpu.VMEM((width, hidden), BF16),
-            pltpu.VMEM((rows, width), F32),
-            pltpu.SemaphoreType.DMA((parts, most)),
-            pltpu.SemaphoreType.DMA((parts + 1,)),
-        ],
+        scratch=[pltpu.VMEM((width, hidden), BF16)] + [weight.sems() for _, weight in weights],
         cost=cost(2 * rows * width * hidden, 22 * rows * width),
         name="output",
     )
@@ -648,7 +633,7 @@
             out_weights.sems(),
             pltpu.SemaphoreType.DMA((parts + 3,)),
         ],
-        cost=cost(2 * rows * width * (hidden + 2 * width), 30 * rows * width),
+        cost=cost(8 * rows * width * (hidden + 2 * width), 120 * rows * width),
         name="middle",
     )
 
@@ -736,7 +721,9 @@
         after=after,
         scratch=[pltpu.VMEM((rows, rows), F32), pltpu.VMEM((rows, LANES), F32)],
         cost=cost(
-            20 * rows * rows * LANES * count, 16 * rows * LANES * count, 2 * rows * rows * count
+            (80 if first == 0 else 20) * rows * rows * LANES * count,
+            16 * rows * LANES * count,
+            2 * rows * rows * count,
         ),
         name="attend_back",
     )
@@ -774,71 +761,49 @@
     size = grads[0][0].shape[1]
     flat = [value for group in grads for value in group]
     count = len(flat)
+    by_row = lambda size: pl.BlockSpec((span, size), lambda i: (i, 0))
 
     def kernel(*refs):
-        held, weight, x_in, grad_in, sems, own_sems = refs[-6:]
-        pieces = refs
-        refs = weights.rest(refs)
-        grad_refs = refs[:count]
+        weight, sems = refs[-2:]
+        stream = []
+        for part in range(3):
+            columns = slice(part * width, (part + 1) * width)
+            copies, rest = weights.at(part * width).copies(
+                refs,
+                width,
+                lambda at, lines, columns=columns: weight.at[pl.ds(at, lines), columns],
+                sems.at[part],
+            )
+            stream.append(copies)
+        refs = rest
+        for copies in stream:
+            start_all(copies)
         x_ref, grad_ref, gain_ref, out_ref, ggain_ref, gshift_ref = refs[count : count + 6]
-        stream = Stream()
-        begins = []
-        for index in range(count):
-            group, part = divmod(index, 3)
-            begin = part * width + group * size
-            begins.append(begin)
-            columns = slice(begin, begin + size)
-            copies, _ = weights.at(begin).copies(
-                pieces,
-                size,
-                lambda at, lines, columns=columns: weight.at[pl.ds(at, lines), columns],
-                sems.at[index],
-            )
-            copies.append(
-                pltpu.make_async_copy(grad_refs[index], held.at[index], own_sems.at[index])
-            )
-            stream.add(copies)
-        stream.add(
-            [
-                pltpu.make_async_copy(x_ref, x_in, own_sems.at[count]),
-                pltpu.make_async_copy(grad_ref, grad_in, own_sems.at[count + 1]),
-            ]
-        )
-        stream.start()
+        step = pl.program_id(0)
         total = None
-        for index in range(count):
-            stream.wait(index)
-            columns = slice(begins[index], begins[index] + size)
-            value = dot_nt(held[index], weight[:, columns])
-            total = value if total is None else total + value
-        stream.wait(count)
-        gain = gain_ref[...]
-        sums = [jnp.zeros((1, width), F32)] * 2
-        for start in range(0, rows, span):
-            lines = slice(start, start + span)
-            grad = total[lines]
-            hat, scale = norm_stats(x_in[lines, :].astype(F32))
-            out_ref[lines, :] = grad_in[lines, :] + norm_back(hat, scale, grad * gain)
-            for index, value in enumerate((grad * hat, grad)):
-                sums[index] = sums[index] + jnp.sum(value, axis=0, keepdims=True)
-        ggain_ref[...], gshift_ref[...] = sums
+        for part in range(3):
+            wait_all(stream[part])
+            for group in range(len(grads)):
+                begin = part * width + group * size
+                value = dot_nt(refs[3 * group + part][...], weight[:, begin : begin + size])
+                total = value if total is None else total + value
+        hat, scale = norm_stats(x_ref[...].astype(F32))
+        accumulate(gshift_ref, jnp.sum(total, axis=0, keepdims=True), step == 0)
+        accumulate(ggain_ref, jnp.sum(total * hat, axis=0, keepdims=True), step == 0)
+        out_ref[...] = grad_ref[...] + norm_back(hat, scale, total * gain_ref[...])
 
     vector = ((1, width), F32, whole((1, width)))
     return call(
         kernel,
-        (1,),
+        (rows // span,),
         weights.inputs()
-        + [(value, ANY) for value in flat]
-        + [(x, ANY), (grad_after, ANY), param(small, number, width)],
-        [((rows, width), F32, whole((rows, width))), vector, vector],
+        + [(value, by_row(size)) for value in flat]
+        + [(x, by_row(width)), (grad_after, by_row(width)), param(small, number, width)],
+        [((rows, width), F32, by_row(width)), vector, vector],
         after=after,
         scratch=[
-            pltpu.VMEM((count, rows, size), BF16),
             pltpu.VMEM((width, 3 * width), BF16),
-            pltpu.VMEM((rows, width), BF16),
-            pltpu.VMEM((rows, width), F32),
-            pltpu.SemaphoreType.DMA((count, len(weights.plan))),
-            pltpu.SemaphoreType.DMA((count + 2,)),
+            pltpu.SemaphoreType.DMA((3, len(weights.plan))),
         ],
         cost=cost(6 * rows * width * width, 22 * rows * width),
         name="grad_input",
@@ -855,7 +820,7 @@
 
 
 def run_adam(core, state, groups, span, places, pick, earlier, after=()):
-    half = groups[0][0].shape[1]
+    half = groups[0][0].shape[-2]
     count = len(places)
     table = jnp.array(places, jnp.int32)
     place = pl.BlockSpec((half, span), lambda p, h, c, t: (jnp.bitwise_xor(h, c[0]), t[p]))
@@ -945,20 +910,17 @@
     return ins, outs, run
 
 
-def job_join(pairs, steps):
-    blocks, rows, size = pairs[0][0].shape[1:]
+def job_join(left, right, steps):
+    _, blocks, rows, size = left.shape
     span = rows // steps
     four = lambda i, c: (0, 0, i, 0)
-    count = 2 * len(pairs)
-    ins = [(value, (2, blocks, span, size), four) for pair in pairs for value in pair]
-    outs = [((blocks, count, rows, size), BF16, (blocks, count, span, size), four)]
+    ins = [(value, (2, blocks, span, size), four) for value in (left, right)]
+    outs = [((blocks, 2, rows, size), BF16, (blocks, 2, span, size), four)]
 
     def run(have, give):
-        for number in range(len(pairs)):
-            left, right = have[2 * number : 2 * number + 2]
-            for side in range(2):
-                for block in range(blocks):
-                    give[0][block, 2 * number + side] = left[side, block] + right[side, block]
+        for side in range(2):
+            for block in range(blocks):
+                give[0][block, side] = have[0][side, block] + have[1][side, block]
 
     return ins, outs, run
 
@@ -997,9 +959,9 @@
 
 
 def job_pick(own, received, steps):
-    count, rows, size = own.shape
-    block = (count, rows // steps, size)
-    index = lambda i, c: (0, i, 0)
+    at = own.ndim - 2
+    block = tuple(size // steps if axis == at else size for axis, size in enumerate(own.shape))
+    index = lambda i, c: (0,) * at + (i, 0)
 
     def run(have, give, places):
         give[0][...] = jnp.where(places[2] == 1, have[0][...], have[1][...])
@@ -1234,29 +1196,12 @@
 class Wide:
     def __init__(self, links, joined):
         self.links = links
-        self.stage = 0
-        count, half, size = joined.shape[1:]
-        flat = joined.reshape(links.shards * count * half, size)
-        mine = lax.psum_scatter(flat, "shard", scatter_dimension=0, tiled=True)
-        self.own = mine.reshape(count, half, size)
-
-    def send(self):
-        before = self.own
-        self.received = self.links.along_dp(before, 0)
-        return before
-
-    def job(self, steps):
-        if self.stage == 2:
-            return job_pick(self.own, self.received, steps)
-        return job_add(self.own, self.received, steps)
-
-    def advance(self, results):
-        self.own = results[0]
-        self.stage += 1
-        if self.stage < 3:
-            self.received = self.links.along_dp(self.own, self.stage)
-        else:
-            self.grads = (self.own, self.links.swap(self.own))
+        self.shape = joined.shape[1:]
+        flat = joined.reshape(-1, joined.shape[3])
+        self.own = lax.psum_scatter(flat, "shard", scatter_dimension=0, tiled=True)
+
+    def finish(self):
+        self.own = self.links.over_dp(self.own).reshape(self.shape)
 
 
 class Side:
@@ -1302,8 +1247,7 @@
     pairs = width // LANES
     pad = 16
     core_arr = links.core_arr
-    by_owner = links.turned_offsets(False)
-    around = links.turned_offsets(True) if links.fast else by_owner
+    around = links.turned_offsets(links.fast)
     side = Side(links)
 
     ends = jnp.cumsum(lengths[0], dtype=jnp.int32)
@@ -1321,10 +1265,10 @@
 
     def first_job():
         ins = [
-            (attn_state[0], (half, 3 * width), lambda i, c: (c[0], 0)),
+            (attn_state[0], (half, 4 * width), lambda i, c: (c[0], 0)),
             (small_own, (1, small_size), lambda i, c: (0, 0)),
         ]
-        outs = [((half + pad, 3 * width), BF16, (half + pad, 3 * width), lambda i, c: (0, 0))]
+        outs = [((half + pad, 4 * width), BF16, (half + pad, 4 * width), lambda i, c: (0, 0))]
 
         def job(have, give):
             give[0][:half] = have[0][...].astype(BF16)
@@ -1333,45 +1277,42 @@
 
         return ins, outs, job
 
-    blocks = 4
-    block = hidden // blocks
-    columns = [(attn_state[0], 3, width)]
-    columns += [(mlp_state[0], number, block) for number in (0, 1, blocks, blocks + 1)]
-    more_columns = [
-        (mlp_state[0], number, block) for number in (2, 3, blocks + 2, blocks + 3)
-    ]
+    block = hidden // 2
+    groups = [[(mlp_state[0], number, block) for number in pair] for pair in ((0, 2), (1, 3))]
     (first_half,) = side.jobs([first_job()])
     if links.fast:
-        qkv_gather = Gather(links, first_half, None)
+        attn_gather = Gather(links, first_half, None)
     else:
-        qkv_weights = links.gathered(links.gather(first_half))
-    dy, dyt, grad_bias_dn = side.then(run_cot(half, by_owner, ends, cotangent, after=side.order))
+        attn_weights = links.gathered(links.gather(first_half))
+    dy, dyt, grad_bias_dn = side.then(run_cot(half, around, ends, cotangent, after=side.order))
+    (more_half,) = side.jobs([job_cast(half, groups[1], 1, 4)], steps=4)
     if links.fast:
-        (qkv_gather.own,) = side.jobs(
-            [job_cast(links.rows, [(attn_state[0], 0, 3 * width)], 0, 4)], steps=4
-        )
-        qkv_gather.forward(side.jobs(qkv_gather.jobs()))
-    (out_half,) = side.jobs([job_cast(half, columns, 1, 4)], steps=4)
-    wide = links.gather(out_half)
-    (feed_half,) = side.jobs([job_cast(half, more_columns, 1, 4)], steps=4)
-    more_wide = links.gather(feed_half)
+        (attn_gather.own,) = side.jobs(
+            [job_cast(links.rows, [(attn_state[0], 0, 4 * width)], 0, 4)], steps=4
+        )
+        *copied, feed_half = side.jobs([*attn_gather.jobs(), job_cast(half, groups[0], 1, 1)])
+        attn_gather.forward(copied)
+    else:
+        (feed_half,) = side.jobs([job_cast(half, groups[0], 1, 1)])
+    wide = links.gather(feed_half)
+    more_wide = links.gather(more_half)
     if links.fast:
-        qkv_weights = qkv_gather.weights()
+        attn_weights = attn_gather.weights()
         rows_of = [
             (small_own, 0),
-            (qkv_gather.by_x, half),
-            (qkv_gather.by_y, half),
-            (qkv_gather.far[1], half // 2),
+            (attn_gather.by_x, half),
+            (attn_gather.by_y, half),
+            (attn_gather.far[1], half // 2),
         ]
         (small,) = side.jobs([job_params(rows_of, links.shards, small_size)])
     else:
-        small = qkv_weights.pieces[0].reshape(links.shards, half + pad, 3 * width)
+        small = attn_weights.pieces[0].reshape(links.shards, half + pad, 4 * width)
         small = small[:, half, :small_size].astype(F32).reshape(1, -1)
 
     qkv, turned_one = side.then(
         run_qkv(
             half,
-            qkv_weights,
+            attn_weights,
             around,
             tokens,
             small,
@@ -1379,16 +1320,14 @@
             after=side.order,
         )
     )
-    attended = side.then(run_attend(ends, qkv, 0, pairs // 2, after=side.order))
-    wide = links.gathered(wide, attended[1])
-    mixed, lse = side.then(
-        run_attend(ends, qkv, pairs // 2, pairs // 2, attended, after=(wide.pieces[0],))
-    )
+    mixed, lse = side.then(run_attend(ends, qkv, 0, pairs, after=side.order))
+    wide = links.gathered(wide, lse)
+    side.order += (wide.pieces[0],)
     after, low_two, turned_two, turned_mixed = side.then(
         run_after(
             half,
-            wide,
-            (around, by_owner),
+            attn_weights.at(3 * width),
+            (around, around),
             mixed,
             tokens,
             small,
@@ -1397,45 +1336,45 @@
         )
     )
 
-    passed, grad_bias_up, mlp_grads = [None], [], []
-    feeds = [(0, 2 * block, wide.at(width), wide.at(width + 2 * block))]
-
-    def feed(number):
-        start, size, up_weights, down_weights = feeds[number]
-        act, du, own, sib, gbias = side.then(
-            run_feed(
-                up_weights,
-                down_weights,
-                low_two,
-                turned_two,
-                dy,
-                dyt,
-                small,
-                BIAS_UP * width + start,
-                start,
-                size,
-                passed[-1],
-                after=side.order,
-            )
+    passed, grad_bias_up = [None], []
+    blocked = lambda value: value.reshape(2, links.shards, half, value.shape[2])
+
+    def feed(start, up_weights, down_weights):
+        act, du, own, sib, gbias = run_feed(
+            up_weights,
+            down_weights,
+            low_two,
+            turned_two,
+            dy,
+            dyt,
+            small,
+            BIAS_UP * width + start,
+            start,
+            block,
+            passed[-1],
+            after=side.order,
         )
         side.order = (own,)
         passed.append((act, du))
         grad_bias_up.append(gbias)
-        shape = (2, links.shards, half, size)
-        mlp_grads.append((own.reshape(shape), links.swap(sib).reshape(shape)))
-
-    def join(pairs):
-        return side.jobs([job_join(pairs, half // 16)], steps=half // 16)[0]
-
-    feed(0)
+        return own, sib
+
+    def unit(line, *grads):
+        if links.fast:
+            return Reduce(links, line).add(*grads)
+        return Wide(links, side.jobs([job_join(blocked(grads[0]), blocked(links.swap(grads[1])), 4)], steps=4)[0])
+
+    def reduce(units, jobs=(), steps=2):
+        if links.fast:
+            return side.reduce(units, jobs, steps)
+        return side.jobs(jobs) if jobs else None
+
+    group_a = feed(0, wide, wide.at(block))
     more_wide = links.gathered(more_wide, grad_bias_up[0])
-    feeds += [
-        (2 * block, block, more_wide, more_wide.at(2 * block)),
-        (3 * block, block, more_wide.at(block), more_wide.at(3 * block)),
-    ]
-    feed(1)
-    reduces = [Wide(links, join([mlp_grads[0]]))]
-    feed(2)
+    unit_a = unit(True, *group_a)
+    reduce([unit_a], steps=4)
+    unit_b = unit(True, *feed(block, more_wide, more_wide.at(block)))
+    reduce([unit_a], steps=4)
     (
         grad_after,
         dmix,
@@ -1446,8 +1385,8 @@
         grad_shift_two,
     ) = side.then(
         run_middle(
-            [(item[1], item[2]) for item in feeds],
-            wide,
+            [(block, wide), (block, more_wide)],
+            attn_weights.at(3 * width),
             passed[-1][1],
             after,
             dy,
@@ -1457,11 +1396,8 @@
             after=side.order,
         )
     )
-    reduces.append(Wide(links, join([mlp_grads[1], mlp_grads[2]])))
-    if links.fast:
-        reduces.append(Reduce(links, True).add(own_out, sib_out))
-    else:
-        reduces.append((own_out, sib_out))
+    unit_c = unit(False, own_out, sib_out)
+    reduce([unit_a, unit_b], steps=4)
     grads, biases = [], []
 
     def attend_back(first):
@@ -1472,57 +1408,47 @@
         biases.append((gq, gv))
 
     def project(group):
-        own, sib = side.then(run_project(turned_one, *grads[group], after=side.order))
-        if not links.fast:
-            reduces.append((own, sib))
-        elif group == 0:
-            reduces[2].add(own, sib)
-        else:
-            reduces.append(Reduce(links, False).add(own, sib))
-
-    def reduce(numbers, jobs=()):
-        if links.fast:
-            return side.reduce([reduces[number] for number in numbers], jobs)
-        return side.jobs(jobs) if jobs else None
+        return side.then(run_project(turned_one, *grads[group], after=side.order))
 
     attend_back(0)
+    reduce([unit_a, unit_b], steps=4)
     if links.fast:
-        side.order += (reduces[0].send(),)
-    project(0)
+        unit_c.add(*project(0))
+    else:
+        unit_e = unit(False, *project(0))
     attend_back(pairs // 2)
-    reduce([0, 2])
-    if links.fast:
-        side.order += (reduces[1].send(),)
-    project(1)
-    reduce([2])
+    reduce([unit_a, unit_b, unit_c], steps=4)
+    unit_d = unit(False, *project(1))
     grad_input, grad_gain_one, grad_shift_one = side.then(
-        run_input(
-            qkv_weights, grads, tokens, grad_after, small, GAIN_ONE, after=side.order
-        )
+        run_input(attn_weights, grads, tokens, grad_after, small, GAIN_ONE, after=side.order)
     )
     small_grads = [biases[0][0], biases[1][0], biases[0][1], biases[1][1], grad_bias_o]
     small_grads += grad_bias_up
     small_grads += [grad_bias_dn, grad_gain_one, grad_shift_one, grad_gain_two, grad_shift_two]
-    (grad_small,) = reduce([0, 1, 2, 3], [job_lay(small_grads)])
-    output = run_output(
-        [(item[1], item[3]) for item in feeds],
-        passed[-1][0],
-        after,
-        small,
-        BIAS_DN,
-        after=side.order,
-    )
-    side.then([output])
+    (grad_small,) = reduce([unit_a, unit_b, unit_c, unit_d], [job_lay(small_grads)])
+
+    def pick_feed(number, arrays):
+        return [arrays[0][number]]
+
+    def adam_mlp(number, item, earlier):
+        return side.then(
+            run_adam(
+                core_arr,
+                mlp_state,
+                [item.grads],
+                block,
+                [number, 2 + number],
+                pick_feed,
+                earlier,
+                after=side.order,
+            )
+        )
 
     out_block = width // 2
-    pick_mlp = (
-        lambda number, arrays: [arrays[0][number]],
-        lambda number, arrays: [arrays[0][number], arrays[0][2 + number]],
-    )
 
     def pick_heads(number, arrays):
+        left, right = arrays[0][0], arrays[0][1]
         skip = arrays[0].shape[2] - 3 * out_block // 2
-        left, right = arrays[0][0], arrays[0][1]
         split = skip + out_block // 2
         return (
             [left[:, skip : skip + out_block]],
@@ -1532,13 +1458,12 @@
             [right[:, :skip]],
         )[number]
 
-    def adam_attn(group, earlier):
-        places = [0, 2, 4, 6, 7] if group == 0 else [1, 3, 5]
+    def adam_attn(item, places, earlier):
         return side.then(
             run_adam(
                 core_arr,
                 attn_state,
-                [reduces[2 + group].grads],
+                [item.grads],
                 out_block,
                 places,
                 pick_heads,
@@ -1547,53 +1472,48 @@
             )
         )
 
-    def adam_mlp(group, earlier):
-        return side.then(
-            run_adam(
-                core_arr,
-                mlp_state,
-                [reduces[group].grads],
-                2 * block,
-                [group, blocks // 2 + group],
-                pick_mlp[group],
-                earlier,
-                after=side.order,
-            )
-        )
+    def output_now():
+        out = run_output(
+            [(block, wide.at(block)), (block, more_wide.at(block))],
+            passed[-1][0],
+            after,
+            small,
+            BIAS_DN,
+            after=side.order,
+        )
+        side.then([out])
+        return out
 
     if links.fast:
-
-        def step(numbers, move):
-            (total,) = reduce(numbers, [job_add(grad_small, moved, 2)])
+        shard_move = lambda bit: functools.partial(links.across_shard, bit=bit)
+        dp_move = lambda bit: functools.partial(links.across_dp, bit=bit)
+        moved = links.across_shard(grad_small, 1)
+
+        def step(units, move):
+            (total,) = reduce(units, [job_add(grad_small, moved, 2)])
             return total, move(total) if move else None
 
-        across = lambda bit: functools.partial(links.across_dp, bit=bit)
-        reduce([0, 1, 2, 3])
-        moved = links.across_shard(grad_small, 1)
-        mlp_new = adam_mlp(0, None)
-        grad_small, moved = step([1, 2, 3], functools.partial(links.across_shard, bit=2))
-        mlp_new = adam_mlp(1, mlp_new)
-        grad_small, moved = step([2, 3], links.swap)
-        attn_new = adam_attn(0, None)
-        grad_small, moved = step([3], across(2))
-        grad_small, moved = step([], across(4))
-        attn_new = adam_attn(1, attn_new)
+        mlp_new = adam_mlp(0, unit_a, None)
+        grad_small, moved = step([unit_b, unit_c, unit_d], shard_move(2))
+        output = output_now()
+        grad_small, moved = step([unit_b, unit_c, unit_d], links.swap)
+        mlp_new = adam_mlp(1, unit_b, mlp_new)
+        grad_small, moved = step([unit_c, unit_d], dp_move(2))
+        attn_new = adam_attn(unit_c, [0, 2, 4, 6, 7], None)
+        grad_small, moved = step([unit_d], dp_move(4))
+        attn_new = adam_attn(unit_d, [1, 3, 5], attn_new)
         grad_small, _ = step([], None)
     else:
-        blocked = lambda value: value.reshape(2, links.shards, half, value.shape[2])
-        for number in range(2, len(reduces)):
-            own, sib = reduces[number]
-            pair = (blocked(own), blocked(links.swap(sib)))
-            reduces[number] = Wide(links, join([pair]))
-        for item in reduces:
-            item.own = links.over_dp(item.own)
+        for item in (unit_a, unit_b, unit_c, unit_d, unit_e):
+            item.finish()
+        unit_c.own = jnp.concatenate([unit_c.own, unit_e.own], axis=2)
+        for item in (unit_a, unit_b, unit_c, unit_d):
             item.grads = (item.own, links.swap(item.own))
-        mine = jnp.concatenate([reduces[2].own, reduces[3].own], axis=2)
-        reduces[2].grads = (mine, links.swap(mine))
-        reduces[3] = reduces.pop()
         grad_small = lax.psum(grad_small, ("dp", "shard"))
-        mlp_new = adam_mlp(1, adam_mlp(0, None))
-        attn_new = adam_attn(1, adam_attn(0, None))
+        output = output_now()
+        mlp_new = adam_mlp(1, unit_b, adam_mlp(0, unit_a, None))
+        attn_new = adam_attn(unit_c, [0, 2, 4, 6, 7], None)
+        attn_new = adam_attn(unit_d, [1, 3, 5], attn_new)
     grad_small = lax.dynamic_slice_in_dim(grad_small, links.shard * small_size, small_size, 1)[0]
     small_new = adamw(*small_state, grad_small, 0.4, 0.0)
     return (output, grad_input, *attn_new, *mlp_new, *small_new)

time: 535 us -> 517 us (0.966)
  Pallas kernels: 352 us -> 334 us
    pallas_call x36 -> x33, Pallas kernels: 352 us -> 334 us  [call(): pl.pallas_call(run, grid_spec=pltpu.PrefetchScalarGridSpec(num_scalar_pre...]
    ppermute x21 -> x22, waiting for transfers between devices: 31 us -> 43.7 us  [across_dp(): lax.ppermute(value, 'dp', [(d, d ^ bit) for d in range(self.replicas)])]
    ppermute x9 -> x6, starting transfers between devices: 27.8 us -> 17.3 us  [along_dp(): return lax.ppermute(value, 'dp', pairs)]
    ppermute x14 -> x22, starting transfers between devices: 15.7 us -> 24.3 us  [across_shard(): lax.ppermute(value, 'shard', [(s, s ^ bit) for s in range(self.shards)])]
    ppermute x9 -> x6, waiting for transfers between devices: 12.2 us -> 5.63 us  [along_dp(): return lax.ppermute(value, 'dp', pairs)]
    all_gather x2, waiting for transfers between devices: 15.6 us -> 9.19 us  [gather(): return lax.all_gather(half_rows, 'shard', axis=0, tiled=True)]
    ppermute x21 -> x22, starting transfers between devices: 7.57 us -> 12.4 us  [across_dp(): lax.ppermute(value, 'dp', [(d, d ^ bit) for d in range(self.replicas)])]
    ppermute x14 -> x22, waiting for transfers between devices: 41.7 us -> 44.8 us  [across_shard(): lax.ppermute(value, 'shard', [(s, s ^ bit) for s in range(self.shards)])]
  transfers between devices with their start and end apart: 48 -> 52, of which waited for: 14 -> 17; matrix products, arithmetic and copies ran while one was open for 1% -> 1% of each run, Pallas kernels for 58% -> 53%
where the time goes in v2:
time: 517 us; the launch traced here: 512 us
  Pallas kernels  334 us (65%)
  waiting for transfers between devices  103 us (20%)
  starting transfers between devices  54.1 us (10%)
  between operations  14.7 us (3%)
    pallas_call x33, Pallas kernels, call(): pl.pallas_call(run, grid_spec=pltpu.PrefetchScalarGridSpec(num_scalar_pre...  334 us
    ppermute x22, waiting for transfers between devices, across_shard(): lax.ppermute(value, 'shard', [(s, s ^ bit) for s in range(self.shards)])  44.8 us
    ppermute x22, waiting for transfers between devices, across_dp(): lax.ppermute(value, 'dp', [(d, d ^ bit) for d in range(self.replicas)])  43.7 us
    ppermute x22, starting transfers between devices, across_shard(): lax.ppermute(value, 'shard', [(s, s ^ bit) for s in range(self.shards)])  24.3 us
    ppermute x6, starting transfers between devices, along_dp(): return lax.ppermute(value, 'dp', pairs)  17.3 us
    ppermute x22, starting transfers between devices, across_dp(): lax.ppermute(value, 'dp', [(d, d ^ bit) for d in range(self.replicas)])  12.4 us
  transfers between devices with their start and end apart: 52, of which 17 were waited for; matrix products, arithmetic and copies ran while one was open for 1% of the time, Pallas kernels for 53%

profile of v2, /device:TPU:0, one launch (start us, length us, event | category | flops | bytes accessed | tf_op | source)
XLA Modules:
  0.0 512.5 jit_solution(1463294415278993328)
XLA Ops:
  31.3 9.2 %collective-permute-done.refs_1_.refs_3_.refs_15_ = bf16[144,4096]{1,0:T(8,128)(2,1)} collective-permute-done((bf16[144,4096]{1,0:T(8,128)(2,1)}, bf16[144,4096]{1,0:T(8,128)(2,1)}, u32[]{:S(2)}, u32[]{:S(2)}) %collective-permute-start) | collective-permute-done | bytes 1179680 | tf_op jit(solution)/shard_map/ppermute | solution.py:1078
  48.9 19.5 %collective-permute-done.5.refs_4_.refs_7_.refs_19_ = bf16[80,4096]{1,0:T(8,128)(2,1)} collective-permute-done((bf16[80,4096]{1,0:T(8,128)(2,1)}, bf16[80,4096]{1,0:T(8,128)(2,1)}, u32[]{:S(2)}, u32[]{:S(2)}) %collective-permute-start.5) | collective-permute-done | bytes 655392 | tf_op jit(solution)/shard_map/ppermute | solution.py:1078
  71.9 14.2 %qkv.1 = (bf16[1024,3072]{1,0:T(8,128)(2,1)}, bf16[1024,1024]{1,0:T(8,128)(2,1)}) custom-call(s32[9]{0:T(128)} %stack.59.refs_0_.refs_12_, bf16[256,4096]{1,0:T(8,128)(2,1)} %side.18.refs_5_.refs_1_.refs_13_, bf16[144,4096]{1,0:T(8,128)(2,1)} %collective-permute-done.1.refs_2_.refs_14_, bf16[144,4096]{1,0:T(8,128)(2,1)} %collective-permute-done.refs_1_.refs_3_.refs_15_, ...), custom_call_target="tpu_custom_call" | custom-call | flops 6442450944 | bytes 16777216 | tf_op jit(solution)/shard_map/qkv/pallas_call | solution.py:60
  86.2 22.9 %attend.1 = (bf16[1024,1024]{1,0:T(8,128)(2,1)}, f32[8,2,1024]{2,1,0:T(2,128)}) custom-call(s32[4]{0:T(128)} %bitcast.47, bf16[1024,3072]{1,0:T(8,128)(2,1)} %get-tuple-element.120.refs_1_.refs_2_.refs_3_.refs_4_, bf16[1024,3072]{1,0:T(8,128)(2,1)} %get-tuple-element.120.refs_1_.refs_2_.refs_3_.refs_4_, ...), custom_call_target="tpu_custom_call" | custom-call | flops 8589934592 | bytes 8388608 | tf_op jit(solution)/shard_map/attend/pallas_call | solution.py:60
  109.7 10.4 %after.1 = (f32[1024,1024]{1,0:T(8,128)}, bf16[1024,1024]{1,0:T(8,128)(2,1)}, bf16[1024,1024]{1,0:T(8,128)(2,1)}, bf16[1024,1024]{1,0:T(8,128)(2,1)}) custom-call(s32[9]{0:T(128)} %stack.59.refs_0_.refs_12_, bf16[256,4096]{1,0:T(8,128)(2,1)} %side.18.refs_5_.refs_1_.refs_13_, bf16[144,4096]{1,0:T(8,128)(2,1)} %collective-permute-done.1.refs_2_.refs_14_, ...), custom_call_target="tpu_custom_call" | custom-call | flops 2147483648 | bytes 14680064 | tf_op jit(solution)/shard_map/after/pallas_call | solution.py:60
  120.1 29.1 %feed.2 = (bf16[1024,4096]{1,0:T(8,128)(2,1)}, bf16[1024,4096]{1,0:T(8,128)(2,1)}, bf16[2,512,2048]{2,1,0:T(8,128)(2,1)}, bf16[2,512,2048]{2,1,0:T(8,128)(2,1)}, f32[1,2048]{1,0:T(1,128)}) custom-call(s32[8]{0:T(128)} %pad_add_fusion.refs_0_.refs_3_.refs_6_.refs_9_, bf16[512,4096]{1,0:T(8,128)(2,1)} %all-gather.3.cloned.1.call-done.refs_18_.refs_1_.refs_4_, ...), custom_call_target="tpu_custom_call" | custom-call | flops 17179869184 | bytes 50331648 | tf_op jit(solution)/shard_map/feed/pallas_call | solution.py:60
  149.8 9.2 %all-gather.5.cloned.1.call-done.refs_1_.refs_4_.refs_7_.refs_10_ = bf16[512,4096]{1,0:T(8,128)(2,1)} async-done(((bf16[128,4096]{1,0:T(8,128)(2,1)}), bf16[512,4096]{1,0:T(8,128)(2,1)}) %all-gather.5.cloned.1.call-update) | async-done | bytes 4194320 | tf_op jit(solution)/shard_map/all_gather | solution.py:1089
  167.5 29.6 %feed.3 = (bf16[1024,4096]{1,0:T(8,128)(2,1)}, bf16[1024,4096]{1,0:T(8,128)(2,1)}, bf16[2,512,2048]{2,1,0:T(8,128)(2,1)}, bf16[2,512,2048]{2,1,0:T(8,128)(2,1)}, f32[1,2048]{1,0:T(1,128)}) custom-call(s32[8]{0:T(128)} %pad_add_fusion.refs_0_.refs_3_.refs_6_.refs_9_, ...), custom_call_target="tpu_custom_call", output_to_operand_aliasing={{0}: (12, {}), {1}: (13, {})} | custom-call | flops 17179869184 | bytes 50331648 | tf_op jit(solution)/shard_map/feed/pallas_call | solution.py:60
  204.1 24.6 %middle.1 = (f32[1024,1024]{1,0:T(8,128)}, bf16[1024,1024]{1,0:T(8,128)(2,1)}, bf16[2,512,512]{2,1,0:T(8,128)(2,1)}, bf16[2,512,512]{2,1,0:T(8,128)(2,1)}, f32[1...) custom-call(s32[8]{0:T(128)} %pad_add_fusion.refs_0_.refs_3_.refs_6_.refs_9_, ...), custom_call_target="tpu_custom_call" | custom-call | flops 51539607552 | bytes 125829120 | tf_op jit(solution)/shard_map/middle/pallas_call | solution.py:60
  228.7 7.3 %side.23 = (bf16[2,1,128,2048]{3,2,1,0:T(8,128)(2,1)}, bf16[2,2,128,2048]{3,2,1,0:T(8,128)(2,1)}, bf16[2,128,2048]{2,1,0:T(8,128)(2,1)}, bf16[2,128,2048]{2,1,0:T(8,128)(2,1)}) custom-call(s32[3]{0:T(128)} %pad_add_fusion.1.refs_0_, bf16[2,1,128,2048]{3,2,1,0:T(8,128)(2,1)} %get-tuple-element.139.refs_27_.refs_1_, ...), custom_call_target="tpu_custom_call" | custom-call | bytes 20971520 | tf_op jit(solution)/shard_map/side/pallas_call | solution.py:60
  242.3 18.8 %attend_back.2 = (bf16[1024,512]{1,0:T(8,128)(2,1)}, bf16[1024,512]{1,0:T(8,128)(2,1)}, bf16[1024,512]{1,0:T(8,128)(2,1)}, f32[1,512]{1,0:T(1,128)}, f32[1,512]{1,0:T(1,128)}) custom-call(s32[4]{0:T(128)} %bitcast.48, bf16[1024,3072]{1,0:T(8,128)(2,1)} %get-tuple-element.120.refs_1_.refs_2_.refs_3_.refs_4_, ...), custom_call_target="tpu_custom_call" | custom-call | flops 42949672960 | bytes 8388608 | tf_op jit(solution)/shard_map/attend_back/pallas_call | solution.py:60
  272.1 7.1 %project.2 = (bf16[2,512,768]{2,1,0:T(8,128)(2,1)}, bf16[2,512,768]{2,1,0:T(8,128)(2,1)}) custom-call(bf16[1024,1024]{1,0:T(8,128)(2,1)} %get-tuple-element.158.refs_0_, bf16[1024,512]{1,0:T(8,128)(2,1)} %get-tuple-element.151.refs_6_.refs_1_.refs_10_, bf16[1024,512]{1,0:T(8,128)(2,1)} %get-tuple-element.159.refs_2_.refs_11_, ...), custom_call_target="tpu_custom_call" | custom-call | flops 3221225472 | bytes 7340032 | tf_op jit(solution)/shard_map/project/pallas_call | solution.py:60
  283.3 19.1 %attend_back.3 = (bf16[1024,512]{1,0:T(8,128)(2,1)}, bf16[1024,512]{1,0:T(8,128)(2,1)}, bf16[1024,512]{1,0:T(8,128)(2,1)}, f32[1,512]{1,0:T(1,128)}, f32[1,512]{1,0:T(1,128)}) custom-call(s32[4]{0:T(128)} %bitcast.49, bf16[1024,3072]{1,0:T(8,128)(2,1)} %get-tuple-element.120.refs_1_.refs_2_.refs_3_.refs_4_, ...), custom_call_target="tpu_custom_call" | custom-call | flops 10737418240 | bytes 8388608 | tf_op jit(solution)/shard_map/attend_back/pallas_call | solution.py:60
  309.3 7.1 %project.3 = (bf16[2,512,768]{2,1,0:T(8,128)(2,1)}, bf16[2,512,768]{2,1,0:T(8,128)(2,1)}) custom-call(bf16[1024,1024]{1,0:T(8,128)(2,1)} %get-tuple-element.158.refs_0_, bf16[1024,512]{1,0:T(8,128)(2,1)} %get-tuple-element.163.refs_10_.refs_1_.refs_13_, bf16[1024,512]{1,0:T(8,128)(2,1)} %get-tuple-element.169.refs_2_.refs_14_, ...), custom_call_target="tpu_custom_call" | custom-call | flops 3221225472 | bytes 7340032 | tf_op jit(solution)/shard_map/project/pallas_call | solution.py:60
  326.6 15.6 %grad_input.1 = (f32[1024,1024]{1,0:T(8,128)}, f32[1,1024]{1,0:T(1,128)}, f32[1,1024]{1,0:T(1,128)}) custom-call(s32[9]{0:T(128)} %stack.59.refs_0_.refs_12_, bf16[256,4096]{1,0:T(8,128)(2,1)} %side.18.refs_5_.refs_1_.refs_13_, bf16[144,4096]{1,0:T(8,128)(2,1)} %collective-permute-done.1.refs_2_.refs_14_, ...), custom_call_target="tpu_custom_call" | custom-call | flops 6442450944 | bytes 23068672 | tf_op jit(solution)/shard_map/grad_input/pallas_call | solution.py:60
  358.6 10.0 %collective-permute-done.34.refs_10_ = f32[1,12288]{1,0:T(1,128)} collective-permute-done((f32[1,12288]{1,0:T(1,128)}, f32[1,12288]{1,0:T(1,128)}, u32[]{:S(2)}, u32[]{:S(2)}) %collective-permute-start.34) | collective-permute-done | bytes 49184 | tf_op jit(solution)/shard_map/ppermute | solution.py:1078
  371.2 12.7 %adam.4 = (f32[256,8192]{1,0:T(8,128)}, f32[256,8192]{1,0:T(8,128)}, f32[256,8192]{1,0:T(8,128)}) custom-call(s32[3]{0:T(128)} %pad_add_fusion.1.refs_0_, s32[2]{0:T(128)} %iota_multiply_fusion.1.refs_1_, f32[256,8192]{1,0:T(8,128)} %refs_2_.9, f32[256,8192]{1,0:T(8,128)} %refs_3_.7, f32[256,8192]{1,0:T(8,128)} %refs_4_.7, ...), custom_call_target="tpu_custom_call" | custom-call | flops 20971520 | bytes 27262976 | tf_op jit(solution)/shard_map/adam/pallas_call | solution.py:60
  397.4 15.3 %output.1.refs_10_ = bf16[1024,1024]{1,0:T(8,128)(2,1)} custom-call(s32[8]{0:T(128)} %pad_add_fusion.refs_0_.refs_3_.refs_6_.refs_9_, bf16[512,4096]{1,0:T(8,128)(2,1)} %all-gather.3.cloned.1.call-done.refs_18_.refs_1_.refs_4_, bf16[512,4096]{1,0:T(8,128)(2,1)} %collective-permute-done.8.refs_2_.refs_5_, s32[8]{0:T(128)} %pad_add_fusion.refs_0_.refs_3_.refs_6_.refs_9_, ...), custom_call_target="tpu_custom_call" | custom-call | flops 8589934592 | bytes 23068672 | tf_op jit(solution)/shard_map/output/pallas_call | solution.py:60
  412.8 17.3 %collective-permute-done.37.refs_4_ = bf16[2,128,1280]{2,1,0:T(8,128)(2,1)} collective-permute-done((bf16[2,128,1280]{2,1,0:T(8,128)(2,1)}, bf16[2,128,1280]{2,1,0:T(8,128)(2,1)}, u32[]{:S(2)}, u32[]{:S(2)}) %collective-permute-start.37) | collective-permute-done | bytes 655392 | tf_op jit(solution)/shard_map/ppermute | solution.py:1070
  437.0 12.4 %adam.5 = (f32[256,8192]{1,0:T(8,128)}, f32[256,8192]{1,0:T(8,128)}, f32[256,8192]{1,0:T(8,128)}) custom-call(s32[3]{0:T(128)} %pad_add_fusion.1.refs_0_, s32[2]{0:T(128)} %constant.87.clone.refs_1_, f32[256,8192]{1,0:T(8,128)} %refs_2_.9, f32[256,8192]{1,0:T(8,128)} %refs_3_.7, ...), custom_call_target="tpu_custom_call", output_to_operand_aliasing={{0}: (8, {}), {1}: (9, {}), {2}: (10, {})} | custom-call | flops 20971520 | bytes 27262976 | tf_op jit(solution)/shard_map/adam/pallas_call | solution.py:60
  449.5 8.3 %collective-permute-done.42.refs_4_ = bf16[2,128,768]{2,1,0:T(8,128)(2,1)} collective-permute-done((bf16[2,128,768]{2,1,0:T(8,128)(2,1)}, bf16[2,128,768]{2,1,0:T(8,128)(2,1)}, u32[]{:S(2)}, u32[]{:S(2)}) %collective-permute-start.42) | collective-permute-done | bytes 393248 | tf_op jit(solution)/shard_map/ppermute | solution.py:1070
  457.8 7.7 %collective-permute-done.41.refs_2_ = bf16[2,128,1280]{2,1,0:T(8,128)(2,1)} collective-permute-done((bf16[2,128,1280]{2,1,0:T(8,128)(2,1)}, bf16[2,128,1280]{2,1,0:T(8,128)(2,1)}, u32[]{:S(2)}, u32[]{:S(2)}) %collective-permute-start.41) | collective-permute-done | bytes 655392 | tf_op jit(solution)/shard_map/ppermute | solution.py:1070
  471.5 10.3 %adam.6 = (f32[256,4096]{1,0:T(8,128)}, f32[256,4096]{1,0:T(8,128)}, f32[256,4096]{1,0:T(8,128)}) custom-call(s32[3]{0:T(128)} %pad_add_fusion.1.refs_0_, s32[5]{0:T(128)} %constant.88.clone.refs_1_, f32[256,4096]{1,0:T(8,128)} %refs_2_.11, f32[256,4096]{1,0:T(8,128)} %refs_3_.9, f32[256,4096]{1,0:T(8,128)} %refs_4_.9, ...), custom_call_target="tpu_custom_call" | custom-call | flops 13107200 | bytes 17039360 | tf_op jit(solution)/shard_map/adam/pallas_call | solution.py:60
  481.8 7.6 %collective-permute-done.45.refs_2_ = bf16[2,128,768]{2,1,0:T(8,128)(2,1)} collective-permute-done((bf16[2,128,768]{2,1,0:T(8,128)(2,1)}, bf16[2,128,768]{2,1,0:T(8,128)(2,1)}, u32[]{:S(2)}, u32[]{:S(2)}) %collective-permute-start.45) | collective-permute-done | bytes 393248 | tf_op jit(solution)/shard_map/ppermute | solution.py:1070
  (124 shorter events, 152.6 us)
Async XLA Ops:
  7.2 101.9 %all-gather.3.cloned.1.call-start = ((), (), s32[]{:S(2)}) async-start(), calls=%async_computation | async-start | bytes 5242880 | tf_op jit(solution)/shard_map/all_gather | solution.py:1089
  11.2 29.2 %collective-permute-start = (bf16[144,4096]{1,0:T(8,128)(2,1)}, bf16[144,4096]{1,0:T(8,128)(2,1)}, u32[]{:S(2)}, u32[]{:S(2)}) collective-permute-start(bf16[144,4096]{1,0:T(8,128)(2,1)} %side.16.refs_3_), channel_id=1, source_target_pairs={{0,2},{1,3},{2,0},{3,1},{4,6},{5,7},{6,4},{7,5},{8,10},{9,11},{10,... | collective-permute-start | bytes 3538952 | tf_op jit(solution)/shard_map/ppermute | solution.py:1078
  14.2 27.7 %collective-permute-start.1 = (bf16[144,4096]{1,0:T(8,128)(2,1)}, bf16[144,4096]{1,0:T(8,128)(2,1)}, u32[]{:S(2)}, u32[]{:S(2)}) collective-permute-start(bf16[144,4096]{1,0:T(8,128)(2,1)} %side.16.refs_3_), channel_id=1, source_target_pairs={{0,1},{1,0},{2,3},{3,2},{4,5},{5,4},{6,7},{7,6},{8,9},{9,8},{10,11... | collective-permute-start | bytes 3538952 | tf_op jit(solution)/shard_map/ppermute | solution.py:1078
  46.3 112.7 %all-gather.5.cloned.1.call-start = ((), (), s32[]{:S(2)}) async-start(), calls=%async_computation.1 | async-start | bytes 5242880 | tf_op jit(solution)/shard_map/all_gather | solution.py:1089
  46.7 25.2 %collective-permute-start.2 = (bf16[144,4096]{1,0:T(8,128)(2,1)}, bf16[144,4096]{1,0:T(8,128)(2,1)}, u32[]{:S(2)}, u32[]{:S(2)}) collective-permute-start(bf16[144,4096]{1,0:T(8,128)(2,1)} %collective-permute-done.1.refs_2_.refs_14_), channel_id=1, source_target_pairs={{0,4},{4,0},{8,12},{12,8},{16,20},{20,16},{24,28},{28,24},{1,5},{5... | collective-permute-start | bytes 3538952 | tf_op jit(solution)/shard_map/ppermute | solution.py:1070
  46.7 25.2 %collective-permute-start.3 = (bf16[144,4096]{1,0:T(8,128)(2,1)}, bf16[144,4096]{1,0:T(8,128)(2,1)}, u32[]{:S(2)}, u32[]{:S(2)}) collective-permute-start(bf16[144,4096]{1,0:T(8,128)(2,1)} %collective-permute-done.refs_1_.refs_3_.refs_15_), channel_id=1, source_target_pairs={{0,4},{4,0},{8,12},{12,8},{16,20},{20,16},{24,28},{28,24},{1,5},{5... | collective-permute-start | bytes 3538952 | tf_op jit(solution)/shard_map/ppermute | solution.py:1070
  165.5 31.7 %collective-permute-start.11 = (bf16[2,128,2048]{2,1,0:T(8,128)(2,1)}, bf16[2,128,2048]{2,1,0:T(8,128)(2,1)}, u32[]{:S(2)}, u32[]{:S(2)}) collective-permute-start(bf16[2,128,2048]{2,1,0:T(8,128)(2,1)} %get-tuple-element.136), channel_id=1, source_target_pairs={{0,1},{1,0},{2,3},{3,2},{4,5},{5,4},{6,7},{7,6},{8,9},{9,8},{10,11... | collective-permute-start | bytes 3145736 | tf_op jit(solution)/shard_map/ppermute | solution.py:1078
  167.0 30.2 %collective-permute-start.12 = (bf16[2,128,2048]{2,1,0:T(8,128)(2,1)}, bf16[2,128,2048]{2,1,0:T(8,128)(2,1)}, u32[]{:S(2)}, u32[]{:S(2)}) collective-permute-start(bf16[2,128,2048]{2,1,0:T(8,128)(2,1)} %get-tuple-element.137), channel_id=1, source_target_pairs={{0,2},{1,3},{2,0},{3,1},{4,6},{5,7},{6,4},{7,5},{8,10},{9,11},{10,... | collective-permute-start | bytes 3145736 | tf_op jit(solution)/shard_map/ppermute | solution.py:1078
  197.1 31.6 %collective-permute-start.15 = (bf16[2,512,2048]{2,1,0:T(8,128)(2,1)}, bf16[2,512,2048]{2,1,0:T(8,128)(2,1)}, u32[]{:S(2)}, u32[]{:S(2)}) collective-permute-start(bf16[2,512,2048]{2,1,0:T(8,128)(2,1)} %get-tuple-element.142), channel_id=1, source_target_pairs={{0,4},{4,0},{8,12},{12,8},{16,20},{20,16},{24,28},{28,24},{1,5},{5... | collective-permute-start | bytes 12582920 | tf_op jit(solution)/shard_map/ppermute | solution.py:1070
  202.0 26.6 %collective-permute-start.13 = (bf16[1,128,2048]{2,1,0:T(8,128)(2,1)}, bf16[1,128,2048]{2,1,0:T(8,128)(2,1)}, u32[]{:S(2)}, u32[]{:S(2)}) collective-permute-start(bf16[1,128,2048]{2,1,0:T(8,128)(2,1)} %get-tuple-element.140), channel_id=1, source_target_pairs={{0,2},{1,3},{2,0},{3,1},{4,6},{5,7},{6,4},{7,5},{8,10},{9,11},{10,... | collective-permute-start | bytes 1572872 | tf_op jit(solution)/shard_map/ppermute | solution.py:1078
  203.5 25.2 %collective-permute-start.14 = (bf16[1,128,2048]{2,1,0:T(8,128)(2,1)}, bf16[1,128,2048]{2,1,0:T(8,128)(2,1)}, u32[]{:S(2)}, u32[]{:S(2)}) collective-permute-start(bf16[1,128,2048]{2,1,0:T(8,128)(2,1)} %get-tuple-element.141), channel_id=1, source_target_pairs={{0,1},{1,0},{2,3},{3,2},{4,5},{5,4},{6,7},{7,6},{8,9},{9,8},{10,11... | collective-permute-start | bytes 1572872 | tf_op jit(solution)/shard_map/ppermute | solution.py:1078
  236.0 26.2 %collective-permute-start.16 = (bf16[2,128,2048]{2,1,0:T(8,128)(2,1)}, bf16[2,128,2048]{2,1,0:T(8,128)(2,1)}, u32[]{:S(2)}, u32[]{:S(2)}) collective-permute-start(bf16[2,128,2048]{2,1,0:T(8,128)(2,1)} %bitcast.37), channel_id=1, source_target_pairs={{0,8},{4,12},{24,16},{28,20},{1,9},{5,13},{25,17},{29,21},{2,10},{... | collective-permute-start | bytes 3145736 | tf_op jit(solution)/shard_map/ppermute | solution.py:1075
  240.3 25.0 %collective-permute-start.17 = (bf16[2,128,2048]{2,1,0:T(8,128)(2,1)}, bf16[2,128,2048]{2,1,0:T(8,128)(2,1)}, u32[]{:S(2)}, u32[]{:S(2)}) collective-permute-start(bf16[2,128,2048]{2,1,0:T(8,128)(2,1)} %get-tuple-element.148), channel_id=1, source_target_pairs={{0,1},{1,0},{2,3},{3,2},{4,5},{5,4},{6,7},{7,6},{8,9},{9,8},{10,11... | collective-permute-start | bytes 3145736 | tf_op jit(solution)/shard_map/ppermute | solution.py:1078
  241.8 24.7 %collective-permute-start.18 = (bf16[2,128,2048]{2,1,0:T(8,128)(2,1)}, bf16[2,128,2048]{2,1,0:T(8,128)(2,1)}, u32[]{:S(2)}, u32[]{:S(2)}) collective-permute-start(bf16[2,128,2048]{2,1,0:T(8,128)(2,1)} %get-tuple-element.149), channel_id=1, source_target_pairs={{0,2},{1,3},{2,0},{3,1},{4,6},{5,7},{6,4},{7,5},{8,10},{9,11},{10,... | collective-permute-start | bytes 3145736 | tf_op jit(solution)/shard_map/ppermute | solution.py:1078
  316.3 30.7 %collective-permute-start.28 = (bf16[2,512,768]{2,1,0:T(8,128)(2,1)}, bf16[2,512,768]{2,1,0:T(8,128)(2,1)}, u32[]{:S(2)}, u32[]{:S(2)}) collective-permute-start(bf16[2,512,768]{2,1,0:T(8,128)(2,1)} %get-tuple-element.172), channel_id=1, source_target_pairs={{0,4},{4,0},{8,12},{12,8},{16,20},{20,16},{24,28},{28,24},{1,5},{5... | collective-permute-start | bytes 4718600 | tf_op jit(solution)/shard_map/ppermute | solution.py:1070
  316.3 28.5 %collective-permute-start.24 = (bf16[2,128,2048]{2,1,0:T(8,128)(2,1)}, bf16[2,128,2048]{2,1,0:T(8,128)(2,1)}, u32[]{:S(2)}, u32[]{:S(2)}) collective-permute-start(bf16[2,128,2048]{2,1,0:T(8,128)(2,1)} %get-tuple-element.164.refs_4_.refs_1_), channel_id=1, source_target_pairs={{8,0},{12,4},{16,24},{20,28},{9,1},{13,5},{17,25},{21,29},{10,2},{... | collective-permute-start | bytes 3145736 | tf_op jit(solution)/shard_map/ppermute | solution.py:1075
  317.6 29.4 %collective-permute-start.25 = (bf16[2,128,2048]{2,1,0:T(8,128)(2,1)}, bf16[2,128,2048]{2,1,0:T(8,128)(2,1)}, u32[]{:S(2)}, u32[]{:S(2)}) collective-permute-start(bf16[2,128,2048]{2,1,0:T(8,128)(2,1)} %bitcast.34), channel_id=1, source_target_pairs={{0,8},{4,12},{24,16},{28,20},{1,9},{5,13},{25,17},{29,21},{2,10},{... | collective-permute-start | bytes 3145736 | tf_op jit(solution)/shard_map/ppermute | solution.py:1075
  354.1 29.8 %collective-permute-start.29 = (bf16[2,128,2048]{2,1,0:T(8,128)(2,1)}, bf16[2,128,2048]{2,1,0:T(8,128)(2,1)}, u32[]{:S(2)}, u32[]{:S(2)}) collective-permute-start(bf16[2,128,2048]{2,1,0:T(8,128)(2,1)} %get-tuple-element.185.refs_1_), channel_id=1, source_target_pairs={{8,16},{12,20},{16,8},{20,12},{9,17},{13,21},{17,9},{21,13},{10,18... | collective-permute-start | bytes 3145736 | tf_op jit(solution)/shard_map/ppermute | solution.py:1075
  355.8 28.1 %collective-permute-start.32 = (bf16[2,128,768]{2,1,0:T(8,128)(2,1)}, bf16[2,128,768]{2,1,0:T(8,128)(2,1)}, u32[]{:S(2)}, u32[]{:S(2)}) collective-permute-start(bf16[2,128,768]{2,1,0:T(8,128)(2,1)} %get-tuple-element.190), channel_id=1, source_target_pairs={{0,1},{1,0},{2,3},{3,2},{4,5},{5,4},{6,7},{7,6},{8,9},{9,8},{10,11... | collective-permute-start | bytes 1179656 | tf_op jit(solution)/shard_map/ppermute | solution.py:1078
  356.6 27.3 %collective-permute-start.33 = (bf16[2,128,768]{2,1,0:T(8,128)(2,1)}, bf16[2,128,768]{2,1,0:T(8,128)(2,1)}, u32[]{:S(2)}, u32[]{:S(2)}) collective-permute-start(bf16[2,128,768]{2,1,0:T(8,128)(2,1)} %get-tuple-element.191), channel_id=1, source_target_pairs={{0,2},{1,3},{2,0},{3,1},{4,6},{5,7},{6,4},{7,5},{8,10},{9,11},{10,... | collective-permute-start | bytes 1179656 | tf_op jit(solution)/shard_map/ppermute | solution.py:1078
  388.2 41.8 %collective-permute-start.36 = (bf16[2,128,2048]{2,1,0:T(8,128)(2,1)}, bf16[2,128,2048]{2,1,0:T(8,128)(2,1)}, u32[]{:S(2)}, u32[]{:S(2)}) collective-permute-start(bf16[2,128,2048]{2,1,0:T(8,128)(2,1)} %get-tuple-element.195.refs_9_.refs_1_), channel_id=1, source_target_pairs={{8,0},{12,4},{16,24},{20,28},{9,1},{13,5},{17,25},{21,29},{10,2},{... | collective-permute-start | bytes 3145736 | tf_op jit(solution)/shard_map/ppermute | solution.py:1075
  389.5 40.5 %collective-permute-start.37 = (bf16[2,128,1280]{2,1,0:T(8,128)(2,1)}, bf16[2,128,1280]{2,1,0:T(8,128)(2,1)}, u32[]{:S(2)}, u32[]{:S(2)}) collective-permute-start(bf16[2,128,1280]{2,1,0:T(8,128)(2,1)} %bitcast.39), channel_id=1, source_target_pairs={{0,8},{4,12},{8,0},{12,4},{16,24},{20,28},{24,16},{28,20},{1,9},{5... | collective-permute-start | bytes 1966088 | tf_op jit(solution)/shard_map/ppermute | solution.py:1070
  434.1 31.4 %collective-permute-start.41 = (bf16[2,128,1280]{2,1,0:T(8,128)(2,1)}, bf16[2,128,1280]{2,1,0:T(8,128)(2,1)}, u32[]{:S(2)}, u32[]{:S(2)}) collective-permute-start(bf16[2,128,1280]{2,1,0:T(8,128)(2,1)} %get-tuple-element.201.refs_1_), channel_id=1, source_target_pairs={{0,16},{4,20},{8,24},{12,28},{16,0},{20,4},{24,8},{28,12},{1,17},{... | collective-permute-start | bytes 1966088 | tf_op jit(solution)/shard_map/ppermute | solution.py:1070
  434.1 23.6 %collective-permute-start.42 = (bf16[2,128,768]{2,1,0:T(8,128)(2,1)}, bf16[2,128,768]{2,1,0:T(8,128)(2,1)}, u32[]{:S(2)}, u32[]{:S(2)}) collective-permute-start(bf16[2,128,768]{2,1,0:T(8,128)(2,1)} %bitcast.41), channel_id=1, source_target_pairs={{0,8},{4,12},{8,0},{12,4},{16,24},{20,28},{24,16},{28,20},{1,9},{5... | collective-permute-start | bytes 1179656 | tf_op jit(solution)/shard_map/ppermute | solution.py:1070
  (28 other events, 397.2 us)
Sparse Core Ops, SparseCore 0:
  46.4 57.9 all-gather.2
  106.3 52.6 all-gather.4

commit v3 on v2

--- a/solution.py
+++ b/solution.py
@@ -721,9 +721,7 @@
         after=after,
         scratch=[pltpu.VMEM((rows, rows), F32), pltpu.VMEM((rows, LANES), F32)],
         cost=cost(
-            (80 if first == 0 else 20) * rows * rows * LANES * count,
-            16 * rows * LANES * count,
-            2 * rows * rows * count,
+            (80 if first == 0 else 2) * rows * rows * LANES * count, rows * LANES * count
         ),
         name="attend_back",
     )
@@ -1141,10 +1139,13 @@
         return Weights(pieces, plan, jnp.stack(offs).astype(jnp.int32))
 
 
+LINE, AT_ONCE, EXCHANGE = range(3)
+
+
 class Reduce:
-    def __init__(self, links, line):
+    def __init__(self, links, way):
         self.links = links
-        self.line = line
+        self.way = way
         self.stage = 0
         self.groups = []
 
@@ -1156,7 +1157,7 @@
     def job(self, steps):
         if self.stage > 2:
             own, received = self.groups[0]
-            if self.line and self.stage == 5:
+            if self.way == LINE and self.stage == 5:
                 return job_pick(own, received, steps)
             return job_add(own, received, steps)
         blocks = self.groups[0][0].shape[1]
@@ -1185,12 +1186,18 @@
             return
         if stage == 2:
             own = own.reshape(2, own.shape[2], own.shape[3])
-        if self.line and stage < 5:
+        if self.way == AT_ONCE:
+            self.own = links.over_dp(own)
+        elif self.way == LINE and stage < 5:
             self.groups = [(own, links.along_dp(own, stage - 2))]
-        elif not self.line and stage < 4:
+        elif self.way == EXCHANGE and stage < 4:
             self.groups = [(own, links.across_dp(own, 2 * (stage - 1)))]
         else:
             self.grads = (own, links.swap(own))
+
+    def close(self, behind):
+        mine, _ = lax.optimization_barrier((self.own, behind))
+        self.grads = (mine, self.links.swap(mine))
 
 
 class Wide:
@@ -1359,9 +1366,9 @@
         grad_bias_up.append(gbias)
         return own, sib
 
-    def unit(line, *grads):
+    def unit(way, *grads):
         if links.fast:
-            return Reduce(links, line).add(*grads)
+            return Reduce(links, way).add(*grads)
         return Wide(links, side.jobs([job_join(blocked(grads[0]), blocked(links.swap(grads[1])), 4)], steps=4)[0])
 
     def reduce(units, jobs=(), steps=2):
@@ -1371,9 +1378,9 @@
 
     group_a = feed(0, wide, wide.at(block))
     more_wide = links.gathered(more_wide, grad_bias_up[0])
-    unit_a = unit(True, *group_a)
+    unit_a = unit(LINE, *group_a)
     reduce([unit_a], steps=4)
-    unit_b = unit(True, *feed(block, more_wide, more_wide.at(block)))
+    unit_b = unit(AT_ONCE, *feed(block, more_wide, more_wide.at(block)))
     reduce([unit_a], steps=4)
     (
         grad_after,
@@ -1396,8 +1403,11 @@
             after=side.order,
         )
     )
-    unit_c = unit(False, own_out, sib_out)
-    reduce([unit_a, unit_b], steps=4)
+    if links.fast:
+        unit_b.add(own_out, sib_out)
+    else:
+        unit_e = unit(AT_ONCE, own_out, sib_out)
+    reduce([unit_a])
     grads, biases = [], []
 
     def attend_back(first):
@@ -1412,13 +1422,11 @@
 
     attend_back(0)
     reduce([unit_a, unit_b], steps=4)
-    if links.fast:
-        unit_c.add(*project(0))
-    else:
-        unit_e = unit(False, *project(0))
+    unit_c = unit(EXCHANGE, *project(0))
     attend_back(pairs // 2)
     reduce([unit_a, unit_b, unit_c], steps=4)
-    unit_d = unit(False, *project(1))
+    unit_d = unit(EXCHANGE, *project(1))
+    reduce([unit_c])
     grad_input, grad_gain_one, grad_shift_one = side.then(
         run_input(attn_weights, grads, tokens, grad_after, small, GAIN_ONE, after=side.order)
     )
@@ -1428,7 +1436,7 @@
     (grad_small,) = reduce([unit_a, unit_b, unit_c, unit_d], [job_lay(small_grads)])
 
     def pick_feed(number, arrays):
-        return [arrays[0][number]]
+        return [arrays[0][number, :, :block]]
 
     def adam_mlp(number, item, earlier):
         return side.then(
@@ -1448,22 +1456,21 @@
 
     def pick_heads(number, arrays):
         left, right = arrays[0][0], arrays[0][1]
-        skip = arrays[0].shape[2] - 3 * out_block // 2
-        split = skip + out_block // 2
+        split = out_block // 2
+        if number > 2:
+            return [arrays[1][number - 3, :, block:]]
         return (
-            [left[:, skip : skip + out_block]],
-            [left[:, skip + out_block :], right[:, skip:split]],
+            [left[:, :out_block]],
+            [left[:, out_block:], right[:, :split]],
             [right[:, split:]],
-            [left[:, :skip]],
-            [right[:, :skip]],
         )[number]
 
-    def adam_attn(item, places, earlier):
+    def adam_attn(items, places, earlier):
         return side.then(
             run_adam(
                 core_arr,
                 attn_state,
-                [item.grads],
+                [item.grads for item in items],
                 out_block,
                 places,
                 pick_heads,
@@ -1494,26 +1501,27 @@
             return total, move(total) if move else None
 
         mlp_new = adam_mlp(0, unit_a, None)
-        grad_small, moved = step([unit_b, unit_c, unit_d], shard_move(2))
+        grad_small, moved = step([unit_c, unit_d], shard_move(2))
         output = output_now()
-        grad_small, moved = step([unit_b, unit_c, unit_d], links.swap)
+        grad_small, moved = step([unit_c, unit_d], links.swap)
+        unit_b.close(grad_small)
+        attn_new = adam_attn([unit_c], [0, 2, 4], None)
+        grad_small, moved = step([unit_d], dp_move(2))
         mlp_new = adam_mlp(1, unit_b, mlp_new)
-        grad_small, moved = step([unit_c, unit_d], dp_move(2))
-        attn_new = adam_attn(unit_c, [0, 2, 4, 6, 7], None)
         grad_small, moved = step([unit_d], dp_move(4))
-        attn_new = adam_attn(unit_d, [1, 3, 5], attn_new)
+        attn_new = adam_attn([unit_d, unit_b], [1, 3, 5, 6, 7], attn_new)
         grad_small, _ = step([], None)
     else:
         for item in (unit_a, unit_b, unit_c, unit_d, unit_e):
             item.finish()
-        unit_c.own = jnp.concatenate([unit_c.own, unit_e.own], axis=2)
+        unit_b.own = jnp.concatenate([unit_b.own, unit_e.own], axis=2)
         for item in (unit_a, unit_b, unit_c, unit_d):
             item.grads = (item.own, links.swap(item.own))
         grad_small = lax.psum(grad_small, ("dp", "shard"))
         output = output_now()
         mlp_new = adam_mlp(1, unit_b, adam_mlp(0, unit_a, None))
-        attn_new = adam_attn(unit_c, [0, 2, 4, 6, 7], None)
-        attn_new = adam_attn(unit_d, [1, 3, 5], attn_new)
+        attn_new = adam_attn([unit_c], [0, 2, 4], None)
+        attn_new = adam_attn([unit_d, unit_b], [1, 3, 5, 6, 7], attn_new)
     grad_small = lax.dynamic_slice_in_dim(grad_small, links.shard * small_size, small_size, 1)[0]
     small_new = adamw(*small_state, grad_small, 0.4, 0.0)
     return (output, grad_input, *attn_new, *mlp_new, *small_new)

time: 517 us -> 506 us (0.979)
  starting transfers between devices: 54.1 us -> 40.9 us
    ppermute x22, waiting for transfers between devices: 43.7 us -> 20.9 us  [across_dp(): lax.ppermute(value, 'dp', [(d, d ^ bit) for d in range(self.replicas)])]
    psum x0 -> x1, waiting for transfers between devices: none -> 19.5 us  [over_dp(): return lax.psum(values, 'dp', axis_index_groups=groups)]
    ppermute x6 -> x3, starting transfers between devices: 17.3 us -> 7.27 us  [along_dp(): return lax.ppermute(value, 'dp', pairs)]
    ppermute x22, waiting for transfers between devices: 44.8 us -> 53.6 us  [across_shard(): lax.ppermute(value, 'shard', [(s, s ^ bit) for s in range(self.shards)])]
    pallas_call x33 -> x34, Pallas kernels: 334 us -> 333 us  [call(): pl.pallas_call(run, grid_spec=pltpu.PrefetchScalarGridSpec(num_scalar_pre...]
  transfers between devices with their start and end apart: 52 -> 50, of which waited for: 17 -> 17; matrix products, arithmetic and copies ran while one was open for 1% -> 1% of each run, Pallas kernels for 53% -> 57%
where the time goes in v3:
time: 506 us; the launch traced here: 502 us
  Pallas kernels  333 us (66%)
  waiting for transfers between devices  107 us (21%)
  starting transfers between devices  40.9 us (8%)
  between operations  14.4 us (3%)
  other arithmetic  5.54 us (1%)
    pallas_call x34, Pallas kernels, call(): pl.pallas_call(run, grid_spec=pltpu.PrefetchScalarGridSpec(num_scalar_pre...  333 us
    ppermute x22, waiting for transfers between devices, across_shard(): lax.ppermute(value, 'shard', [(s, s ^ bit) for s in range(self.shards)])  53.6 us
    ppermute x22, starting transfers between devices, across_shard(): lax.ppermute(value, 'shard', [(s, s ^ bit) for s in range(self.shards)])  24.2 us
    ppermute x22, waiting for transfers between devices, across_dp(): lax.ppermute(value, 'dp', [(d, d ^ bit) for d in range(self.replicas)])  20.9 us
    psum x1, waiting for transfers between devices, over_dp(): return lax.psum(values, 'dp', axis_index_groups=groups)  19.5 us
  transfers between devices with their start and end apart: 50, of which 17 were waited for; matrix products, arithmetic and copies ran while one was open for 1% of the time, Pallas kernels for 57%

profile of v3, /device:TPU:0, one launch (start us, length us, event | category | flops | bytes accessed | tf_op | source)
XLA Modules:
  0.0 501.8 jit_solution(9001539394610777981)
XLA Ops:
  31.3 9.2 %collective-permute-done.refs_1_.refs_3_.refs_15_ = bf16[144,4096]{1,0:T(8,128)(2,1)} collective-permute-done((bf16[144,4096]{1,0:T(8,128)(2,1)}, bf16[144,4096]{1,0:T(8,128)(2,1)}, u32[]{:S(2)}, u32[]{:S(2)}) %collective-permute-start) | collective-permute-done | bytes 1179680 | tf_op jit(solution)/shard_map/ppermute | solution.py:1076
  48.9 19.5 %collective-permute-done.5.refs_4_.refs_7_.refs_19_ = bf16[80,4096]{1,0:T(8,128)(2,1)} collective-permute-done((bf16[80,4096]{1,0:T(8,128)(2,1)}, bf16[80,4096]{1,0:T(8,128)(2,1)}, u32[]{:S(2)}, u32[]{:S(2)}) %collective-permute-start.5) | collective-permute-done | bytes 655392 | tf_op jit(solution)/shard_map/ppermute | solution.py:1076
  72.1 14.2 %qkv.1 = (bf16[1024,3072]{1,0:T(8,128)(2,1)}, bf16[1024,1024]{1,0:T(8,128)(2,1)}) custom-call(s32[9]{0:T(128)} %stack.59.refs_0_.refs_12_, bf16[256,4096]{1,0:T(8,128)(2,1)} %side.19.refs_5_.refs_1_.refs_13_, bf16[144,4096]{1,0:T(8,128)(2,1)} %collective-permute-done.1.refs_2_.refs_14_, bf16[144,4096]{1,0:T(8,128)(2,1)} %collective-permute-done.refs_1_.refs_3_.refs_15_, ...), custom_call_target="tpu_custom_call" | custom-call | flops 6442450944 | bytes 16777216 | tf_op jit(solution)/shard_map/qkv/pallas_call | solution.py:60
  86.3 22.9 %attend.1 = (bf16[1024,1024]{1,0:T(8,128)(2,1)}, f32[8,2,1024]{2,1,0:T(2,128)}) custom-call(s32[4]{0:T(128)} %bitcast.46, bf16[1024,3072]{1,0:T(8,128)(2,1)} %get-tuple-element.117.refs_1_.refs_2_.refs_3_.refs_4_, bf16[1024,3072]{1,0:T(8,128)(2,1)} %get-tuple-element.117.refs_1_.refs_2_.refs_3_.refs_4_, ...), custom_call_target="tpu_custom_call" | custom-call | flops 8589934592 | bytes 8388608 | tf_op jit(solution)/shard_map/attend/pallas_call | solution.py:60
  109.9 10.4 %after.1 = (f32[1024,1024]{1,0:T(8,128)}, bf16[1024,1024]{1,0:T(8,128)(2,1)}, bf16[1024,1024]{1,0:T(8,128)(2,1)}, bf16[1024,1024]{1,0:T(8,128)(2,1)}) custom-call(s32[9]{0:T(128)} %stack.59.refs_0_.refs_12_, bf16[256,4096]{1,0:T(8,128)(2,1)} %side.19.refs_5_.refs_1_.refs_13_, bf16[144,4096]{1,0:T(8,128)(2,1)} %collective-permute-done.1.refs_2_.refs_14_, ...), custom_call_target="tpu_custom_call" | custom-call | flops 2147483648 | bytes 14680064 | tf_op jit(solution)/shard_map/after/pallas_call | solution.py:60
  120.3 29.1 %feed.2 = (bf16[1024,4096]{1,0:T(8,128)(2,1)}, bf16[1024,4096]{1,0:T(8,128)(2,1)}, bf16[2,512,2048]{2,1,0:T(8,128)(2,1)}, bf16[2,512,2048]{2,1,0:T(8,128)(2,1)}, f32[1,2048]{1,0:T(1,128)}) custom-call(s32[8]{0:T(128)} %pad_add_fusion.refs_0_.refs_3_.refs_6_.refs_9_, bf16[512,4096]{1,0:T(8,128)(2,1)} %all-gather.3.cloned.1.call-done.refs_18_.refs_1_.refs_4_, ...), custom_call_target="tpu_custom_call" | custom-call | flops 17179869184 | bytes 50331648 | tf_op jit(solution)/shard_map/feed/pallas_call | solution.py:60
  150.0 9.0 %all-gather.5.cloned.1.call-done.refs_1_.refs_4_.refs_7_.refs_10_ = bf16[512,4096]{1,0:T(8,128)(2,1)} async-done(((bf16[128,4096]{1,0:T(8,128)(2,1)}), bf16[512,4096]{1,0:T(8,128)(2,1)}) %all-gather.5.cloned.1.call-update) | async-done | bytes 4194320 | tf_op jit(solution)/shard_map/all_gather | solution.py:1087
  167.5 29.6 %feed.3 = (bf16[1024,4096]{1,0:T(8,128)(2,1)}, bf16[1024,4096]{1,0:T(8,128)(2,1)}, bf16[2,512,2048]{2,1,0:T(8,128)(2,1)}, bf16[2,512,2048]{2,1,0:T(8,128)(2,1)}, f32[1,2048]{1,0:T(1,128)}) custom-call(s32[8]{0:T(128)} %pad_add_fusion.refs_0_.refs_3_.refs_6_.refs_9_, ...), custom_call_target="tpu_custom_call", output_to_operand_aliasing={{0}: (12, {}), {1}: (13, {})} | custom-call | flops 17179869184 | bytes 50331648 | tf_op jit(solution)/shard_map/feed/pallas_call | solution.py:60
  204.1 24.5 %middle.1 = (f32[1024,1024]{1,0:T(8,128)}, bf16[1024,1024]{1,0:T(8,128)(2,1)}, bf16[2,512,512]{2,1,0:T(8,128)(2,1)}, bf16[2,512,512]{2,1,0:T(8,128)(2,1)}, f32[1...) custom-call(s32[8]{0:T(128)} %pad_add_fusion.refs_0_.refs_3_.refs_6_.refs_9_, ...), custom_call_target="tpu_custom_call" | custom-call | flops 51539607552 | bytes 125829120 | tf_op jit(solution)/shard_map/middle/pallas_call | solution.py:60
  236.1 18.8 %attend_back.2 = (bf16[1024,512]{1,0:T(8,128)(2,1)}, bf16[1024,512]{1,0:T(8,128)(2,1)}, bf16[1024,512]{1,0:T(8,128)(2,1)}, f32[1,512]{1,0:T(1,128)}, f32[1,512]{1,0:T(1,128)}) custom-call(s32[4]{0:T(128)} %bitcast.47, bf16[1024,3072]{1,0:T(8,128)(2,1)} %get-tuple-element.117.refs_1_.refs_2_.refs_3_.refs_4_, ...), custom_call_target="tpu_custom_call" | custom-call | flops 42949672960 | bytes 524288 | tf_op jit(solution)/shard_map/attend_back/pallas_call | solution.py:60
  258.5 7.9 %side.25 = (bf16[2,128,2048]{2,1,0:T(8,128)(2,1)}, bf16[2,2,128,2560]{3,2,1,0:T(8,128)(2,1)}, bf16[2,128,2560]{2,1,0:T(8,128)(2,1)}, bf16[2,128,2560]{2,1,0:T(8,128)(2,1)}) custom-call(s32[3]{0:T(128)} %pad_add_fusion.1.refs_0_, bf16[2,128,2048]{2,1,0:T(8,128)(2,1)} %bitcast.35, bf16[2,128,2048]{2,1,0:T(8,128)(2,1)} %collective-permute-done.15.refs_2_, ...), custom_call_target="tpu_custom_call" | custom-call | bytes 25165824 | tf_op jit(solution)/shard_map/side/pallas_call | solution.py:60
  266.4 7.1 %project.2 = (bf16[2,512,768]{2,1,0:T(8,128)(2,1)}, bf16[2,512,768]{2,1,0:T(8,128)(2,1)}) custom-call(bf16[1024,1024]{1,0:T(8,128)(2,1)} %get-tuple-element.151.refs_0_, bf16[1024,512]{1,0:T(8,128)(2,1)} %get-tuple-element.146.refs_7_.refs_1_.refs_10_, bf16[1024,512]{1,0:T(8,128)(2,1)} %get-tuple-element.152.refs_2_.refs_11_, ...), custom_call_target="tpu_custom_call" | custom-call | flops 3221225472 | bytes 7340032 | tf_op jit(solution)/shard_map/project/pallas_call | solution.py:60
  277.2 19.0 %attend_back.3 = (bf16[1024,512]{1,0:T(8,128)(2,1)}, bf16[1024,512]{1,0:T(8,128)(2,1)}, bf16[1024,512]{1,0:T(8,128)(2,1)}, f32[1,512]{1,0:T(1,128)}, f32[1,512]{1,0:T(1,128)}) custom-call(s32[4]{0:T(128)} %bitcast.48, bf16[1024,3072]{1,0:T(8,128)(2,1)} %get-tuple-element.117.refs_1_.refs_2_.refs_3_.refs_4_, ...), custom_call_target="tpu_custom_call" | custom-call | flops 1073741824 | bytes 524288 | tf_op jit(solution)/shard_map/attend_back/pallas_call | solution.py:60
  296.2 8.8 %collective-permute-done.19.refs_4_ = bf16[2,128,2560]{2,1,0:T(8,128)(2,1)} collective-permute-done((bf16[2,128,2560]{2,1,0:T(8,128)(2,1)}, bf16[2,128,2560]{2,1,0:T(8,128)(2,1)}, u32[]{:S(2)}, u32[]{:S(2)}) %collective-permute-start.19) | collective-permute-done | bytes 1310752 | tf_op jit(solution)/shard_map/ppermute | solution.py:1076
  306.2 7.2 %side.26 = (bf16[2,128,2048]{2,1,0:T(8,128)(2,1)}, bf16[2,1,128,2560]{3,2,1,0:T(8,128)(2,1)}, bf16[1,128,2560]{2,1,0:T(8,128)(2,1)}, bf16[1,128,2560]{2,1,0:T(8,...) custom-call(s32[3]{0:T(128)} %pad_add_fusion.1.refs_0_, ...), custom_call_target="tpu_custom_call" | custom-call | bytes 20971520 | tf_op jit(solution)/shard_map/side/pallas_call | solution.py:60
  313.4 7.1 %project.3 = (bf16[2,512,768]{2,1,0:T(8,128)(2,1)}, bf16[2,512,768]{2,1,0:T(8,128)(2,1)}) custom-call(bf16[1024,1024]{1,0:T(8,128)(2,1)} %get-tuple-element.151.refs_0_, bf16[1024,512]{1,0:T(8,128)(2,1)} %get-tuple-element.156.refs_8_.refs_1_.refs_13_, bf16[1024,512]{1,0:T(8,128)(2,1)} %get-tuple-element.164.refs_2_.refs_14_, ...), custom_call_target="tpu_custom_call" | custom-call | flops 3221225472 | bytes 7340032 | tf_op jit(solution)/shard_map/project/pallas_call | solution.py:60
  323.7 8.6 %collective-permute-done.25.refs_2_ = bf16[2,128,768]{2,1,0:T(8,128)(2,1)} collective-permute-done((bf16[2,128,768]{2,1,0:T(8,128)(2,1)}, bf16[2,128,768]{2,1,0:T(8,128)(2,1)}, u32[]{:S(2)}, u32[]{:S(2)}) %collective-permute-start.25) | collective-permute-done | bytes 393248 | tf_op jit(solution)/shard_map/ppermute | solution.py:1076
  345.3 15.7 %grad_input.1 = (f32[1024,1024]{1,0:T(8,128)}, f32[1,1024]{1,0:T(1,128)}, f32[1,1024]{1,0:T(1,128)}) custom-call(s32[9]{0:T(128)} %stack.59.refs_0_.refs_12_, bf16[256,4096]{1,0:T(8,128)(2,1)} %side.19.refs_5_.refs_1_.refs_13_, bf16[144,4096]{1,0:T(8,128)(2,1)} %collective-permute-done.1.refs_2_.refs_14_, ...), custom_call_target="tpu_custom_call" | custom-call | flops 6442450944 | bytes 23068672 | tf_op jit(solution)/shard_map/grad_input/pallas_call | solution.py:60
  372.9 12.4 %adam.4 = (f32[256,8192]{1,0:T(8,128)}, f32[256,8192]{1,0:T(8,128)}, f32[256,8192]{1,0:T(8,128)}) custom-call(s32[3]{0:T(128)} %pad_add_fusion.1.refs_0_, s32[2]{0:T(128)} %iota_multiply_fusion.2.refs_1_, f32[256,8192]{1,0:T(8,128)} %refs_2_.10, f32[256,8192]{1,0:T(8,128)} %refs_3_.8, f32[256,8192]{1,0:T(8,128)} %refs_4_.8, ...), custom_call_target="tpu_custom_call" | custom-call | flops 20971520 | bytes 27262976 | tf_op jit(solution)/shard_map/adam/pallas_call | solution.py:60
  396.6 15.4 %output.1.refs_8_ = bf16[1024,1024]{1,0:T(8,128)(2,1)} custom-call(s32[8]{0:T(128)} %pad_add_fusion.refs_0_.refs_3_.refs_6_.refs_9_, bf16[512,4096]{1,0:T(8,128)(2,1)} %all-gather.3.cloned.1.call-done.refs_18_.refs_1_.refs_4_, bf16[512,4096]{1,0:T(8,128)(2,1)} %collective-permute-done.8.refs_2_.refs_5_, s32[8]{0:T(128)} %pad_add_fusion.refs_0_.refs_3_.refs_6_.refs_9_, ...), custom_call_target="tpu_custom_call" | custom-call | flops 8589934592 | bytes 23068672 | tf_op jit(solution)/shard_map/output/pallas_call | solution.py:60
  421.2 19.5 %all-reduce.2.cloned.1.call-done.refs_5_.refs_7_ = bf16[2,128,2560]{2,1,0:T(8,128)(2,1)} async-done(((bf16[2,128,2560]{2,1,0:T(8,128)(2,1)}), bf16[2,128,2560]{2,1,0:T(8,128)(2,1)}) %all-reduce.2.cloned.1.call-update) | async-done | bytes 1310736 | tf_op jit(solution)/shard_map/psum | solution.py:1102
  444.6 7.0 %adam.5 = (f32[256,4096]{1,0:T(8,128)}, f32[256,4096]{1,0:T(8,128)}, f32[256,4096]{1,0:T(8,128)}) custom-call(s32[3]{0:T(128)} %pad_add_fusion.1.refs_0_, s32[3]{0:T(128)} %iota_multiply_fusion.1.refs_1_, f32[256,4096]{1,0:T(8,128)} %refs_2_.11, f32[256,4096]{1,0:T(8,128)} %refs_3_.9, f32[256,4096]{1,0:T(8,128)} %refs_4_.9, ...), custom_call_target="tpu_custom_call" | custom-call | flops 7864320 | bytes 10223616 | tf_op jit(solution)/shard_map/adam/pallas_call | solution.py:60
  457.9 12.6 %adam.6 = (f32[256,8192]{1,0:T(8,128)}, f32[256,8192]{1,0:T(8,128)}, f32[256,8192]{1,0:T(8,128)}) custom-call(s32[3]{0:T(128)} %pad_add_fusion.1.refs_0_, s32[2]{0:T(128)} %constant.88.clone.refs_1_, f32[256,8192]{1,0:T(8,128)} %refs_2_.10, f32[256,8192]{1,0:T(8,128)} %refs_3_.8, ...), custom_call_target="tpu_custom_call", output_to_operand_aliasing={{0}: (8, {}), {1}: (9, {}), {2}: (10, {})} | custom-call | flops 20971520 | bytes 27262976 | tf_op jit(solution)/shard_map/adam/pallas_call | solution.py:60
  479.9 10.9 %adam.7 = (f32[256,4096]{1,0:T(8,128)}, f32[256,4096]{1,0:T(8,128)}, f32[256,4096]{1,0:T(8,128)}) custom-call(s32[3]{0:T(128)} %pad_add_fusion.1.refs_0_, s32[5]{0:T(128)} %constant.89.clone.refs_1_, f32[256,4096]{1,0:T(8,128)} %refs_2_.11, f32[256,4096]{1,0:T(8,128)} %refs_3_.9, ...), custom_call_target="tpu_custom_call", output_to_operand_aliasing={{0}: (10, {}), {1}: (11, {}), {2}: (12, {})} | custom-call | flops 13107200 | bytes 17039360 | tf_op jit(solution)/shard_map/adam/pallas_call | solution.py:60
  (123 shorter events, 141.1 us)
Async XLA Ops:
  7.2 102.1 %all-gather.3.cloned.1.call-start = ((), (), s32[]{:S(2)}) async-start(), calls=%async_computation | async-start | bytes 5242880 | tf_op jit(solution)/shard_map/all_gather | solution.py:1087
  11.3 29.2 %collective-permute-start = (bf16[144,4096]{1,0:T(8,128)(2,1)}, bf16[144,4096]{1,0:T(8,128)(2,1)}, u32[]{:S(2)}, u32[]{:S(2)}) collective-permute-start(bf16[144,4096]{1,0:T(8,128)(2,1)} %side.17.refs_3_), channel_id=1, source_target_pairs={{0,2},{1,3},{2,0},{3,1},{4,6},{5,7},{6,4},{7,5},{8,10},{9,11},{10,... | collective-permute-start | bytes 3538952 | tf_op jit(solution)/shard_map/ppermute | solution.py:1076
  14.2 27.7 %collective-permute-start.1 = (bf16[144,4096]{1,0:T(8,128)(2,1)}, bf16[144,4096]{1,0:T(8,128)(2,1)}, u32[]{:S(2)}, u32[]{:S(2)}) collective-permute-start(bf16[144,4096]{1,0:T(8,128)(2,1)} %side.17.refs_3_), channel_id=1, source_target_pairs={{0,1},{1,0},{2,3},{3,2},{4,5},{5,4},{6,7},{7,6},{8,9},{9,8},{10,11... | collective-permute-start | bytes 3538952 | tf_op jit(solution)/shard_map/ppermute | solution.py:1076
  46.3 112.7 %all-gather.5.cloned.1.call-start = ((), (), s32[]{:S(2)}) async-start(), calls=%async_computation.1 | async-start | bytes 5242880 | tf_op jit(solution)/shard_map/all_gather | solution.py:1087
  46.4 22.1 %collective-permute-start.5 = (bf16[80,4096]{1,0:T(8,128)(2,1)}, bf16[80,4096]{1,0:T(8,128)(2,1)}, u32[]{:S(2)}, u32[]{:S(2)}) collective-permute-start(bf16[80,4096]{1,0:T(8,128)(2,1)} %get-tuple-element.116), channel_id=1, source_target_pairs={{0,2},{1,3},{2,0},{3,1},{4,6},{5,7},{6,4},{7,5},{8,10},{9,11},{10,... | collective-permute-start | bytes 1966088 | tf_op jit(solution)/shard_map/ppermute | solution.py:1076
  46.7 25.4 %collective-permute-start.2 = (bf16[144,4096]{1,0:T(8,128)(2,1)}, bf16[144,4096]{1,0:T(8,128)(2,1)}, u32[]{:S(2)}, u32[]{:S(2)}) collective-permute-start(bf16[144,4096]{1,0:T(8,128)(2,1)} %collective-permute-done.1.refs_2_.refs_14_), channel_id=1, source_target_pairs={{0,4},{4,0},{8,12},{12,8},{16,20},{20,16},{24,28},{28,24},{1,5},{5... | collective-permute-start | bytes 3538952 | tf_op jit(solution)/shard_map/ppermute | solution.py:1068
  46.7 25.4 %collective-permute-start.3 = (bf16[144,4096]{1,0:T(8,128)(2,1)}, bf16[144,4096]{1,0:T(8,128)(2,1)}, u32[]{:S(2)}, u32[]{:S(2)}) collective-permute-start(bf16[144,4096]{1,0:T(8,128)(2,1)} %collective-permute-done.refs_1_.refs_3_.refs_15_), channel_id=1, source_target_pairs={{0,4},{4,0},{8,12},{12,8},{16,20},{20,16},{24,28},{28,24},{1,5},{5... | collective-permute-start | bytes 3538952 | tf_op jit(solution)/shard_map/ppermute | solution.py:1068
  69.0 371.7 %all-reduce.2.cloned.1.call-start = ((), (), s32[]{:S(2)}) async-start(), calls=%async_computation.2 | async-start | bytes 2621440 | tf_op jit(solution)/shard_map/psum | solution.py:1102
  165.5 31.7 %collective-permute-start.11 = (bf16[2,128,2048]{2,1,0:T(8,128)(2,1)}, bf16[2,128,2048]{2,1,0:T(8,128)(2,1)}, u32[]{:S(2)}, u32[]{:S(2)}) collective-permute-start(bf16[2,128,2048]{2,1,0:T(8,128)(2,1)} %get-tuple-element.133), channel_id=1, source_target_pairs={{0,1},{1,0},{2,3},{3,2},{4,5},{5,4},{6,7},{7,6},{8,9},{9,8},{10,11... | collective-permute-start | bytes 3145736 | tf_op jit(solution)/shard_map/ppermute | solution.py:1076
  167.0 30.2 %collective-permute-start.12 = (bf16[2,128,2048]{2,1,0:T(8,128)(2,1)}, bf16[2,128,2048]{2,1,0:T(8,128)(2,1)}, u32[]{:S(2)}, u32[]{:S(2)}) collective-permute-start(bf16[2,128,2048]{2,1,0:T(8,128)(2,1)} %get-tuple-element.134), channel_id=1, source_target_pairs={{0,2},{1,3},{2,0},{3,1},{4,6},{5,7},{6,4},{7,5},{8,10},{9,11},{10,... | collective-permute-start | bytes 3145736 | tf_op jit(solution)/shard_map/ppermute | solution.py:1076
  197.1 61.4 %collective-permute-start.16 = (bf16[2,512,2048]{2,1,0:T(8,128)(2,1)}, bf16[2,512,2048]{2,1,0:T(8,128)(2,1)}, u32[]{:S(2)}, u32[]{:S(2)}) collective-permute-start(bf16[2,512,2048]{2,1,0:T(8,128)(2,1)} %get-tuple-element.142), channel_id=1, source_target_pairs={{0,4},{4,0},{8,12},{12,8},{16,20},{20,16},{24,28},{28,24},{1,5},{5... | collective-permute-start | bytes 12582920 | tf_op jit(solution)/shard_map/ppermute | solution.py:1068
  202.0 26.7 %collective-permute-start.13 = (bf16[1,128,2048]{2,1,0:T(8,128)(2,1)}, bf16[1,128,2048]{2,1,0:T(8,128)(2,1)}, u32[]{:S(2)}, u32[]{:S(2)}) collective-permute-start(bf16[1,128,2048]{2,1,0:T(8,128)(2,1)} %get-tuple-element.137), channel_id=1, source_target_pairs={{0,2},{1,3},{2,0},{3,1},{4,6},{5,7},{6,4},{7,5},{8,10},{9,11},{10,... | collective-permute-start | bytes 1572872 | tf_op jit(solution)/shard_map/ppermute | solution.py:1076
  203.5 25.2 %collective-permute-start.14 = (bf16[1,128,2048]{2,1,0:T(8,128)(2,1)}, bf16[1,128,2048]{2,1,0:T(8,128)(2,1)}, u32[]{:S(2)}, u32[]{:S(2)}) collective-permute-start(bf16[1,128,2048]{2,1,0:T(8,128)(2,1)} %get-tuple-element.138), channel_id=1, source_target_pairs={{0,1},{1,0},{2,3},{3,2},{4,5},{5,4},{6,7},{7,6},{8,9},{9,8},{10,11... | collective-permute-start | bytes 1572872 | tf_op jit(solution)/shard_map/ppermute | solution.py:1076
  228.6 26.3 %collective-permute-start.17 = (bf16[2,512,512]{2,1,0:T(8,128)(2,1)}, bf16[2,512,512]{2,1,0:T(8,128)(2,1)}, u32[]{:S(2)}, u32[]{:S(2)}) collective-permute-start(bf16[2,512,512]{2,1,0:T(8,128)(2,1)} %get-tuple-element.144), channel_id=1, source_target_pairs={{0,4},{4,0},{8,12},{12,8},{16,20},{20,16},{24,28},{28,24},{1,5},{5... | collective-permute-start | bytes 3145736 | tf_op jit(solution)/shard_map/ppermute | solution.py:1068
  231.8 26.7 %collective-permute-start.15 = (bf16[2,128,2048]{2,1,0:T(8,128)(2,1)}, bf16[2,128,2048]{2,1,0:T(8,128)(2,1)}, u32[]{:S(2)}, u32[]{:S(2)}) collective-permute-start(bf16[2,128,2048]{2,1,0:T(8,128)(2,1)} %bitcast.34), channel_id=1, source_target_pairs={{0,8},{4,12},{24,16},{28,20},{1,9},{5,13},{25,17},{29,21},{2,10},{... | collective-permute-start | bytes 3145736 | tf_op jit(solution)/shard_map/ppermute | solution.py:1073
  273.5 32.7 %collective-permute-start.21 = (bf16[2,512,768]{2,1,0:T(8,128)(2,1)}, bf16[2,512,768]{2,1,0:T(8,128)(2,1)}, u32[]{:S(2)}, u32[]{:S(2)}) collective-permute-start(bf16[2,512,768]{2,1,0:T(8,128)(2,1)} %get-tuple-element.155), channel_id=1, source_target_pairs={{0,4},{4,0},{8,12},{12,8},{16,20},{20,16},{24,28},{28,24},{1,5},{5... | collective-permute-start | bytes 4718600 | tf_op jit(solution)/shard_map/ppermute | solution.py:1068
  273.5 31.5 %collective-permute-start.19 = (bf16[2,128,2560]{2,1,0:T(8,128)(2,1)}, bf16[2,128,2560]{2,1,0:T(8,128)(2,1)}, u32[]{:S(2)}, u32[]{:S(2)}) collective-permute-start(bf16[2,128,2560]{2,1,0:T(8,128)(2,1)} %get-tuple-element.149), channel_id=1, source_target_pairs={{0,1},{1,0},{2,3},{3,2},{4,5},{5,4},{6,7},{7,6},{8,9},{9,8},{10,11... | collective-permute-start | bytes 3932168 | tf_op jit(solution)/shard_map/ppermute | solution.py:1076
  275.0 31.2 %collective-permute-start.20 = (bf16[2,128,2560]{2,1,0:T(8,128)(2,1)}, bf16[2,128,2560]{2,1,0:T(8,128)(2,1)}, u32[]{:S(2)}, u32[]{:S(2)}) collective-permute-start(bf16[2,128,2560]{2,1,0:T(8,128)(2,1)} %get-tuple-element.150), channel_id=1, source_target_pairs={{0,2},{1,3},{2,0},{3,1},{4,6},{5,7},{6,4},{7,5},{8,10},{9,11},{10,... | collective-permute-start | bytes 3932168 | tf_op jit(solution)/shard_map/ppermute | solution.py:1076
  320.4 40.5 %collective-permute-start.29 = (bf16[2,512,768]{2,1,0:T(8,128)(2,1)}, bf16[2,512,768]{2,1,0:T(8,128)(2,1)}, u32[]{:S(2)}, u32[]{:S(2)}) collective-permute-start(bf16[2,512,768]{2,1,0:T(8,128)(2,1)} %get-tuple-element.170), channel_id=1, source_target_pairs={{0,4},{4,0},{8,12},{12,8},{16,20},{20,16},{24,28},{28,24},{1,5},{5... | collective-permute-start | bytes 4718600 | tf_op jit(solution)/shard_map/ppermute | solution.py:1068
  322.4 38.5 %collective-permute-start.22 = (bf16[2,128,2048]{2,1,0:T(8,128)(2,1)}, bf16[2,128,2048]{2,1,0:T(8,128)(2,1)}, u32[]{:S(2)}, u32[]{:S(2)}) collective-permute-start(bf16[2,128,2048]{2,1,0:T(8,128)(2,1)} %get-tuple-element.157.refs_4_.refs_1_), channel_id=1, source_target_pairs={{8,0},{12,4},{16,24},{20,28},{9,1},{13,5},{17,25},{21,29},{10,2},{... | collective-permute-start | bytes 3145736 | tf_op jit(solution)/shard_map/ppermute | solution.py:1073
  337.1 23.9 %collective-permute-start.23 = (bf16[1,128,2560]{2,1,0:T(8,128)(2,1)}, bf16[1,128,2560]{2,1,0:T(8,128)(2,1)}, u32[]{:S(2)}, u32[]{:S(2)}) collective-permute-start(bf16[1,128,2560]{2,1,0:T(8,128)(2,1)} %get-tuple-element.159), channel_id=1, source_target_pairs={{0,2},{1,3},{2,0},{3,1},{4,6},{5,7},{6,4},{7,5},{8,10},{9,11},{10,... | collective-permute-start | bytes 1966088 | tf_op jit(solution)/shard_map/ppermute | solution.py:1076
  337.6 23.3 %collective-permute-start.24 = (bf16[1,128,2560]{2,1,0:T(8,128)(2,1)}, bf16[1,128,2560]{2,1,0:T(8,128)(2,1)}, u32[]{:S(2)}, u32[]{:S(2)}) collective-permute-start(bf16[1,128,2560]{2,1,0:T(8,128)(2,1)} %get-tuple-element.160), channel_id=1, source_target_pairs={{0,1},{1,0},{2,3},{3,2},{4,5},{5,4},{6,7},{7,6},{8,9},{9,8},{10,11... | collective-permute-start | bytes 1966088 | tf_op jit(solution)/shard_map/ppermute | solution.py:1076
  367.3 23.8 %collective-permute-start.30 = (bf16[2,128,768]{2,1,0:T(8,128)(2,1)}, bf16[2,128,768]{2,1,0:T(8,128)(2,1)}, u32[]{:S(2)}, u32[]{:S(2)}) collective-permute-start(bf16[2,128,768]{2,1,0:T(8,128)(2,1)} %bitcast.38), channel_id=1, source_target_pairs={{0,8},{4,12},{8,0},{12,4},{16,24},{20,28},{24,16},{28,20},{1,9},{5... | collective-permute-start | bytes 1179656 | tf_op jit(solution)/shard_map/ppermute | solution.py:1068
  394.4 23.8 %collective-permute-start.35 = (bf16[2,128,768]{2,1,0:T(8,128)(2,1)}, bf16[2,128,768]{2,1,0:T(8,128)(2,1)}, u32[]{:S(2)}, u32[]{:S(2)}) collective-permute-start(bf16[2,128,768]{2,1,0:T(8,128)(2,1)} %get-tuple-element.190.refs_9_.refs_1_), channel_id=1, source_target_pairs={{0,16},{4,20},{8,24},{12,28},{16,0},{20,4},{24,8},{28,12},{1,17},{... | collective-permute-start | bytes 1179656 | tf_op jit(solution)/shard_map/ppermute | solution.py:1068
  (26 other events, 330.1 us)
Sparse Core Ops, SparseCore 0:
  46.4 57.9 all-gather.2
  106.3 52.6 all-gather.4
  367.4 73.2 all-reduce.1

commit v4 on v3

--- a/solution.py
+++ b/solution.py
@@ -534,7 +534,7 @@
         [((rows, width), BF16, by_row(width))],
         after=after,
         scratch=[pltpu.VMEM((width, hidden), BF16)] + [weight.sems() for _, weight in weights],
-        cost=cost(2 * rows * width * hidden, 22 * rows * width),
+        cost=cost(rows * width * hidden // 5, 2 * rows * width),
         name="output",
     )
     return out
@@ -851,7 +851,7 @@
         reuse=[] if earlier is None else [(value, n) for n, value in enumerate(earlier)],
         prefetch=(core, table),
         scratch=[pltpu.VMEM((half, span), BF16)],
-        cost=cost(20 * moved, 26 * moved),
+        cost=cost(2 * moved, 2 * moved),
         name="adam",
     )
 
@@ -908,17 +908,18 @@
     return ins, outs, run
 
 
-def job_join(left, right, steps):
+def job_join(left, right, steps, around):
     _, blocks, rows, size = left.shape
     span = rows // steps
     four = lambda i, c: (0, 0, i, 0)
     ins = [(value, (2, blocks, span, size), four) for value in (left, right)]
     outs = [((blocks, 2, rows, size), BF16, (blocks, 2, span, size), four)]
 
-    def run(have, give):
+    def run(have, give, places):
         for side in range(2):
             for block in range(blocks):
-                give[0][block, side] = have[0][side, block] + have[1][side, block]
+                owner = jnp.bitwise_xor(places[1], block) if around else block
+                give[0][owner, side] = have[0][side, block] + have[1][side, block]
 
     return ins, outs, run
 
@@ -1143,9 +1144,10 @@
 
 
 class Reduce:
-    def __init__(self, links, way):
+    def __init__(self, links, way, bits=((1, 2), (2, 1))):
         self.links = links
         self.way = way
+        self.bits = bits
         self.stage = 0
         self.groups = []
 
@@ -1161,15 +1163,19 @@
                 return job_pick(own, received, steps)
             return job_add(own, received, steps)
         blocks = self.groups[0][0].shape[1]
-        odd = lambda block: block % 2 == 1
-        late = lambda block: block >= blocks // 2
-        goes = [odd, late]
-        if blocks == 2:
-            goes = [odd, odd]
-        if blocks == 1:
-            goes = [lambda block: False] * 2
-        keep = [[block for block in range(blocks) if not go(block)] for go in goes]
-        send = [[block for block in range(blocks) if go(block)] for go in goes]
+        sides = []
+        for number in range(2):
+            order = self.bits[number % len(self.bits)]
+            if blocks == 1:
+                sides.append(())
+            elif blocks == 2:
+                sides.append((1,))
+            else:
+                sides.append(tuple(block for block in range(blocks) if block & order[0]))
+        keep = [[block for block in range(blocks) if block not in gone] for gone in sides]
+        send = [list(gone) for gone in sides]
+        if len(self.bits) == 1 and blocks > 1:
+            send = send[:1]
         return job_sum(self.groups, keep, send, steps)
 
     def advance(self, results):
@@ -1178,16 +1184,16 @@
         stage = self.stage
         self.stage += 1
         if stage < 2:
-            bits = (1, 2) if stage == 0 else (2, 1)
             received = tuple(
-                links.across_shard(value, bit) for value, bit in zip(results[1:], bits)
+                links.across_shard(value, order[stage])
+                for value, order in zip(results[1:], self.bits)
             )
             self.groups = [(own, received)]
             return
         if stage == 2:
             own = own.reshape(2, own.shape[2], own.shape[3])
         if self.way == AT_ONCE:
-            self.own = links.over_dp(own)
+            self.own = own
         elif self.way == LINE and stage < 5:
             self.groups = [(own, links.along_dp(own, stage - 2))]
         elif self.way == EXCHANGE and stage < 4:
@@ -1209,6 +1215,10 @@
 
     def finish(self):
         self.own = self.links.over_dp(self.own).reshape(self.shape)
+
+    def close(self, behind):
+        mine, _ = lax.optimization_barrier((self.own, behind))
+        self.grads = (mine, self.links.swap(mine))
 
 
 class Side:
@@ -1366,15 +1376,18 @@
         grad_bias_up.append(gbias)
         return own, sib
 
-    def unit(way, *grads):
+    def unit(way, own, sib, bits=((1, 2), (2, 1))):
         if links.fast:
-            return Reduce(links, way).add(*grads)
-        return Wide(links, side.jobs([job_join(blocked(grads[0]), blocked(links.swap(grads[1])), 4)], steps=4)[0])
+            return Reduce(links, way, bits).add(own, sib)
+        return Wide(links, side.jobs([join(own, links.swap(sib))], steps=4)[0])
+
+    def join(own, received):
+        return job_join(blocked(own), blocked(received), 4, links.fast)
 
     def reduce(units, jobs=(), steps=2):
         if links.fast:
             return side.reduce(units, jobs, steps)
-        return side.jobs(jobs) if jobs else None
+        return side.jobs(jobs, steps) if jobs else None
 
     group_a = feed(0, wide, wide.at(block))
     more_wide = links.gathered(more_wide, grad_bias_up[0])
@@ -1403,11 +1416,8 @@
             after=side.order,
         )
     )
-    if links.fast:
-        unit_b.add(own_out, sib_out)
-    else:
-        unit_e = unit(AT_ONCE, own_out, sib_out)
-    reduce([unit_a])
+    received_out = links.swap(sib_out)
+    reduce([unit_a, unit_b], steps=4)
     grads, biases = [], []
 
     def attend_back(first):
@@ -1421,22 +1431,26 @@
         return side.then(run_project(turned_one, *grads[group], after=side.order))
 
     attend_back(0)
-    reduce([unit_a, unit_b], steps=4)
-    unit_c = unit(EXCHANGE, *project(0))
+    (joined,) = reduce([unit_a, unit_b], [join(own_out, received_out)], steps=4)
+    unit_e = Wide(links, joined)
+    unit_c = unit(EXCHANGE, *project(0), ((1, 2),))
     attend_back(pairs // 2)
+    if links.fast:
+        side.order += (unit_e.own,)
     reduce([unit_a, unit_b, unit_c], steps=4)
-    unit_d = unit(EXCHANGE, *project(1))
-    reduce([unit_c])
+    if links.fast:
+        unit_b.own, unit_e.own = links.over_dp((unit_b.own, unit_e.own.reshape(unit_e.shape)))
+    unit_d = unit(EXCHANGE, *project(1), ((2, 1),))
     grad_input, grad_gain_one, grad_shift_one = side.then(
         run_input(attn_weights, grads, tokens, grad_after, small, GAIN_ONE, after=side.order)
     )
     small_grads = [biases[0][0], biases[1][0], biases[0][1], biases[1][1], grad_bias_o]
     small_grads += grad_bias_up
     small_grads += [grad_bias_dn, grad_gain_one, grad_shift_one, grad_gain_two, grad_shift_two]
-    (grad_small,) = reduce([unit_a, unit_b, unit_c, unit_d], [job_lay(small_grads)])
+    (grad_small,) = reduce([unit_a, unit_c, unit_d], [job_lay(small_grads)])
 
     def pick_feed(number, arrays):
-        return [arrays[0][number, :, :block]]
+        return [arrays[0][number]]
 
     def adam_mlp(number, item, earlier):
         return side.then(
@@ -1458,7 +1472,7 @@
         left, right = arrays[0][0], arrays[0][1]
         split = out_block // 2
         if number > 2:
-            return [arrays[1][number - 3, :, block:]]
+            return [arrays[1][number - 3]]
         return (
             [left[:, :out_block]],
             [left[:, out_block:], right[:, :split]],
@@ -1505,23 +1519,22 @@
         output = output_now()
         grad_small, moved = step([unit_c, unit_d], links.swap)
         unit_b.close(grad_small)
+        unit_e.close(grad_small)
+        mlp_new = adam_mlp(1, unit_b, mlp_new)
+        grad_small, moved = step([unit_c, unit_d], dp_move(2))
         attn_new = adam_attn([unit_c], [0, 2, 4], None)
-        grad_small, moved = step([unit_d], dp_move(2))
-        mlp_new = adam_mlp(1, unit_b, mlp_new)
         grad_small, moved = step([unit_d], dp_move(4))
-        attn_new = adam_attn([unit_d, unit_b], [1, 3, 5, 6, 7], attn_new)
+        attn_new = adam_attn([unit_d, unit_e], [1, 3, 5, 6, 7], attn_new)
         grad_small, _ = step([], None)
     else:
         for item in (unit_a, unit_b, unit_c, unit_d, unit_e):
             item.finish()
-        unit_b.own = jnp.concatenate([unit_b.own, unit_e.own], axis=2)
-        for item in (unit_a, unit_b, unit_c, unit_d):
-            item.grads = (item.own, links.swap(item.own))
+            item.close(grad_input)
         grad_small = lax.psum(grad_small, ("dp", "shard"))
         output = output_now()
         mlp_new = adam_mlp(1, unit_b, adam_mlp(0, unit_a, None))
         attn_new = adam_attn([unit_c], [0, 2, 4], None)
-        attn_new = adam_attn([unit_d, unit_b], [1, 3, 5, 6, 7], attn_new)
+        attn_new = adam_attn([unit_d, unit_e], [1, 3, 5, 6, 7], attn_new)
     grad_small = lax.dynamic_slice_in_dim(grad_small, links.shard * small_size, small_size, 1)[0]
     small_new = adamw(*small_state, grad_small, 0.4, 0.0)
     return (output, grad_input, *attn_new, *mlp_new, *small_new)

time: 506 us -> 492 us (0.972)
  waiting for transfers between devices: 107 us -> 98.9 us
    psum x1, waiting for transfers between devices: 19.5 us -> 3.13 us  [over_dp(): return lax.psum(values, 'dp', axis_index_groups=groups)]
    ppermute x22 -> x23, waiting for transfers between devices: 20.9 us -> 27 us  [across_dp(): lax.ppermute(value, 'dp', [(d, d ^ bit) for d in range(self.replicas)])]
    ppermute x3, waiting for transfers between devices: 3.58 us -> 8.95 us  [along_dp(): return lax.ppermute(value, 'dp', pairs)]
    ppermute x22 -> x18, starting transfers between devices: 24.2 us -> 20.6 us  [across_shard(): lax.ppermute(value, 'shard', [(s, s ^ bit) for s in range(self.shards)])]
    ppermute x22 -> x18, waiting for transfers between devices: 53.6 us -> 50.8 us  [across_shard(): lax.ppermute(value, 'shard', [(s, s ^ bit) for s in range(self.shards)])]
    pallas_call x34 -> x33, Pallas kernels: 333 us -> 331 us  [call(): pl.pallas_call(run, grid_spec=pltpu.PrefetchScalarGridSpec(num_scalar_pre...]
  transfers between devices with their start and end apart: 50 -> 48, of which waited for: 17 -> 16; matrix products, arithmetic and copies ran while one was open for 1% -> 1% of each run, Pallas kernels for 57% -> 60%
where the time goes in v4:
time: 492 us; the launch traced here: 487 us
  Pallas kernels  331 us (67%)
  waiting for transfers between devices  98.9 us (20%)
  starting transfers between devices  36.7 us (7%)
  between operations  14.4 us (3%)
  other arithmetic  5.61 us (1%)
    pallas_call x33, Pallas kernels, call(): pl.pallas_call(run, grid_spec=pltpu.PrefetchScalarGridSpec(num_scalar_pre...  331 us
    ppermute x18, waiting for transfers between devices, across_shard(): lax.ppermute(value, 'shard', [(s, s ^ bit) for s in range(self.shards)])  50.8 us
    ppermute x23, waiting for transfers between devices, across_dp(): lax.ppermute(value, 'dp', [(d, d ^ bit) for d in range(self.replicas)])  27 us
    ppermute x18, starting transfers between devices, across_shard(): lax.ppermute(value, 'shard', [(s, s ^ bit) for s in range(self.shards)])  20.6 us
  transfers between devices with their start and end apart: 48, of which 16 were waited for; matrix products, arithmetic and copies ran while one was open for 1% of the time, Pallas kernels for 60%

profile of v4, /device:TPU:0, one launch (start us, length us, event | category | flops | bytes accessed | tf_op | source)
XLA Modules:
  0.0 487.5 jit_solution(14134467334211788670)
XLA Ops:
  31.3 9.2 %collective-permute-done.refs_1_.refs_3_.refs_15_ = bf16[144,4096]{1,0:T(8,128)(2,1)} collective-permute-done((bf16[144,4096]{1,0:T(8,128)(2,1)}, bf16[144,4096]{1,0:T(8,128)(2,1)}, u32[]{:S(2)}, u32[]{:S(2)}) %collective-permute-start) | collective-permute-done | bytes 1179680 | tf_op jit(solution)/shard_map/ppermute | solution.py:1077
  49.0 19.5 %collective-permute-done.5.refs_4_.refs_7_.refs_19_ = bf16[80,4096]{1,0:T(8,128)(2,1)} collective-permute-done((bf16[80,4096]{1,0:T(8,128)(2,1)}, bf16[80,4096]{1,0:T(8,128)(2,1)}, u32[]{:S(2)}, u32[]{:S(2)}) %collective-permute-start.5) | collective-permute-done | bytes 655392 | tf_op jit(solution)/shard_map/ppermute | solution.py:1077
  72.1 14.2 %qkv.1 = (bf16[1024,3072]{1,0:T(8,128)(2,1)}, bf16[1024,1024]{1,0:T(8,128)(2,1)}) custom-call(s32[9]{0:T(128)} %stack.59.refs_0_.refs_12_, bf16[256,4096]{1,0:T(8,128)(2,1)} %side.18.refs_5_.refs_1_.refs_13_, bf16[144,4096]{1,0:T(8,128)(2,1)} %collective-permute-done.1.refs_2_.refs_14_, bf16[144,4096]{1,0:T(8,128)(2,1)} %collective-permute-done.refs_1_.refs_3_.refs_15_, ...), custom_call_target="tpu_custom_call" | custom-call | flops 6442450944 | bytes 16777216 | tf_op jit(solution)/shard_map/qkv/pallas_call | solution.py:60
  86.4 22.9 %attend.1 = (bf16[1024,1024]{1,0:T(8,128)(2,1)}, f32[8,2,1024]{2,1,0:T(2,128)}) custom-call(s32[4]{0:T(128)} %bitcast.50, bf16[1024,3072]{1,0:T(8,128)(2,1)} %get-tuple-element.116.refs_1_.refs_2_.refs_3_.refs_4_, bf16[1024,3072]{1,0:T(8,128)(2,1)} %get-tuple-element.116.refs_1_.refs_2_.refs_3_.refs_4_, ...), custom_call_target="tpu_custom_call" | custom-call | flops 8589934592 | bytes 8388608 | tf_op jit(solution)/shard_map/attend/pallas_call | solution.py:60
  109.9 10.4 %after.1 = (f32[1024,1024]{1,0:T(8,128)}, bf16[1024,1024]{1,0:T(8,128)(2,1)}, bf16[1024,1024]{1,0:T(8,128)(2,1)}, bf16[1024,1024]{1,0:T(8,128)(2,1)}) custom-call(s32[9]{0:T(128)} %stack.59.refs_0_.refs_12_, bf16[256,4096]{1,0:T(8,128)(2,1)} %side.18.refs_5_.refs_1_.refs_13_, bf16[144,4096]{1,0:T(8,128)(2,1)} %collective-permute-done.1.refs_2_.refs_14_, ...), custom_call_target="tpu_custom_call" | custom-call | flops 2147483648 | bytes 14680064 | tf_op jit(solution)/shard_map/after/pallas_call | solution.py:60
  120.3 29.1 %feed.2 = (bf16[1024,4096]{1,0:T(8,128)(2,1)}, bf16[1024,4096]{1,0:T(8,128)(2,1)}, bf16[2,512,2048]{2,1,0:T(8,128)(2,1)}, bf16[2,512,2048]{2,1,0:T(8,128)(2,1)}, f32[1,2048]{1,0:T(1,128)}) custom-call(s32[8]{0:T(128)} %pad_add_fusion.refs_0_.refs_3_.refs_6_.refs_9_, bf16[512,4096]{1,0:T(8,128)(2,1)} %all-gather.3.cloned.1.call-done.refs_18_.refs_1_.refs_4_, ...), custom_call_target="tpu_custom_call" | custom-call | flops 17179869184 | bytes 50331648 | tf_op jit(solution)/shard_map/feed/pallas_call | solution.py:60
  150.1 9.0 %all-gather.5.cloned.1.call-done.refs_1_.refs_4_.refs_7_.refs_10_ = bf16[512,4096]{1,0:T(8,128)(2,1)} async-done(((bf16[128,4096]{1,0:T(8,128)(2,1)}), bf16[512,4096]{1,0:T(8,128)(2,1)}) %all-gather.5.cloned.1.call-update) | async-done | bytes 4194320 | tf_op jit(solution)/shard_map/all_gather | solution.py:1088
  167.6 29.6 %feed.3 = (bf16[1024,4096]{1,0:T(8,128)(2,1)}, bf16[1024,4096]{1,0:T(8,128)(2,1)}, bf16[2,512,2048]{2,1,0:T(8,128)(2,1)}, bf16[2,512,2048]{2,1,0:T(8,128)(2,1)}, f32[1,2048]{1,0:T(1,128)}) custom-call(s32[8]{0:T(128)} %pad_add_fusion.refs_0_.refs_3_.refs_6_.refs_9_, ...), custom_call_target="tpu_custom_call", output_to_operand_aliasing={{0}: (12, {}), {1}: (13, {})} | custom-call | flops 17179869184 | bytes 50331648 | tf_op jit(solution)/shard_map/feed/pallas_call | solution.py:60
  204.1 24.6 %middle.1 = (f32[1024,1024]{1,0:T(8,128)}, bf16[1024,1024]{1,0:T(8,128)(2,1)}, bf16[2,512,512]{2,1,0:T(8,128)(2,1)}, bf16[2,512,512]{2,1,0:T(8,128)(2,1)}, f32[1...) custom-call(s32[8]{0:T(128)} %pad_add_fusion.refs_0_.refs_3_.refs_6_.refs_9_, ...), custom_call_target="tpu_custom_call" | custom-call | flops 51539607552 | bytes 125829120 | tf_op jit(solution)/shard_map/middle/pallas_call | solution.py:60
  228.9 7.3 %side.23 = (bf16[2,1,128,2048]{3,2,1,0:T(8,128)(2,1)}, bf16[2,2,128,2048]{3,2,1,0:T(8,128)(2,1)}, bf16[2,128,2048]{2,1,0:T(8,128)(2,1)}, bf16[2,128,2048]{2,1,0:T(8,128)(2,1)}) custom-call(s32[3]{0:T(128)} %pad_add_fusion.1.refs_0_, bf16[2,1,128,2048]{3,2,1,0:T(8,128)(2,1)} %get-tuple-element.135.refs_27_.refs_1_, ...), custom_call_target="tpu_custom_call" | custom-call | bytes 20971520 | tf_op jit(solution)/shard_map/side/pallas_call | solution.py:60
  242.5 18.9 %attend_back.2 = (bf16[1024,512]{1,0:T(8,128)(2,1)}, bf16[1024,512]{1,0:T(8,128)(2,1)}, bf16[1024,512]{1,0:T(8,128)(2,1)}, f32[1,512]{1,0:T(1,128)}, f32[1,512]{1,0:T(1,128)}) custom-call(s32[4]{0:T(128)} %bitcast.51, bf16[1024,3072]{1,0:T(8,128)(2,1)} %get-tuple-element.116.refs_1_.refs_2_.refs_3_.refs_4_, ...), custom_call_target="tpu_custom_call" | custom-call | flops 42949672960 | bytes 524288 | tf_op jit(solution)/shard_map/attend_back/pallas_call | solution.py:60
  273.7 7.1 %project.2 = (bf16[2,512,768]{2,1,0:T(8,128)(2,1)}, bf16[2,512,768]{2,1,0:T(8,128)(2,1)}) custom-call(bf16[1024,1024]{1,0:T(8,128)(2,1)} %get-tuple-element.154.refs_0_, bf16[1024,512]{1,0:T(8,128)(2,1)} %get-tuple-element.149.refs_8_.refs_1_.refs_10_, bf16[1024,512]{1,0:T(8,128)(2,1)} %get-tuple-element.155.refs_2_.refs_11_, ...), custom_call_target="tpu_custom_call" | custom-call | flops 3221225472 | bytes 7340032 | tf_op jit(solution)/shard_map/project/pallas_call | solution.py:60
  284.4 19.1 %attend_back.3 = (bf16[1024,512]{1,0:T(8,128)(2,1)}, bf16[1024,512]{1,0:T(8,128)(2,1)}, bf16[1024,512]{1,0:T(8,128)(2,1)}, f32[1,512]{1,0:T(1,128)}, f32[1,512]{1,0:T(1,128)}) custom-call(s32[4]{0:T(128)} %bitcast.52, bf16[1024,3072]{1,0:T(8,128)(2,1)} %get-tuple-element.116.refs_1_.refs_2_.refs_3_.refs_4_, ...), custom_call_target="tpu_custom_call" | custom-call | flops 1073741824 | bytes 524288 | tf_op jit(solution)/shard_map/attend_back/pallas_call | solution.py:60
  309.5 7.1 %project.3 = (bf16[2,512,768]{2,1,0:T(8,128)(2,1)}, bf16[2,512,768]{2,1,0:T(8,128)(2,1)}) custom-call(bf16[1024,1024]{1,0:T(8,128)(2,1)} %get-tuple-element.154.refs_0_, bf16[1024,512]{1,0:T(8,128)(2,1)} %get-tuple-element.159.refs_8_.refs_1_.refs_13_, bf16[1024,512]{1,0:T(8,128)(2,1)} %get-tuple-element.164.refs_2_.refs_14_, ...), custom_call_target="tpu_custom_call" | custom-call | flops 3221225472 | bytes 7340032 | tf_op jit(solution)/shard_map/project/pallas_call | solution.py:60
  318.9 15.9 %grad_input.1 = (f32[1024,1024]{1,0:T(8,128)}, f32[1,1024]{1,0:T(1,128)}, f32[1,1024]{1,0:T(1,128)}) custom-call(s32[9]{0:T(128)} %stack.59.refs_0_.refs_12_, bf16[256,4096]{1,0:T(8,128)(2,1)} %side.18.refs_5_.refs_1_.refs_13_, bf16[144,4096]{1,0:T(8,128)(2,1)} %collective-permute-done.1.refs_2_.refs_14_, ...), custom_call_target="tpu_custom_call" | custom-call | flops 6442450944 | bytes 23068672 | tf_op jit(solution)/shard_map/grad_input/pallas_call | solution.py:60
  338.2 7.5 %collective-permute-done.24.refs_2_ = bf16[2,128,2048]{2,1,0:T(8,128)(2,1)} collective-permute-done((bf16[2,128,2048]{2,1,0:T(8,128)(2,1)}, bf16[2,128,2048]{2,1,0:T(8,128)(2,1)}, u32[]{:S(2)}, u32[]{:S(2)}) %collective-permute-start.24) | collective-permute-done | bytes 1048608 | tf_op jit(solution)/shard_map/ppermute | solution.py:1074
  354.3 12.5 %adam.4 = (f32[256,8192]{1,0:T(8,128)}, f32[256,8192]{1,0:T(8,128)}, f32[256,8192]{1,0:T(8,128)}) custom-call(s32[3]{0:T(128)} %pad_add_fusion.1.refs_0_, s32[2]{0:T(128)} %iota_multiply_fusion.2.refs_1_, f32[256,8192]{1,0:T(8,128)} %refs_2_.9, f32[256,8192]{1,0:T(8,128)} %refs_3_.7, f32[256,8192]{1,0:T(8,128)} %refs_4_.7, ...), custom_call_target="tpu_custom_call" | custom-call | flops 2097152 | bytes 2097152 | tf_op jit(solution)/shard_map/adam/pallas_call | solution.py:60
  366.9 12.8 %collective-permute-done.27.refs_2_ = bf16[2,1,128,768]{3,2,1,0:T(8,128)(2,1)} collective-permute-done((bf16[2,1,128,768]{3,2,1,0:T(8,128)(2,1)}, bf16[2,1,128,768]{3,2,1,0:T(8,128)(2,1)}, u32[]{:S(2)}, u32[]{:S(2)}) %collective-permute-start.27) | collective-permute-done | bytes 393248 | tf_op jit(solution)/shard_map/ppermute | solution.py:1077
  385.2 15.6 %output.1.refs_7_ = bf16[1024,1024]{1,0:T(8,128)(2,1)} custom-call(s32[8]{0:T(128)} %pad_add_fusion.refs_0_.refs_3_.refs_6_.refs_9_, bf16[512,4096]{1,0:T(8,128)(2,1)} %all-gather.3.cloned.1.call-done.refs_18_.refs_1_.refs_4_, bf16[512,4096]{1,0:T(8,128)(2,1)} %collective-permute-done.8.refs_2_.refs_5_, s32[8]{0:T(128)} %pad_add_fusion.refs_0_.refs_3_.refs_6_.refs_9_, ...), custom_call_target="tpu_custom_call" | custom-call | flops 858993472 | bytes 2097152 | tf_op jit(solution)/shard_map/output/pallas_call | solution.py:60
  400.8 8.7 %collective-permute-done.31.refs_2_ = bf16[2,128,768]{2,1,0:T(8,128)(2,1)} collective-permute-done((bf16[2,128,768]{2,1,0:T(8,128)(2,1)}, bf16[2,128,768]{2,1,0:T(8,128)(2,1)}, u32[]{:S(2)}, u32[]{:S(2)}) %collective-permute-start.31) | collective-permute-done | bytes 393248 | tf_op jit(solution)/shard_map/ppermute | solution.py:1069
  418.7 12.4 %adam.5 = (f32[256,8192]{1,0:T(8,128)}, f32[256,8192]{1,0:T(8,128)}, f32[256,8192]{1,0:T(8,128)}) custom-call(s32[3]{0:T(128)} %pad_add_fusion.1.refs_0_, s32[2]{0:T(128)} %constant.88.clone.refs_1_, f32[256,8192]{1,0:T(8,128)} %refs_2_.9, f32[256,8192]{1,0:T(8,128)} %refs_3_.7, ...), custom_call_target="tpu_custom_call", output_to_operand_aliasing={{0}: (8, {}), {1}: (9, {}), {2}: (10, {})} | custom-call | flops 2097152 | bytes 2097152 | tf_op jit(solution)/shard_map/adam/pallas_call | solution.py:60
  443.5 7.0 %adam.6 = (f32[256,4096]{1,0:T(8,128)}, f32[256,4096]{1,0:T(8,128)}, f32[256,4096]{1,0:T(8,128)}) custom-call(s32[3]{0:T(128)} %pad_add_fusion.1.refs_0_, s32[3]{0:T(128)} %iota_multiply_fusion.1.refs_1_, f32[256,4096]{1,0:T(8,128)} %refs_2_.11, f32[256,4096]{1,0:T(8,128)} %refs_3_.9, f32[256,4096]{1,0:T(8,128)} %refs_4_.9, ...), custom_call_target="tpu_custom_call" | custom-call | flops 786432 | bytes 786432 | tf_op jit(solution)/shard_map/adam/pallas_call | solution.py:60
  452.5 8.7 %collective-permute-done.38.refs_2_ = bf16[2,128,768]{2,1,0:T(8,128)(2,1)} collective-permute-done((bf16[2,128,768]{2,1,0:T(8,128)(2,1)}, bf16[2,128,768]{2,1,0:T(8,128)(2,1)}, u32[]{:S(2)}, u32[]{:S(2)}) %collective-permute-start.38) | collective-permute-done | bytes 393248 | tf_op jit(solution)/shard_map/ppermute | solution.py:1069
  466.3 10.2 %adam.7 = (f32[256,4096]{1,0:T(8,128)}, f32[256,4096]{1,0:T(8,128)}, f32[256,4096]{1,0:T(8,128)}) custom-call(s32[3]{0:T(128)} %pad_add_fusion.1.refs_0_, s32[5]{0:T(128)} %constant.89.clone.refs_1_, f32[256,4096]{1,0:T(8,128)} %refs_2_.11, f32[256,4096]{1,0:T(8,128)} %refs_3_.9, ...), custom_call_target="tpu_custom_call", output_to_operand_aliasing={{0}: (10, {}), {1}: (11, {}), {2}: (12, {})} | custom-call | flops 1310720 | bytes 1310720 | tf_op jit(solution)/shard_map/adam/pallas_call | solution.py:60
  (119 shorter events, 133.9 us)
Async XLA Ops:
  7.2 102.1 %all-gather.3.cloned.1.call-start = ((), (), s32[]{:S(2)}) async-start(), calls=%async_computation.1 | async-start | bytes 5242880 | tf_op jit(solution)/shard_map/all_gather | solution.py:1088
  11.3 29.2 %collective-permute-start = (bf16[144,4096]{1,0:T(8,128)(2,1)}, bf16[144,4096]{1,0:T(8,128)(2,1)}, u32[]{:S(2)}, u32[]{:S(2)}) collective-permute-start(bf16[144,4096]{1,0:T(8,128)(2,1)} %side.16.refs_3_), channel_id=1, source_target_pairs={{0,2},{1,3},{2,0},{3,1},{4,6},{5,7},{6,4},{7,5},{8,10},{9,11},{10,... | collective-permute-start | bytes 3538952 | tf_op jit(solution)/shard_map/ppermute | solution.py:1077
  14.3 27.7 %collective-permute-start.1 = (bf16[144,4096]{1,0:T(8,128)(2,1)}, bf16[144,4096]{1,0:T(8,128)(2,1)}, u32[]{:S(2)}, u32[]{:S(2)}) collective-permute-start(bf16[144,4096]{1,0:T(8,128)(2,1)} %side.16.refs_3_), channel_id=1, source_target_pairs={{0,1},{1,0},{2,3},{3,2},{4,5},{5,4},{6,7},{7,6},{8,9},{9,8},{10,11... | collective-permute-start | bytes 3538952 | tf_op jit(solution)/shard_map/ppermute | solution.py:1077
  46.3 112.7 %all-gather.5.cloned.1.call-start = ((), (), s32[]{:S(2)}) async-start(), calls=%async_computation.2 | async-start | bytes 5242880 | tf_op jit(solution)/shard_map/all_gather | solution.py:1088
  46.8 25.3 %collective-permute-start.2 = (bf16[144,4096]{1,0:T(8,128)(2,1)}, bf16[144,4096]{1,0:T(8,128)(2,1)}, u32[]{:S(2)}, u32[]{:S(2)}) collective-permute-start(bf16[144,4096]{1,0:T(8,128)(2,1)} %collective-permute-done.1.refs_2_.refs_14_), channel_id=1, source_target_pairs={{0,4},{4,0},{8,12},{12,8},{16,20},{20,16},{24,28},{28,24},{1,5},{5... | collective-permute-start | bytes 3538952 | tf_op jit(solution)/shard_map/ppermute | solution.py:1069
  46.8 25.3 %collective-permute-start.3 = (bf16[144,4096]{1,0:T(8,128)(2,1)}, bf16[144,4096]{1,0:T(8,128)(2,1)}, u32[]{:S(2)}, u32[]{:S(2)}) collective-permute-start(bf16[144,4096]{1,0:T(8,128)(2,1)} %collective-permute-done.refs_1_.refs_3_.refs_15_), channel_id=1, source_target_pairs={{0,4},{4,0},{8,12},{12,8},{16,20},{20,16},{24,28},{28,24},{1,5},{5... | collective-permute-start | bytes 3538952 | tf_op jit(solution)/shard_map/ppermute | solution.py:1069
  69.0 234.6 %reduce-scatter.2.cloned.1.call-start = ((), (), s32[]{:S(2)}) async-start(), calls=%async_computation.3 | async-start | bytes 1310720 | tf_op jit(solution)/shard_map/reduce_scatter | solution.py:1214
  165.5 31.7 %collective-permute-start.11 = (bf16[2,128,2048]{2,1,0:T(8,128)(2,1)}, bf16[2,128,2048]{2,1,0:T(8,128)(2,1)}, u32[]{:S(2)}, u32[]{:S(2)}) collective-permute-start(bf16[2,128,2048]{2,1,0:T(8,128)(2,1)} %get-tuple-element.132), channel_id=1, source_target_pairs={{0,1},{1,0},{2,3},{3,2},{4,5},{5,4},{6,7},{7,6},{8,9},{9,8},{10,11... | collective-permute-start | bytes 3145736 | tf_op jit(solution)/shard_map/ppermute | solution.py:1077
  167.0 30.2 %collective-permute-start.12 = (bf16[2,128,2048]{2,1,0:T(8,128)(2,1)}, bf16[2,128,2048]{2,1,0:T(8,128)(2,1)}, u32[]{:S(2)}, u32[]{:S(2)}) collective-permute-start(bf16[2,128,2048]{2,1,0:T(8,128)(2,1)} %get-tuple-element.133), channel_id=1, source_target_pairs={{0,2},{1,3},{2,0},{3,1},{4,6},{5,7},{6,4},{7,5},{8,10},{9,11},{10,... | collective-permute-start | bytes 3145736 | tf_op jit(solution)/shard_map/ppermute | solution.py:1077
  197.1 31.7 %collective-permute-start.15 = (bf16[2,512,2048]{2,1,0:T(8,128)(2,1)}, bf16[2,512,2048]{2,1,0:T(8,128)(2,1)}, u32[]{:S(2)}, u32[]{:S(2)}) collective-permute-start(bf16[2,512,2048]{2,1,0:T(8,128)(2,1)} %get-tuple-element.138), channel_id=1, source_target_pairs={{0,4},{4,0},{8,12},{12,8},{16,20},{20,16},{24,28},{28,24},{1,5},{5... | collective-permute-start | bytes 12582920 | tf_op jit(solution)/shard_map/ppermute | solution.py:1069
  202.1 26.7 %collective-permute-start.13 = (bf16[1,128,2048]{2,1,0:T(8,128)(2,1)}, bf16[1,128,2048]{2,1,0:T(8,128)(2,1)}, u32[]{:S(2)}, u32[]{:S(2)}) collective-permute-start(bf16[1,128,2048]{2,1,0:T(8,128)(2,1)} %get-tuple-element.136), channel_id=1, source_target_pairs={{0,2},{1,3},{2,0},{3,1},{4,6},{5,7},{6,4},{7,5},{8,10},{9,11},{10,... | collective-permute-start | bytes 1572872 | tf_op jit(solution)/shard_map/ppermute | solution.py:1077
  203.6 25.3 %collective-permute-start.14 = (bf16[1,128,2048]{2,1,0:T(8,128)(2,1)}, bf16[1,128,2048]{2,1,0:T(8,128)(2,1)}, u32[]{:S(2)}, u32[]{:S(2)}) collective-permute-start(bf16[1,128,2048]{2,1,0:T(8,128)(2,1)} %get-tuple-element.137), channel_id=1, source_target_pairs={{0,1},{1,0},{2,3},{3,2},{4,5},{5,4},{6,7},{7,6},{8,9},{9,8},{10,11... | collective-permute-start | bytes 1572872 | tf_op jit(solution)/shard_map/ppermute | solution.py:1077
  228.7 32.6 %collective-permute-start.19 = (bf16[2,512,512]{2,1,0:T(8,128)(2,1)}, bf16[2,512,512]{2,1,0:T(8,128)(2,1)}, u32[]{:S(2)}, u32[]{:S(2)}) collective-permute-start(bf16[2,512,512]{2,1,0:T(8,128)(2,1)} %get-tuple-element.147), channel_id=1, source_target_pairs={{0,4},{4,0},{8,12},{12,8},{16,20},{20,16},{24,28},{28,24},{1,5},{5... | collective-permute-start | bytes 3145736 | tf_op jit(solution)/shard_map/ppermute | solution.py:1069
  236.1 26.7 %collective-permute-start.16 = (bf16[2,128,2048]{2,1,0:T(8,128)(2,1)}, bf16[2,128,2048]{2,1,0:T(8,128)(2,1)}, u32[]{:S(2)}, u32[]{:S(2)}) collective-permute-start(bf16[2,128,2048]{2,1,0:T(8,128)(2,1)} %bitcast.39), channel_id=1, source_target_pairs={{0,8},{4,12},{24,16},{28,20},{1,9},{5,13},{25,17},{29,21},{2,10},{... | collective-permute-start | bytes 3145736 | tf_op jit(solution)/shard_map/ppermute | solution.py:1074
  240.5 25.6 %collective-permute-start.17 = (bf16[2,128,2048]{2,1,0:T(8,128)(2,1)}, bf16[2,128,2048]{2,1,0:T(8,128)(2,1)}, u32[]{:S(2)}, u32[]{:S(2)}) collective-permute-start(bf16[2,128,2048]{2,1,0:T(8,128)(2,1)} %get-tuple-element.144), channel_id=1, source_target_pairs={{0,1},{1,0},{2,3},{3,2},{4,5},{5,4},{6,7},{7,6},{8,9},{9,8},{10,11... | collective-permute-start | bytes 3145736 | tf_op jit(solution)/shard_map/ppermute | solution.py:1077
  241.9 25.3 %collective-permute-start.18 = (bf16[2,128,2048]{2,1,0:T(8,128)(2,1)}, bf16[2,128,2048]{2,1,0:T(8,128)(2,1)}, u32[]{:S(2)}, u32[]{:S(2)}) collective-permute-start(bf16[2,128,2048]{2,1,0:T(8,128)(2,1)} %get-tuple-element.145), channel_id=1, source_target_pairs={{0,2},{1,3},{2,0},{3,1},{4,6},{5,7},{6,4},{7,5},{8,10},{9,11},{10,... | collective-permute-start | bytes 3145736 | tf_op jit(solution)/shard_map/ppermute | solution.py:1077
  273.6 142.1 %all-reduce.3.cloned.1.call-start = ((), (), s32[]{:S(2)}) async-start(), calls=%async_computation.4 | async-start | bytes 2621440 | tf_op jit(solution)/shard_map/psum | solution.py:1103
  280.7 22.8 %collective-permute-start.23 = (bf16[2,512,768]{2,1,0:T(8,128)(2,1)}, bf16[2,512,768]{2,1,0:T(8,128)(2,1)}, u32[]{:S(2)}, u32[]{:S(2)}) collective-permute-start(bf16[2,512,768]{2,1,0:T(8,128)(2,1)} %get-tuple-element.158), channel_id=1, source_target_pairs={{0,4},{4,0},{8,12},{12,8},{16,20},{20,16},{24,28},{28,24},{1,5},{5... | collective-permute-start | bytes 4718600 | tf_op jit(solution)/shard_map/ppermute | solution.py:1069
  316.6 29.1 %collective-permute-start.26 = (bf16[2,512,768]{2,1,0:T(8,128)(2,1)}, bf16[2,512,768]{2,1,0:T(8,128)(2,1)}, u32[]{:S(2)}, u32[]{:S(2)}) collective-permute-start(bf16[2,512,768]{2,1,0:T(8,128)(2,1)} %get-tuple-element.167), channel_id=1, source_target_pairs={{0,4},{4,0},{8,12},{12,8},{16,20},{20,16},{24,28},{28,24},{1,5},{5... | collective-permute-start | bytes 4718600 | tf_op jit(solution)/shard_map/ppermute | solution.py:1069
  316.6 29.1 %collective-permute-start.24 = (bf16[2,128,2048]{2,1,0:T(8,128)(2,1)}, bf16[2,128,2048]{2,1,0:T(8,128)(2,1)}, u32[]{:S(2)}, u32[]{:S(2)}) collective-permute-start(bf16[2,128,2048]{2,1,0:T(8,128)(2,1)} %get-tuple-element.161.refs_4_.refs_1_), channel_id=1, source_target_pairs={{8,0},{12,4},{16,24},{20,28},{9,1},{13,5},{17,25},{21,29},{10,2},{... | collective-permute-start | bytes 3145736 | tf_op jit(solution)/shard_map/ppermute | solution.py:1074
  350.9 28.8 %collective-permute-start.28 = (bf16[2,2,128,768]{3,2,1,0:T(8,128)(2,1)}, bf16[2,2,128,768]{3,2,1,0:T(8,128)(2,1)}, u32[]{:S(2)}, u32[]{:S(2)}) collective-permute-start(bf16[2,2,128,768]{3,2,1,0:T(8,128)(2,1)} %get-tuple-element.183), channel_id=1, source_target_pairs={{0,2},{1,3},{2,0},{3,1},{4,6},{5,7},{6,4},{7,5},{8,10},{9,11},{10,... | collective-permute-start | bytes 2359304 | tf_op jit(solution)/shard_map/ppermute | solution.py:1077
  351.8 27.9 %collective-permute-start.27 = (bf16[2,1,128,768]{3,2,1,0:T(8,128)(2,1)}, bf16[2,1,128,768]{3,2,1,0:T(8,128)(2,1)}, u32[]{:S(2)}, u32[]{:S(2)}) collective-permute-start(bf16[2,1,128,768]{3,2,1,0:T(8,128)(2,1)} %get-tuple-element.181), channel_id=1, source_target_pairs={{0,2},{1,3},{2,0},{3,1},{4,6},{5,7},{6,4},{7,5},{8,10},{9,11},{10,... | collective-permute-start | bytes 1179656 | tf_op jit(solution)/shard_map/ppermute | solution.py:1077
  383.0 26.6 %collective-permute-start.31 = (bf16[2,128,768]{2,1,0:T(8,128)(2,1)}, bf16[2,128,768]{2,1,0:T(8,128)(2,1)}, u32[]{:S(2)}, u32[]{:S(2)}) collective-permute-start(bf16[2,128,768]{2,1,0:T(8,128)(2,1)} %bitcast.35), channel_id=1, source_target_pairs={{0,8},{4,12},{8,0},{12,4},{16,24},{20,28},{24,16},{28,20},{1,9},{5... | collective-permute-start | bytes 1179656 | tf_op jit(solution)/shard_map/ppermute | solution.py:1069
  383.1 26.5 %collective-permute-start.32 = (bf16[2,1,128,768]{3,2,1,0:T(8,128)(2,1)}, bf16[2,1,128,768]{3,2,1,0:T(8,128)(2,1)}, u32[]{:S(2)}, u32[]{:S(2)}) collective-permute-start(bf16[2,1,128,768]{3,2,1,0:T(8,128)(2,1)} %get-tuple-element.189), channel_id=1, source_target_pairs={{0,1},{1,0},{2,3},{3,2},{4,5},{5,4},{6,7},{7,6},{8,9},{9,8},{10,11... | collective-permute-start | bytes 1179656 | tf_op jit(solution)/shard_map/ppermute | solution.py:1077
  (24 other events, 306.2 us)
Sparse Core Ops, SparseCore 0:
  46.5 57.9 all-gather.2
  106.3 52.6 all-gather.4
  273.7 29.2 reduce-scatter.1
  351.0 64.5 all-reduce.2

commit v5 on v4

--- a/solution.py
+++ b/solution.py
@@ -721,7 +721,7 @@
         after=after,
         scratch=[pltpu.VMEM((rows, rows), F32), pltpu.VMEM((rows, LANES), F32)],
         cost=cost(
-            (80 if first == 0 else 2) * rows * rows * LANES * count, rows * LANES * count
+            80 * rows * rows * LANES * count, rows * LANES * count
         ),
         name="attend_back",
     )
@@ -803,7 +803,7 @@
             pltpu.VMEM((width, 3 * width), BF16),
             pltpu.SemaphoreType.DMA((3, len(weights.plan))),
         ],
-        cost=cost(6 * rows * width * width, 22 * rows * width),
+        cost=cost(24 * rows * width * width, 88 * rows * width),
         name="grad_input",
     )
 
@@ -1440,7 +1440,7 @@
     reduce([unit_a, unit_b, unit_c], steps=4)
     if links.fast:
         unit_b.own, unit_e.own = links.over_dp((unit_b.own, unit_e.own.reshape(unit_e.shape)))
-    unit_d = unit(EXCHANGE, *project(1), ((2, 1),))
+    unit_d = unit(EXCHANGE, *project(1), ((1, 2),))
     grad_input, grad_gain_one, grad_shift_one = side.then(
         run_input(attn_weights, grads, tokens, grad_after, small, GAIN_ONE, after=side.order)
     )
@@ -1515,6 +1515,7 @@
             return total, move(total) if move else None
 
         mlp_new = adam_mlp(0, unit_a, None)
+        side.order += (unit_b.own,)
         grad_small, moved = step([unit_c, unit_d], shard_move(2))
         output = output_now()
         grad_small, moved = step([unit_c, unit_d], links.swap)

time: 492 us -> 501 us (1.018)
  waiting for transfers between devices: 98.9 us -> 107 us
    ppermute x18, waiting for transfers between devices: 50.8 us -> 37.5 us  [across_shard(): lax.ppermute(value, 'shard', [(s, s ^ bit) for s in range(self.shards)])]
    reduce_scatter x1, waiting for transfers between devices: 0.02 us -> 10.7 us  [__init__(): self.own = lax.psum_scatter(flat, 'shard', scatter_dimension=0, tiled=True)]
    psum x1, waiting for transfers between devices: 3.13 us -> 12.8 us  [over_dp(): return lax.psum(values, 'dp', axis_index_groups=groups)]
    ppermute x3, waiting for transfers between devices: 8.95 us -> 18.3 us  [along_dp(): return lax.ppermute(value, 'dp', pairs)]
    ppermute x23, waiting for transfers between devices: 27 us -> 18.7 us  [across_dp(): lax.ppermute(value, 'dp', [(d, d ^ bit) for d in range(self.replicas)])]
where the time goes in v5:
time: 501 us; the launch traced here: 497 us
  Pallas kernels  330 us (66%)
  waiting for transfers between devices  107 us (21%)
  starting transfers between devices  38.4 us (8%)
  between operations  14.4 us (3%)
  other arithmetic  5.61 us (1%)
    pallas_call x33, Pallas kernels, call(): pl.pallas_call(run, grid_spec=pltpu.PrefetchScalarGridSpec(num_scalar_pre...  330 us
    ppermute x18, waiting for transfers between devices, across_shard(): lax.ppermute(value, 'shard', [(s, s ^ bit) for s in range(self.shards)])  37.5 us
    ppermute x18, starting transfers between devices, across_shard(): lax.ppermute(value, 'shard', [(s, s ^ bit) for s in range(self.shards)])  21.5 us
    ppermute x23, waiting for transfers between devices, across_dp(): lax.ppermute(value, 'dp', [(d, d ^ bit) for d in range(self.replicas)])  18.7 us
    ppermute x3, waiting for transfers between devices, along_dp(): return lax.ppermute(value, 'dp', pairs)  18.3 us
    psum x1, waiting for transfers between devices, over_dp(): return lax.psum(values, 'dp', axis_index_groups=groups)  12.8 us
    reduce_scatter x1, waiting for transfers between devices, __init__(): self.own = lax.psum_scatter(flat, 'shard', scatter_dimension=0, tiled=True)  10.7 us
  transfers between devices with their start and end apart: 48, of which 16 were waited for; matrix products, arithmetic and copies ran while one was open for 1% of the time, Pallas kernels for 60%

profile of v5, /device:TPU:0, one launch (start us, length us, event | category | flops | bytes accessed | tf_op | source)
XLA Modules:
  0.0 497.0 jit_solution(9410296976895901508)
XLA Ops:
  31.3 9.2 %collective-permute-done.refs_1_.refs_3_.refs_15_ = bf16[144,4096]{1,0:T(8,128)(2,1)} collective-permute-done((bf16[144,4096]{1,0:T(8,128)(2,1)}, bf16[144,4096]{1,0:T(8,128)(2,1)}, u32[]{:S(2)}, u32[]{:S(2)}) %collective-permute-start) | collective-permute-done | bytes 1179680 | tf_op jit(solution)/shard_map/ppermute | solution.py:1077
  49.0 19.5 %collective-permute-done.5.refs_4_.refs_7_.refs_19_ = bf16[80,4096]{1,0:T(8,128)(2,1)} collective-permute-done((bf16[80,4096]{1,0:T(8,128)(2,1)}, bf16[80,4096]{1,0:T(8,128)(2,1)}, u32[]{:S(2)}, u32[]{:S(2)}) %collective-permute-start.5) | collective-permute-done | bytes 655392 | tf_op jit(solution)/shard_map/ppermute | solution.py:1077
  72.1 14.2 %qkv.1 = (bf16[1024,3072]{1,0:T(8,128)(2,1)}, bf16[1024,1024]{1,0:T(8,128)(2,1)}) custom-call(s32[9]{0:T(128)} %stack.59.refs_0_.refs_12_, bf16[256,4096]{1,0:T(8,128)(2,1)} %side.18.refs_5_.refs_1_.refs_13_, bf16[144,4096]{1,0:T(8,128)(2,1)} %collective-permute-done.1.refs_2_.refs_14_, bf16[144,4096]{1,0:T(8,128)(2,1)} %collective-permute-done.refs_1_.refs_3_.refs_15_, ...), custom_call_target="tpu_custom_call" | custom-call | flops 6442450944 | bytes 16777216 | tf_op jit(solution)/shard_map/qkv/pallas_call | solution.py:60
  86.4 22.9 %attend.1 = (bf16[1024,1024]{1,0:T(8,128)(2,1)}, f32[8,2,1024]{2,1,0:T(2,128)}) custom-call(s32[4]{0:T(128)} %bitcast.50, bf16[1024,3072]{1,0:T(8,128)(2,1)} %get-tuple-element.116.refs_1_.refs_2_.refs_3_.refs_4_, bf16[1024,3072]{1,0:T(8,128)(2,1)} %get-tuple-element.116.refs_1_.refs_2_.refs_3_.refs_4_, ...), custom_call_target="tpu_custom_call" | custom-call | flops 8589934592 | bytes 8388608 | tf_op jit(solution)/shard_map/attend/pallas_call | solution.py:60
  109.9 10.4 %after.1 = (f32[1024,1024]{1,0:T(8,128)}, bf16[1024,1024]{1,0:T(8,128)(2,1)}, bf16[1024,1024]{1,0:T(8,128)(2,1)}, bf16[1024,1024]{1,0:T(8,128)(2,1)}) custom-call(s32[9]{0:T(128)} %stack.59.refs_0_.refs_12_, bf16[256,4096]{1,0:T(8,128)(2,1)} %side.18.refs_5_.refs_1_.refs_13_, bf16[144,4096]{1,0:T(8,128)(2,1)} %collective-permute-done.1.refs_2_.refs_14_, ...), custom_call_target="tpu_custom_call" | custom-call | flops 2147483648 | bytes 14680064 | tf_op jit(solution)/shard_map/after/pallas_call | solution.py:60
  120.3 29.1 %feed.2 = (bf16[1024,4096]{1,0:T(8,128)(2,1)}, bf16[1024,4096]{1,0:T(8,128)(2,1)}, bf16[2,512,2048]{2,1,0:T(8,128)(2,1)}, bf16[2,512,2048]{2,1,0:T(8,128)(2,1)}, f32[1,2048]{1,0:T(1,128)}) custom-call(s32[8]{0:T(128)} %pad_add_fusion.refs_0_.refs_3_.refs_6_.refs_9_, bf16[512,4096]{1,0:T(8,128)(2,1)} %all-gather.3.cloned.1.call-done.refs_18_.refs_1_.refs_4_, ...), custom_call_target="tpu_custom_call" | custom-call | flops 17179869184 | bytes 50331648 | tf_op jit(solution)/shard_map/feed/pallas_call | solution.py:60
  150.1 9.0 %all-gather.5.cloned.1.call-done.refs_1_.refs_4_.refs_7_.refs_10_ = bf16[512,4096]{1,0:T(8,128)(2,1)} async-done(((bf16[128,4096]{1,0:T(8,128)(2,1)}), bf16[512,4096]{1,0:T(8,128)(2,1)}) %all-gather.5.cloned.1.call-update) | async-done | bytes 4194320 | tf_op jit(solution)/shard_map/all_gather | solution.py:1088
  167.6 29.6 %feed.3 = (bf16[1024,4096]{1,0:T(8,128)(2,1)}, bf16[1024,4096]{1,0:T(8,128)(2,1)}, bf16[2,512,2048]{2,1,0:T(8,128)(2,1)}, bf16[2,512,2048]{2,1,0:T(8,128)(2,1)}, f32[1,2048]{1,0:T(1,128)}) custom-call(s32[8]{0:T(128)} %pad_add_fusion.refs_0_.refs_3_.refs_6_.refs_9_, ...), custom_call_target="tpu_custom_call", output_to_operand_aliasing={{0}: (12, {}), {1}: (13, {})} | custom-call | flops 17179869184 | bytes 50331648 | tf_op jit(solution)/shard_map/feed/pallas_call | solution.py:60
  204.1 24.6 %middle.1 = (f32[1024,1024]{1,0:T(8,128)}, bf16[1024,1024]{1,0:T(8,128)(2,1)}, bf16[2,512,512]{2,1,0:T(8,128)(2,1)}, bf16[2,512,512]{2,1,0:T(8,128)(2,1)}, f32[1...) custom-call(s32[8]{0:T(128)} %pad_add_fusion.refs_0_.refs_3_.refs_6_.refs_9_, ...), custom_call_target="tpu_custom_call" | custom-call | flops 51539607552 | bytes 125829120 | tf_op jit(solution)/shard_map/middle/pallas_call | solution.py:60
  228.9 7.3 %side.23 = (bf16[2,1,128,2048]{3,2,1,0:T(8,128)(2,1)}, bf16[2,2,128,2048]{3,2,1,0:T(8,128)(2,1)}, bf16[2,128,2048]{2,1,0:T(8,128)(2,1)}, bf16[2,128,2048]{2,1,0:T(8,128)(2,1)}) custom-call(s32[3]{0:T(128)} %pad_add_fusion.1.refs_0_, bf16[2,1,128,2048]{3,2,1,0:T(8,128)(2,1)} %get-tuple-element.135.refs_27_.refs_1_, ...), custom_call_target="tpu_custom_call" | custom-call | bytes 20971520 | tf_op jit(solution)/shard_map/side/pallas_call | solution.py:60
  242.5 18.9 %attend_back.2 = (bf16[1024,512]{1,0:T(8,128)(2,1)}, bf16[1024,512]{1,0:T(8,128)(2,1)}, bf16[1024,512]{1,0:T(8,128)(2,1)}, f32[1,512]{1,0:T(1,128)}, f32[1,512]{1,0:T(1,128)}) custom-call(s32[4]{0:T(128)} %bitcast.51, bf16[1024,3072]{1,0:T(8,128)(2,1)} %get-tuple-element.116.refs_1_.refs_2_.refs_3_.refs_4_, ...), custom_call_target="tpu_custom_call" | custom-call | flops 42949672960 | bytes 524288 | tf_op jit(solution)/shard_map/attend_back/pallas_call | solution.py:60
  275.3 7.1 %project.2 = (bf16[2,512,768]{2,1,0:T(8,128)(2,1)}, bf16[2,512,768]{2,1,0:T(8,128)(2,1)}) custom-call(bf16[1024,1024]{1,0:T(8,128)(2,1)} %get-tuple-element.154.refs_0_, bf16[1024,512]{1,0:T(8,128)(2,1)} %get-tuple-element.149.refs_8_.refs_1_.refs_10_, bf16[1024,512]{1,0:T(8,128)(2,1)} %get-tuple-element.155.refs_2_.refs_11_, ...), custom_call_target="tpu_custom_call" | custom-call | flops 3221225472 | bytes 7340032 | tf_op jit(solution)/shard_map/project/pallas_call | solution.py:60
  284.4 19.0 %attend_back.3 = (bf16[1024,512]{1,0:T(8,128)(2,1)}, bf16[1024,512]{1,0:T(8,128)(2,1)}, bf16[1024,512]{1,0:T(8,128)(2,1)}, f32[1,512]{1,0:T(1,128)}, f32[1,512]{1,0:T(1,128)}) custom-call(s32[4]{0:T(128)} %bitcast.52, bf16[1024,3072]{1,0:T(8,128)(2,1)} %get-tuple-element.116.refs_1_.refs_2_.refs_3_.refs_4_, ...), custom_call_target="tpu_custom_call" | custom-call | flops 42949672960 | bytes 524288 | tf_op jit(solution)/shard_map/attend_back/pallas_call | solution.py:60
  303.5 10.7 %reduce-scatter.2.cloned.1.call-done.refs_9_ = bf16[256,512]{1,0:T(8,128)(2,1)} async-done(((bf16[1024,512]{1,0:T(8,128)(2,1)}), bf16[256,512]{1,0:T(8,128)(2,1)}) %reduce-scatter.2.cloned.1.call-update) | async-done | bytes 262160 | tf_op jit(solution)/shard_map/reduce_scatter | solution.py:1214
  321.4 7.1 %project.3 = (bf16[2,512,768]{2,1,0:T(8,128)(2,1)}, bf16[2,512,768]{2,1,0:T(8,128)(2,1)}) custom-call(bf16[1024,1024]{1,0:T(8,128)(2,1)} %get-tuple-element.154.refs_0_, bf16[1024,512]{1,0:T(8,128)(2,1)} %get-tuple-element.159.refs_8_.refs_1_.refs_13_, bf16[1024,512]{1,0:T(8,128)(2,1)} %get-tuple-element.164.refs_2_.refs_14_, ...), custom_call_target="tpu_custom_call" | custom-call | flops 3221225472 | bytes 7340032 | tf_op jit(solution)/shard_map/project/pallas_call | solution.py:60
  329.9 16.0 %grad_input.1 = (f32[1024,1024]{1,0:T(8,128)}, f32[1,1024]{1,0:T(1,128)}, f32[1,1024]{1,0:T(1,128)}) custom-call(s32[9]{0:T(128)} %stack.59.refs_0_.refs_12_, bf16[256,4096]{1,0:T(8,128)(2,1)} %side.18.refs_5_.refs_1_.refs_13_, bf16[144,4096]{1,0:T(8,128)(2,1)} %collective-permute-done.1.refs_2_.refs_14_, ...), custom_call_target="tpu_custom_call" | custom-call | flops 25769803776 | bytes 92274688 | tf_op jit(solution)/shard_map/grad_input/pallas_call | solution.py:60
  348.7 16.8 %collective-permute-done.24.refs_2_ = bf16[2,128,2048]{2,1,0:T(8,128)(2,1)} collective-permute-done((bf16[2,128,2048]{2,1,0:T(8,128)(2,1)}, bf16[2,128,2048]{2,1,0:T(8,128)(2,1)}, u32[]{:S(2)}, u32[]{:S(2)}) %collective-permute-start.24) | collective-permute-done | bytes 1048608 | tf_op jit(solution)/shard_map/ppermute | solution.py:1074
  374.7 12.6 %adam.4 = (f32[256,8192]{1,0:T(8,128)}, f32[256,8192]{1,0:T(8,128)}, f32[256,8192]{1,0:T(8,128)}) custom-call(s32[3]{0:T(128)} %pad_add_fusion.1.refs_0_, s32[2]{0:T(128)} %iota_multiply_fusion.2.refs_1_, f32[256,8192]{1,0:T(8,128)} %refs_2_.9, f32[256,8192]{1,0:T(8,128)} %refs_3_.7, f32[256,8192]{1,0:T(8,128)} %refs_4_.7, ...), custom_call_target="tpu_custom_call" | custom-call | flops 2097152 | bytes 2097152 | tf_op jit(solution)/shard_map/adam/pallas_call | solution.py:60
  387.3 12.8 %all-reduce.3.cloned.1.call-done = (bf16[2,128,2048]{2,1,0:T(8,128)(2,1)}, bf16[2,128,512]{2,1,0:T(8,128)(2,1)}) async-done(((bf16[2,128,2048]{2,1,0:T(8,128)(2,1)}, bf16[2,128,512]{2,1,0:T(8,128)(2,1)}), (bf16[2,128,2048]{2,1,0:T(8,128)(2,1)}, bf16[2,128,512]{2,1,0:T(8,128)(2,1)})) %all-reduce.3.cloned.1.call-update) | async-done | bytes 1310736 | tf_op jit(solution)/shard_map/psum | solution.py:1103
  406.9 15.3 %output.1.refs_7_ = bf16[1024,1024]{1,0:T(8,128)(2,1)} custom-call(s32[8]{0:T(128)} %pad_add_fusion.refs_0_.refs_3_.refs_6_.refs_9_, bf16[512,4096]{1,0:T(8,128)(2,1)} %all-gather.3.cloned.1.call-done.refs_18_.refs_1_.refs_4_, bf16[512,4096]{1,0:T(8,128)(2,1)} %collective-permute-done.8.refs_2_.refs_5_, s32[8]{0:T(128)} %pad_add_fusion.refs_0_.refs_3_.refs_6_.refs_9_, ...), custom_call_target="tpu_custom_call" | custom-call | flops 858993472 | bytes 2097152 | tf_op jit(solution)/shard_map/output/pallas_call | solution.py:60
  428.4 12.4 %adam.5 = (f32[256,8192]{1,0:T(8,128)}, f32[256,8192]{1,0:T(8,128)}, f32[256,8192]{1,0:T(8,128)}) custom-call(s32[3]{0:T(128)} %pad_add_fusion.1.refs_0_, s32[2]{0:T(128)} %constant.88.clone.refs_1_, f32[256,8192]{1,0:T(8,128)} %refs_2_.9, f32[256,8192]{1,0:T(8,128)} %refs_3_.7, ...), custom_call_target="tpu_custom_call", output_to_operand_aliasing={{0}: (8, {}), {1}: (9, {}), {2}: (10, {})} | custom-call | flops 2097152 | bytes 2097152 | tf_op jit(solution)/shard_map/adam/pallas_call | solution.py:60
  452.9 7.0 %adam.6 = (f32[256,4096]{1,0:T(8,128)}, f32[256,4096]{1,0:T(8,128)}, f32[256,4096]{1,0:T(8,128)}) custom-call(s32[3]{0:T(128)} %pad_add_fusion.1.refs_0_, s32[3]{0:T(128)} %iota_multiply_fusion.1.refs_1_, f32[256,4096]{1,0:T(8,128)} %refs_2_.11, f32[256,4096]{1,0:T(8,128)} %refs_3_.9, f32[256,4096]{1,0:T(8,128)} %refs_4_.9, ...), custom_call_target="tpu_custom_call" | custom-call | flops 786432 | bytes 786432 | tf_op jit(solution)/shard_map/adam/pallas_call | solution.py:60
  460.8 9.9 %collective-permute-done.38.refs_2_ = bf16[2,128,768]{2,1,0:T(8,128)(2,1)} collective-permute-done((bf16[2,128,768]{2,1,0:T(8,128)(2,1)}, bf16[2,128,768]{2,1,0:T(8,128)(2,1)}, u32[]{:S(2)}, u32[]{:S(2)}) %collective-permute-start.38) | collective-permute-done | bytes 393248 | tf_op jit(solution)/shard_map/ppermute | solution.py:1069
  475.8 10.2 %adam.7 = (f32[256,4096]{1,0:T(8,128)}, f32[256,4096]{1,0:T(8,128)}, f32[256,4096]{1,0:T(8,128)}) custom-call(s32[3]{0:T(128)} %pad_add_fusion.1.refs_0_, s32[5]{0:T(128)} %constant.89.clone.refs_1_, f32[256,4096]{1,0:T(8,128)} %refs_2_.11, f32[256,4096]{1,0:T(8,128)} %refs_3_.9, ...), custom_call_target="tpu_custom_call", output_to_operand_aliasing={{0}: (10, {}), {1}: (11, {}), {2}: (12, {})} | custom-call | flops 1310720 | bytes 1310720 | tf_op jit(solution)/shard_map/adam/pallas_call | solution.py:60
  (119 shorter events, 131.2 us)
Async XLA Ops:
  7.2 102.1 %all-gather.3.cloned.1.call-start = ((), (), s32[]{:S(2)}) async-start(), calls=%async_computation.1 | async-start | bytes 5242880 | tf_op jit(solution)/shard_map/all_gather | solution.py:1088
  11.3 29.2 %collective-permute-start = (bf16[144,4096]{1,0:T(8,128)(2,1)}, bf16[144,4096]{1,0:T(8,128)(2,1)}, u32[]{:S(2)}, u32[]{:S(2)}) collective-permute-start(bf16[144,4096]{1,0:T(8,128)(2,1)} %side.16.refs_3_), channel_id=1, source_target_pairs={{0,2},{1,3},{2,0},{3,1},{4,6},{5,7},{6,4},{7,5},{8,10},{9,11},{10,... | collective-permute-start | bytes 3538952 | tf_op jit(solution)/shard_map/ppermute | solution.py:1077
  14.3 27.7 %collective-permute-start.1 = (bf16[144,4096]{1,0:T(8,128)(2,1)}, bf16[144,4096]{1,0:T(8,128)(2,1)}, u32[]{:S(2)}, u32[]{:S(2)}) collective-permute-start(bf16[144,4096]{1,0:T(8,128)(2,1)} %side.16.refs_3_), channel_id=1, source_target_pairs={{0,1},{1,0},{2,3},{3,2},{4,5},{5,4},{6,7},{7,6},{8,9},{9,8},{10,11... | collective-permute-start | bytes 3538952 | tf_op jit(solution)/shard_map/ppermute | solution.py:1077
  46.3 112.7 %all-gather.5.cloned.1.call-start = ((), (), s32[]{:S(2)}) async-start(), calls=%async_computation.2 | async-start | bytes 5242880 | tf_op jit(solution)/shard_map/all_gather | solution.py:1088
  46.4 22.1 %collective-permute-start.5 = (bf16[80,4096]{1,0:T(8,128)(2,1)}, bf16[80,4096]{1,0:T(8,128)(2,1)}, u32[]{:S(2)}, u32[]{:S(2)}) collective-permute-start(bf16[80,4096]{1,0:T(8,128)(2,1)} %get-tuple-element.115), channel_id=1, source_target_pairs={{0,2},{1,3},{2,0},{3,1},{4,6},{5,7},{6,4},{7,5},{8,10},{9,11},{10,... | collective-permute-start | bytes 1966088 | tf_op jit(solution)/shard_map/ppermute | solution.py:1077
  46.8 25.3 %collective-permute-start.2 = (bf16[144,4096]{1,0:T(8,128)(2,1)}, bf16[144,4096]{1,0:T(8,128)(2,1)}, u32[]{:S(2)}, u32[]{:S(2)}) collective-permute-start(bf16[144,4096]{1,0:T(8,128)(2,1)} %collective-permute-done.1.refs_2_.refs_14_), channel_id=1, source_target_pairs={{0,4},{4,0},{8,12},{12,8},{16,20},{20,16},{24,28},{28,24},{1,5},{5... | collective-permute-start | bytes 3538952 | tf_op jit(solution)/shard_map/ppermute | solution.py:1069
  46.8 25.3 %collective-permute-start.3 = (bf16[144,4096]{1,0:T(8,128)(2,1)}, bf16[144,4096]{1,0:T(8,128)(2,1)}, u32[]{:S(2)}, u32[]{:S(2)}) collective-permute-start(bf16[144,4096]{1,0:T(8,128)(2,1)} %collective-permute-done.refs_1_.refs_3_.refs_15_), channel_id=1, source_target_pairs={{0,4},{4,0},{8,12},{12,8},{16,20},{20,16},{24,28},{28,24},{1,5},{5... | collective-permute-start | bytes 3538952 | tf_op jit(solution)/shard_map/ppermute | solution.py:1069
  69.0 245.2 %reduce-scatter.2.cloned.1.call-start = ((), (), s32[]{:S(2)}) async-start(), calls=%async_computation.3 | async-start | bytes 1310720 | tf_op jit(solution)/shard_map/reduce_scatter | solution.py:1214
  165.5 31.7 %collective-permute-start.11 = (bf16[2,128,2048]{2,1,0:T(8,128)(2,1)}, bf16[2,128,2048]{2,1,0:T(8,128)(2,1)}, u32[]{:S(2)}, u32[]{:S(2)}) collective-permute-start(bf16[2,128,2048]{2,1,0:T(8,128)(2,1)} %get-tuple-element.132), channel_id=1, source_target_pairs={{0,1},{1,0},{2,3},{3,2},{4,5},{5,4},{6,7},{7,6},{8,9},{9,8},{10,11... | collective-permute-start | bytes 3145736 | tf_op jit(solution)/shard_map/ppermute | solution.py:1077
  167.0 30.2 %collective-permute-start.12 = (bf16[2,128,2048]{2,1,0:T(8,128)(2,1)}, bf16[2,128,2048]{2,1,0:T(8,128)(2,1)}, u32[]{:S(2)}, u32[]{:S(2)}) collective-permute-start(bf16[2,128,2048]{2,1,0:T(8,128)(2,1)} %get-tuple-element.133), channel_id=1, source_target_pairs={{0,2},{1,3},{2,0},{3,1},{4,6},{5,7},{6,4},{7,5},{8,10},{9,11},{10,... | collective-permute-start | bytes 3145736 | tf_op jit(solution)/shard_map/ppermute | solution.py:1077
  197.1 31.7 %collective-permute-start.15 = (bf16[2,512,2048]{2,1,0:T(8,128)(2,1)}, bf16[2,512,2048]{2,1,0:T(8,128)(2,1)}, u32[]{:S(2)}, u32[]{:S(2)}) collective-permute-start(bf16[2,512,2048]{2,1,0:T(8,128)(2,1)} %get-tuple-element.138), channel_id=1, source_target_pairs={{0,4},{4,0},{8,12},{12,8},{16,20},{20,16},{24,28},{28,24},{1,5},{5... | collective-permute-start | bytes 12582920 | tf_op jit(solution)/shard_map/ppermute | solution.py:1069
  202.1 26.7 %collective-permute-start.13 = (bf16[1,128,2048]{2,1,0:T(8,128)(2,1)}, bf16[1,128,2048]{2,1,0:T(8,128)(2,1)}, u32[]{:S(2)}, u32[]{:S(2)}) collective-permute-start(bf16[1,128,2048]{2,1,0:T(8,128)(2,1)} %get-tuple-element.136), channel_id=1, source_target_pairs={{0,2},{1,3},{2,0},{3,1},{4,6},{5,7},{6,4},{7,5},{8,10},{9,11},{10,... | collective-permute-start | bytes 1572872 | tf_op jit(solution)/shard_map/ppermute | solution.py:1077
  203.6 25.3 %collective-permute-start.14 = (bf16[1,128,2048]{2,1,0:T(8,128)(2,1)}, bf16[1,128,2048]{2,1,0:T(8,128)(2,1)}, u32[]{:S(2)}, u32[]{:S(2)}) collective-permute-start(bf16[1,128,2048]{2,1,0:T(8,128)(2,1)} %get-tuple-element.137), channel_id=1, source_target_pairs={{0,1},{1,0},{2,3},{3,2},{4,5},{5,4},{6,7},{7,6},{8,9},{9,8},{10,11... | collective-permute-start | bytes 1572872 | tf_op jit(solution)/shard_map/ppermute | solution.py:1077
  228.7 32.6 %collective-permute-start.19 = (bf16[2,512,512]{2,1,0:T(8,128)(2,1)}, bf16[2,512,512]{2,1,0:T(8,128)(2,1)}, u32[]{:S(2)}, u32[]{:S(2)}) collective-permute-start(bf16[2,512,512]{2,1,0:T(8,128)(2,1)} %get-tuple-element.147), channel_id=1, source_target_pairs={{0,4},{4,0},{8,12},{12,8},{16,20},{20,16},{24,28},{28,24},{1,5},{5... | collective-permute-start | bytes 3145736 | tf_op jit(solution)/shard_map/ppermute | solution.py:1069
  236.1 26.7 %collective-permute-start.16 = (bf16[2,128,2048]{2,1,0:T(8,128)(2,1)}, bf16[2,128,2048]{2,1,0:T(8,128)(2,1)}, u32[]{:S(2)}, u32[]{:S(2)}) collective-permute-start(bf16[2,128,2048]{2,1,0:T(8,128)(2,1)} %bitcast.39), channel_id=1, source_target_pairs={{0,8},{4,12},{24,16},{28,20},{1,9},{5,13},{25,17},{29,21},{2,10},{... | collective-permute-start | bytes 3145736 | tf_op jit(solution)/shard_map/ppermute | solution.py:1074
  240.5 25.6 %collective-permute-start.17 = (bf16[2,128,2048]{2,1,0:T(8,128)(2,1)}, bf16[2,128,2048]{2,1,0:T(8,128)(2,1)}, u32[]{:S(2)}, u32[]{:S(2)}) collective-permute-start(bf16[2,128,2048]{2,1,0:T(8,128)(2,1)} %get-tuple-element.144), channel_id=1, source_target_pairs={{0,1},{1,0},{2,3},{3,2},{4,5},{5,4},{6,7},{7,6},{8,9},{9,8},{10,11... | collective-permute-start | bytes 3145736 | tf_op jit(solution)/shard_map/ppermute | solution.py:1077
  241.9 25.3 %collective-permute-start.18 = (bf16[2,128,2048]{2,1,0:T(8,128)(2,1)}, bf16[2,128,2048]{2,1,0:T(8,128)(2,1)}, u32[]{:S(2)}, u32[]{:S(2)}) collective-permute-start(bf16[2,128,2048]{2,1,0:T(8,128)(2,1)} %get-tuple-element.145), channel_id=1, source_target_pairs={{0,2},{1,3},{2,0},{3,1},{4,6},{5,7},{6,4},{7,5},{8,10},{9,11},{10,... | collective-permute-start | bytes 3145736 | tf_op jit(solution)/shard_map/ppermute | solution.py:1077
  273.6 29.9 %collective-permute-start.20 = (bf16[2,128,2048]{2,1,0:T(8,128)(2,1)}, bf16[2,128,2048]{2,1,0:T(8,128)(2,1)}, u32[]{:S(2)}, u32[]{:S(2)}) collective-permute-start(bf16[2,128,2048]{2,1,0:T(8,128)(2,1)} %get-tuple-element.150.refs_4_.refs_1_), channel_id=1, source_target_pairs={{8,16},{12,20},{16,8},{20,12},{9,17},{13,21},{17,9},{21,13},{10,18... | collective-permute-start | bytes 3145736 | tf_op jit(solution)/shard_map/ppermute | solution.py:1074
  284.4 115.7 %all-reduce.3.cloned.1.call-start = ((), (), s32[]{:S(2)}) async-start(), calls=%async_computation.4 | async-start | bytes 2621440 | tf_op jit(solution)/shard_map/psum | solution.py:1103
  320.1 45.4 %collective-permute-start.24 = (bf16[2,128,2048]{2,1,0:T(8,128)(2,1)}, bf16[2,128,2048]{2,1,0:T(8,128)(2,1)}, u32[]{:S(2)}, u32[]{:S(2)}) collective-permute-start(bf16[2,128,2048]{2,1,0:T(8,128)(2,1)} %get-tuple-element.161.refs_4_.refs_1_), channel_id=1, source_target_pairs={{8,0},{12,4},{16,24},{20,28},{9,1},{13,5},{17,25},{21,29},{10,2},{... | collective-permute-start | bytes 3145736 | tf_op jit(solution)/shard_map/ppermute | solution.py:1074
  328.5 37.0 %collective-permute-start.26 = (bf16[2,512,768]{2,1,0:T(8,128)(2,1)}, bf16[2,512,768]{2,1,0:T(8,128)(2,1)}, u32[]{:S(2)}, u32[]{:S(2)}) collective-permute-start(bf16[2,512,768]{2,1,0:T(8,128)(2,1)} %get-tuple-element.167), channel_id=1, source_target_pairs={{0,4},{4,0},{8,12},{12,8},{16,20},{20,16},{24,28},{28,24},{1,5},{5... | collective-permute-start | bytes 4718600 | tf_op jit(solution)/shard_map/ppermute | solution.py:1069
  370.8 29.3 %collective-permute-start.28 = (bf16[2,2,128,768]{3,2,1,0:T(8,128)(2,1)}, bf16[2,2,128,768]{3,2,1,0:T(8,128)(2,1)}, u32[]{:S(2)}, u32[]{:S(2)}) collective-permute-start(bf16[2,2,128,768]{3,2,1,0:T(8,128)(2,1)} %get-tuple-element.183), channel_id=1, source_target_pairs={{0,1},{1,0},{2,3},{3,2},{4,5},{5,4},{6,7},{7,6},{8,9},{9,8},{10,11... | collective-permute-start | bytes 2359304 | tf_op jit(solution)/shard_map/ppermute | solution.py:1077
  372.2 27.9 %collective-permute-start.27 = (bf16[2,1,128,768]{3,2,1,0:T(8,128)(2,1)}, bf16[2,1,128,768]{3,2,1,0:T(8,128)(2,1)}, u32[]{:S(2)}, u32[]{:S(2)}) collective-permute-start(bf16[2,1,128,768]{3,2,1,0:T(8,128)(2,1)} %get-tuple-element.181), channel_id=1, source_target_pairs={{0,2},{1,3},{2,0},{3,1},{4,6},{5,7},{6,4},{7,5},{8,10},{9,11},{10,... | collective-permute-start | bytes 1179656 | tf_op jit(solution)/shard_map/ppermute | solution.py:1077
  372.2 27.9 %collective-permute-start.29 = (f32[1,12288]{1,0:T(1,128)}, f32[1,12288]{1,0:T(1,128)}, u32[]{:S(2)}, u32[]{:S(2)}) collective-permute-start(f32[1,12288]{1,0:T(1,128)} %get-tuple-element.184.refs_5_), channel_id=1, source_target_pairs={{0,1},{1,0},{2,3},{3,2},{4,5},{5,4},{6,7},{7,6},{8,9},{9,8},{10,11... | collective-permute-start | bytes 147464 | tf_op jit(solution)/shard_map/ppermute | solution.py:1077
  (24 other events, 305.5 us)
Sparse Core Ops, SparseCore 0:
  46.5 57.9 all-gather.2
  106.3 52.6 all-gather.4
  284.5 29.6 reduce-scatter.1
  330.0 69.9 all-reduce.2

commit v6 on v5

--- a/solution.py
+++ b/solution.py
@@ -1435,11 +1435,9 @@
     unit_e = Wide(links, joined)
     unit_c = unit(EXCHANGE, *project(0), ((1, 2),))
     attend_back(pairs // 2)
-    if links.fast:
-        side.order += (unit_e.own,)
     reduce([unit_a, unit_b, unit_c], steps=4)
     if links.fast:
-        unit_b.own, unit_e.own = links.over_dp((unit_b.own, unit_e.own.reshape(unit_e.shape)))
+        unit_b.own = links.over_dp(unit_b.own)
     unit_d = unit(EXCHANGE, *project(1), ((1, 2),))
     grad_input, grad_gain_one, grad_shift_one = side.then(
         run_input(attn_weights, grads, tokens, grad_after, small, GAIN_ONE, after=side.order)
@@ -1447,6 +1445,8 @@
     small_grads = [biases[0][0], biases[1][0], biases[0][1], biases[1][1], grad_bias_o]
     small_grads += grad_bias_up
     small_grads += [grad_bias_dn, grad_gain_one, grad_shift_one, grad_gain_two, grad_shift_two]
+    if links.fast:
+        side.order += (unit_e.own,)
     (grad_small,) = reduce([unit_a, unit_c, unit_d], [job_lay(small_grads)])
 
     def pick_feed(number, arrays):
@@ -1515,14 +1515,15 @@
             return total, move(total) if move else None
 
         mlp_new = adam_mlp(0, unit_a, None)
-        side.order += (unit_b.own,)
         grad_small, moved = step([unit_c, unit_d], shard_move(2))
         output = output_now()
         grad_small, moved = step([unit_c, unit_d], links.swap)
         unit_b.close(grad_small)
-        unit_e.close(grad_small)
+        unit_e.own, _ = lax.optimization_barrier((unit_e.own, unit_b.own))
+        unit_e.finish()
         mlp_new = adam_mlp(1, unit_b, mlp_new)
         grad_small, moved = step([unit_c, unit_d], dp_move(2))
+        unit_e.close(grad_small)
         attn_new = adam_attn([unit_c], [0, 2, 4], None)
         grad_small, moved = step([unit_d], dp_move(4))
         attn_new = adam_attn([unit_d, unit_e], [1, 3, 5, 6, 7], attn_new)

time: 501 us -> 497 us (level)
  waiting for transfers between devices: 107 us -> 100 us
    ppermute x3, waiting for transfers between devices: 18.3 us -> 1.49 us  [along_dp(): return lax.ppermute(value, 'dp', pairs)]
    reduce_scatter x1, waiting for transfers between devices: 10.7 us -> 0.02 us  [__init__(): self.own = lax.psum_scatter(flat, 'shard', scatter_dimension=0, tiled=True)]
    psum x1 -> x2, waiting for transfers between devices: 12.8 us -> 22.1 us  [over_dp(): return lax.psum(values, 'dp', axis_index_groups=groups)]
    ppermute x18, waiting for transfers between devices: 37.5 us -> 46.7 us  [across_shard(): lax.ppermute(value, 'shard', [(s, s ^ bit) for s in range(self.shards)])]
  transfers between devices with their start and end apart: 48 -> 49, of which waited for: 16 -> 14; matrix products, arithmetic and copies ran while one was open for 1% -> 1% of each run, Pallas kernels for 60% -> 62%
where the time goes in v6:
time: 497 us; the launch traced here: 493 us
  Pallas kernels  330 us (66%)
  waiting for transfers between devices  100 us (20%)
  starting transfers between devices  41.5 us (8%)
  between operations  14.4 us (3%)
  other arithmetic  5.61 us (1%)
    pallas_call x33, Pallas kernels, call(): pl.pallas_call(run, grid_spec=pltpu.PrefetchScalarGridSpec(num_scalar_pre...  330 us
    ppermute x18, waiting for transfers between devices, across_shard(): lax.ppermute(value, 'shard', [(s, s ^ bit) for s in range(self.shards)])  46.7 us
    psum x2, waiting for transfers between devices, over_dp(): return lax.psum(values, 'dp', axis_index_groups=groups)  22.1 us
    ppermute x23, waiting for transfers between devices, across_dp(): lax.ppermute(value, 'dp', [(d, d ^ bit) for d in range(self.replicas)])  20.6 us
    ppermute x18, starting transfers between devices, across_shard(): lax.ppermute(value, 'shard', [(s, s ^ bit) for s in range(self.shards)])  19.9 us
    ppermute x23, starting transfers between devices, across_dp(): lax.ppermute(value, 'dp', [(d, d ^ bit) for d in range(self.replicas)])  14.1 us
  transfers between devices with their start and end apart: 49, of which 14 were waited for; matrix products, arithmetic and copies ran while one was open for 1% of the time, Pallas kernels for 62%

profile of v6, /device:TPU:0, one launch (start us, length us, event | category | flops | bytes accessed | tf_op | source)
XLA Modules:
  0.0 493.2 jit_solution(5112942221609756739)
XLA Ops:
  31.3 9.2 %collective-permute-done.refs_1_.refs_3_.refs_15_ = bf16[144,4096]{1,0:T(8,128)(2,1)} collective-permute-done((bf16[144,4096]{1,0:T(8,128)(2,1)}, bf16[144,4096]{1,0:T(8,128)(2,1)}, u32[]{:S(2)}, u32[]{:S(2)}) %collective-permute-start) | collective-permute-done | bytes 1179680 | tf_op jit(solution)/shard_map/ppermute | solution.py:1077
  49.0 19.5 %collective-permute-done.5.refs_4_.refs_7_.refs_19_ = bf16[80,4096]{1,0:T(8,128)(2,1)} collective-permute-done((bf16[80,4096]{1,0:T(8,128)(2,1)}, bf16[80,4096]{1,0:T(8,128)(2,1)}, u32[]{:S(2)}, u32[]{:S(2)}) %collective-permute-start.5) | collective-permute-done | bytes 655392 | tf_op jit(solution)/shard_map/ppermute | solution.py:1077
  72.1 14.2 %qkv.1 = (bf16[1024,3072]{1,0:T(8,128)(2,1)}, bf16[1024,1024]{1,0:T(8,128)(2,1)}) custom-call(s32[9]{0:T(128)} %stack.59.refs_0_.refs_12_, bf16[256,4096]{1,0:T(8,128)(2,1)} %side.18.refs_5_.refs_1_.refs_13_, bf16[144,4096]{1,0:T(8,128)(2,1)} %collective-permute-done.1.refs_2_.refs_14_, bf16[144,4096]{1,0:T(8,128)(2,1)} %collective-permute-done.refs_1_.refs_3_.refs_15_, ...), custom_call_target="tpu_custom_call" | custom-call | flops 6442450944 | bytes 16777216 | tf_op jit(solution)/shard_map/qkv/pallas_call | solution.py:60
  86.3 22.9 %attend.1 = (bf16[1024,1024]{1,0:T(8,128)(2,1)}, f32[8,2,1024]{2,1,0:T(2,128)}) custom-call(s32[4]{0:T(128)} %bitcast.50, bf16[1024,3072]{1,0:T(8,128)(2,1)} %get-tuple-element.117.refs_1_.refs_2_.refs_3_.refs_4_, bf16[1024,3072]{1,0:T(8,128)(2,1)} %get-tuple-element.117.refs_1_.refs_2_.refs_3_.refs_4_, ...), custom_call_target="tpu_custom_call" | custom-call | flops 8589934592 | bytes 8388608 | tf_op jit(solution)/shard_map/attend/pallas_call | solution.py:60
  109.9 10.4 %after.1 = (f32[1024,1024]{1,0:T(8,128)}, bf16[1024,1024]{1,0:T(8,128)(2,1)}, bf16[1024,1024]{1,0:T(8,128)(2,1)}, bf16[1024,1024]{1,0:T(8,128)(2,1)}) custom-call(s32[9]{0:T(128)} %stack.59.refs_0_.refs_12_, bf16[256,4096]{1,0:T(8,128)(2,1)} %side.18.refs_5_.refs_1_.refs_13_, bf16[144,4096]{1,0:T(8,128)(2,1)} %collective-permute-done.1.refs_2_.refs_14_, ...), custom_call_target="tpu_custom_call" | custom-call | flops 2147483648 | bytes 14680064 | tf_op jit(solution)/shard_map/after/pallas_call | solution.py:60
  120.4 29.1 %feed.2 = (bf16[1024,4096]{1,0:T(8,128)(2,1)}, bf16[1024,4096]{1,0:T(8,128)(2,1)}, bf16[2,512,2048]{2,1,0:T(8,128)(2,1)}, bf16[2,512,2048]{2,1,0:T(8,128)(2,1)}, f32[1,2048]{1,0:T(1,128)}) custom-call(s32[8]{0:T(128)} %pad_add_fusion.refs_0_.refs_3_.refs_6_.refs_9_, bf16[512,4096]{1,0:T(8,128)(2,1)} %all-gather.3.cloned.1.call-done.refs_18_.refs_1_.refs_4_, ...), custom_call_target="tpu_custom_call" | custom-call | flops 17179869184 | bytes 50331648 | tf_op jit(solution)/shard_map/feed/pallas_call | solution.py:60
  150.1 8.9 %all-gather.5.cloned.1.call-done.refs_1_.refs_4_.refs_7_.refs_10_ = bf16[512,4096]{1,0:T(8,128)(2,1)} async-done(((bf16[128,4096]{1,0:T(8,128)(2,1)}), bf16[512,4096]{1,0:T(8,128)(2,1)}) %all-gather.5.cloned.1.call-update) | async-done | bytes 4194320 | tf_op jit(solution)/shard_map/all_gather | solution.py:1088
  159.1 6.4 %side.21 = (bf16[2,2,128,2048]{3,2,1,0:T(8,128)(2,1)}, bf16[2,128,2048]{2,1,0:T(8,128)(2,1)}, bf16[2,128,2048]{2,1,0:T(8,128)(2,1)}) custom-call(s32[3]{0:T(128)} %pad_add_fusion.1.refs_0_, bf16[2,4,128,2048]{3,2,1,0:T(8,128)(2,1)} %bitcast.33, bf16[2,4,128,2048]{3,2,1,0:T(8,128)(2,1)} %bitcast.16.refs_2_, bf16[2,512,2048]{2,1,0:T(8,128)(2,1)} %get-tuple-element.127.refs_3_), custom_call_target="tpu_custom_call" | custom-call | bytes 16777216 | tf_op jit(solution)/shard_map/side/pallas_call | solution.py:60
  167.5 29.6 %feed.3 = (bf16[1024,4096]{1,0:T(8,128)(2,1)}, bf16[1024,4096]{1,0:T(8,128)(2,1)}, bf16[2,512,2048]{2,1,0:T(8,128)(2,1)}, bf16[2,512,2048]{2,1,0:T(8,128)(2,1)}, f32[1,2048]{1,0:T(1,128)}) custom-call(s32[8]{0:T(128)} %pad_add_fusion.refs_0_.refs_3_.refs_6_.refs_9_, ...), custom_call_target="tpu_custom_call", output_to_operand_aliasing={{0}: (12, {}), {1}: (13, {})} | custom-call | flops 17179869184 | bytes 50331648 | tf_op jit(solution)/shard_map/feed/pallas_call | solution.py:60
  204.1 24.5 %middle.1 = (f32[1024,1024]{1,0:T(8,128)}, bf16[1024,1024]{1,0:T(8,128)(2,1)}, bf16[2,512,512]{2,1,0:T(8,128)(2,1)}, bf16[2,512,512]{2,1,0:T(8,128)(2,1)}, f32[1...) custom-call(s32[8]{0:T(128)} %pad_add_fusion.refs_0_.refs_3_.refs_6_.refs_9_, ...), custom_call_target="tpu_custom_call" | custom-call | flops 51539607552 | bytes 125829120 | tf_op jit(solution)/shard_map/middle/pallas_call | solution.py:60
  228.7 7.2 %side.23 = (bf16[2,1,128,2048]{3,2,1,0:T(8,128)(2,1)}, bf16[2,2,128,2048]{3,2,1,0:T(8,128)(2,1)}, bf16[2,128,2048]{2,1,0:T(8,128)(2,1)}, bf16[2,128,2048]{2,1,0:T(8,128)(2,1)}) custom-call(s32[3]{0:T(128)} %pad_add_fusion.1.refs_0_, bf16[2,1,128,2048]{3,2,1,0:T(8,128)(2,1)} %get-tuple-element.136.refs_27_.refs_1_, ...), custom_call_target="tpu_custom_call" | custom-call | bytes 20971520 | tf_op jit(solution)/shard_map/side/pallas_call | solution.py:60
  242.4 18.8 %attend_back.2 = (bf16[1024,512]{1,0:T(8,128)(2,1)}, bf16[1024,512]{1,0:T(8,128)(2,1)}, bf16[1024,512]{1,0:T(8,128)(2,1)}, f32[1,512]{1,0:T(1,128)}, f32[1,512]{1,0:T(1,128)}) custom-call(s32[4]{0:T(128)} %bitcast.51, bf16[1024,3072]{1,0:T(8,128)(2,1)} %get-tuple-element.117.refs_1_.refs_2_.refs_3_.refs_4_, ...), custom_call_target="tpu_custom_call" | custom-call | flops 42949672960 | bytes 524288 | tf_op jit(solution)/shard_map/attend_back/pallas_call | solution.py:60
  275.2 7.1 %project.2 = (bf16[2,512,768]{2,1,0:T(8,128)(2,1)}, bf16[2,512,768]{2,1,0:T(8,128)(2,1)}) custom-call(bf16[1024,1024]{1,0:T(8,128)(2,1)} %get-tuple-element.155.refs_0_, bf16[1024,512]{1,0:T(8,128)(2,1)} %get-tuple-element.150.refs_8_.refs_1_.refs_10_, bf16[1024,512]{1,0:T(8,128)(2,1)} %get-tuple-element.156.refs_2_.refs_11_, ...), custom_call_target="tpu_custom_call" | custom-call | flops 3221225472 | bytes 7340032 | tf_op jit(solution)/shard_map/project/pallas_call | solution.py:60
  284.2 19.0 %attend_back.3 = (bf16[1024,512]{1,0:T(8,128)(2,1)}, bf16[1024,512]{1,0:T(8,128)(2,1)}, bf16[1024,512]{1,0:T(8,128)(2,1)}, f32[1,512]{1,0:T(1,128)}, f32[1,512]{1,0:T(1,128)}) custom-call(s32[4]{0:T(128)} %bitcast.52, bf16[1024,3072]{1,0:T(8,128)(2,1)} %get-tuple-element.117.refs_1_.refs_2_.refs_3_.refs_4_, ...), custom_call_target="tpu_custom_call" | custom-call | flops 42949672960 | bytes 524288 | tf_op jit(solution)/shard_map/attend_back/pallas_call | solution.py:60
  310.6 7.1 %project.3 = (bf16[2,512,768]{2,1,0:T(8,128)(2,1)}, bf16[2,512,768]{2,1,0:T(8,128)(2,1)}) custom-call(bf16[1024,1024]{1,0:T(8,128)(2,1)} %get-tuple-element.155.refs_0_, bf16[1024,512]{1,0:T(8,128)(2,1)} %get-tuple-element.160.refs_8_.refs_1_.refs_13_, bf16[1024,512]{1,0:T(8,128)(2,1)} %get-tuple-element.164.refs_2_.refs_14_, ...), custom_call_target="tpu_custom_call" | custom-call | flops 3221225472 | bytes 7340032 | tf_op jit(solution)/shard_map/project/pallas_call | solution.py:60
  318.3 15.7 %grad_input.1 = (f32[1024,1024]{1,0:T(8,128)}, f32[1,1024]{1,0:T(1,128)}, f32[1,1024]{1,0:T(1,128)}) custom-call(s32[9]{0:T(128)} %stack.59.refs_0_.refs_12_, bf16[256,4096]{1,0:T(8,128)(2,1)} %side.18.refs_5_.refs_1_.refs_13_, bf16[144,4096]{1,0:T(8,128)(2,1)} %collective-permute-done.1.refs_2_.refs_14_, ...), custom_call_target="tpu_custom_call" | custom-call | flops 25769803776 | bytes 92274688 | tf_op jit(solution)/shard_map/grad_input/pallas_call | solution.py:60
  334.0 6.7 %collective-permute-done.25.refs_4_ = bf16[2,2,128,768]{3,2,1,0:T(8,128)(2,1)} collective-permute-done((bf16[2,2,128,768]{3,2,1,0:T(8,128)(2,1)}, bf16[2,2,128,768]{3,2,1,0:T(8,128)(2,1)}, u32[]{:S(2)}, u32[]{:S(2)}) %collective-permute-start.25) | collective-permute-done | bytes 786464 | tf_op jit(solution)/shard_map/ppermute | solution.py:1077
  349.3 12.7 %adam.4 = (f32[256,8192]{1,0:T(8,128)}, f32[256,8192]{1,0:T(8,128)}, f32[256,8192]{1,0:T(8,128)}) custom-call(s32[3]{0:T(128)} %pad_add_fusion.1.refs_0_, s32[2]{0:T(128)} %iota_multiply_fusion.2.refs_1_, f32[256,8192]{1,0:T(8,128)} %refs_2_.9, f32[256,8192]{1,0:T(8,128)} %refs_3_.7, f32[256,8192]{1,0:T(8,128)} %refs_4_.7, ...), custom_call_target="tpu_custom_call" | custom-call | flops 2097152 | bytes 2097152 | tf_op jit(solution)/shard_map/adam/pallas_call | solution.py:60
  376.6 15.6 %output.1.refs_7_ = bf16[1024,1024]{1,0:T(8,128)(2,1)} custom-call(s32[8]{0:T(128)} %pad_add_fusion.refs_0_.refs_3_.refs_6_.refs_9_, bf16[512,4096]{1,0:T(8,128)(2,1)} %all-gather.3.cloned.1.call-done.refs_18_.refs_1_.refs_4_, bf16[512,4096]{1,0:T(8,128)(2,1)} %collective-permute-done.8.refs_2_.refs_5_, s32[8]{0:T(128)} %pad_add_fusion.refs_0_.refs_3_.refs_6_.refs_9_, ...), custom_call_target="tpu_custom_call" | custom-call | flops 858993472 | bytes 2097152 | tf_op jit(solution)/shard_map/output/pallas_call | solution.py:60
  403.9 12.4 %adam.5 = (f32[256,8192]{1,0:T(8,128)}, f32[256,8192]{1,0:T(8,128)}, f32[256,8192]{1,0:T(8,128)}) custom-call(s32[3]{0:T(128)} %pad_add_fusion.1.refs_0_, s32[2]{0:T(128)} %constant.88.clone.refs_1_, f32[256,8192]{1,0:T(8,128)} %refs_2_.9, f32[256,8192]{1,0:T(8,128)} %refs_3_.7, ...), custom_call_target="tpu_custom_call", output_to_operand_aliasing={{0}: (8, {}), {1}: (9, {}), {2}: (10, {})} | custom-call | flops 2097152 | bytes 2097152 | tf_op jit(solution)/shard_map/adam/pallas_call | solution.py:60
  428.9 7.0 %adam.6 = (f32[256,4096]{1,0:T(8,128)}, f32[256,4096]{1,0:T(8,128)}, f32[256,4096]{1,0:T(8,128)}) custom-call(s32[3]{0:T(128)} %pad_add_fusion.1.refs_0_, s32[3]{0:T(128)} %iota_multiply_fusion.1.refs_1_, f32[256,4096]{1,0:T(8,128)} %refs_2_.11, f32[256,4096]{1,0:T(8,128)} %refs_3_.9, f32[256,4096]{1,0:T(8,128)} %refs_4_.9, ...), custom_call_target="tpu_custom_call" | custom-call | flops 786432 | bytes 786432 | tf_op jit(solution)/shard_map/adam/pallas_call | solution.py:60
  439.4 11.3 %collective-permute-done.38.refs_2_ = bf16[2,128,768]{2,1,0:T(8,128)(2,1)} collective-permute-done((bf16[2,128,768]{2,1,0:T(8,128)(2,1)}, bf16[2,128,768]{2,1,0:T(8,128)(2,1)}, u32[]{:S(2)}, u32[]{:S(2)}) %collective-permute-start.38) | collective-permute-done | bytes 393248 | tf_op jit(solution)/shard_map/ppermute | solution.py:1069
  453.4 16.4 %all-reduce.5.cloned.1.call-done.refs_7_ = bf16[2,128,512]{2,1,0:T(8,128)(2,1)} async-done(((bf16[2,128,512]{2,1,0:T(8,128)(2,1)}), bf16[2,128,512]{2,1,0:T(8,128)(2,1)}) %all-reduce.5.cloned.1.call-update) | async-done | bytes 262160 | tf_op jit(solution)/shard_map/psum | solution.py:1103
  472.0 10.2 %adam.7 = (f32[256,4096]{1,0:T(8,128)}, f32[256,4096]{1,0:T(8,128)}, f32[256,4096]{1,0:T(8,128)}) custom-call(s32[3]{0:T(128)} %pad_add_fusion.1.refs_0_, s32[5]{0:T(128)} %constant.89.clone.refs_1_, f32[256,4096]{1,0:T(8,128)} %refs_2_.11, f32[256,4096]{1,0:T(8,128)} %refs_3_.9, ...), custom_call_target="tpu_custom_call", output_to_operand_aliasing={{0}: (10, {}), {1}: (11, {}), {2}: (12, {})} | custom-call | flops 1310720 | bytes 1310720 | tf_op jit(solution)/shard_map/adam/pallas_call | solution.py:60
  (122 shorter events, 136.6 us)
Async XLA Ops:
  7.2 102.1 %all-gather.3.cloned.1.call-start = ((), (), s32[]{:S(2)}) async-start(), calls=%async_computation.1 | async-start | bytes 5242880 | tf_op jit(solution)/shard_map/all_gather | solution.py:1088
  11.3 29.2 %collective-permute-start = (bf16[144,4096]{1,0:T(8,128)(2,1)}, bf16[144,4096]{1,0:T(8,128)(2,1)}, u32[]{:S(2)}, u32[]{:S(2)}) collective-permute-start(bf16[144,4096]{1,0:T(8,128)(2,1)} %side.16.refs_3_), channel_id=1, source_target_pairs={{0,2},{1,3},{2,0},{3,1},{4,6},{5,7},{6,4},{7,5},{8,10},{9,11},{10,... | collective-permute-start | bytes 3538952 | tf_op jit(solution)/shard_map/ppermute | solution.py:1077
  14.3 27.7 %collective-permute-start.1 = (bf16[144,4096]{1,0:T(8,128)(2,1)}, bf16[144,4096]{1,0:T(8,128)(2,1)}, u32[]{:S(2)}, u32[]{:S(2)}) collective-permute-start(bf16[144,4096]{1,0:T(8,128)(2,1)} %side.16.refs_3_), channel_id=1, source_target_pairs={{0,1},{1,0},{2,3},{3,2},{4,5},{5,4},{6,7},{7,6},{8,9},{9,8},{10,11... | collective-permute-start | bytes 3538952 | tf_op jit(solution)/shard_map/ppermute | solution.py:1077
  46.3 112.7 %all-gather.5.cloned.1.call-start = ((), (), s32[]{:S(2)}) async-start(), calls=%async_computation.2 | async-start | bytes 5242880 | tf_op jit(solution)/shard_map/all_gather | solution.py:1088
  46.4 22.1 %collective-permute-start.5 = (bf16[80,4096]{1,0:T(8,128)(2,1)}, bf16[80,4096]{1,0:T(8,128)(2,1)}, u32[]{:S(2)}, u32[]{:S(2)}) collective-permute-start(bf16[80,4096]{1,0:T(8,128)(2,1)} %get-tuple-element.116), channel_id=1, source_target_pairs={{0,2},{1,3},{2,0},{3,1},{4,6},{5,7},{6,4},{7,5},{8,10},{9,11},{10,... | collective-permute-start | bytes 1966088 | tf_op jit(solution)/shard_map/ppermute | solution.py:1077
  46.7 25.3 %collective-permute-start.2 = (bf16[144,4096]{1,0:T(8,128)(2,1)}, bf16[144,4096]{1,0:T(8,128)(2,1)}, u32[]{:S(2)}, u32[]{:S(2)}) collective-permute-start(bf16[144,4096]{1,0:T(8,128)(2,1)} %collective-permute-done.1.refs_2_.refs_14_), channel_id=1, source_target_pairs={{0,4},{4,0},{8,12},{12,8},{16,20},{20,16},{24,28},{28,24},{1,5},{5... | collective-permute-start | bytes 3538952 | tf_op jit(solution)/shard_map/ppermute | solution.py:1069
  46.7 25.3 %collective-permute-start.3 = (bf16[144,4096]{1,0:T(8,128)(2,1)}, bf16[144,4096]{1,0:T(8,128)(2,1)}, u32[]{:S(2)}, u32[]{:S(2)}) collective-permute-start(bf16[144,4096]{1,0:T(8,128)(2,1)} %collective-permute-done.refs_1_.refs_3_.refs_15_), channel_id=1, source_target_pairs={{0,4},{4,0},{8,12},{12,8},{16,20},{20,16},{24,28},{28,24},{1,5},{5... | collective-permute-start | bytes 3538952 | tf_op jit(solution)/shard_map/ppermute | solution.py:1069
  69.0 265.0 %reduce-scatter.2.cloned.1.call-start = ((), (), s32[]{:S(2)}) async-start(), calls=%async_computation.3 | async-start | bytes 1310720 | tf_op jit(solution)/shard_map/reduce_scatter | solution.py:1214
  165.5 31.7 %collective-permute-start.11 = (bf16[2,128,2048]{2,1,0:T(8,128)(2,1)}, bf16[2,128,2048]{2,1,0:T(8,128)(2,1)}, u32[]{:S(2)}, u32[]{:S(2)}) collective-permute-start(bf16[2,128,2048]{2,1,0:T(8,128)(2,1)} %get-tuple-element.133), channel_id=1, source_target_pairs={{0,1},{1,0},{2,3},{3,2},{4,5},{5,4},{6,7},{7,6},{8,9},{9,8},{10,11... | collective-permute-start | bytes 3145736 | tf_op jit(solution)/shard_map/ppermute | solution.py:1077
  167.0 30.2 %collective-permute-start.12 = (bf16[2,128,2048]{2,1,0:T(8,128)(2,1)}, bf16[2,128,2048]{2,1,0:T(8,128)(2,1)}, u32[]{:S(2)}, u32[]{:S(2)}) collective-permute-start(bf16[2,128,2048]{2,1,0:T(8,128)(2,1)} %get-tuple-element.134), channel_id=1, source_target_pairs={{0,2},{1,3},{2,0},{3,1},{4,6},{5,7},{6,4},{7,5},{8,10},{9,11},{10,... | collective-permute-start | bytes 3145736 | tf_op jit(solution)/shard_map/ppermute | solution.py:1077
  197.1 31.6 %collective-permute-start.15 = (bf16[2,512,2048]{2,1,0:T(8,128)(2,1)}, bf16[2,512,2048]{2,1,0:T(8,128)(2,1)}, u32[]{:S(2)}, u32[]{:S(2)}) collective-permute-start(bf16[2,512,2048]{2,1,0:T(8,128)(2,1)} %get-tuple-element.139), channel_id=1, source_target_pairs={{0,4},{4,0},{8,12},{12,8},{16,20},{20,16},{24,28},{28,24},{1,5},{5... | collective-permute-start | bytes 12582920 | tf_op jit(solution)/shard_map/ppermute | solution.py:1069
  202.1 26.6 %collective-permute-start.13 = (bf16[1,128,2048]{2,1,0:T(8,128)(2,1)}, bf16[1,128,2048]{2,1,0:T(8,128)(2,1)}, u32[]{:S(2)}, u32[]{:S(2)}) collective-permute-start(bf16[1,128,2048]{2,1,0:T(8,128)(2,1)} %get-tuple-element.137), channel_id=1, source_target_pairs={{0,2},{1,3},{2,0},{3,1},{4,6},{5,7},{6,4},{7,5},{8,10},{9,11},{10,... | collective-permute-start | bytes 1572872 | tf_op jit(solution)/shard_map/ppermute | solution.py:1077
  203.6 25.2 %collective-permute-start.14 = (bf16[1,128,2048]{2,1,0:T(8,128)(2,1)}, bf16[1,128,2048]{2,1,0:T(8,128)(2,1)}, u32[]{:S(2)}, u32[]{:S(2)}) collective-permute-start(bf16[1,128,2048]{2,1,0:T(8,128)(2,1)} %get-tuple-element.138), channel_id=1, source_target_pairs={{0,1},{1,0},{2,3},{3,2},{4,5},{5,4},{6,7},{7,6},{8,9},{9,8},{10,11... | collective-permute-start | bytes 1572872 | tf_op jit(solution)/shard_map/ppermute | solution.py:1077
  228.6 32.6 %collective-permute-start.19 = (bf16[2,512,512]{2,1,0:T(8,128)(2,1)}, bf16[2,512,512]{2,1,0:T(8,128)(2,1)}, u32[]{:S(2)}, u32[]{:S(2)}) collective-permute-start(bf16[2,512,512]{2,1,0:T(8,128)(2,1)} %get-tuple-element.148), channel_id=1, source_target_pairs={{0,4},{4,0},{8,12},{12,8},{16,20},{20,16},{24,28},{28,24},{1,5},{5... | collective-permute-start | bytes 3145736 | tf_op jit(solution)/shard_map/ppermute | solution.py:1069
  236.0 26.7 %collective-permute-start.16 = (bf16[2,128,2048]{2,1,0:T(8,128)(2,1)}, bf16[2,128,2048]{2,1,0:T(8,128)(2,1)}, u32[]{:S(2)}, u32[]{:S(2)}) collective-permute-start(bf16[2,128,2048]{2,1,0:T(8,128)(2,1)} %bitcast.39), channel_id=1, source_target_pairs={{0,8},{4,12},{24,16},{28,20},{1,9},{5,13},{25,17},{29,21},{2,10},{... | collective-permute-start | bytes 3145736 | tf_op jit(solution)/shard_map/ppermute | solution.py:1074
  240.3 25.6 %collective-permute-start.17 = (bf16[2,128,2048]{2,1,0:T(8,128)(2,1)}, bf16[2,128,2048]{2,1,0:T(8,128)(2,1)}, u32[]{:S(2)}, u32[]{:S(2)}) collective-permute-start(bf16[2,128,2048]{2,1,0:T(8,128)(2,1)} %get-tuple-element.145), channel_id=1, source_target_pairs={{0,1},{1,0},{2,3},{3,2},{4,5},{5,4},{6,7},{7,6},{8,9},{9,8},{10,11... | collective-permute-start | bytes 3145736 | tf_op jit(solution)/shard_map/ppermute | solution.py:1077
  241.8 25.3 %collective-permute-start.18 = (bf16[2,128,2048]{2,1,0:T(8,128)(2,1)}, bf16[2,128,2048]{2,1,0:T(8,128)(2,1)}, u32[]{:S(2)}, u32[]{:S(2)}) collective-permute-start(bf16[2,128,2048]{2,1,0:T(8,128)(2,1)} %get-tuple-element.146), channel_id=1, source_target_pairs={{0,2},{1,3},{2,0},{3,1},{4,6},{5,7},{6,4},{7,5},{8,10},{9,11},{10,... | collective-permute-start | bytes 3145736 | tf_op jit(solution)/shard_map/ppermute | solution.py:1077
  273.5 29.8 %collective-permute-start.20 = (bf16[2,128,2048]{2,1,0:T(8,128)(2,1)}, bf16[2,128,2048]{2,1,0:T(8,128)(2,1)}, u32[]{:S(2)}, u32[]{:S(2)}) collective-permute-start(bf16[2,128,2048]{2,1,0:T(8,128)(2,1)} %get-tuple-element.151.refs_4_.refs_1_), channel_id=1, source_target_pairs={{8,16},{12,20},{16,8},{20,12},{9,17},{13,21},{17,9},{21,13},{10,18... | collective-permute-start | bytes 3145736 | tf_op jit(solution)/shard_map/ppermute | solution.py:1074
  303.3 97.7 %all-reduce.3.cloned.1.call-start = ((), (), s32[]{:S(2)}) async-start(), calls=%async_computation.4 | async-start | bytes 2097152 | tf_op jit(solution)/shard_map/psum | solution.py:1103
  309.4 31.4 %collective-permute-start.24 = (bf16[2,128,2048]{2,1,0:T(8,128)(2,1)}, bf16[2,128,2048]{2,1,0:T(8,128)(2,1)}, u32[]{:S(2)}, u32[]{:S(2)}) collective-permute-start(bf16[2,128,2048]{2,1,0:T(8,128)(2,1)} %get-tuple-element.161.refs_4_.refs_1_), channel_id=1, source_target_pairs={{8,0},{12,4},{16,24},{20,28},{9,1},{13,5},{17,25},{21,29},{10,2},{... | collective-permute-start | bytes 3145736 | tf_op jit(solution)/shard_map/ppermute | solution.py:1074
  317.7 23.1 %collective-permute-start.26 = (bf16[2,512,768]{2,1,0:T(8,128)(2,1)}, bf16[2,512,768]{2,1,0:T(8,128)(2,1)}, u32[]{:S(2)}, u32[]{:S(2)}) collective-permute-start(bf16[2,512,768]{2,1,0:T(8,128)(2,1)} %get-tuple-element.167), channel_id=1, source_target_pairs={{0,4},{4,0},{8,12},{12,8},{16,20},{20,16},{24,28},{28,24},{1,5},{5... | collective-permute-start | bytes 4718600 | tf_op jit(solution)/shard_map/ppermute | solution.py:1069
  317.7 23.1 %collective-permute-start.25 = (bf16[2,2,128,768]{3,2,1,0:T(8,128)(2,1)}, bf16[2,2,128,768]{3,2,1,0:T(8,128)(2,1)}, u32[]{:S(2)}, u32[]{:S(2)}) collective-permute-start(bf16[2,2,128,768]{3,2,1,0:T(8,128)(2,1)} %get-tuple-element.163), channel_id=1, source_target_pairs={{0,1},{1,0},{2,3},{3,2},{4,5},{5,4},{6,7},{7,6},{8,9},{9,8},{10,11... | collective-permute-start | bytes 2359304 | tf_op jit(solution)/shard_map/ppermute | solution.py:1077
  346.7 123.2 %all-reduce.5.cloned.1.call-start = ((), (), s32[]{:S(2)}) async-start(), calls=%async_computation.5 | async-start | bytes 524288 | tf_op jit(solution)/shard_map/psum | solution.py:1103
  425.3 25.4 %collective-permute-start.38 = (bf16[2,128,768]{2,1,0:T(8,128)(2,1)}, bf16[2,128,768]{2,1,0:T(8,128)(2,1)}, u32[]{:S(2)}, u32[]{:S(2)}) collective-permute-start(bf16[2,128,768]{2,1,0:T(8,128)(2,1)} %get-tuple-element.200.refs_1_), channel_id=1, source_target_pairs={{0,16},{4,20},{8,24},{12,28},{16,0},{20,4},{24,8},{28,12},{1,17},{... | collective-permute-start | bytes 1179656 | tf_op jit(solution)/shard_map/ppermute | solution.py:1069
  (25 other events, 345.0 us)
Sparse Core Ops, SparseCore 0:
  46.5 57.9 all-gather.2
  106.3 52.6 all-gather.4
  303.4 29.6 reduce-scatter.1
  346.8 54.1 all-reduce.2
  427.5 42.3 all-reduce.4

commit v7 on v5

--- a/solution.py
+++ b/solution.py
@@ -1435,8 +1435,6 @@
     unit_e = Wide(links, joined)
     unit_c = unit(EXCHANGE, *project(0), ((1, 2),))
     attend_back(pairs // 2)
-    if links.fast:
-        side.order += (unit_e.own,)
     reduce([unit_a, unit_b, unit_c], steps=4)
     if links.fast:
         unit_b.own, unit_e.own = links.over_dp((unit_b.own, unit_e.own.reshape(unit_e.shape)))
@@ -1515,7 +1513,6 @@
             return total, move(total) if move else None
 
         mlp_new = adam_mlp(0, unit_a, None)
-        side.order += (unit_b.own,)
         grad_small, moved = step([unit_c, unit_d], shard_move(2))
         output = output_now()
         grad_small, moved = step([unit_c, unit_d], links.swap)

time: 501 us -> 486 us (0.970)
  waiting for transfers between devices: 107 us -> 92.2 us
    ppermute x3, waiting for transfers between devices: 18.3 us -> 1.57 us  [along_dp(): return lax.ppermute(value, 'dp', pairs)]
    reduce_scatter x1, waiting for transfers between devices: 10.7 us -> 0.02 us  [__init__(): self.own = lax.psum_scatter(flat, 'shard', scatter_dimension=0, tiled=True)]
    ppermute x18, waiting for transfers between devices: 37.5 us -> 47.1 us  [across_shard(): lax.ppermute(value, 'shard', [(s, s ^ bit) for s in range(self.shards)])]
  transfers between devices with their start and end apart: 48 -> 48, of which waited for: 16 -> 15; matrix products, arithmetic and copies ran while one was open for 1% -> 1% of each run, Pallas kernels for 60% -> 64%
where the time goes in v7:
time: 486 us; the launch traced here: 482 us
  Pallas kernels  330 us (68%)
  waiting for transfers between devices  92.2 us (19%)
  starting transfers between devices  38 us (8%)
  between operations  14.4 us (3%)
  other arithmetic  5.61 us (1%)
    pallas_call x33, Pallas kernels, call(): pl.pallas_call(run, grid_spec=pltpu.PrefetchScalarGridSpec(num_scalar_pre...  330 us
    ppermute x18, waiting for transfers between devices, across_shard(): lax.ppermute(value, 'shard', [(s, s ^ bit) for s in range(self.shards)])  47.1 us
    ppermute x23, waiting for transfers between devices, across_dp(): lax.ppermute(value, 'dp', [(d, d ^ bit) for d in range(self.replicas)])  19.9 us
    ppermute x18, starting transfers between devices, across_shard(): lax.ppermute(value, 'shard', [(s, s ^ bit) for s in range(self.shards)])  19.8 us
    psum x1, waiting for transfers between devices, over_dp(): return lax.psum(values, 'dp', axis_index_groups=groups)  14.6 us
    ppermute x23, starting transfers between devices, across_dp(): lax.ppermute(value, 'dp', [(d, d ^ bit) for d in range(self.replicas)])  10.9 us
  transfers between devices with their start and end apart: 48, of which 15 were waited for; matrix products, arithmetic and copies ran while one was open for 1% of the time, Pallas kernels for 64%

profile of v7, /device:TPU:0, one launch (start us, length us, event | category | flops | bytes accessed | tf_op | source)
XLA Modules:
  0.0 481.6 jit_solution(14349806022150393777)
XLA Ops:
  31.3 9.2 %collective-permute-done.refs_1_.refs_3_.refs_15_ = bf16[144,4096]{1,0:T(8,128)(2,1)} collective-permute-done((bf16[144,4096]{1,0:T(8,128)(2,1)}, bf16[144,4096]{1,0:T(8,128)(2,1)}, u32[]{:S(2)}, u32[]{:S(2)}) %collective-permute-start) | collective-permute-done | bytes 1179680 | tf_op jit(solution)/shard_map/ppermute | solution.py:1077
  49.0 19.5 %collective-permute-done.5.refs_4_.refs_7_.refs_19_ = bf16[80,4096]{1,0:T(8,128)(2,1)} collective-permute-done((bf16[80,4096]{1,0:T(8,128)(2,1)}, bf16[80,4096]{1,0:T(8,128)(2,1)}, u32[]{:S(2)}, u32[]{:S(2)}) %collective-permute-start.5) | collective-permute-done | bytes 655392 | tf_op jit(solution)/shard_map/ppermute | solution.py:1077
  72.1 14.2 %qkv.1 = (bf16[1024,3072]{1,0:T(8,128)(2,1)}, bf16[1024,1024]{1,0:T(8,128)(2,1)}) custom-call(s32[9]{0:T(128)} %stack.59.refs_0_.refs_12_, bf16[256,4096]{1,0:T(8,128)(2,1)} %side.18.refs_5_.refs_1_.refs_13_, bf16[144,4096]{1,0:T(8,128)(2,1)} %collective-permute-done.1.refs_2_.refs_14_, bf16[144,4096]{1,0:T(8,128)(2,1)} %collective-permute-done.refs_1_.refs_3_.refs_15_, ...), custom_call_target="tpu_custom_call" | custom-call | flops 6442450944 | bytes 16777216 | tf_op jit(solution)/shard_map/qkv/pallas_call | solution.py:60
  86.4 22.9 %attend.1 = (bf16[1024,1024]{1,0:T(8,128)(2,1)}, f32[8,2,1024]{2,1,0:T(2,128)}) custom-call(s32[4]{0:T(128)} %bitcast.50, bf16[1024,3072]{1,0:T(8,128)(2,1)} %get-tuple-element.116.refs_1_.refs_2_.refs_3_.refs_4_, bf16[1024,3072]{1,0:T(8,128)(2,1)} %get-tuple-element.116.refs_1_.refs_2_.refs_3_.refs_4_, ...), custom_call_target="tpu_custom_call" | custom-call | flops 8589934592 | bytes 8388608 | tf_op jit(solution)/shard_map/attend/pallas_call | solution.py:60
  109.9 10.4 %after.1 = (f32[1024,1024]{1,0:T(8,128)}, bf16[1024,1024]{1,0:T(8,128)(2,1)}, bf16[1024,1024]{1,0:T(8,128)(2,1)}, bf16[1024,1024]{1,0:T(8,128)(2,1)}) custom-call(s32[9]{0:T(128)} %stack.59.refs_0_.refs_12_, bf16[256,4096]{1,0:T(8,128)(2,1)} %side.18.refs_5_.refs_1_.refs_13_, bf16[144,4096]{1,0:T(8,128)(2,1)} %collective-permute-done.1.refs_2_.refs_14_, ...), custom_call_target="tpu_custom_call" | custom-call | flops 2147483648 | bytes 14680064 | tf_op jit(solution)/shard_map/after/pallas_call | solution.py:60
  120.3 29.1 %feed.2 = (bf16[1024,4096]{1,0:T(8,128)(2,1)}, bf16[1024,4096]{1,0:T(8,128)(2,1)}, bf16[2,512,2048]{2,1,0:T(8,128)(2,1)}, bf16[2,512,2048]{2,1,0:T(8,128)(2,1)}, f32[1,2048]{1,0:T(1,128)}) custom-call(s32[8]{0:T(128)} %pad_add_fusion.refs_0_.refs_3_.refs_6_.refs_9_, bf16[512,4096]{1,0:T(8,128)(2,1)} %all-gather.3.cloned.1.call-done.refs_18_.refs_1_.refs_4_, ...), custom_call_target="tpu_custom_call" | custom-call | flops 17179869184 | bytes 50331648 | tf_op jit(solution)/shard_map/feed/pallas_call | solution.py:60
  150.1 9.0 %all-gather.5.cloned.1.call-done.refs_1_.refs_4_.refs_7_.refs_10_ = bf16[512,4096]{1,0:T(8,128)(2,1)} async-done(((bf16[128,4096]{1,0:T(8,128)(2,1)}), bf16[512,4096]{1,0:T(8,128)(2,1)}) %all-gather.5.cloned.1.call-update) | async-done | bytes 4194320 | tf_op jit(solution)/shard_map/all_gather | solution.py:1088
  159.1 6.5 %side.21 = (bf16[2,2,128,2048]{3,2,1,0:T(8,128)(2,1)}, bf16[2,128,2048]{2,1,0:T(8,128)(2,1)}, bf16[2,128,2048]{2,1,0:T(8,128)(2,1)}) custom-call(s32[3]{0:T(128)} %pad_add_fusion.1.refs_0_, bf16[2,4,128,2048]{3,2,1,0:T(8,128)(2,1)} %bitcast.33, bf16[2,4,128,2048]{3,2,1,0:T(8,128)(2,1)} %bitcast.16.refs_2_, bf16[2,512,2048]{2,1,0:T(8,128)(2,1)} %get-tuple-element.126.refs_3_), custom_call_target="tpu_custom_call" | custom-call | bytes 16777216 | tf_op jit(solution)/shard_map/side/pallas_call | solution.py:60
  167.6 29.6 %feed.3 = (bf16[1024,4096]{1,0:T(8,128)(2,1)}, bf16[1024,4096]{1,0:T(8,128)(2,1)}, bf16[2,512,2048]{2,1,0:T(8,128)(2,1)}, bf16[2,512,2048]{2,1,0:T(8,128)(2,1)}, f32[1,2048]{1,0:T(1,128)}) custom-call(s32[8]{0:T(128)} %pad_add_fusion.refs_0_.refs_3_.refs_6_.refs_9_, ...), custom_call_target="tpu_custom_call", output_to_operand_aliasing={{0}: (12, {}), {1}: (13, {})} | custom-call | flops 17179869184 | bytes 50331648 | tf_op jit(solution)/shard_map/feed/pallas_call | solution.py:60
  204.1 24.6 %middle.1 = (f32[1024,1024]{1,0:T(8,128)}, bf16[1024,1024]{1,0:T(8,128)(2,1)}, bf16[2,512,512]{2,1,0:T(8,128)(2,1)}, bf16[2,512,512]{2,1,0:T(8,128)(2,1)}, f32[1...) custom-call(s32[8]{0:T(128)} %pad_add_fusion.refs_0_.refs_3_.refs_6_.refs_9_, ...), custom_call_target="tpu_custom_call" | custom-call | flops 51539607552 | bytes 125829120 | tf_op jit(solution)/shard_map/middle/pallas_call | solution.py:60
  228.8 7.3 %side.23 = (bf16[2,1,128,2048]{3,2,1,0:T(8,128)(2,1)}, bf16[2,2,128,2048]{3,2,1,0:T(8,128)(2,1)}, bf16[2,128,2048]{2,1,0:T(8,128)(2,1)}, bf16[2,128,2048]{2,1,0:T(8,128)(2,1)}) custom-call(s32[3]{0:T(128)} %pad_add_fusion.1.refs_0_, bf16[2,1,128,2048]{3,2,1,0:T(8,128)(2,1)} %get-tuple-element.135.refs_27_.refs_1_, ...), custom_call_target="tpu_custom_call" | custom-call | bytes 20971520 | tf_op jit(solution)/shard_map/side/pallas_call | solution.py:60
  242.5 18.8 %attend_back.2 = (bf16[1024,512]{1,0:T(8,128)(2,1)}, bf16[1024,512]{1,0:T(8,128)(2,1)}, bf16[1024,512]{1,0:T(8,128)(2,1)}, f32[1,512]{1,0:T(1,128)}, f32[1,512]{1,0:T(1,128)}) custom-call(s32[4]{0:T(128)} %bitcast.51, bf16[1024,3072]{1,0:T(8,128)(2,1)} %get-tuple-element.116.refs_1_.refs_2_.refs_3_.refs_4_, ...), custom_call_target="tpu_custom_call" | custom-call | flops 42949672960 | bytes 524288 | tf_op jit(solution)/shard_map/attend_back/pallas_call | solution.py:60
  275.3 7.1 %project.2 = (bf16[2,512,768]{2,1,0:T(8,128)(2,1)}, bf16[2,512,768]{2,1,0:T(8,128)(2,1)}) custom-call(bf16[1024,1024]{1,0:T(8,128)(2,1)} %get-tuple-element.154.refs_0_, bf16[1024,512]{1,0:T(8,128)(2,1)} %get-tuple-element.149.refs_8_.refs_1_.refs_10_, bf16[1024,512]{1,0:T(8,128)(2,1)} %get-tuple-element.155.refs_2_.refs_11_, ...), custom_call_target="tpu_custom_call" | custom-call | flops 3221225472 | bytes 7340032 | tf_op jit(solution)/shard_map/project/pallas_call | solution.py:60
  284.3 19.0 %attend_back.3 = (bf16[1024,512]{1,0:T(8,128)(2,1)}, bf16[1024,512]{1,0:T(8,128)(2,1)}, bf16[1024,512]{1,0:T(8,128)(2,1)}, f32[1,512]{1,0:T(1,128)}, f32[1,512]{1,0:T(1,128)}) custom-call(s32[4]{0:T(128)} %bitcast.52, bf16[1024,3072]{1,0:T(8,128)(2,1)} %get-tuple-element.116.refs_1_.refs_2_.refs_3_.refs_4_, ...), custom_call_target="tpu_custom_call" | custom-call | flops 42949672960 | bytes 524288 | tf_op jit(solution)/shard_map/attend_back/pallas_call | solution.py:60
  310.7 7.1 %project.3 = (bf16[2,512,768]{2,1,0:T(8,128)(2,1)}, bf16[2,512,768]{2,1,0:T(8,128)(2,1)}) custom-call(bf16[1024,1024]{1,0:T(8,128)(2,1)} %get-tuple-element.154.refs_0_, bf16[1024,512]{1,0:T(8,128)(2,1)} %get-tuple-element.159.refs_8_.refs_1_.refs_13_, bf16[1024,512]{1,0:T(8,128)(2,1)} %get-tuple-element.163.refs_2_.refs_14_, ...), custom_call_target="tpu_custom_call" | custom-call | flops 3221225472 | bytes 7340032 | tf_op jit(solution)/shard_map/project/pallas_call | solution.py:60
  318.3 15.9 %grad_input.1 = (f32[1024,1024]{1,0:T(8,128)}, f32[1,1024]{1,0:T(1,128)}, f32[1,1024]{1,0:T(1,128)}) custom-call(s32[9]{0:T(128)} %stack.59.refs_0_.refs_12_, bf16[256,4096]{1,0:T(8,128)(2,1)} %side.18.refs_5_.refs_1_.refs_13_, bf16[144,4096]{1,0:T(8,128)(2,1)} %collective-permute-done.1.refs_2_.refs_14_, ...), custom_call_target="tpu_custom_call" | custom-call | flops 25769803776 | bytes 92274688 | tf_op jit(solution)/shard_map/grad_input/pallas_call | solution.py:60
  334.2 6.7 %collective-permute-done.25.refs_4_ = bf16[2,2,128,768]{3,2,1,0:T(8,128)(2,1)} collective-permute-done((bf16[2,2,128,768]{3,2,1,0:T(8,128)(2,1)}, bf16[2,2,128,768]{3,2,1,0:T(8,128)(2,1)}, u32[]{:S(2)}, u32[]{:S(2)}) %collective-permute-start.25) | collective-permute-done | bytes 786464 | tf_op jit(solution)/shard_map/ppermute | solution.py:1077
  349.3 12.4 %adam.4 = (f32[256,8192]{1,0:T(8,128)}, f32[256,8192]{1,0:T(8,128)}, f32[256,8192]{1,0:T(8,128)}) custom-call(s32[3]{0:T(128)} %pad_add_fusion.1.refs_0_, s32[2]{0:T(128)} %iota_multiply_fusion.2.refs_1_, f32[256,8192]{1,0:T(8,128)} %refs_2_.9, f32[256,8192]{1,0:T(8,128)} %refs_3_.7, f32[256,8192]{1,0:T(8,128)} %refs_4_.7, ...), custom_call_target="tpu_custom_call" | custom-call | flops 2097152 | bytes 2097152 | tf_op jit(solution)/shard_map/adam/pallas_call | solution.py:60
  376.7 15.4 %output.1.refs_7_ = bf16[1024,1024]{1,0:T(8,128)(2,1)} custom-call(s32[8]{0:T(128)} %pad_add_fusion.refs_0_.refs_3_.refs_6_.refs_9_, bf16[512,4096]{1,0:T(8,128)(2,1)} %all-gather.3.cloned.1.call-done.refs_18_.refs_1_.refs_4_, bf16[512,4096]{1,0:T(8,128)(2,1)} %collective-permute-done.8.refs_2_.refs_5_, s32[8]{0:T(128)} %pad_add_fusion.refs_0_.refs_3_.refs_6_.refs_9_, ...), custom_call_target="tpu_custom_call" | custom-call | flops 858993472 | bytes 2097152 | tf_op jit(solution)/shard_map/output/pallas_call | solution.py:60
  395.1 14.6 %all-reduce.3.cloned.1.call-done = (bf16[2,128,2048]{2,1,0:T(8,128)(2,1)}, bf16[2,128,512]{2,1,0:T(8,128)(2,1)}) async-done(((bf16[2,128,2048]{2,1,0:T(8,128)(2,1)}, bf16[2,128,512]{2,1,0:T(8,128)(2,1)}), (bf16[2,128,2048]{2,1,0:T(8,128)(2,1)}, bf16[2,128,512]{2,1,0:T(8,128)(2,1)})) %all-reduce.3.cloned.1.call-update) | async-done | bytes 1310736 | tf_op jit(solution)/shard_map/psum | solution.py:1103
  412.8 12.4 %adam.5 = (f32[256,8192]{1,0:T(8,128)}, f32[256,8192]{1,0:T(8,128)}, f32[256,8192]{1,0:T(8,128)}) custom-call(s32[3]{0:T(128)} %pad_add_fusion.1.refs_0_, s32[2]{0:T(128)} %constant.88.clone.refs_1_, f32[256,8192]{1,0:T(8,128)} %refs_2_.9, f32[256,8192]{1,0:T(8,128)} %refs_3_.7, ...), custom_call_target="tpu_custom_call", output_to_operand_aliasing={{0}: (8, {}), {1}: (9, {}), {2}: (10, {})} | custom-call | flops 2097152 | bytes 2097152 | tf_op jit(solution)/shard_map/adam/pallas_call | solution.py:60
  436.9 7.0 %adam.6 = (f32[256,4096]{1,0:T(8,128)}, f32[256,4096]{1,0:T(8,128)}, f32[256,4096]{1,0:T(8,128)}) custom-call(s32[3]{0:T(128)} %pad_add_fusion.1.refs_0_, s32[3]{0:T(128)} %iota_multiply_fusion.1.refs_1_, f32[256,4096]{1,0:T(8,128)} %refs_2_.11, f32[256,4096]{1,0:T(8,128)} %refs_3_.9, f32[256,4096]{1,0:T(8,128)} %refs_4_.9, ...), custom_call_target="tpu_custom_call" | custom-call | flops 786432 | bytes 786432 | tf_op jit(solution)/shard_map/adam/pallas_call | solution.py:60
  445.6 9.7 %collective-permute-done.38.refs_2_ = bf16[2,128,768]{2,1,0:T(8,128)(2,1)} collective-permute-done((bf16[2,128,768]{2,1,0:T(8,128)(2,1)}, bf16[2,128,768]{2,1,0:T(8,128)(2,1)}, u32[]{:S(2)}, u32[]{:S(2)}) %collective-permute-start.38) | collective-permute-done | bytes 393248 | tf_op jit(solution)/shard_map/ppermute | solution.py:1069
  460.4 10.2 %adam.7 = (f32[256,4096]{1,0:T(8,128)}, f32[256,4096]{1,0:T(8,128)}, f32[256,4096]{1,0:T(8,128)}) custom-call(s32[3]{0:T(128)} %pad_add_fusion.1.refs_0_, s32[5]{0:T(128)} %constant.89.clone.refs_1_, f32[256,4096]{1,0:T(8,128)} %refs_2_.11, f32[256,4096]{1,0:T(8,128)} %refs_3_.9, ...), custom_call_target="tpu_custom_call", output_to_operand_aliasing={{0}: (10, {}), {1}: (11, {}), {2}: (12, {})} | custom-call | flops 1310720 | bytes 1310720 | tf_op jit(solution)/shard_map/adam/pallas_call | solution.py:60
  (119 shorter events, 128.8 us)
Async XLA Ops:
  7.2 102.1 %all-gather.3.cloned.1.call-start = ((), (), s32[]{:S(2)}) async-start(), calls=%async_computation.1 | async-start | bytes 5242880 | tf_op jit(solution)/shard_map/all_gather | solution.py:1088
  11.3 29.2 %collective-permute-start = (bf16[144,4096]{1,0:T(8,128)(2,1)}, bf16[144,4096]{1,0:T(8,128)(2,1)}, u32[]{:S(2)}, u32[]{:S(2)}) collective-permute-start(bf16[144,4096]{1,0:T(8,128)(2,1)} %side.16.refs_3_), channel_id=1, source_target_pairs={{0,2},{1,3},{2,0},{3,1},{4,6},{5,7},{6,4},{7,5},{8,10},{9,11},{10,... | collective-permute-start | bytes 3538952 | tf_op jit(solution)/shard_map/ppermute | solution.py:1077
  14.3 27.7 %collective-permute-start.1 = (bf16[144,4096]{1,0:T(8,128)(2,1)}, bf16[144,4096]{1,0:T(8,128)(2,1)}, u32[]{:S(2)}, u32[]{:S(2)}) collective-permute-start(bf16[144,4096]{1,0:T(8,128)(2,1)} %side.16.refs_3_), channel_id=1, source_target_pairs={{0,1},{1,0},{2,3},{3,2},{4,5},{5,4},{6,7},{7,6},{8,9},{9,8},{10,11... | collective-permute-start | bytes 3538952 | tf_op jit(solution)/shard_map/ppermute | solution.py:1077
  46.3 112.7 %all-gather.5.cloned.1.call-start = ((), (), s32[]{:S(2)}) async-start(), calls=%async_computation.2 | async-start | bytes 5242880 | tf_op jit(solution)/shard_map/all_gather | solution.py:1088
  46.4 22.1 %collective-permute-start.5 = (bf16[80,4096]{1,0:T(8,128)(2,1)}, bf16[80,4096]{1,0:T(8,128)(2,1)}, u32[]{:S(2)}, u32[]{:S(2)}) collective-permute-start(bf16[80,4096]{1,0:T(8,128)(2,1)} %get-tuple-element.115), channel_id=1, source_target_pairs={{0,2},{1,3},{2,0},{3,1},{4,6},{5,7},{6,4},{7,5},{8,10},{9,11},{10,... | collective-permute-start | bytes 1966088 | tf_op jit(solution)/shard_map/ppermute | solution.py:1077
  46.8 25.3 %collective-permute-start.2 = (bf16[144,4096]{1,0:T(8,128)(2,1)}, bf16[144,4096]{1,0:T(8,128)(2,1)}, u32[]{:S(2)}, u32[]{:S(2)}) collective-permute-start(bf16[144,4096]{1,0:T(8,128)(2,1)} %collective-permute-done.1.refs_2_.refs_14_), channel_id=1, source_target_pairs={{0,4},{4,0},{8,12},{12,8},{16,20},{20,16},{24,28},{28,24},{1,5},{5... | collective-permute-start | bytes 3538952 | tf_op jit(solution)/shard_map/ppermute | solution.py:1069
  46.8 25.3 %collective-permute-start.3 = (bf16[144,4096]{1,0:T(8,128)(2,1)}, bf16[144,4096]{1,0:T(8,128)(2,1)}, u32[]{:S(2)}, u32[]{:S(2)}) collective-permute-start(bf16[144,4096]{1,0:T(8,128)(2,1)} %collective-permute-done.refs_1_.refs_3_.refs_15_), channel_id=1, source_target_pairs={{0,4},{4,0},{8,12},{12,8},{16,20},{20,16},{24,28},{28,24},{1,5},{5... | collective-permute-start | bytes 3538952 | tf_op jit(solution)/shard_map/ppermute | solution.py:1069
  69.0 277.1 %reduce-scatter.2.cloned.1.call-start = ((), (), s32[]{:S(2)}) async-start(), calls=%async_computation.3 | async-start | bytes 1310720 | tf_op jit(solution)/shard_map/reduce_scatter | solution.py:1214
  165.6 31.7 %collective-permute-start.11 = (bf16[2,128,2048]{2,1,0:T(8,128)(2,1)}, bf16[2,128,2048]{2,1,0:T(8,128)(2,1)}, u32[]{:S(2)}, u32[]{:S(2)}) collective-permute-start(bf16[2,128,2048]{2,1,0:T(8,128)(2,1)} %get-tuple-element.132), channel_id=1, source_target_pairs={{0,1},{1,0},{2,3},{3,2},{4,5},{5,4},{6,7},{7,6},{8,9},{9,8},{10,11... | collective-permute-start | bytes 3145736 | tf_op jit(solution)/shard_map/ppermute | solution.py:1077
  167.0 30.3 %collective-permute-start.12 = (bf16[2,128,2048]{2,1,0:T(8,128)(2,1)}, bf16[2,128,2048]{2,1,0:T(8,128)(2,1)}, u32[]{:S(2)}, u32[]{:S(2)}) collective-permute-start(bf16[2,128,2048]{2,1,0:T(8,128)(2,1)} %get-tuple-element.133), channel_id=1, source_target_pairs={{0,2},{1,3},{2,0},{3,1},{4,6},{5,7},{6,4},{7,5},{8,10},{9,11},{10,... | collective-permute-start | bytes 3145736 | tf_op jit(solution)/shard_map/ppermute | solution.py:1077
  197.2 31.6 %collective-permute-start.15 = (bf16[2,512,2048]{2,1,0:T(8,128)(2,1)}, bf16[2,512,2048]{2,1,0:T(8,128)(2,1)}, u32[]{:S(2)}, u32[]{:S(2)}) collective-permute-start(bf16[2,512,2048]{2,1,0:T(8,128)(2,1)} %get-tuple-element.138), channel_id=1, source_target_pairs={{0,4},{4,0},{8,12},{12,8},{16,20},{20,16},{24,28},{28,24},{1,5},{5... | collective-permute-start | bytes 12582920 | tf_op jit(solution)/shard_map/ppermute | solution.py:1069
  202.1 26.6 %collective-permute-start.13 = (bf16[1,128,2048]{2,1,0:T(8,128)(2,1)}, bf16[1,128,2048]{2,1,0:T(8,128)(2,1)}, u32[]{:S(2)}, u32[]{:S(2)}) collective-permute-start(bf16[1,128,2048]{2,1,0:T(8,128)(2,1)} %get-tuple-element.136), channel_id=1, source_target_pairs={{0,2},{1,3},{2,0},{3,1},{4,6},{5,7},{6,4},{7,5},{8,10},{9,11},{10,... | collective-permute-start | bytes 1572872 | tf_op jit(solution)/shard_map/ppermute | solution.py:1077
  203.6 25.2 %collective-permute-start.14 = (bf16[1,128,2048]{2,1,0:T(8,128)(2,1)}, bf16[1,128,2048]{2,1,0:T(8,128)(2,1)}, u32[]{:S(2)}, u32[]{:S(2)}) collective-permute-start(bf16[1,128,2048]{2,1,0:T(8,128)(2,1)} %get-tuple-element.137), channel_id=1, source_target_pairs={{0,1},{1,0},{2,3},{3,2},{4,5},{5,4},{6,7},{7,6},{8,9},{9,8},{10,11... | collective-permute-start | bytes 1572872 | tf_op jit(solution)/shard_map/ppermute | solution.py:1077
  228.7 32.6 %collective-permute-start.19 = (bf16[2,512,512]{2,1,0:T(8,128)(2,1)}, bf16[2,512,512]{2,1,0:T(8,128)(2,1)}, u32[]{:S(2)}, u32[]{:S(2)}) collective-permute-start(bf16[2,512,512]{2,1,0:T(8,128)(2,1)} %get-tuple-element.147), channel_id=1, source_target_pairs={{0,4},{4,0},{8,12},{12,8},{16,20},{20,16},{24,28},{28,24},{1,5},{5... | collective-permute-start | bytes 3145736 | tf_op jit(solution)/shard_map/ppermute | solution.py:1069
  236.1 26.8 %collective-permute-start.16 = (bf16[2,128,2048]{2,1,0:T(8,128)(2,1)}, bf16[2,128,2048]{2,1,0:T(8,128)(2,1)}, u32[]{:S(2)}, u32[]{:S(2)}) collective-permute-start(bf16[2,128,2048]{2,1,0:T(8,128)(2,1)} %bitcast.39), channel_id=1, source_target_pairs={{0,8},{4,12},{24,16},{28,20},{1,9},{5,13},{25,17},{29,21},{2,10},{... | collective-permute-start | bytes 3145736 | tf_op jit(solution)/shard_map/ppermute | solution.py:1074
  240.4 25.6 %collective-permute-start.17 = (bf16[2,128,2048]{2,1,0:T(8,128)(2,1)}, bf16[2,128,2048]{2,1,0:T(8,128)(2,1)}, u32[]{:S(2)}, u32[]{:S(2)}) collective-permute-start(bf16[2,128,2048]{2,1,0:T(8,128)(2,1)} %get-tuple-element.144), channel_id=1, source_target_pairs={{0,1},{1,0},{2,3},{3,2},{4,5},{5,4},{6,7},{7,6},{8,9},{9,8},{10,11... | collective-permute-start | bytes 3145736 | tf_op jit(solution)/shard_map/ppermute | solution.py:1077
  241.9 25.3 %collective-permute-start.18 = (bf16[2,128,2048]{2,1,0:T(8,128)(2,1)}, bf16[2,128,2048]{2,1,0:T(8,128)(2,1)}, u32[]{:S(2)}, u32[]{:S(2)}) collective-permute-start(bf16[2,128,2048]{2,1,0:T(8,128)(2,1)} %get-tuple-element.145), channel_id=1, source_target_pairs={{0,2},{1,3},{2,0},{3,1},{4,6},{5,7},{6,4},{7,5},{8,10},{9,11},{10,... | collective-permute-start | bytes 3145736 | tf_op jit(solution)/shard_map/ppermute | solution.py:1077
  273.6 29.8 %collective-permute-start.20 = (bf16[2,128,2048]{2,1,0:T(8,128)(2,1)}, bf16[2,128,2048]{2,1,0:T(8,128)(2,1)}, u32[]{:S(2)}, u32[]{:S(2)}) collective-permute-start(bf16[2,128,2048]{2,1,0:T(8,128)(2,1)} %get-tuple-element.150.refs_4_.refs_1_), channel_id=1, source_target_pairs={{8,16},{12,20},{16,8},{20,12},{9,17},{13,21},{17,9},{21,13},{10,18... | collective-permute-start | bytes 3145736 | tf_op jit(solution)/shard_map/ppermute | solution.py:1074
  303.4 106.4 %all-reduce.3.cloned.1.call-start = ((), (), s32[]{:S(2)}) async-start(), calls=%async_computation.4 | async-start | bytes 2621440 | tf_op jit(solution)/shard_map/psum | solution.py:1103
  309.4 31.4 %collective-permute-start.24 = (bf16[2,128,2048]{2,1,0:T(8,128)(2,1)}, bf16[2,128,2048]{2,1,0:T(8,128)(2,1)}, u32[]{:S(2)}, u32[]{:S(2)}) collective-permute-start(bf16[2,128,2048]{2,1,0:T(8,128)(2,1)} %get-tuple-element.160.refs_4_.refs_1_), channel_id=1, source_target_pairs={{8,0},{12,4},{16,24},{20,28},{9,1},{13,5},{17,25},{21,29},{10,2},{... | collective-permute-start | bytes 3145736 | tf_op jit(solution)/shard_map/ppermute | solution.py:1074
  317.8 23.1 %collective-permute-start.26 = (bf16[2,512,768]{2,1,0:T(8,128)(2,1)}, bf16[2,512,768]{2,1,0:T(8,128)(2,1)}, u32[]{:S(2)}, u32[]{:S(2)}) collective-permute-start(bf16[2,512,768]{2,1,0:T(8,128)(2,1)} %get-tuple-element.166), channel_id=1, source_target_pairs={{0,4},{4,0},{8,12},{12,8},{16,20},{20,16},{24,28},{28,24},{1,5},{5... | collective-permute-start | bytes 4718600 | tf_op jit(solution)/shard_map/ppermute | solution.py:1069
  317.8 23.1 %collective-permute-start.25 = (bf16[2,2,128,768]{3,2,1,0:T(8,128)(2,1)}, bf16[2,2,128,768]{3,2,1,0:T(8,128)(2,1)}, u32[]{:S(2)}, u32[]{:S(2)}) collective-permute-start(bf16[2,2,128,768]{3,2,1,0:T(8,128)(2,1)} %get-tuple-element.162), channel_id=1, source_target_pairs={{0,1},{1,0},{2,3},{3,2},{4,5},{5,4},{6,7},{7,6},{8,9},{9,8},{10,11... | collective-permute-start | bytes 2359304 | tf_op jit(solution)/shard_map/ppermute | solution.py:1077
  346.1 21.4 %collective-permute-start.28 = (bf16[2,2,128,768]{3,2,1,0:T(8,128)(2,1)}, bf16[2,2,128,768]{3,2,1,0:T(8,128)(2,1)}, u32[]{:S(2)}, u32[]{:S(2)}) collective-permute-start(bf16[2,2,128,768]{3,2,1,0:T(8,128)(2,1)} %get-tuple-element.182), channel_id=1, source_target_pairs={{0,1},{1,0},{2,3},{3,2},{4,5},{5,4},{6,7},{7,6},{8,9},{9,8},{10,11... | collective-permute-start | bytes 2359304 | tf_op jit(solution)/shard_map/ppermute | solution.py:1077
  370.8 21.3 %collective-permute-start.31 = (bf16[2,128,768]{2,1,0:T(8,128)(2,1)}, bf16[2,128,768]{2,1,0:T(8,128)(2,1)}, u32[]{:S(2)}, u32[]{:S(2)}) collective-permute-start(bf16[2,128,768]{2,1,0:T(8,128)(2,1)} %bitcast.34), channel_id=1, source_target_pairs={{0,8},{4,12},{8,0},{12,4},{16,24},{20,28},{24,16},{28,20},{1,9},{5... | collective-permute-start | bytes 1179656 | tf_op jit(solution)/shard_map/ppermute | solution.py:1069
  (24 other events, 306.5 us)
Sparse Core Ops, SparseCore 0:
  46.5 57.9 all-gather.2
  106.3 52.6 all-gather.4
  303.5 29.6 reduce-scatter.1
  346.2 63.4 all-reduce.2

commit v8 on v7

--- a/solution.py
+++ b/solution.py
@@ -1506,16 +1506,16 @@
     if links.fast:
         shard_move = lambda bit: functools.partial(links.across_shard, bit=bit)
         dp_move = lambda bit: functools.partial(links.across_dp, bit=bit)
-        moved = links.across_shard(grad_small, 1)
+        moved = links.swap(grad_small)
 
         def step(units, move):
             (total,) = reduce(units, [job_add(grad_small, moved, 2)])
             return total, move(total) if move else None
 
         mlp_new = adam_mlp(0, unit_a, None)
+        grad_small, moved = step([unit_c, unit_d], shard_move(1))
+        output = output_now()
         grad_small, moved = step([unit_c, unit_d], shard_move(2))
-        output = output_now()
-        grad_small, moved = step([unit_c, unit_d], links.swap)
         unit_b.close(grad_small)
         unit_e.close(grad_small)
         mlp_new = adam_mlp(1, unit_b, mlp_new)

time: 486 us -> 487 us (level)
  no operation moved by 1% of the time
where the time goes in v8:
time: 487 us; the launch traced here: 482 us
  Pallas kernels  330 us (68%)
  waiting for transfers between devices  91 us (19%)
  starting transfers between devices  39.8 us (8%)
  between operations  14.4 us (3%)
  other arithmetic  5.61 us (1%)
    pallas_call x33, Pallas kernels, call(): pl.pallas_call(run, grid_spec=pltpu.PrefetchScalarGridSpec(num_scalar_pre...  330 us
    ppermute x18, waiting for transfers between devices, across_shard(): lax.ppermute(value, 'shard', [(s, s ^ bit) for s in range(self.shards)])  46.2 us
    ppermute x18, starting transfers between devices, across_shard(): lax.ppermute(value, 'shard', [(s, s ^ bit) for s in range(self.shards)])  20.7 us
    ppermute x23, waiting for transfers between devices, across_dp(): lax.ppermute(value, 'dp', [(d, d ^ bit) for d in range(self.replicas)])  17.9 us
    psum x1, waiting for transfers between devices, over_dp(): return lax.psum(values, 'dp', axis_index_groups=groups)  16.3 us
    ppermute x23, starting transfers between devices, across_dp(): lax.ppermute(value, 'dp', [(d, d ^ bit) for d in range(self.replicas)])  11.7 us
  transfers between devices with their start and end apart: 48, of which 15 were waited for; matrix products, arithmetic and copies ran while one was open for 1% of the time, Pallas kernels for 64%

profile of v8, /device:TPU:0, one launch (start us, length us, event | category | flops | bytes accessed | tf_op | source)
XLA Modules:
  0.0 482.2 jit_solution(6700334705069981005)
XLA Ops:
  31.3 9.2 %collective-permute-done.refs_1_.refs_3_.refs_15_ = bf16[144,4096]{1,0:T(8,128)(2,1)} collective-permute-done((bf16[144,4096]{1,0:T(8,128)(2,1)}, bf16[144,4096]{1,0:T(8,128)(2,1)}, u32[]{:S(2)}, u32[]{:S(2)}) %collective-permute-start) | collective-permute-done | bytes 1179680 | tf_op jit(solution)/shard_map/ppermute | solution.py:1077
  49.0 19.5 %collective-permute-done.5.refs_4_.refs_7_.refs_19_ = bf16[80,4096]{1,0:T(8,128)(2,1)} collective-permute-done((bf16[80,4096]{1,0:T(8,128)(2,1)}, bf16[80,4096]{1,0:T(8,128)(2,1)}, u32[]{:S(2)}, u32[]{:S(2)}) %collective-permute-start.5) | collective-permute-done | bytes 655392 | tf_op jit(solution)/shard_map/ppermute | solution.py:1077
  72.1 14.2 %qkv.1 = (bf16[1024,3072]{1,0:T(8,128)(2,1)}, bf16[1024,1024]{1,0:T(8,128)(2,1)}) custom-call(s32[9]{0:T(128)} %stack.59.refs_0_.refs_12_, bf16[256,4096]{1,0:T(8,128)(2,1)} %side.18.refs_5_.refs_1_.refs_13_, bf16[144,4096]{1,0:T(8,128)(2,1)} %collective-permute-done.1.refs_2_.refs_14_, bf16[144,4096]{1,0:T(8,128)(2,1)} %collective-permute-done.refs_1_.refs_3_.refs_15_, ...), custom_call_target="tpu_custom_call" | custom-call | flops 6442450944 | bytes 16777216 | tf_op jit(solution)/shard_map/qkv/pallas_call | solution.py:60
  86.4 22.9 %attend.1 = (bf16[1024,1024]{1,0:T(8,128)(2,1)}, f32[8,2,1024]{2,1,0:T(2,128)}) custom-call(s32[4]{0:T(128)} %bitcast.50, bf16[1024,3072]{1,0:T(8,128)(2,1)} %get-tuple-element.116.refs_1_.refs_2_.refs_3_.refs_4_, bf16[1024,3072]{1,0:T(8,128)(2,1)} %get-tuple-element.116.refs_1_.refs_2_.refs_3_.refs_4_, ...), custom_call_target="tpu_custom_call" | custom-call | flops 8589934592 | bytes 8388608 | tf_op jit(solution)/shard_map/attend/pallas_call | solution.py:60
  109.9 10.4 %after.1 = (f32[1024,1024]{1,0:T(8,128)}, bf16[1024,1024]{1,0:T(8,128)(2,1)}, bf16[1024,1024]{1,0:T(8,128)(2,1)}, bf16[1024,1024]{1,0:T(8,128)(2,1)}) custom-call(s32[9]{0:T(128)} %stack.59.refs_0_.refs_12_, bf16[256,4096]{1,0:T(8,128)(2,1)} %side.18.refs_5_.refs_1_.refs_13_, bf16[144,4096]{1,0:T(8,128)(2,1)} %collective-permute-done.1.refs_2_.refs_14_, ...), custom_call_target="tpu_custom_call" | custom-call | flops 2147483648 | bytes 14680064 | tf_op jit(solution)/shard_map/after/pallas_call | solution.py:60
  120.3 29.1 %feed.2 = (bf16[1024,4096]{1,0:T(8,128)(2,1)}, bf16[1024,4096]{1,0:T(8,128)(2,1)}, bf16[2,512,2048]{2,1,0:T(8,128)(2,1)}, bf16[2,512,2048]{2,1,0:T(8,128)(2,1)}, f32[1,2048]{1,0:T(1,128)}) custom-call(s32[8]{0:T(128)} %pad_add_fusion.refs_0_.refs_3_.refs_6_.refs_9_, bf16[512,4096]{1,0:T(8,128)(2,1)} %all-gather.3.cloned.1.call-done.refs_18_.refs_1_.refs_4_, ...), custom_call_target="tpu_custom_call" | custom-call | flops 17179869184 | bytes 50331648 | tf_op jit(solution)/shard_map/feed/pallas_call | solution.py:60
  150.1 9.0 %all-gather.5.cloned.1.call-done.refs_1_.refs_4_.refs_7_.refs_10_ = bf16[512,4096]{1,0:T(8,128)(2,1)} async-done(((bf16[128,4096]{1,0:T(8,128)(2,1)}), bf16[512,4096]{1,0:T(8,128)(2,1)}) %all-gather.5.cloned.1.call-update) | async-done | bytes 4194320 | tf_op jit(solution)/shard_map/all_gather | solution.py:1088
  159.1 6.5 %side.21 = (bf16[2,2,128,2048]{3,2,1,0:T(8,128)(2,1)}, bf16[2,128,2048]{2,1,0:T(8,128)(2,1)}, bf16[2,128,2048]{2,1,0:T(8,128)(2,1)}) custom-call(s32[3]{0:T(128)} %pad_add_fusion.1.refs_0_, bf16[2,4,128,2048]{3,2,1,0:T(8,128)(2,1)} %bitcast.33, bf16[2,4,128,2048]{3,2,1,0:T(8,128)(2,1)} %bitcast.16.refs_2_, bf16[2,512,2048]{2,1,0:T(8,128)(2,1)} %get-tuple-element.126.refs_3_), custom_call_target="tpu_custom_call" | custom-call | bytes 16777216 | tf_op jit(solution)/shard_map/side/pallas_call | solution.py:60
  167.6 29.6 %feed.3 = (bf16[1024,4096]{1,0:T(8,128)(2,1)}, bf16[1024,4096]{1,0:T(8,128)(2,1)}, bf16[2,512,2048]{2,1,0:T(8,128)(2,1)}, bf16[2,512,2048]{2,1,0:T(8,128)(2,1)}, f32[1,2048]{1,0:T(1,128)}) custom-call(s32[8]{0:T(128)} %pad_add_fusion.refs_0_.refs_3_.refs_6_.refs_9_, ...), custom_call_target="tpu_custom_call", output_to_operand_aliasing={{0}: (12, {}), {1}: (13, {})} | custom-call | flops 17179869184 | bytes 50331648 | tf_op jit(solution)/shard_map/feed/pallas_call | solution.py:60
  204.1 24.6 %middle.1 = (f32[1024,1024]{1,0:T(8,128)}, bf16[1024,1024]{1,0:T(8,128)(2,1)}, bf16[2,512,512]{2,1,0:T(8,128)(2,1)}, bf16[2,512,512]{2,1,0:T(8,128)(2,1)}, f32[1...) custom-call(s32[8]{0:T(128)} %pad_add_fusion.refs_0_.refs_3_.refs_6_.refs_9_, ...), custom_call_target="tpu_custom_call" | custom-call | flops 51539607552 | bytes 125829120 | tf_op jit(solution)/shard_map/middle/pallas_call | solution.py:60
  228.8 7.3 %side.23 = (bf16[2,1,128,2048]{3,2,1,0:T(8,128)(2,1)}, bf16[2,2,128,2048]{3,2,1,0:T(8,128)(2,1)}, bf16[2,128,2048]{2,1,0:T(8,128)(2,1)}, bf16[2,128,2048]{2,1,0:T(8,128)(2,1)}) custom-call(s32[3]{0:T(128)} %pad_add_fusion.1.refs_0_, bf16[2,1,128,2048]{3,2,1,0:T(8,128)(2,1)} %get-tuple-element.135.refs_27_.refs_1_, ...), custom_call_target="tpu_custom_call" | custom-call | bytes 20971520 | tf_op jit(solution)/shard_map/side/pallas_call | solution.py:60
  242.5 18.8 %attend_back.2 = (bf16[1024,512]{1,0:T(8,128)(2,1)}, bf16[1024,512]{1,0:T(8,128)(2,1)}, bf16[1024,512]{1,0:T(8,128)(2,1)}, f32[1,512]{1,0:T(1,128)}, f32[1,512]{1,0:T(1,128)}) custom-call(s32[4]{0:T(128)} %bitcast.51, bf16[1024,3072]{1,0:T(8,128)(2,1)} %get-tuple-element.116.refs_1_.refs_2_.refs_3_.refs_4_, ...), custom_call_target="tpu_custom_call" | custom-call | flops 42949672960 | bytes 524288 | tf_op jit(solution)/shard_map/attend_back/pallas_call | solution.py:60
  275.3 7.1 %project.2 = (bf16[2,512,768]{2,1,0:T(8,128)(2,1)}, bf16[2,512,768]{2,1,0:T(8,128)(2,1)}) custom-call(bf16[1024,1024]{1,0:T(8,128)(2,1)} %get-tuple-element.154.refs_0_, bf16[1024,512]{1,0:T(8,128)(2,1)} %get-tuple-element.149.refs_8_.refs_1_.refs_10_, bf16[1024,512]{1,0:T(8,128)(2,1)} %get-tuple-element.155.refs_2_.refs_11_, ...), custom_call_target="tpu_custom_call" | custom-call | flops 3221225472 | bytes 7340032 | tf_op jit(solution)/shard_map/project/pallas_call | solution.py:60
  284.3 19.0 %attend_back.3 = (bf16[1024,512]{1,0:T(8,128)(2,1)}, bf16[1024,512]{1,0:T(8,128)(2,1)}, bf16[1024,512]{1,0:T(8,128)(2,1)}, f32[1,512]{1,0:T(1,128)}, f32[1,512]{1,0:T(1,128)}) custom-call(s32[4]{0:T(128)} %bitcast.52, bf16[1024,3072]{1,0:T(8,128)(2,1)} %get-tuple-element.116.refs_1_.refs_2_.refs_3_.refs_4_, ...), custom_call_target="tpu_custom_call" | custom-call | flops 42949672960 | bytes 524288 | tf_op jit(solution)/shard_map/attend_back/pallas_call | solution.py:60
  310.7 7.1 %project.3 = (bf16[2,512,768]{2,1,0:T(8,128)(2,1)}, bf16[2,512,768]{2,1,0:T(8,128)(2,1)}) custom-call(bf16[1024,1024]{1,0:T(8,128)(2,1)} %get-tuple-element.154.refs_0_, bf16[1024,512]{1,0:T(8,128)(2,1)} %get-tuple-element.159.refs_8_.refs_1_.refs_13_, bf16[1024,512]{1,0:T(8,128)(2,1)} %get-tuple-element.163.refs_2_.refs_14_, ...), custom_call_target="tpu_custom_call" | custom-call | flops 3221225472 | bytes 7340032 | tf_op jit(solution)/shard_map/project/pallas_call | solution.py:60
  318.3 15.9 %grad_input.1 = (f32[1024,1024]{1,0:T(8,128)}, f32[1,1024]{1,0:T(1,128)}, f32[1,1024]{1,0:T(1,128)}) custom-call(s32[9]{0:T(128)} %stack.59.refs_0_.refs_12_, bf16[256,4096]{1,0:T(8,128)(2,1)} %side.18.refs_5_.refs_1_.refs_13_, bf16[144,4096]{1,0:T(8,128)(2,1)} %collective-permute-done.1.refs_2_.refs_14_, ...), custom_call_target="tpu_custom_call" | custom-call | flops 25769803776 | bytes 92274688 | tf_op jit(solution)/shard_map/grad_input/pallas_call | solution.py:60
  334.2 6.7 %collective-permute-done.25.refs_4_ = bf16[2,2,128,768]{3,2,1,0:T(8,128)(2,1)} collective-permute-done((bf16[2,2,128,768]{3,2,1,0:T(8,128)(2,1)}, bf16[2,2,128,768]{3,2,1,0:T(8,128)(2,1)}, u32[]{:S(2)}, u32[]{:S(2)}) %collective-permute-start.25) | collective-permute-done | bytes 786464 | tf_op jit(solution)/shard_map/ppermute | solution.py:1077
  349.1 12.4 %adam.4 = (f32[256,8192]{1,0:T(8,128)}, f32[256,8192]{1,0:T(8,128)}, f32[256,8192]{1,0:T(8,128)}) custom-call(s32[3]{0:T(128)} %pad_add_fusion.1.refs_0_, s32[2]{0:T(128)} %iota_multiply_fusion.2.refs_1_, f32[256,8192]{1,0:T(8,128)} %refs_2_.9, f32[256,8192]{1,0:T(8,128)} %refs_3_.7, f32[256,8192]{1,0:T(8,128)} %refs_4_.7, ...), custom_call_target="tpu_custom_call" | custom-call | flops 2097152 | bytes 2097152 | tf_op jit(solution)/shard_map/adam/pallas_call | solution.py:60
  375.7 15.4 %output.1.refs_7_ = bf16[1024,1024]{1,0:T(8,128)(2,1)} custom-call(s32[8]{0:T(128)} %pad_add_fusion.refs_0_.refs_3_.refs_6_.refs_9_, bf16[512,4096]{1,0:T(8,128)(2,1)} %all-gather.3.cloned.1.call-done.refs_18_.refs_1_.refs_4_, bf16[512,4096]{1,0:T(8,128)(2,1)} %collective-permute-done.8.refs_2_.refs_5_, s32[8]{0:T(128)} %pad_add_fusion.refs_0_.refs_3_.refs_6_.refs_9_, ...), custom_call_target="tpu_custom_call" | custom-call | flops 858993472 | bytes 2097152 | tf_op jit(solution)/shard_map/output/pallas_call | solution.py:60
  394.1 16.3 %all-reduce.3.cloned.1.call-done = (bf16[2,128,2048]{2,1,0:T(8,128)(2,1)}, bf16[2,128,512]{2,1,0:T(8,128)(2,1)}) async-done(((bf16[2,128,2048]{2,1,0:T(8,128)(2,1)}, bf16[2,128,512]{2,1,0:T(8,128)(2,1)}), (bf16[2,128,2048]{2,1,0:T(8,128)(2,1)}, bf16[2,128,512]{2,1,0:T(8,128)(2,1)})) %all-reduce.3.cloned.1.call-update) | async-done | bytes 1310736 | tf_op jit(solution)/shard_map/psum | solution.py:1103
  414.5 12.4 %adam.5 = (f32[256,8192]{1,0:T(8,128)}, f32[256,8192]{1,0:T(8,128)}, f32[256,8192]{1,0:T(8,128)}) custom-call(s32[3]{0:T(128)} %pad_add_fusion.1.refs_0_, s32[2]{0:T(128)} %constant.88.clone.refs_1_, f32[256,8192]{1,0:T(8,128)} %refs_2_.9, f32[256,8192]{1,0:T(8,128)} %refs_3_.7, ...), custom_call_target="tpu_custom_call", output_to_operand_aliasing={{0}: (8, {}), {1}: (9, {}), {2}: (10, {})} | custom-call | flops 2097152 | bytes 2097152 | tf_op jit(solution)/shard_map/adam/pallas_call | solution.py:60
  437.9 7.0 %adam.6 = (f32[256,4096]{1,0:T(8,128)}, f32[256,4096]{1,0:T(8,128)}, f32[256,4096]{1,0:T(8,128)}) custom-call(s32[3]{0:T(128)} %pad_add_fusion.1.refs_0_, s32[3]{0:T(128)} %iota_multiply_fusion.1.refs_1_, f32[256,4096]{1,0:T(8,128)} %refs_2_.11, f32[256,4096]{1,0:T(8,128)} %refs_3_.9, f32[256,4096]{1,0:T(8,128)} %refs_4_.9, ...), custom_call_target="tpu_custom_call" | custom-call | flops 786432 | bytes 786432 | tf_op jit(solution)/shard_map/adam/pallas_call | solution.py:60
  446.6 9.2 %collective-permute-done.38.refs_2_ = bf16[2,128,768]{2,1,0:T(8,128)(2,1)} collective-permute-done((bf16[2,128,768]{2,1,0:T(8,128)(2,1)}, bf16[2,128,768]{2,1,0:T(8,128)(2,1)}, u32[]{:S(2)}, u32[]{:S(2)}) %collective-permute-start.38) | collective-permute-done | bytes 393248 | tf_op jit(solution)/shard_map/ppermute | solution.py:1069
  461.0 10.2 %adam.7 = (f32[256,4096]{1,0:T(8,128)}, f32[256,4096]{1,0:T(8,128)}, f32[256,4096]{1,0:T(8,128)}) custom-call(s32[3]{0:T(128)} %pad_add_fusion.1.refs_0_, s32[5]{0:T(128)} %constant.89.clone.refs_1_, f32[256,4096]{1,0:T(8,128)} %refs_2_.11, f32[256,4096]{1,0:T(8,128)} %refs_3_.9, ...), custom_call_target="tpu_custom_call", output_to_operand_aliasing={{0}: (10, {}), {1}: (11, {}), {2}: (12, {})} | custom-call | flops 1310720 | bytes 1310720 | tf_op jit(solution)/shard_map/adam/pallas_call | solution.py:60
  (119 shorter events, 128.1 us)
Async XLA Ops:
  7.2 102.1 %all-gather.3.cloned.1.call-start = ((), (), s32[]{:S(2)}) async-start(), calls=%async_computation.1 | async-start | bytes 5242880 | tf_op jit(solution)/shard_map/all_gather | solution.py:1088
  11.3 29.2 %collective-permute-start = (bf16[144,4096]{1,0:T(8,128)(2,1)}, bf16[144,4096]{1,0:T(8,128)(2,1)}, u32[]{:S(2)}, u32[]{:S(2)}) collective-permute-start(bf16[144,4096]{1,0:T(8,128)(2,1)} %side.16.refs_3_), channel_id=1, source_target_pairs={{0,2},{1,3},{2,0},{3,1},{4,6},{5,7},{6,4},{7,5},{8,10},{9,11},{10,... | collective-permute-start | bytes 3538952 | tf_op jit(solution)/shard_map/ppermute | solution.py:1077
  14.3 27.7 %collective-permute-start.1 = (bf16[144,4096]{1,0:T(8,128)(2,1)}, bf16[144,4096]{1,0:T(8,128)(2,1)}, u32[]{:S(2)}, u32[]{:S(2)}) collective-permute-start(bf16[144,4096]{1,0:T(8,128)(2,1)} %side.16.refs_3_), channel_id=1, source_target_pairs={{0,1},{1,0},{2,3},{3,2},{4,5},{5,4},{6,7},{7,6},{8,9},{9,8},{10,11... | collective-permute-start | bytes 3538952 | tf_op jit(solution)/shard_map/ppermute | solution.py:1077
  46.3 112.7 %all-gather.5.cloned.1.call-start = ((), (), s32[]{:S(2)}) async-start(), calls=%async_computation.2 | async-start | bytes 5242880 | tf_op jit(solution)/shard_map/all_gather | solution.py:1088
  46.4 22.1 %collective-permute-start.5 = (bf16[80,4096]{1,0:T(8,128)(2,1)}, bf16[80,4096]{1,0:T(8,128)(2,1)}, u32[]{:S(2)}, u32[]{:S(2)}) collective-permute-start(bf16[80,4096]{1,0:T(8,128)(2,1)} %get-tuple-element.115), channel_id=1, source_target_pairs={{0,2},{1,3},{2,0},{3,1},{4,6},{5,7},{6,4},{7,5},{8,10},{9,11},{10,... | collective-permute-start | bytes 1966088 | tf_op jit(solution)/shard_map/ppermute | solution.py:1077
  46.8 25.3 %collective-permute-start.2 = (bf16[144,4096]{1,0:T(8,128)(2,1)}, bf16[144,4096]{1,0:T(8,128)(2,1)}, u32[]{:S(2)}, u32[]{:S(2)}) collective-permute-start(bf16[144,4096]{1,0:T(8,128)(2,1)} %collective-permute-done.1.refs_2_.refs_14_), channel_id=1, source_target_pairs={{0,4},{4,0},{8,12},{12,8},{16,20},{20,16},{24,28},{28,24},{1,5},{5... | collective-permute-start | bytes 3538952 | tf_op jit(solution)/shard_map/ppermute | solution.py:1069
  46.8 25.3 %collective-permute-start.3 = (bf16[144,4096]{1,0:T(8,128)(2,1)}, bf16[144,4096]{1,0:T(8,128)(2,1)}, u32[]{:S(2)}, u32[]{:S(2)}) collective-permute-start(bf16[144,4096]{1,0:T(8,128)(2,1)} %collective-permute-done.refs_1_.refs_3_.refs_15_), channel_id=1, source_target_pairs={{0,4},{4,0},{8,12},{12,8},{16,20},{20,16},{24,28},{28,24},{1,5},{5... | collective-permute-start | bytes 3538952 | tf_op jit(solution)/shard_map/ppermute | solution.py:1069
  47.3 21.2 %collective-permute-start.4 = (bf16[64,4096]{1,0:T(8,128)(2,1)}, bf16[64,4096]{1,0:T(8,128)(2,1)}, u32[]{:S(2)}, u32[]{:S(2)}) collective-permute-start(bf16[64,4096]{1,0:T(8,128)(2,1)} %get-tuple-element.114.refs_5_), channel_id=1, source_target_pairs={{0,1},{1,0},{2,3},{3,2},{4,5},{5,4},{6,7},{7,6},{8,9},{9,8},{10,11... | collective-permute-start | bytes 1572872 | tf_op jit(solution)/shard_map/ppermute | solution.py:1077
  69.0 277.1 %reduce-scatter.2.cloned.1.call-start = ((), (), s32[]{:S(2)}) async-start(), calls=%async_computation.3 | async-start | bytes 1310720 | tf_op jit(solution)/shard_map/reduce_scatter | solution.py:1214
  165.6 31.7 %collective-permute-start.11 = (bf16[2,128,2048]{2,1,0:T(8,128)(2,1)}, bf16[2,128,2048]{2,1,0:T(8,128)(2,1)}, u32[]{:S(2)}, u32[]{:S(2)}) collective-permute-start(bf16[2,128,2048]{2,1,0:T(8,128)(2,1)} %get-tuple-element.132), channel_id=1, source_target_pairs={{0,1},{1,0},{2,3},{3,2},{4,5},{5,4},{6,7},{7,6},{8,9},{9,8},{10,11... | collective-permute-start | bytes 3145736 | tf_op jit(solution)/shard_map/ppermute | solution.py:1077
  167.0 30.3 %collective-permute-start.12 = (bf16[2,128,2048]{2,1,0:T(8,128)(2,1)}, bf16[2,128,2048]{2,1,0:T(8,128)(2,1)}, u32[]{:S(2)}, u32[]{:S(2)}) collective-permute-start(bf16[2,128,2048]{2,1,0:T(8,128)(2,1)} %get-tuple-element.133), channel_id=1, source_target_pairs={{0,2},{1,3},{2,0},{3,1},{4,6},{5,7},{6,4},{7,5},{8,10},{9,11},{10,... | collective-permute-start | bytes 3145736 | tf_op jit(solution)/shard_map/ppermute | solution.py:1077
  197.2 31.6 %collective-permute-start.15 = (bf16[2,512,2048]{2,1,0:T(8,128)(2,1)}, bf16[2,512,2048]{2,1,0:T(8,128)(2,1)}, u32[]{:S(2)}, u32[]{:S(2)}) collective-permute-start(bf16[2,512,2048]{2,1,0:T(8,128)(2,1)} %get-tuple-element.138), channel_id=1, source_target_pairs={{0,4},{4,0},{8,12},{12,8},{16,20},{20,16},{24,28},{28,24},{1,5},{5... | collective-permute-start | bytes 12582920 | tf_op jit(solution)/shard_map/ppermute | solution.py:1069
  202.1 26.6 %collective-permute-start.13 = (bf16[1,128,2048]{2,1,0:T(8,128)(2,1)}, bf16[1,128,2048]{2,1,0:T(8,128)(2,1)}, u32[]{:S(2)}, u32[]{:S(2)}) collective-permute-start(bf16[1,128,2048]{2,1,0:T(8,128)(2,1)} %get-tuple-element.136), channel_id=1, source_target_pairs={{0,2},{1,3},{2,0},{3,1},{4,6},{5,7},{6,4},{7,5},{8,10},{9,11},{10,... | collective-permute-start | bytes 1572872 | tf_op jit(solution)/shard_map/ppermute | solution.py:1077
  203.6 25.2 %collective-permute-start.14 = (bf16[1,128,2048]{2,1,0:T(8,128)(2,1)}, bf16[1,128,2048]{2,1,0:T(8,128)(2,1)}, u32[]{:S(2)}, u32[]{:S(2)}) collective-permute-start(bf16[1,128,2048]{2,1,0:T(8,128)(2,1)} %get-tuple-element.137), channel_id=1, source_target_pairs={{0,1},{1,0},{2,3},{3,2},{4,5},{5,4},{6,7},{7,6},{8,9},{9,8},{10,11... | collective-permute-start | bytes 1572872 | tf_op jit(solution)/shard_map/ppermute | solution.py:1077
  228.7 32.6 %collective-permute-start.19 = (bf16[2,512,512]{2,1,0:T(8,128)(2,1)}, bf16[2,512,512]{2,1,0:T(8,128)(2,1)}, u32[]{:S(2)}, u32[]{:S(2)}) collective-permute-start(bf16[2,512,512]{2,1,0:T(8,128)(2,1)} %get-tuple-element.147), channel_id=1, source_target_pairs={{0,4},{4,0},{8,12},{12,8},{16,20},{20,16},{24,28},{28,24},{1,5},{5... | collective-permute-start | bytes 3145736 | tf_op jit(solution)/shard_map/ppermute | solution.py:1069
  236.1 26.8 %collective-permute-start.16 = (bf16[2,128,2048]{2,1,0:T(8,128)(2,1)}, bf16[2,128,2048]{2,1,0:T(8,128)(2,1)}, u32[]{:S(2)}, u32[]{:S(2)}) collective-permute-start(bf16[2,128,2048]{2,1,0:T(8,128)(2,1)} %bitcast.39), channel_id=1, source_target_pairs={{0,8},{4,12},{24,16},{28,20},{1,9},{5,13},{25,17},{29,21},{2,10},{... | collective-permute-start | bytes 3145736 | tf_op jit(solution)/shard_map/ppermute | solution.py:1074
  240.4 25.6 %collective-permute-start.17 = (bf16[2,128,2048]{2,1,0:T(8,128)(2,1)}, bf16[2,128,2048]{2,1,0:T(8,128)(2,1)}, u32[]{:S(2)}, u32[]{:S(2)}) collective-permute-start(bf16[2,128,2048]{2,1,0:T(8,128)(2,1)} %get-tuple-element.144), channel_id=1, source_target_pairs={{0,1},{1,0},{2,3},{3,2},{4,5},{5,4},{6,7},{7,6},{8,9},{9,8},{10,11... | collective-permute-start | bytes 3145736 | tf_op jit(solution)/shard_map/ppermute | solution.py:1077
  241.9 25.3 %collective-permute-start.18 = (bf16[2,128,2048]{2,1,0:T(8,128)(2,1)}, bf16[2,128,2048]{2,1,0:T(8,128)(2,1)}, u32[]{:S(2)}, u32[]{:S(2)}) collective-permute-start(bf16[2,128,2048]{2,1,0:T(8,128)(2,1)} %get-tuple-element.145), channel_id=1, source_target_pairs={{0,2},{1,3},{2,0},{3,1},{4,6},{5,7},{6,4},{7,5},{8,10},{9,11},{10,... | collective-permute-start | bytes 3145736 | tf_op jit(solution)/shard_map/ppermute | solution.py:1077
  273.6 29.8 %collective-permute-start.20 = (bf16[2,128,2048]{2,1,0:T(8,128)(2,1)}, bf16[2,128,2048]{2,1,0:T(8,128)(2,1)}, u32[]{:S(2)}, u32[]{:S(2)}) collective-permute-start(bf16[2,128,2048]{2,1,0:T(8,128)(2,1)} %get-tuple-element.150.refs_4_.refs_1_), channel_id=1, source_target_pairs={{8,16},{12,20},{16,8},{20,12},{9,17},{13,21},{17,9},{21,13},{10,18... | collective-permute-start | bytes 3145736 | tf_op jit(solution)/shard_map/ppermute | solution.py:1074
  303.4 107.0 %all-reduce.3.cloned.1.call-start = ((), (), s32[]{:S(2)}) async-start(), calls=%async_computation.4 | async-start | bytes 2621440 | tf_op jit(solution)/shard_map/psum | solution.py:1103
  309.4 31.4 %collective-permute-start.24 = (bf16[2,128,2048]{2,1,0:T(8,128)(2,1)}, bf16[2,128,2048]{2,1,0:T(8,128)(2,1)}, u32[]{:S(2)}, u32[]{:S(2)}) collective-permute-start(bf16[2,128,2048]{2,1,0:T(8,128)(2,1)} %get-tuple-element.160.refs_4_.refs_1_), channel_id=1, source_target_pairs={{8,0},{12,4},{16,24},{20,28},{9,1},{13,5},{17,25},{21,29},{10,2},{... | collective-permute-start | bytes 3145736 | tf_op jit(solution)/shard_map/ppermute | solution.py:1074
  317.8 23.1 %collective-permute-start.26 = (bf16[2,512,768]{2,1,0:T(8,128)(2,1)}, bf16[2,512,768]{2,1,0:T(8,128)(2,1)}, u32[]{:S(2)}, u32[]{:S(2)}) collective-permute-start(bf16[2,512,768]{2,1,0:T(8,128)(2,1)} %get-tuple-element.166), channel_id=1, source_target_pairs={{0,4},{4,0},{8,12},{12,8},{16,20},{20,16},{24,28},{28,24},{1,5},{5... | collective-permute-start | bytes 4718600 | tf_op jit(solution)/shard_map/ppermute | solution.py:1069
  317.8 23.1 %collective-permute-start.25 = (bf16[2,2,128,768]{3,2,1,0:T(8,128)(2,1)}, bf16[2,2,128,768]{3,2,1,0:T(8,128)(2,1)}, u32[]{:S(2)}, u32[]{:S(2)}) collective-permute-start(bf16[2,2,128,768]{3,2,1,0:T(8,128)(2,1)} %get-tuple-element.162), channel_id=1, source_target_pairs={{0,1},{1,0},{2,3},{3,2},{4,5},{5,4},{6,7},{7,6},{8,9},{9,8},{10,11... | collective-permute-start | bytes 2359304 | tf_op jit(solution)/shard_map/ppermute | solution.py:1077
  369.8 21.3 %collective-permute-start.31 = (bf16[2,128,768]{2,1,0:T(8,128)(2,1)}, bf16[2,128,768]{2,1,0:T(8,128)(2,1)}, u32[]{:S(2)}, u32[]{:S(2)}) collective-permute-start(bf16[2,128,768]{2,1,0:T(8,128)(2,1)} %bitcast.34), channel_id=1, source_target_pairs={{0,8},{4,12},{8,0},{12,4},{16,24},{20,28},{24,16},{28,20},{1,9},{5... | collective-permute-start | bytes 1179656 | tf_op jit(solution)/shard_map/ppermute | solution.py:1069
  (24 other events, 295.3 us)
Sparse Core Ops, SparseCore 0:
  46.5 57.9 all-gather.2
  106.3 52.6 all-gather.4
  303.5 29.6 reduce-scatter.1
  346.2 64.1 all-reduce.2
